TPU v7x, 32 devices: a whole 2x2x4 slice. The times are simulated.
32 devices in a mesh: dp: 16 (over z, x, core), tensor: 2 (over y).
Axes of the slice: x: 2, y: 2, z: 4, core: 2. Of those that a mesh axis runs over, the one named last changes fastest.
Arguments:
- hidden: bfloat16 [32, 1024, 1024], P('dp'), may hold values from -6 to 6
- segment_ids: int32 [32, 1024], P('dp'), may hold values from 0 to 3, never falling along the last dimension, each value on 1 to 800 neighbouring positions
- norm_gain: float32 [1024], replicated, may hold values from 0.1 to 1.9
- proj_gate: bfloat16 [1024, 2048], P(None, 'tensor'), may hold values from -0.1875 to 0.1875
- proj_value: bfloat16 [1024, 2048], P(None, 'tensor'), may hold values from -0.1875 to 0.1875
- proj_state: bfloat16 [1024, 256], replicated, may hold values from -0.1875 to 0.1875
- proj_step: bfloat16 [1024, 32], P(None, 'tensor'), may hold values from -0.1875 to 0.1875
- conv_value: float32 [4, 2048], P(None, 'tensor'), may hold values from -3 to 3
- conv_value_bias: float32 [2048], P('tensor'), may hold values from -3 to 3
- conv_state: float32 [4, 256], replicated, may hold values from -3 to 3
- conv_state_bias: float32 [256], replicated, may hold values from -3 to 3
- step_bias: float32 [32], P('tensor'), may hold values from -6 to -2
- decay_log: float32 [32], P('tensor'), may hold values from 0 to 2.77
- skip_gain: float32 [32], P('tensor'), may hold values from 0.5 to 1.5
- gate_gain: float32 [2048], P('tensor'), may hold values from 0.1 to 1.9
- proj_out: bfloat16 [1024, 2048], P(None, 'tensor'), may hold values from -0.125 to 0.125
- out_grad: bfloat16 [32, 1024, 1024], P('dp'), may hold values from -6 to 6
Outputs:
- block_out: bfloat16 [32, 1024, 1024], P('dp')
- grad_hidden: float32 [32, 1024, 1024], P('dp')
- grad_norm_gain: float32 [1024], replicated
- grad_proj_gate: float32 [1024, 2048], P('dp', 'tensor')
- grad_proj_value: float32 [1024, 2048], P('dp', 'tensor')
- grad_proj_state: float32 [1024, 256], P('dp')
- grad_proj_step: float32 [1024, 32], P('dp', 'tensor')
- grad_conv_value: float32 [4, 2048], P(None, 'tensor')
- grad_conv_value_bias: float32 [2048], P('tensor')
- grad_conv_state: float32 [4, 256], replicated
- grad_conv_state_bias: float32 [256], replicated
- grad_step_bias: float32 [32], P('tensor')
- grad_decay_log: float32 [32], P('tensor')
- grad_skip_gain: float32 [32], P('tensor')
- grad_gate_gain: float32 [2048], P('tensor')
- grad_proj_out: float32 [1024, 2048], P('dp', 'tensor')
Inputs may be any that keep to these rules, and one draw needn't show every extreme that they name: `segment_ids`: tokens of a sequence with the same number form one document; numbers never fall along a sequence; each sequence holds 4 documents of 1 to 800 tokens, one of exactly 800.
All inputs are finite; a program needn't handle non-finite values.
Results may differ from a plain program's by a relative error of at most 0.019.
Values sent between devices are 32-bit elements; how exact they have to be, the bound alone decides.
A program may use at most 192 MiB of HBM per device.

v0:
```python
import functools

import jax
import jax.numpy as jnp
from jax import lax
from jax.sharding import PartitionSpec as P

HEAD_DIM = 64
STATE = 128
KERNEL = 4


epsilon = 1e-05
precise = lax.Precision.HIGHEST


def lag_masks(segment_row):
    length = segment_row.shape[0]
    result = [jnp.ones((length,), jnp.float32)]
    for delay in range(1, KERNEL):
        earlier = jnp.concatenate(
            [jnp.full((delay,), -1, jnp.int32), segment_row[: length - delay]]
        )
        result.append((earlier == segment_row).astype(jnp.float32))
    return result


def causal_conv(values, weight, conv_bias, doc_masks):
    length = values.shape[0]
    summed = conv_bias[None, :] + weight[KERNEL - 1][None, :] * values
    for delay in range(1, KERNEL):
        earlier = jnp.concatenate(
            [jnp.zeros((delay, values.shape[1]), jnp.float32), values[: length - delay]], axis=0
        )
        summed = summed + weight[KERNEL - 1 - delay][None, :] * earlier * doc_masks[delay][:, None]
    return jax.nn.silu(summed)


CHUNK = 128


def head_mix(values, states, step_raw, segment_row, step_bias, decay_log, skip_gain):
    length, inner = values.shape
    heads = step_raw.shape[1]
    chunks = length // CHUNK
    step_size = jax.nn.softplus(step_raw + step_bias[None, :])
    decay_rate = -jnp.exp(decay_log)
    places = jnp.arange(CHUNK)
    lower = places[:, None] >= places[None, :]
    drop = (step_size * decay_rate[None, :]).reshape(chunks, CHUNK, heads)
    running = jnp.einsum("ts,csh->cth", lower.astype(jnp.float32), drop, precision=precise)
    segments = segment_row.reshape(chunks, CHUNK)
    last = segments[:, -1]
    before = jnp.concatenate([jnp.full((1,), -1, jnp.int32), last[:-1]])
    allowed = lower[None] & (segments[:, :, None] == segments[:, None, :])
    state_in = states[:, :STATE].astype(jnp.bfloat16).reshape(chunks, CHUNK, STATE)
    state_out = states[:, STATE:].astype(jnp.bfloat16).reshape(chunks, CHUNK, STATE)
    affinity = jnp.einsum("ctn,csn->cts", state_out, state_in, preferred_element_type=jnp.float32)
    running_head = running.transpose(0, 2, 1)
    step_head = step_size.reshape(chunks, CHUNK, heads).transpose(0, 2, 1)
    decays = jnp.exp(
        jnp.where(
            allowed[:, None], running_head[:, :, :, None] - running_head[:, :, None, :], -1e30
        )
    )
    mixing = (decays * affinity[:, None] * step_head[:, :, None, :]).astype(jnp.bfloat16)
    low_head = values.astype(jnp.bfloat16).reshape(chunks, CHUNK, heads, HEAD_DIM)
    near = jnp.einsum("chts,cshp->cthp", mixing, low_head, preferred_element_type=jnp.float32)
    near = near.reshape(chunks, CHUNK, inner)

    spread = (jnp.arange(inner)[None, :] // HEAD_DIM == jnp.arange(heads)[:, None]).astype(
        jnp.float32
    )
    total = running[:, -1, :]
    at_end = (segments == last[:, None]).astype(jnp.float32)
    from_start = (segments == before[:, None]).astype(jnp.float32)
    keep_scale = (
        jnp.exp(total[:, None, :] - running)
        * step_size.reshape(chunks, CHUNK, heads)
        * at_end[:, :, None]
    )
    read_scale = jnp.exp(running) * from_start[:, :, None]
    carry = jnp.exp(total) * (last == before).astype(jnp.float32)[:, None]
    keep_wide = jnp.einsum("cth,hi->cti", keep_scale, spread, precision=lax.Precision.HIGH)
    read_wide = jnp.einsum("cth,hi->cti", read_scale, spread, precision=lax.Precision.HIGH)
    carry_wide = jnp.einsum("ch,hi->ci", carry, spread, precision=precise)
    kept = (values.reshape(chunks, CHUNK, inner) * keep_wide).astype(jnp.bfloat16)
    gained = jnp.einsum("csn,csi->cni", state_in, kept, preferred_element_type=jnp.float32)
    held = jnp.zeros((STATE, inner), jnp.float32)
    entry = []
    for c in range(chunks):
        entry.append(held.astype(jnp.bfloat16))
        held = held * carry_wide[c][None, :] + gained[c]
    entry = jnp.stack(entry)
    far = jnp.einsum("ctn,cni->cti", state_out, entry, preferred_element_type=jnp.float32)
    mixed = (near + far * read_wide).reshape(length, inner)
    return mixed + jnp.repeat(skip_gain, HEAD_DIM)[None, :] * values


def mixer(
    segment_row,
    value_row,
    state_row,
    step_row,
    conv_value,
    conv_value_bias,
    conv_state,
    conv_state_bias,
    step_bias,
    decay_log,
    skip_gain,
):
    doc_masks = lag_masks(segment_row)
    value_conv = causal_conv(value_row, conv_value, conv_value_bias, doc_masks)
    state_conv = causal_conv(state_row, conv_state, conv_state_bias, doc_masks)
    return head_mix(value_conv, state_conv, step_row, segment_row, step_bias, decay_log, skip_gain)


def right_product(left, weight):
    return lax.dot_general(
        left, weight, (((1,), (1,)), ((), ())), preferred_element_type=jnp.float32
    )


def token_product(left, right):
    return lax.dot_general(
        left, right, (((0,), (0,)), ((), ())), preferred_element_type=jnp.float32
    )


def tensor_others(part):
    count = lax.axis_size("tensor")
    if count == 2:
        return lax.ppermute(part, "tensor", [(0, 1), (1, 0)])
    return lax.psum(part, "tensor")


def tensor_join(part, others):
    return part + others if lax.axis_size("tensor") == 2 else others


def after(value, *earlier):
    return lax.optimization_barrier((value, *earlier))[0]


def local(
    hidden,
    segment_ids,
    norm_gain,
    proj_gate,
    proj_value,
    proj_state,
    proj_step,
    conv_value,
    conv_value_bias,
    conv_state,
    conv_state_bias,
    step_bias,
    decay_log,
    skip_gain,
    gate_gain,
    proj_out,
    out_grad,
):
    seq_count, length, width = hidden.shape
    local_inner = proj_gate.shape[1]
    local_heads = proj_step.shape[1]
    state_width = proj_state.shape[1]
    tensor_count = lax.axis_size("tensor")
    inner_total = local_inner * tensor_count
    every = range(seq_count)

    wides = [hidden[s].astype(jnp.float32) for s in every]
    row_scales = [
        lax.rsqrt(jnp.mean(w * w, axis=-1, keepdims=True) + epsilon) for w in wides
    ]
    normeds = [
        (w * r * norm_gain[None, :]).astype(jnp.bfloat16) for w, r in zip(wides, row_scales)
    ]
    params = (
        conv_value,
        conv_value_bias,
        conv_state,
        conv_state_bias,
        step_bias,
        decay_log,
        skip_gain,
    )
    gate_raws, mixed_outs, mixer_backs, gateds, squares = [], [], [], [], []
    for s in every:
        gate_raw = jnp.dot(normeds[s], proj_gate, preferred_element_type=jnp.float32)
        value_raw = jnp.dot(normeds[s], proj_value, preferred_element_type=jnp.float32)
        state_raw = jnp.dot(normeds[s], proj_state, preferred_element_type=jnp.float32)
        step_raw = jnp.dot(normeds[s], proj_step, preferred_element_type=jnp.float32)
        mixed_out, back = jax.vjp(
            jax.checkpoint(functools.partial(mixer, segment_ids[s])),
            value_raw,
            state_raw,
            step_raw,
            *params,
        )
        gated = mixed_out * jax.nn.silu(gate_raw)
        gate_raws.append(gate_raw)
        mixed_outs.append(mixed_out)
        mixer_backs.append(back)
        gateds.append(gated)
        squares.append(jnp.sum(gated * gated, axis=-1))

    d_output_ins = [
        jnp.dot(out_grad[s], proj_out, preferred_element_type=jnp.float32) for s in every
    ]
    inners = [
        jnp.sum(d_output_ins[s] * gate_gain[None, :] * gateds[s], axis=-1) for s in every
    ]
    both = lax.psum(jnp.stack(squares + inners), "tensor")
    branches, received, output_ins, d_gates, d_mixeds = [], [], [], [], []
    grad_gate_gain = jnp.zeros((local_inner,), jnp.float32)
    for s in every:
        gated, gate_raw = gateds[s], gate_raws[s]
        gated_scale = lax.rsqrt(both[s] / inner_total + epsilon)[:, None]
        gate_inner = both[seq_count + s][:, None]
        output_in = (gated * gated_scale * gate_gain[None, :]).astype(jnp.bfloat16)
        branches.append(right_product(output_in, proj_out))
        received.append(tensor_others(branches[s]))
        d_output_in = d_output_ins[s]
        grad_gate_gain = grad_gate_gain + jnp.sum(d_output_in * gated * gated_scale, axis=0)
        weighted = d_output_in * gate_gain[None, :]
        d_gated = gated_scale * weighted - gated_scale**3 * gated * gate_inner / inner_total
        sigma = jax.nn.sigmoid(gate_raw)
        d_mixeds.append(d_gated * gate_raw * sigma)
        d_gates.append(
            (d_gated * mixed_outs[s] * sigma * (1.0 + gate_raw * (1.0 - sigma))).astype(
                jnp.bfloat16
            )
        )
        output_ins.append(output_in)

    normed_all = jnp.concatenate(normeds, axis=0)
    early_part = jnp.concatenate(
        [
            token_product(normed_all, jnp.concatenate(d_gates, axis=0)),
            token_product(
                out_grad.reshape(seq_count * length, width),
                jnp.concatenate(output_ins, axis=0),
            ),
        ],
        axis=1,
    )
    early = lax.psum_scatter(early_part, "dp", scatter_dimension=0, tiled=True)

    late_weight = jnp.concatenate([proj_value, proj_state, proj_step], axis=1)
    param_grads, lates, parts, others, grad_hiddens = None, [], [], [], []
    waits = (early_part, *branches)
    grad_norm_gain = jnp.zeros((width,), jnp.float32)
    for s in every:
        d_value, d_state, d_step, *grads = mixer_backs[s](after(d_mixeds[s], *waits))
        param_grads = grads if s == 0 else [a + b for a, b in zip(param_grads, grads)]
        late = jnp.concatenate([d_value, d_state, d_step], axis=1).astype(jnp.bfloat16)
        lates.append(late)
        part = right_product(d_gates[s], proj_gate) + right_product(late, late_weight)
        grad_norm_gain = grad_norm_gain + jnp.sum(part * wides[s] * row_scales[s], axis=0)
        parts.append(part)
        if s < seq_count - 1:
            parts[s] = after(part, received[s])
            others.append(tensor_others(parts[s]))
            waits = (part, received[s])
    edge_state = local_inner + state_width
    g_cv, g_cvb, g_cs, g_csb, g_sb, g_dl, g_sg = param_grads
    own = [g_cv, g_cvb, g_sb, g_dl, g_sg, grad_gate_gain]
    shared = [g_cs, g_csb, grad_norm_gain]
    own_flat = jnp.concatenate([g.reshape(-1) for g in own])
    place = lax.axis_index("tensor")
    mine = (jnp.arange(tensor_count) == place)[:, None]
    slots = jnp.where(mine, own_flat[None, :], 0.0).reshape(-1)
    packed = lax.psum(
        after(
            jnp.concatenate([slots] + [g.reshape(-1) for g in shared]),
            early,
            received[-1],
            *others,
        ),
        ("dp", "tensor"),
    )
    own_sum = lax.dynamic_slice(packed, (place * own_flat.shape[0],), (own_flat.shape[0],))
    shared_sum = packed[slots.shape[0] :]

    later = lax.psum_scatter(
        token_product(normed_all, after(jnp.concatenate(lates, axis=0), packed)),
        "dp",
        scatter_dimension=0,
        tiled=True,
    )
    block_outs = []
    for s in every:
        if s == seq_count - 1:
            parts[s] = after(parts[s], packed)
            others.append(tensor_others(parts[s]))
        d_scaled = tensor_join(parts[s], others[s]) * norm_gain[None, :]
        row_scale, wide = row_scales[s], wides[s]
        norm_inner = jnp.sum(d_scaled * wide, axis=-1, keepdims=True)
        grad_hiddens.append(
            out_grad[s].astype(jnp.float32)
            + row_scale * d_scaled
            - row_scale**3 * wide * norm_inner / width
        )
        branch = tensor_join(branches[s], received[s])
        block_outs.append((wide + branch).astype(jnp.bfloat16))
    grad_proj_state = lax.psum(later[:, local_inner:edge_state], "tensor")

    def split(flat, like):
        result, edge = [], 0
        for g in like:
            result.append(flat[edge : edge + g.size].reshape(g.shape))
            edge += g.size
        return result

    r_cv, r_cvb, r_sb, r_dl, r_sg, r_gg = split(own_sum, own)
    r_cs, r_csb, r_ng = split(shared_sum, shared)
    return (
        jnp.stack(block_outs),
        jnp.stack(grad_hiddens),
        r_ng,
        early[:, :local_inner],
        later[:, :local_inner],
        grad_proj_state,
        later[:, edge_state:],
        r_cv,
        r_cvb,
        r_cs,
        r_csb,
        r_sb,
        r_dl,
        r_sg,
        r_gg,
        early[:, local_inner:],
    )


def solution(mesh):
    in_specs = (
        P("dp", None, None),
        P("dp", None),
        P(),
        P(None, "tensor"),
        P(None, "tensor"),
        P(),
        P(None, "tensor"),
        P(None, "tensor"),
        P("tensor"),
        P(),
        P(),
        P("tensor"),
        P("tensor"),
        P("tensor"),
        P("tensor"),
        P(None, "tensor"),
        P("dp", None, None),
    )
    out_specs = (
        P("dp", None, None),
        P("dp", None, None),
        P(),
        P("dp", "tensor"),
        P("dp", "tensor"),
        P("dp", None),
        P("dp", "tensor"),
        P(None, "tensor"),
        P("tensor"),
        P(),
        P(),
        P("tensor"),
        P("tensor"),
        P("tensor"),
        P("tensor"),
        P("dp", "tensor"),
    )
    return jax.shard_map(local, mesh=mesh, in_specs=in_specs, out_specs=out_specs, check_vma=False)
```

profile of v0, /device:TPU:0, one launch (start us, length us, event | category | flops | bytes accessed | tf_op | source)
XLA Modules:
  0.0 794.7 jit_solution(9242613608619532424)
XLA Ops:
  11.0 3.1 fusion.28
  16.3 4.3 fusion.459
  20.6 4.3 fusion.466
  30.7 4.4 fusion.465
  35.1 4.4 fusion.472
  41.6 5.6 multiply_convert_fusion.23
  50.2 22.6 %fusion.435 = (bf16[1024,1024]{1,0:T(8,128)(2,1)}, f32[1024,1024]{1,0:T(8,128)}, bf16[1024,1024]{1,0:T(8,128)(2,1)}, f32[1024,1024]{1,0:T(8,128)S(1)}) fusion(f32[1024]{0:T(1024)S(1)} %get-tuple-element.468, f32[1021,1024]{1,0:T(8,128)} %bitcast.722, f32[1024]{0:T(1024)S(1)} %bitcast.950, f32[1024]{0:T(1024)S(1)} %get-tuple-element.467, ...), kind=kLoop, calls=%fused_computation.717 | loop fusion | flops 33554432 | bytes 46133248 | tf_op jit(solution)/shard_map/jvp()/convert_element_type | solution.py:67
  79.6 6.4 reshape.1877
  87.0 7.6 fusion.19
  94.7 5.6 copy.290
  101.0 3.8 multiply_convert_fusion.15
  109.9 6.5 reshape.1876
  116.5 7.6 fusion.18
  124.0 5.3 copy.280
  129.6 6.0 fusion.128
  135.6 3.9 multiply_add_fusion.2
  140.6 3.8 multiply_add_fusion.3
  144.4 14.7 %multiply_reduce_fusion.15 = (f32[1024]{0:T(1024)S(1)}, f32[1024]{0:T(1024)S(1)}, f32[1024,1024]{1,0:T(8,128)}, f32[1024]{0:T(1024)S(1)}, f32[1024]{0:T(1024)S(1...) fusion(f32[1024]{0:T(1024)S(1)} %copy-done.208, f32[1024,1024]{1,0:T(8,128)} %fusion.465, ...), kind=kOutput, calls=%fused_computation.169 | convolution fusion | flops 2172645376 | bytes 46161920 | tf_op jit(solution)/shard_map/dot_general | solution.py:210
  159.1 9.7 %psum.21 = f32[4,1024]{1,0:T(4,128)S(1)} all-reduce(f32[4,1024]{1,0:T(4,128)S(1)} %pad_maximum_fusion.9), channel_id=1, replica_groups=mesh['dp'=16,'tensor'=2] {'tensor'}, use_global_device_ids=true, to_apply=%region_6.7 | all-reduce | flops 4096 | bytes 32768 | tf_op jit(solution)/shard_map/psum | solution.py:215
  168.9 19.2 %multiply_multiply_fusion.1 = (f32[1024,1024]{1,0:T(8,128)}, bf16[1024,1024]{1,0:T(8,128)(2,1)S(1)}, f32[1024]{0:T(1024)}, bf16[1024,1024]{1,0:T(8,128)(2,1)S(1)...) fusion(f32[1024,1024]{1,0:T(8,128)} %fusion.465, ...), kind=kLoop, calls=%fused_computation.152 | loop fusion | flops 54523904 | bytes 58761216 | tf_op jit(solution)/shard_map/mul | solution.py:230
  188.1 4.5 fusion.473
  193.3 4.6 fusion.50
  197.9 6.2 fusion.123
  204.1 4.2 pad_maximum_fusion
  208.3 9.2 %copy.351 = f32[1024,2048]{1,0:T(8,128)} copy(f32[1024,2048]{0,1:T(8,128)} %pad_maximum_fusion) | data formatting | bytes 16777216
  217.6 6.0 fusion.474
  231.4 4.9 copy.295
  238.8 3.9 convolution_multiply_fusion.1
  248.1 13.2 %multiply_reduce_fusion.3 = (f32[1024]{0:T(1024)}, f32[1024,1024]{1,0:T(8,128)S(1)}, f32[1024,1024]{1,0:T(8,128)}) fusion(f32[1024,1024]{1,0:T(8,128)} %get-tuple-element.53, f32[1024]{0:T(1024)} %copy-done.130, f32[1021,1024]{1,0:T(8,128)} %bitcast.725, f32[1024]{0:T(1024)} %bitcast.927, f32[1024]{0:T(1024)} %copy-done.125, f32[1022,1024]{1,0:T(8,128)} %bitcast.726, ...), kind=kLoop, calls=%fused_computation.115 | loop fusion | flops 17824768 | bytes 29372416 | tf_op jit(solution)/shard_map/transpose(jvp(jvp()))/checkpoint/reduce_sum | solution.py:97
  265.4 4.0 convert_multiply_fusion.17
  281.4 6.0 convert_bitcast_fusion.1
  287.4 7.3 copy.345
  294.8 7.7 reshape.1878
  305.1 11.4 %multiply_reduce_fusion.11 = (f32[1024]{0:T(1024)}, f32[1024,1024]{1,0:T(8,128)S(1)}, f32[1024,1024]{1,0:T(8,128)}) fusion(f32[1021,1024]{1,0:T(8,128)} %bitcast.728, f32[1024]{0:T(1024)} %copy-done.130, f32[1024,1024]{1,0:T(8,128)} %get-tuple-element.223, f32[1024,1024]{1,0:T(8,128)} %reshape.1878, f32[8,128,1024]{2,1,0:T(8,128)} %get-tuple-element.312, ...), kind=kLoop, calls=%fused_computation.123 | loop fusion | flops 15727616 | bytes 29360128 | tf_op jit(solution)/shard_map/transpose(jvp(jvp()))/checkpoint/reduce_sum | solution.py:35
  319.4 6.4 reshape.1879
  325.8 12.3 %fusion.15 = (f32[8,16,128]{2,1,0:T(8,128)}, f32[8,16,128]{2,1,0:T(8,128)}, f32[8,16,128]{2,1,0:T(8,128)S(1)}, bf16[8,128,128]{2,1,0:T(8,128)(2,1)S(1)}) fusion(f32[8,16,128]{2,1,0:T(8,128)} %copy.296, f32[8,128,128]{2,1,0:T(8,128)} %fusion.476, f32[8,16,128]{2,1,0:T(8,128)S(1)} %fusion.291, pred[8,128,128]{2,1,0:T(8,128)(4,1)} %compare_and_fusion.1, ...), kind=kOutput, calls=%fused_computation.39 | convolution fusion | flops 297615360 | bytes 5439488 | tf_op jit(solution)/shard_map/transpose(jvp(jvp()))/checkpoint/chts,cshp->cthp/dot_general | solution.py:68
  352.5 4.8 fusion.187
  365.5 4.4 multiply_reduce_fusion.10
  373.2 4.4 fusion.475
  377.6 4.3 fusion.479
  381.9 3.5 fusion.422
  385.5 8.5 %fusion.135 = f32[1024,1024]{1,0:T(8,128)} fusion(f32[1024,1024]{1,0:T(8,128)} %fusion.475, bf16[1024,16]{1,0:T(8,128)(2,1)S(1)} %get-tuple-element.227, bf16[1024,256]{1,0:T(8,128)(2,1)S(1)} %get-tuple-element.318, bf16[1024,1024]{1,0:T(8,128)(2,1)S(1)} %get-tuple-element.304, bf16[1024,16]{1,0:T(8,128)(2,1)S(1)} %copy-done.96, ...), kind=kOutput, calls=%fused_computation.223 | convolution fusion | flops 2734882816 | bytes 13697024 | tf_op jit(solution)/shard_map/dot_general | solution.py:120
  400.0 4.6 copy.314
  408.1 5.9 convert_bitcast_fusion
  414.1 7.1 copy.348
  421.2 7.6 reshape.1880
  430.2 3.6 convolution_multiply_fusion
  438.3 13.2 %multiply_reduce_fusion.2 = (f32[1024]{0:T(1024)}, f32[1024,1024]{1,0:T(8,128)S(1)}, f32[1024,1024]{1,0:T(8,128)}) fusion(f32[1024,1024]{1,0:T(8,128)} %get-tuple-element.69, f32[1024]{0:T(1024)} %copy-done.128, f32[1021,1024]{1,0:T(8,128)} %bitcast.716, f32[1024]{0:T(1024)} %bitcast.925, f32[1024]{0:T(1024)} %copy-done.120, f32[1022,1024]{1,0:T(8,128)} %bitcast.717, ...), kind=kLoop, calls=%fused_computation.114 | loop fusion | flops 17824768 | bytes 29372416 | tf_op jit(solution)/shard_map/transpose(jvp(jvp()))/checkpoint/reduce_sum | solution.py:97
  455.2 6.4 reshape.1881
  461.6 11.3 %fusion.17 = (f32[8,16,128]{2,1,0:T(8,128)}, f32[8,16,128]{2,1,0:T(8,128)}, f32[8,16,128]{2,1,0:T(8,128)S(1)}, bf16[8,128,128]{2,1,0:T(8,128)(2,1)}) fusion(f32[8,16,128]{2,1,0:T(8,128)S(1)} %copy-done.141, f32[8,128,128]{2,1,0:T(8,128)S(1)} %fusion.480, f32[8,16,128]{2,1,0:T(8,128)S(1)} %fusion.288, pred[8,128,128]{2,1,0:T(8,128)(4,1)S(1)} %copy-done.105, ...), kind=kOutput, calls=%fused_computation.41 | convolution fusion | flops 297615360 | bytes 5439488 | tf_op jit(solution)/shard_map/transpose(jvp(jvp()))/checkpoint/chts,cshp->cthp/dot_general | solution.py:68
  476.2 4.2 convert_multiply_fusion.15
  500.0 9.2 %multiply_reduce_fusion.7 = (f32[1024]{0:T(1024)S(1)}, f32[1024,1024]{1,0:T(8,128)S(1)}, f32[1024,1024]{1,0:T(8,128)S(1)}) fusion(f32[1021,1024]{1,0:T(8,128)} %bitcast.719, f32[1024]{0:T(1024)S(1)} %copy-done.129, f32[1024,1024]{1,0:T(8,128)} %get-tuple-element.220, f32[1024,1024]{1,0:T(8,128)} %reshape.1880, f32[8,128,1024]{2,1,0:T(8,128)} %get-tuple-element.308, ...), kind=kLoop, calls=%fused_computation.119 | loop fusion | flops 15727616 | bytes 29360128 | tf_op jit(solution)/shard_map/transpose(jvp(jvp()))/checkpoint/reduce_sum | solution.py:35
  515.8 3.8 fusion.421
  526.3 9.6 %fusion.44 = (f32[1024]{0:T(1024)S(1)}, f32[1024]{0:T(1024)S(1)}, f32[1024,1024]{1,0:T(8,128)}) fusion(f32[1024]{0:T(1024)S(1)} %copy-done.152, bf16[2,1024,1024]{2,1,0:T(8,128)(2,1)} %param.18, f32[1024]{0:T(1024)S(1)} %copy-done.154, f32[1024,1024]{1,0:T(8,128)} %fusion.135, f32[1024,1024]{1,0:T(8,128)} %fusion.479, bf16[1024,16]{1,0:T(8,128)(2,1)} %copy.309, ...), kind=kOutput, calls=%fused_computation.75 | convolution fusion | flops 2743269376 | bytes 22102016 | tf_op jit(solution)/shard_map/dot_general | solution.py:120
  536.0 26.3 %maximum_maximum_fusion = bf16[2048,1296]{1,0:T(8,128)(2,1)} fusion(bf16[1024,16]{1,0:T(8,128)(2,1)} %get-tuple-element.225, bf16[1024,256]{1,0:T(8,128)(2,1)S(1)} %get-tuple-element.319, bf16[1024,1024]{1,0:T(8,128)(2,1)} %get-tuple-element.305, bf16[1024,16]{1,0:T(8,128)(2,1)S(1)} %get-tuple-element.227, bf16[1024,256]{1,0:T(8,128)(2,1)S(1)} %copy-done.63, ...), kind=kLoop, calls=%fused_computation.44 | loop fusion | flops 31850496 | bytes 10616832 | tf_op jit(solution)/shard_map/concatenate | solution.py:288
  563.7 25.9 %collective-permute-done.2 = f32[1024,1024]{1,0:T(8,128)} collective-permute-done((f32[1024,1024]{1,0:T(8,128)}, f32[1024,1024]{1,0:T(8,128)}, u32[]{:S(2)}, u32[]{:S(2)}) %collective-permute-start.2) | collective-permute-done | bytes 4194336 | tf_op jit(solution)/shard_map/ppermute | solution.py:134
  589.6 40.5 %psum.22 = f32[14688]{0:T(1024)S(1)} all-reduce(f32[14688]{0:T(1024)S(1)} %concatenate.230), channel_id=1, replica_groups=mesh['dp'=16,'tensor'=2] {'dp','tensor'}, use_global_device_ids=true, to_apply=%region_65.67 | all-reduce | flops 14688 | bytes 117504 | tf_op jit(solution)/shard_map/psum | solution.py:275
  630.2 11.5 %fusion.112 = f32[1024,1296]{1,0:T(8,128)} fusion(bf16[2048,1296]{1,0:T(8,128)(2,1)} %maximum_maximum_fusion, bf16[1024,1024]{1,0:T(8,128)(2,1)} %copy-done.43, bf16[1024,1024]{1,0:T(8,128)(2,1)S(1)} %copy-done.42), kind=kOutput, calls=%fused_computation.204 | convolution fusion | flops 5444206592 | bytes 14811136 | tf_op jit(solution)/shard_map/dot_general | solution.py:126
  649.3 84.6 %collective-permute-done.3 = f32[1024,1024]{1,0:T(8,128)} collective-permute-done((f32[1024,1024]{1,0:T(8,128)}, f32[1024,1024]{1,0:T(8,128)}, u32[]{:S(2)}, u32[]{:S(2)}) %collective-permute-start.3) | collective-permute-done | bytes 4194336 | tf_op jit(solution)/shard_map/ppermute | solution.py:134
  734.0 11.7 %fusion.36 = (f32[1024]{0:T(1024)S(1)}, f32[1024]{0:T(1024)S(1)}, bf16[1,1024,1024]{2,1,0:T(8,128)(2,1)}) fusion(f32[1024]{0:T(1024)S(1)} %copy-done.148, f32[1024,1024]{1,0:T(8,128)} %fusion.135, f32[1024,1024]{1,0:T(8,128)} %collective-permute-done.2, bf16[2,1024,1024]{2,1,0:T(8,128)(2,1)} %param.18, f32[1024,1024]{1,0:T(8,128)} %get-tuple-element.82, ...), kind=kLoop, calls=%fused_computation.67 | loop fusion | flops 13629440 | bytes 31469568 | tf_op jit(solution)/shard_map/reduce_sum | solution.py:300
  745.8 11.8 %fusion.35 = (f32[1,1024,1024]{2,1,0:T(8,128)S(1)}, f32[1,1024,1024]{2,1,0:T(8,128)}, bf16[1,1024,1024]{2,1,0:T(8,128)(2,1)}) fusion(f32[1024]{0:T(1024)S(1)} %get-tuple-element.178, f32[1024]{0:T(1024)S(1)} %copy-done.176, f32[1024]{0:T(1024)S(1)} %copy-done.154, bf16[2,1024,1024]{2,1,0:T(8,128)(2,1)} %param.34, f32[1024]{0:T(1024)S(1)} %copy-done.148, ...), kind=kLoop, calls=%fused_computation.66 | loop fusion | flops 24117248 | bytes 44068864 | tf_op jit(solution)/shard_map/stack | solution.py:321
  757.5 6.8 pad_maximum_fusion.1
  765.9 4.8 pad_maximum_fusion.2
  772.1 14.4 %all-reduce.96.cloned.1.call-done = f32[64,256]{1,0:T(8,128)} async-done(((f32[64,256]{1,0:T(8,128)}), f32[64,256]{1,0:T(8,128)}) %all-reduce.96.cloned.1.call-update) | async-done | bytes 65552 | tf_op jit(solution)/shard_map/psum | solution.py:308
  (726 shorter events, 162.3 us)
Async XLA Ops:
  7.2 122.4 %copy-start = (bf16[1024,1024]{1,0:T(8,128)(2,1)S(1)}, bf16[1024,1024]{1,0:T(8,128)(2,1)}, u32[]{:S(2)}) copy-start(bf16[1024,1024]{1,0:T(8,128)(2,1)} %param.33) | copy-start | bytes 6291460
  7.2 7.5 copy-start.147
  7.2 555.1 %reduce-scatter.7.cloned.1.call-start = ((), (), s32[]{:S(2)}) async-start(), calls=%async_computation.4 | async-start | bytes 8912896
  7.3 7.4 copy-start.8
  8.1 77.9 %copy-start.72 = (s32[1,1024]{1,0:T(1,128)}, s32[1,1024]{1,0:T(1,128)S(1)}, u32[]{:S(2)}) copy-start(s32[1,1024]{1,0:T(1,128)S(1)} %get-tuple-element.415) | copy-start | bytes 12292
  16.0 14.7 %copy-start.40 = (bf16[1024,1024]{1,0:T(8,128)(2,1)}, bf16[1024,1024]{1,0:T(8,128)(2,1)S(1)}, u32[]{:S(2)}) copy-start(bf16[1024,1024]{1,0:T(8,128)(2,1)S(1)} %get-tuple-element.300) | copy-start | bytes 6291460
  16.0 19.0 %copy-start.43 = (bf16[1024,1024]{1,0:T(8,128)(2,1)}, bf16[1024,1024]{1,0:T(8,128)(2,1)S(1)}, u32[]{:S(2)}) copy-start(bf16[1024,1024]{1,0:T(8,128)(2,1)S(1)} %get-tuple-element.301) | copy-start | bytes 6291460
  26.3 13.8 %copy-start.75 = (f32[1024,16]{0,1:T(8,128)}, f32[1024,16]{0,1:T(8,128)S(1)}, u32[]{:S(2)}) copy-start(f32[1024,16]{0,1:T(8,128)S(1)} %fusion.467) | copy-start | bytes 196612
  28.9 12.8 %copy-start.5 = (f32[1024,256]{1,0:T(8,128)}, f32[1024,256]{1,0:T(8,128)S(1)}, u32[]{:S(2)}) copy-start(f32[1024,256]{1,0:T(8,128)S(1)} %fusion.468) | copy-start | bytes 3145732
  29.9 195.1 %copy-start.94 = (pred[128,128]{1,0:T(8,128)(4,1)}, pred[128,128]{1,0:T(8,128)(4,1)S(1)}, u32[]{:S(2)}) copy-start(pred[128,128]{1,0:T(8,128)(4,1)S(1)} %iota_compare_fusion.7) | copy-start | bytes 49156
  35.0 6.5 copy-start.163
  35.0 6.6 copy-start.199
  41.2 6.7 copy-start.178
  41.6 8.5 %copy-start.146 = (f32[1024]{0:T(1024)S(1)}, f32[1024]{0:T(1024)}, u32[]{:S(2)}) copy-start(f32[1024]{0:T(1024)} %param.26) | copy-start | bytes 12292
  50.2 22.6 %copy-start.179 = (f32[8,16]{1,0:T(8,128)S(1)}, f32[8,16]{1,0:T(8,128)}, u32[]{:S(2)}) copy-start(f32[8,16]{1,0:T(8,128)} %copy-done.178) | copy-start | bytes 1540
  109.9 6.5 copy-start.98
  109.9 6.5 copy-start.106
  188.1 9.8 %copy-start.60 = (bf16[1024,1024]{1,0:T(8,128)(2,1)}, bf16[1024,1024]{1,0:T(8,128)(2,1)S(1)}, u32[]{:S(2)}) copy-start(bf16[1024,1024]{1,0:T(8,128)(2,1)S(1)} %get-tuple-element.401) | copy-start | bytes 6291460
  192.6 201.4 %collective-permute-start = (f32[1024,1024]{1,0:T(8,128)}, f32[1024,1024]{1,0:T(8,128)}, u32[]{:S(2)}, u32[]{:S(2)}) collective-permute-start(f32[1024,1024]{1,0:T(8,128)} %fusion.473), channel_id=1, source_target_pairs={{0,1},{1,0},{2,3},{3,2},{4,5},{5,4},{6,7},{7,6},{8,9},{9,8},{10,11... | collective-permute-start | bytes 12582920 | tf_op jit(solution)/shard_map/ppermute | solution.py:134
  217.5 9.5 %copy-start.7 = (f32[1024,256]{1,0:T(8,128)S(1)}, f32[1024,256]{1,0:T(8,128)}, u32[]{:S(2)}) copy-start(f32[1024,256]{1,0:T(8,128)} %fusion.461) | copy-start | bytes 3145732
  217.6 9.5 %copy-start.200 = (f32[256]{0:T(256)S(1)}, f32[256]{0:T(256)}, u32[]{:S(2)}) copy-start(f32[256]{0:T(256)} %param.28) | copy-start | bytes 3076
  217.6 546.8 %reduce-scatter.5.cloned.1.call-start = ((), (), s32[]{:S(2)}) async-start(), calls=%async_computation.2 | async-start | bytes 6127616 | tf_op jit(solution)/shard_map/reduce_scatter | solution.py:287
  223.7 340.0 %collective-permute-start.1 = (f32[1024,1024]{1,0:T(8,128)}, f32[1024,1024]{1,0:T(8,128)}, u32[]{:S(2)}, u32[]{:S(2)}) collective-permute-start(f32[1024,1024]{1,0:T(8,128)} %fusion.474), channel_id=1, source_target_pairs={{0,1},{1,0},{2,3},{3,2},{4,5},{5,4},{6,7},{7,6},{8,9},{9,8},{10,11... | collective-permute-start | bytes 12582920 | tf_op jit(solution)/shard_map/ppermute | solution.py:134
  229.4 7.6 copy-start.51
  229.6 6.7 copy-start.46
  229.7 6.6 copy-start.214
  305.1 11.4 %copy-start.162 = (f32[1,1024]{1,0:T(1,128)S(1)}, f32[1,1024]{1,0:T(1,128)}, u32[]{:S(2)}) copy-start(f32[1,1024]{1,0:T(1,128)} %get-tuple-element.390) | copy-start | bytes 12292
  325.8 12.4 %copy-start.53 = (bf16[1024,128]{1,0:T(8,128)(2,1)S(1)}, bf16[1024,128]{1,0:T(8,128)(2,1)}, u32[]{:S(2)}) copy-start(bf16[1024,128]{1,0:T(8,128)(2,1)} %copy-done.51) | copy-start | bytes 786436
  325.8 12.6 %copy-start.14 = (f32[8,128,1024]{2,1,0:T(8,128)S(1)}, f32[8,128,1024]{2,1,0:T(8,128)}, u32[]{:S(2)}) copy-start(f32[8,128,1024]{2,1,0:T(8,128)} %fusion.477) | copy-start | bytes 12582916
  325.8 12.6 %copy-start.107 = (f32[1,1024]{1,0:T(1,128)S(1)}, f32[1,1024]{1,0:T(1,128)}, u32[]{:S(2)}) copy-start(f32[1,1024]{1,0:T(1,128)} %get-tuple-element.361) | copy-start | bytes 12292
  325.8 12.6 %copy-start.109 = (f32[1,1024]{1,0:T(1,128)S(1)}, f32[1,1024]{1,0:T(1,128)}, u32[]{:S(2)}) copy-start(f32[1,1024]{1,0:T(1,128)} %get-tuple-element.362) | copy-start | bytes 12292
  325.8 12.6 %copy-start.111 = (f32[1,1024]{1,0:T(1,128)S(1)}, f32[1,1024]{1,0:T(1,128)}, u32[]{:S(2)}) copy-start(f32[1,1024]{1,0:T(1,128)} %get-tuple-element.364) | copy-start | bytes 12292
  325.8 12.6 %copy-start.113 = (f32[1,1024]{1,0:T(1,128)S(1)}, f32[1,1024]{1,0:T(1,128)}, u32[]{:S(2)}) copy-start(f32[1,1024]{1,0:T(1,128)} %get-tuple-element.366) | copy-start | bytes 12292
  352.4 7.7 copy-start.167
  352.5 7.6 copy-start.168
  352.5 8.2 %copy-start.35 = (f32[1024,256]{1,0:T(8,128)S(1)}, f32[1024,256]{1,0:T(8,128)}, u32[]{:S(2)}) copy-start(f32[1024,256]{1,0:T(8,128)} %copy-done.34) | copy-start | bytes 3145732
  357.7 7.8 copy-start.124
  357.7 7.8 copy-start.127
  363.7 21.7 %copy-start.62 = (bf16[1024,256]{1,0:T(8,128)(2,1)}, bf16[1024,256]{1,0:T(8,128)(2,1)S(1)}, u32[]{:S(2)}) copy-start(bf16[1024,256]{1,0:T(8,128)(2,1)S(1)} %get-tuple-element.318) | copy-start | bytes 1572868
  385.4 8.5 %copy-start.45 = (bf16[1024,1024]{1,0:T(8,128)(2,1)}, bf16[1024,1024]{1,0:T(8,128)(2,1)S(1)}, u32[]{:S(2)}) copy-start(bf16[1024,1024]{1,0:T(8,128)(2,1)S(1)} %get-tuple-element.304) | copy-start | bytes 6291460
  385.4 8.5 %copy-start.73 = (s32[1,1024]{1,0:T(1,128)S(1)}, s32[1,1024]{1,0:T(1,128)}, u32[]{:S(2)}) copy-start(s32[1,1024]{1,0:T(1,128)} %copy-done.72) | copy-start | bytes 12292
  385.4 8.5 %copy-start.95 = (pred[128,128]{1,0:T(8,128)(4,1)S(1)}, pred[128,128]{1,0:T(8,128)(4,1)}, u32[]{:S(2)}) copy-start(pred[128,128]{1,0:T(8,128)(4,1)} %copy-done.94) | copy-start | bytes 49156
  385.5 9.8 %copy-start.164 = (f32[4,256]{1,0:T(4,128)S(1)}, f32[4,256]{1,0:T(4,128)}, u32[]{:S(2)}) copy-start(f32[4,256]{1,0:T(4,128)} %param.27) | copy-start | bytes 12292
  385.5 9.9 %copy-start.6 = (f32[1024,256]{1,0:T(8,128)S(1)}, f32[1024,256]{1,0:T(8,128)}, u32[]{:S(2)}) copy-start(f32[1024,256]{1,0:T(8,128)} %copy-done.5) | copy-start | bytes 3145732
  385.5 9.9 %copy-start.201 = (f32[256]{0:T(256)S(1)}, f32[256]{0:T(256)}, u32[]{:S(2)}) copy-start(f32[256]{0:T(256)} %param.28) | copy-start | bytes 3076
  421.2 7.6 copy-start.102
  461.6 11.3 %copy-start.20 = (bf16[8,128,1024]{2,1,0:T(8,128)(2,1)S(1)}, bf16[8,128,1024]{2,1,0:T(8,128)(2,1)}, u32[]{:S(2)}) copy-start(bf16[8,128,1024]{2,1,0:T(8,128)(2,1)} %copy-done.19) | copy-start | bytes 6291460
  461.6 11.3 %copy-start.117 = (f32[1,1024]{1,0:T(1,128)S(1)}, f32[1,1024]{1,0:T(1,128)}, u32[]{:S(2)}) copy-start(f32[1,1024]{1,0:T(1,128)} %get-tuple-element.359) | copy-start | bytes 12292
  461.6 11.6 %copy-start.116 = (f32[1,1024]{1,0:T(1,128)S(1)}, f32[1,1024]{1,0:T(1,128)}, u32[]{:S(2)}) copy-start(f32[1,1024]{1,0:T(1,128)} %get-tuple-element.357) | copy-start | bytes 12292
  481.2 7.9 copy-start.15
  499.2 90.4 %collective-permute-start.2 = (f32[1024,1024]{1,0:T(8,128)}, f32[1024,1024]{1,0:T(8,128)}, u32[]{:S(2)}, u32[]{:S(2)}) collective-permute-start(f32[1024,1024]{1,0:T(8,128)} %fusion.135), channel_id=1, source_target_pairs={{0,1},{1,0},{2,3},{3,2},{4,5},{5,4},{6,7},{7,6},{8,9},{9,8},{10,11... | collective-permute-start | bytes 12582920 | tf_op jit(solution)/shard_map/ppermute | solution.py:134
  500.0 9.2 %copy-start.161 = (f32[1,1024]{1,0:T(1,128)S(1)}, f32[1,1024]{1,0:T(1,128)}, u32[]{:S(2)}) copy-start(f32[1,1024]{1,0:T(1,128)} %get-tuple-element.386) | copy-start | bytes 12292
  526.2 9.7 %copy-start.212 = (f32[256]{0:T(256)S(1)}, f32[256]{0:T(256)}, u32[]{:S(2)}) copy-start(f32[256]{0:T(256)} %get-tuple-element.200) | copy-start | bytes 3076
  526.3 9.8 %copy-start.63 = (bf16[1024,256]{1,0:T(8,128)(2,1)S(1)}, bf16[1024,256]{1,0:T(8,128)(2,1)}, u32[]{:S(2)}) copy-start(bf16[1024,256]{1,0:T(8,128)(2,1)} %copy-done.62) | copy-start | bytes 1572868
  536.0 94.1 %copy-start.42 = (bf16[1024,1024]{1,0:T(8,128)(2,1)S(1)}, bf16[1024,1024]{1,0:T(8,128)(2,1)}, u32[]{:S(2)}) copy-start(bf16[1024,1024]{1,0:T(8,128)(2,1)} %copy-done.40) | copy-start | bytes 6291460
  641.7 92.3 %copy-start.148 = (f32[1024]{0:T(1024)S(1)}, f32[1024]{0:T(1024)}, u32[]{:S(2)}) copy-start(f32[1024]{0:T(1024)} %param.20) | copy-start | bytes 12292
  641.7 144.8 %all-reduce.96.cloned.1.call-start = ((), (), s32[]{:S(2)}) async-start(), calls=%async_computation.3 | async-start | bytes 131072 | tf_op jit(solution)/shard_map/psum | solution.py:308
  642.0 92.0 %collective-permute-start.3 = (f32[1024,1024]{1,0:T(8,128)}, f32[1024,1024]{1,0:T(8,128)}, u32[]{:S(2)}, u32[]{:S(2)}) collective-permute-start(f32[1024,1024]{1,0:T(8,128)} %get-tuple-element.82), channel_id=1, source_target_pairs={{0,1},{1,0},{2,3},{3,2},{4,5},{5,4},{6,7},{7,6},{8,9},{9,8},{10,11... | collective-permute-start | bytes 12582920 | tf_op jit(solution)/shard_map/ppermute | solution.py:134
  649.3 96.4 %copy-start.9 = (bf16[2,1024,1024]{2,1,0:T(8,128)(2,1)S(1)}, bf16[2,1024,1024]{2,1,0:T(8,128)(2,1)}, u32[]{:S(2)}) copy-start(bf16[2,1024,1024]{2,1,0:T(8,128)(2,1)} %param.18) | copy-start | bytes 12582916
  649.3 96.4 %copy-start.25 = (f32[1024,1024]{1,0:T(8,128)S(1)}, f32[1024,1024]{1,0:T(8,128)}, u32[]{:S(2)}) copy-start(f32[1024,1024]{1,0:T(8,128)} %fusion.135) | copy-start | bytes 12582916
  649.3 96.4 %copy-start.26 = (f32[1024,1024]{1,0:T(8,128)S(1)}, f32[1024,1024]{1,0:T(8,128)}, u32[]{:S(2)}) copy-start(f32[1024,1024]{1,0:T(8,128)} %get-tuple-element.82) | copy-start | bytes 12582916
  649.3 96.4 %copy-start.175 = (f32[1024]{0:T(1024)S(1)}, f32[1024]{0:T(1024)}, u32[]{:S(2)}) copy-start(f32[1024]{0:T(1024)} %get-tuple-element.420) | copy-start | bytes 12292
  649.3 96.4 %copy-start.176 = (f32[1024]{0:T(1024)S(1)}, f32[1024]{0:T(1024)}, u32[]{:S(2)}) copy-start(f32[1024]{0:T(1024)} %get-tuple-element.466) | copy-start | bytes 12292
  765.9 22.1 %copy-start.1 = (bf16[1024,1024]{1,0:T(8,128)(2,1)S(1)}, bf16[1024,1024]{1,0:T(8,128)(2,1)}, u32[]{:S(2)}) copy-start(bf16[1024,1024]{1,0:T(8,128)(2,1)} %param.33) | copy-start | bytes 6291460
  (181 other events, 571.3 us)
Sparse Core Ops, SparseCore 0:
  217.7 105.6 reduce-scatter.6
  641.8 81.9 reduce-scatter.4
  766.0 20.4 all-reduce.95
where the time goes:
time: 806 us; the launch traced here: 795 us
  other arithmetic  237 us (29%)
  matrix products  220 us (27%)
  local copies, waits for them, and re-layouts  142 us (18%)
  waiting for transfers between devices  125 us (16%)
  blocking collectives  50.2 us (6%)
  between operations  16.9 us (2%)
    ppermute x4, waiting for transfers between devices, tensor_others(): return lax.ppermute(part, 'tensor', [(0, 1), (1, 0)])  111 us
    dot_general x6, matrix products, head_mix(): jnp.einsum('chts,cshp->cthp', mixing, low_head, preferred_element_type=jn...  50.7 us
    psum x1, blocking collectives, local(): lax.psum(after(jnp.concatenate([slots] + [g.reshape(-1) for g in shared])...  40.5 us
    unnamed x495, local copies, waits for them, and re-layouts  39.8 us
    dot_general x6, matrix products, right_product(): lax.dot_general(left, weight, (((1,), (1,)), ((), ())), preferred_element...  37.4 us
    reduce_sum x8, other arithmetic, causal_conv(): weight[KERNEL - 1 - delay][None, :] * earlier * doc_masks[delay][:, None]  30.8 us
    convert_element_type x4, local copies, waits for them, and re-layouts, head_mix(): values.astype(jnp.bfloat16).reshape(chunks, CHUNK, heads, HEAD_DIM)  29.8 us
    reduce_sum x4, other arithmetic, head_mix(): return mixed + jnp.repeat(skip_gain, HEAD_DIM)[None, :] * values  27.3 us
  transfers between devices with their start and end apart: 7, of which 3 were waited for; matrix products, arithmetic and copies ran while one was open for 50% of the time, Pallas kernels for 0%

commit v1 on v0

v1 whole, which is shorter than its diff:
```python
import functools

import jax
import jax.numpy as jnp
from jax import lax
from jax.experimental import pallas as pl
from jax.experimental.pallas import tpu as pltpu
from jax.sharding import PartitionSpec as P

HEAD_DIM = 64
STATE = 128
KERNEL = 4
VMEM_BYTES = 50 * 1024 * 1024

epsilon = 1e-05
precise = lax.Precision.HIGHEST


def lag_masks(segment_row):
    length = segment_row.shape[0]
    result = [jnp.ones((length,), jnp.float32)]
    for delay in range(1, KERNEL):
        earlier = jnp.concatenate(
            [jnp.full((delay,), -1, jnp.int32), segment_row[: length - delay]]
        )
        result.append((earlier == segment_row).astype(jnp.float32))
    return result


def causal_conv(values, weight, conv_bias, doc_masks):
    length = values.shape[0]
    summed = conv_bias[None, :] + weight[KERNEL - 1][None, :] * values
    for delay in range(1, KERNEL):
        earlier = jnp.concatenate(
            [jnp.zeros((delay, values.shape[1]), jnp.float32), values[: length - delay]], axis=0
        )
        summed = summed + weight[KERNEL - 1 - delay][None, :] * earlier * doc_masks[delay][:, None]
    return jax.nn.silu(summed)


CHUNK = 128
PAIR = 2 * HEAD_DIM
LOG2E = 1.4426950408889634
NN = (((1,), (0,)), ((), ()))
NT = (((1,), (1,)), ((), ()))
TN = (((0,), (0,)), ((), ()))
bf16 = jnp.bfloat16


def mxu(a, b, dims=NN):
    return lax.dot_general(a, b, dims, preferred_element_type=jnp.float32)


def sigmoid(z):
    return 0.5 * jnp.tanh(0.5 * z) + 0.5


def pair_wide(rows, at):
    top = jnp.broadcast_to(rows[at : at + 1], (HEAD_DIM, CHUNK))
    low = jnp.broadcast_to(rows[at + 1 : at + 2], (HEAD_DIM, CHUNK))
    return jnp.concatenate([top, low], axis=0)


def decay_block(rows, h):
    run = jnp.broadcast_to(rows[h : h + 1], (CHUNK, CHUNK))
    return jnp.exp2(jnp.minimum(run - run.T, 0.0))


def doc_block(masks):
    segment = jnp.broadcast_to(masks[3:4], (CHUNK, CHUNK))
    source = lax.broadcasted_iota(jnp.int32, (CHUNK, CHUNK), 0)
    target = lax.broadcasted_iota(jnp.int32, (CHUNK, CHUNK), 1)
    return ((segment == segment.T) & (source <= target)).astype(jnp.float32)


def shifted_taps(raw, before, masks):
    lane = lax.broadcasted_iota(jnp.int32, raw.shape, 1)
    taps = [raw]
    for k in range(1, KERNEL):
        moved = pltpu.roll(jnp.where(lane >= CHUNK - k, before, raw), k, 1)
        taps.append(moved * masks[k - 1 : k])
    return taps


def conv_sum(taps, conv_ref, part):
    total = conv_ref[KERNEL, part, :]
    for k in range(KERNEL):
        total = total + conv_ref[KERNEL - 1 - k, part, :] * taps[k]
    return total


def mix_kernel(
    raw_ref, gate_ref, dout_ref, rows_ref, mask_ref, into_ref, outt_ref, conv_ref, gain_ref,
    mixed_ref, entry_ref, sums_ref, held_ref, before_ref,
):
    @pl.when(pl.program_id(1) == 0)
    def _():
        held_ref[...] = jnp.zeros_like(held_ref)
        before_ref[...] = jnp.zeros_like(before_ref)

    masks = mask_ref[0]
    into, outt = into_ref[...], outt_ref[...]
    affinity = mxu(into, outt) * doc_block(masks)

    def body(p, sums):
        part = pl.ds(pl.multiple_of(p * PAIR, PAIR), PAIR)
        rows = rows_ref[0, p]
        raw = raw_ref[part, :].astype(jnp.float32)
        pre = conv_sum(shifted_taps(raw, before_ref[part, :], masks), conv_ref, part)
        value = pre * sigmoid(pre)
        scaled = value * pair_wide(rows, 2)
        low = scaled.astype(bf16)
        near = []
        for h in range(2):
            mixing = (decay_block(rows, h) * affinity).astype(bf16)
            near.append(mxu(low[h * HEAD_DIM : (h + 1) * HEAD_DIM], mixing))
        held = held_ref[part, :]
        held_low = held.astype(bf16)
        entry_ref[0, part, :] = held_low
        far = mxu(held_low, outt) * pair_wide(rows, 6)
        kept = (scaled * pair_wide(rows, 4)).astype(bf16)
        held_ref[part, :] = held * pair_wide(rows, 8) + mxu(kept, into)
        mixed = jnp.concatenate(near, axis=0) + far + pair_wide(rows, 10) * value
        mixed_ref[part, :] = mixed
        before_ref[part, :] = raw
        gate = gate_ref[part, :].astype(jnp.float32)
        gated = mixed * gate * sigmoid(gate)
        square = jnp.sum(gated * gated, axis=0, keepdims=True)
        inner = dout_ref[part, :].astype(jnp.float32) * gain_ref[part, :] * gated
        return sums[0] + square, sums[1] + jnp.sum(inner, axis=0, keepdims=True)

    zero = jnp.zeros((1, CHUNK), jnp.float32)
    square, inner = lax.fori_loop(0, raw_ref.shape[0] // PAIR, body, (zero, zero))
    sums_ref[0, 0:1, :] = square
    sums_ref[0, 1:2, :] = inner


def back_kernel(
    raw_ref, before_ref, mixed_ref, dmix_ref, entry_ref, rows_ref, mask_ref, into_ref, intot_ref,
    out_ref, outt_ref, conv_ref,
    draw_ref, drows_ref, dstate_ref, dconv_ref, dheld_ref, later_ref, latermask_ref, dfar_ref,
):
    step = pl.program_id(1)

    @pl.when((pl.program_id(0) == 0) & (step == 0))
    def _():
        dconv_ref[...] = jnp.zeros_like(dconv_ref)

    @pl.when(step == 0)
    def _():
        dheld_ref[...] = jnp.zeros_like(dheld_ref)
        later_ref[...] = jnp.zeros_like(later_ref)
        latermask_ref[...] = jnp.zeros_like(latermask_ref)

    first = step == pl.num_programs(1) - 1
    masks, later_masks = mask_ref[0], latermask_ref[...]
    into, intot, out, outt = into_ref[...], intot_ref[...], out_ref[...], outt_ref[...]
    allowed = doc_block(masks)
    affinity = mxu(into, outt) * allowed
    dfar_ref[...] = jnp.zeros_like(dfar_ref)
    lane = lax.broadcasted_iota(jnp.int32, (PAIR, CHUNK), 1)
    head_row = lax.broadcasted_iota(jnp.int32, (PAIR, CHUNK), 0) < HEAD_DIM

    def body(p, daffinity):
        part = pl.ds(pl.multiple_of(p * PAIR, PAIR), PAIR)
        rows = rows_ref[0, p]
        raw = raw_ref[part, :].astype(jnp.float32)
        before = jnp.where(first, 0.0, before_ref[part, :].astype(jnp.float32))
        taps = shifted_taps(raw, before, masks)
        pre = conv_sum(taps, conv_ref, part)
        gate = sigmoid(pre)
        value = pre * gate
        step_wide = pair_wide(rows, 2)
        skip_wide = pair_wide(rows, 10)
        keep_wide = pair_wide(rows, 4)
        scaled = value * step_wide
        low = scaled.astype(bf16)
        dmix_low = dmix_ref[part, :]
        dmix = dmix_low.astype(jnp.float32)
        halves = jnp.concatenate(
            [jnp.where(head_row, dmix, 0.0).astype(bf16), jnp.where(head_row, 0.0, dmix).astype(bf16)],
            axis=1,
        )
        dmixing = mxu(low, halves, TN)
        dnear = []
        for h in range(2):
            decay = decay_block(rows, h)
            mixing = (decay * affinity).astype(bf16)
            daffinity = daffinity + dmixing[:, h * CHUNK : (h + 1) * CHUNK] * decay
            dnear.append(mxu(dmix_low[h * HEAD_DIM : (h + 1) * HEAD_DIM], mixing, NT))
        dnear = jnp.concatenate(dnear, axis=0)
        held_low = entry_ref[0, part, :]
        dheld = dheld_ref[part, :]
        dheld_low = dheld.astype(bf16)
        carried = dheld * pair_wide(rows, 8)
        dfar = mxu(dheld_low, intot) * keep_wide
        kept = (scaled * keep_wide).astype(bf16)
        read = (dmix * pair_wide(rows, 6)).astype(bf16)
        dfar_ref[:, :STATE] += mxu(kept, dheld_low, TN)
        dfar_ref[:, STATE:] += mxu(read, held_low, TN)
        dheld_ref[part, :] = carried + mxu(read, out)
        dscaled = dnear + dfar
        scaled_low = low.astype(jnp.float32)
        far_product = scaled * dfar
        running = (
            dmix * (mixed_ref[part, :] - skip_wide * value) - scaled_low * dnear - far_product
        )
        products = (
            running, far_product, carried * held_low.astype(jnp.float32), dscaled * value,
            dmix * value,
        )
        for q, product in enumerate(products):
            for h in range(2):
                drows_ref[0, p, 2 * q + h : 2 * q + h + 1, :] = jnp.sum(
                    product[h * HEAD_DIM : (h + 1) * HEAD_DIM], axis=0, keepdims=True
                )
        dvalue = dscaled * step_wide + skip_wide * dmix
        dpre = dvalue * (gate * (1.0 + pre * (1.0 - gate)))
        later = later_ref[part, :]
        dconv_ref[KERNEL, part, :] += dpre
        dconv_ref[KERNEL - 1, part, :] += dpre * raw
        draw = conv_ref[KERNEL - 1, part, :] * dpre
        for k in range(1, KERNEL):
            dconv_ref[KERNEL - 1 - k, part, :] += dpre * taps[k]
            joined = jnp.where(
                lane < k, later * later_masks[k - 1 : k], dpre * masks[k - 1 : k]
            )
            draw = draw + conv_ref[KERNEL - 1 - k, part, :] * pltpu.roll(joined, CHUNK - k, 1)
        later_ref[part, :] = dpre
        draw_ref[part, :] = draw.astype(bf16)
        return daffinity

    daffinity = lax.fori_loop(
        0, raw_ref.shape[0] // PAIR, body, jnp.zeros((CHUNK, CHUNK), jnp.float32)
    )
    daffinity = (daffinity * allowed).astype(bf16)
    dstate_ref[:, :STATE] = dfar_ref[:, :STATE] + mxu(daffinity, out)
    dstate_ref[:, STATE:] = dfar_ref[:, STATE:] + mxu(daffinity, into, TN)
    latermask_ref[...] = masks


def spec(block, index):
    return pl.BlockSpec(block, index)


def mix_forward(seqs, raw, gate, dout, rows, masks, into, outt, conv, gain):
    ch, tokens = raw.shape
    chunks = tokens // seqs // CHUNK
    at = lambda s, c: (0, s * chunks + c)
    up = lambda s, c: (s * chunks + c, 0)
    slab = spec((ch, CHUNK), at)
    return pl.pallas_call(
        mix_kernel,
        grid=(seqs, chunks),
        in_specs=[
            slab, slab, slab,
            spec((1,) + rows.shape[1:], lambda s, c: (s * chunks + c, 0, 0, 0)),
            spec((1, 8, CHUNK), lambda s, c: (s * chunks + c, 0, 0)),
            spec((CHUNK, STATE), up),
            spec((STATE, CHUNK), at),
            spec(conv.shape, lambda s, c: (0, 0, 0)),
            spec((ch, CHUNK), lambda s, c: (0, 0)),
        ],
        out_specs=[
            slab,
            spec((1, ch, STATE), lambda s, c: (s * chunks + c, 0, 0)),
            spec((1, 8, CHUNK), lambda s, c: (s * chunks + c, 0, 0)),
        ],
        out_shape=[
            jax.ShapeDtypeStruct((ch, tokens), jnp.float32),
            jax.ShapeDtypeStruct((seqs * chunks, ch, STATE), bf16),
            jax.ShapeDtypeStruct((seqs * chunks, 8, CHUNK), jnp.float32),
        ],
        scratch_shapes=[
            pltpu.VMEM((ch, STATE), jnp.float32),
            pltpu.VMEM((ch, CHUNK), jnp.float32),
        ],
        compiler_params=pltpu.CompilerParams(vmem_limit_bytes=VMEM_BYTES),
        cost_estimate=pl.CostEstimate(
            flops=tokens * ch * 1024, bytes_accessed=tokens * ch * 18, transcendentals=tokens * ch * 4
        ),
        name="mix_forward",
    )(raw, gate, dout, rows, masks, into, outt, conv, gain)


def mix_backward(seqs, raw, mixed, dmix, entry, rows, masks, into, intot, out, outt, conv):
    ch, tokens = raw.shape
    chunks = tokens // seqs // CHUNK
    place = lambda s, c: s * chunks + chunks - 1 - c
    at = lambda s, c: (0, place(s, c))
    up = lambda s, c: (place(s, c), 0)
    slab = spec((ch, CHUNK), at)
    row_spec = spec((1,) + rows.shape[1:], lambda s, c: (place(s, c), 0, 0, 0))
    return pl.pallas_call(
        back_kernel,
        grid=(seqs, chunks),
        in_specs=[
            slab,
            spec((ch, CHUNK), lambda s, c: (0, jnp.maximum(place(s, c) - 1, 0))),
            slab, slab,
            spec((1, ch, STATE), lambda s, c: (place(s, c), 0, 0)),
            row_spec,
            spec((1, 8, CHUNK), lambda s, c: (place(s, c), 0, 0)),
            spec((CHUNK, STATE), up),
            spec((STATE, CHUNK), at),
            spec((CHUNK, STATE), up),
            spec((STATE, CHUNK), at),
            spec(conv.shape, lambda s, c: (0, 0, 0)),
        ],
        out_specs=[
            slab,
            row_spec,
            spec((CHUNK, 2 * STATE), up),
            spec(conv.shape, lambda s, c: (0, 0, 0)),
        ],
        out_shape=[
            jax.ShapeDtypeStruct((ch, tokens), bf16),
            jax.ShapeDtypeStruct(rows.shape, jnp.float32),
            jax.ShapeDtypeStruct((tokens, 2 * STATE), jnp.float32),
            jax.ShapeDtypeStruct(conv.shape, jnp.float32),
        ],
        scratch_shapes=[
            pltpu.VMEM((ch, STATE), jnp.float32),
            pltpu.VMEM((ch, CHUNK), jnp.float32),
            pltpu.VMEM((8, CHUNK), jnp.float32),
            pltpu.VMEM((CHUNK, 2 * STATE), jnp.float32),
        ],
        compiler_params=pltpu.CompilerParams(vmem_limit_bytes=VMEM_BYTES),
        cost_estimate=pl.CostEstimate(
            flops=tokens * ch * 2048, bytes_accessed=tokens * ch * 16, transcendentals=tokens * ch * 4
        ),
        name="mix_backward",
    )(raw, raw, mixed, dmix, entry, rows, masks, into, intot, out, outt, conv)


def wide_lanes(columns):
    return jnp.broadcast_to(columns[..., None], columns.shape + (CHUNK,))


def pair_rows(parts, seqs):
    heads, _, chunks, _ = parts[0].shape
    stacked = jnp.stack(parts + [jnp.zeros_like(parts[0])] * (8 - len(parts)))
    stacked = stacked.reshape(8, heads // 2, 2, seqs * chunks, CHUNK)
    return stacked.transpose(3, 1, 0, 2, 4).reshape(seqs * chunks, heads // 2, 16, CHUNK)


def unpair_rows(rows, q, seqs):
    steps, pairs = rows.shape[:2]
    part = rows[:, :, 2 * q : 2 * q + 2, :].transpose(1, 2, 0, 3)
    return part.reshape(2 * pairs, seqs, steps // seqs, CHUNK)


def step_rows(step_raw, step_bias, decay_log, skip_gain, segment_ids):
    seqs, length = segment_ids.shape
    chunks = length // CHUNK
    heads = step_raw.shape[0]
    rate = -jnp.exp(decay_log)
    size = jax.nn.softplus(step_raw + step_bias[:, None]).reshape(heads, seqs, chunks, CHUNK)
    places = jnp.arange(CHUNK)
    upper = (places[:, None] <= places[None, :]).astype(jnp.float32)
    running = jnp.einsum(
        "hqcs,st->hqct", size * rate[:, None, None, None], upper, precision=precise
    )
    segments = segment_ids.reshape(seqs, chunks, CHUNK)
    last = segments[:, :, -1]
    before = jnp.concatenate([jnp.full((seqs, 1), -1, jnp.int32), last[:, :-1]], axis=1)
    total = running[..., -1:]
    at_end = (segments == last[..., None]).astype(jnp.float32)
    from_start = (segments == before[..., None]).astype(jnp.float32)
    through = (last == before).astype(jnp.float32)[..., None]
    full = jnp.ones_like(running)
    parts = [
        running * LOG2E,
        size,
        jnp.exp(total - running) * at_end,
        jnp.exp(running) * from_start,
        jnp.exp(total) * through * full,
        skip_gain[:, None, None, None] * full,
    ]
    lags = [jnp.stack(lag_masks(row)[1:]) for row in segment_ids]
    lags = jnp.stack(lags).reshape(seqs, KERNEL - 1, chunks, CHUNK).transpose(0, 2, 1, 3)
    masks = jnp.concatenate(
        [
            lags,
            segments[:, :, None, :].astype(jnp.float32),
            jnp.zeros((seqs, chunks, 4, CHUNK), jnp.float32),
        ],
        axis=2,
    ).reshape(seqs * chunks, 8, CHUNK)
    return pair_rows(parts, seqs), masks


def step_grads(drows, step_raw, step_bias, decay_log, seqs):
    heads, tokens = step_raw.shape
    running, far, carried, direct, skip = [unpair_rows(drows, q, seqs) for q in range(5)]
    rate = -jnp.exp(decay_log)[:, None, None, None]
    biased = step_raw + step_bias[:, None]
    size = jax.nn.softplus(biased).reshape(running.shape)
    total = jnp.sum(far + carried, axis=-1, keepdims=True)
    places = jnp.arange(CHUNK)
    lower = (places[:, None] >= places[None, :]).astype(jnp.float32)
    ddrop = jnp.einsum("hqct,ts->hqcs", running, lower, precision=precise) + total
    dsize = direct + ddrop * rate
    draw = dsize.reshape(heads, tokens) * jax.nn.sigmoid(biased)
    every = (1, 2, 3)
    return (
        draw,
        jnp.sum(draw, axis=1),
        jnp.sum(ddrop * size * rate, axis=every),
        jnp.sum(skip, axis=every),
    )


def out_product(left, weight):
    return lax.dot_general(left, weight, (((0,), (1,)), ((), ())), preferred_element_type=jnp.float32)


def in_product(weight, tokens):
    return lax.dot_general(weight, tokens, (((0,), (1,)), ((), ())), preferred_element_type=jnp.float32)


def grad_product(tokens, channels):
    return lax.dot_general(
        tokens, channels, (((0,), (1,)), ((), ())), preferred_element_type=jnp.float32
    )


def right_product(left, weight):
    return lax.dot_general(
        left, weight, (((1,), (1,)), ((), ())), preferred_element_type=jnp.float32
    )


def token_product(left, right):
    return lax.dot_general(
        left, right, (((0,), (0,)), ((), ())), preferred_element_type=jnp.float32
    )


def tensor_others(part):
    count = lax.axis_size("tensor")
    if count == 2:
        return lax.ppermute(part, "tensor", [(0, 1), (1, 0)])
    return lax.psum(part, "tensor")


def tensor_join(part, others):
    return part + others if lax.axis_size("tensor") == 2 else others


def after(value, *earlier):
    return lax.optimization_barrier((value, *earlier))[0]


def local(
    hidden,
    segment_ids,
    norm_gain,
    proj_gate,
    proj_value,
    proj_state,
    proj_step,
    conv_value,
    conv_value_bias,
    conv_state,
    conv_state_bias,
    step_bias,
    decay_log,
    skip_gain,
    gate_gain,
    proj_out,
    out_grad,
):
    seq_count, length, width = hidden.shape
    local_inner = proj_gate.shape[1]
    state_width = proj_state.shape[1]
    tensor_count = lax.axis_size("tensor")
    inner_total = local_inner * tensor_count
    every = range(seq_count)

    wides = [hidden[s].astype(jnp.float32) for s in every]
    row_scales = [
        lax.rsqrt(jnp.mean(w * w, axis=-1, keepdims=True) + epsilon) for w in wides
    ]
    normeds = [
        (w * r * norm_gain[None, :]).astype(jnp.bfloat16) for w, r in zip(wides, row_scales)
    ]
    conv_wide = wide_lanes(jnp.concatenate([conv_value, conv_value_bias[None, :]], axis=0))
    gain_wide = wide_lanes(gate_gain)

    gates, douts, raws, steps, rows, masks, states = [], [], [], [], [], [], []
    state_backs, mixeds, entries, boths = [], [], [], []
    for s in every:
        gates.append(in_product(proj_gate, normeds[s]))
        raws.append(in_product(proj_value, normeds[s]))
        steps.append(in_product(proj_step, normeds[s]))
        douts.append(in_product(proj_out, out_grad[s]))
        state_raw = jnp.dot(normeds[s], proj_state, preferred_element_type=jnp.float32)
        state_conv, back = jax.vjp(
            functools.partial(causal_conv, doc_masks=lag_masks(segment_ids[s])),
            state_raw,
            conv_state,
            conv_state_bias,
        )
        state_backs.append(back)
        low = state_conv.astype(jnp.bfloat16)
        into, out = low[:, :STATE], low[:, STATE:]
        states.append((into, into.T, out, out.T))
        row, mask = step_rows(steps[s], step_bias, decay_log, skip_gain, segment_ids[s : s + 1])
        rows.append(row)
        masks.append(mask)
        mixed, entry, sums = mix_forward(
            1, raws[s], gates[s], douts[s], row, mask, into, out.T, conv_wide, gain_wide
        )
        mixeds.append(mixed)
        entries.append(entry)
        sums = sums[:, :2].transpose(1, 0, 2).reshape(2, length)
        boths.append(tensor_join(sums, tensor_others(sums)))

    branches, received, output_ins, d_gates, d_mixeds = [], [], [], [], []
    grad_gate_gain = jnp.zeros((local_inner,), jnp.float32)
    for s in every:
        gate, mixed, dout = gates[s], mixeds[s], douts[s]
        sigma = jax.nn.sigmoid(gate)
        gated = mixed * gate * sigma
        gated_scale = lax.rsqrt(boths[s][0:1] / inner_total + epsilon)
        gate_inner = boths[s][1:2]
        output_in = (gated * gated_scale * gate_gain[:, None]).astype(jnp.bfloat16)
        branches.append(out_product(output_in, proj_out))
        received.append(tensor_others(branches[s]))
        grad_gate_gain = grad_gate_gain + jnp.sum(dout * gated * gated_scale, axis=1)
        weighted = dout * gate_gain[:, None]
        d_gated = gated_scale * weighted - gated_scale**3 * gated * gate_inner / inner_total
        d_mixeds.append((d_gated * gate * sigma).astype(jnp.bfloat16))
        d_gates.append(
            (d_gated * mixed * sigma * (1.0 + gate * (1.0 - sigma))).astype(jnp.bfloat16)
        )
        output_ins.append(output_in)

    normed_all = jnp.concatenate(normeds, axis=0)
    early_part = jnp.stack(
        [
            grad_product(normed_all, jnp.concatenate(d_gates, axis=1)),
            grad_product(
                out_grad.reshape(seq_count * length, width), jnp.concatenate(output_ins, axis=1)
            ),
        ]
    )
    early = lax.psum_scatter(early_part, "dp", scatter_dimension=1, tiled=True)

    param_grads, d_values, d_states, d_steps = None, [], [], []
    parts, others, grad_hiddens = [], [], []
    waits = (early_part, *branches)
    grad_norm_gain = jnp.zeros((width,), jnp.float32)
    for s in every:
        d_value, d_rows, d_state, d_conv = mix_backward(
            1, raws[s], mixeds[s], after(d_mixeds[s], *waits), entries[s], rows[s], masks[s],
            *states[s], conv_wide,
        )
        d_step, g_sb, g_dl, g_sg = step_grads(d_rows, steps[s], step_bias, decay_log, 1)
        d_state = d_state.astype(jnp.bfloat16).astype(jnp.float32)
        d_state, g_cs, g_csb = state_backs[s](d_state)
        d_conv = jnp.sum(d_conv, axis=-1)
        grads = (d_conv[:KERNEL], d_conv[KERNEL], g_cs, g_csb, g_sb, g_dl, g_sg)
        param_grads = grads if s == 0 else [a + b for a, b in zip(param_grads, grads)]
        d_values.append(d_value)
        d_states.append(d_state.astype(jnp.bfloat16))
        d_steps.append(d_step.astype(jnp.bfloat16))
        part = (
            out_product(d_gates[s], proj_gate)
            + out_product(d_value, proj_value)
            + right_product(d_states[s], proj_state)
            + out_product(d_steps[s], proj_step)
        )
        grad_norm_gain = grad_norm_gain + jnp.sum(part * wides[s] * row_scales[s], axis=0)
        parts.append(part)
        if s < seq_count - 1:
            parts[s] = after(part, received[s])
            others.append(tensor_others(parts[s]))
            waits = (part, received[s])
    g_cv, g_cvb, g_cs, g_csb, g_sb, g_dl, g_sg = param_grads
    own = [g_cv, g_cvb, g_sb, g_dl, g_sg, grad_gate_gain]
    shared = [g_cs, g_csb, grad_norm_gain]
    own_flat = jnp.concatenate([g.reshape(-1) for g in own])
    place = lax.axis_index("tensor")
    mine = (jnp.arange(tensor_count) == place)[:, None]
    slots = jnp.where(mine, own_flat[None, :], 0.0).reshape(-1)
    packed = lax.psum(
        after(
            jnp.concatenate([slots] + [g.reshape(-1) for g in shared]),
            early,
            received[-1],
            *others,
        ),
        ("dp", "tensor"),
    )
    own_sum = lax.dynamic_slice(packed, (place * own_flat.shape[0],), (own_flat.shape[0],))
    shared_sum = packed[slots.shape[0] :]

    later_value = lax.psum_scatter(
        grad_product(normed_all, after(jnp.concatenate(d_values, axis=1), packed)),
        "dp",
        scatter_dimension=0,
        tiled=True,
    )
    later_rest = lax.psum_scatter(
        jnp.concatenate(
            [
                token_product(normed_all, jnp.concatenate(d_states, axis=0)),
                grad_product(normed_all, jnp.concatenate(d_steps, axis=1)),
            ],
            axis=1,
        ),
        "dp",
        scatter_dimension=0,
        tiled=True,
    )
    block_outs = []
    for s in every:
        if s == seq_count - 1:
            parts[s] = after(parts[s], packed)
            others.append(tensor_others(parts[s]))
        d_scaled = tensor_join(parts[s], others[s]) * norm_gain[None, :]
        row_scale, wide = row_scales[s], wides[s]
        norm_inner = jnp.sum(d_scaled * wide, axis=-1, keepdims=True)
        grad_hiddens.append(
            out_grad[s].astype(jnp.float32)
            + row_scale * d_scaled
            - row_scale**3 * wide * norm_inner / width
        )
        branch = tensor_join(branches[s], received[s])
        block_outs.append((wide + branch).astype(jnp.bfloat16))
    grad_proj_state = lax.psum(later_rest[:, :state_width], "tensor")

    def split(flat, like):
        result, edge = [], 0
        for g in like:
            result.append(flat[edge : edge + g.size].reshape(g.shape))
            edge += g.size
        return result

    r_cv, r_cvb, r_sb, r_dl, r_sg, r_gg = split(own_sum, own)
    r_cs, r_csb, r_ng = split(shared_sum, shared)
    return (
        jnp.stack(block_outs),
        jnp.stack(grad_hiddens),
        r_ng,
        early[0],
        later_value,
        grad_proj_state,
        later_rest[:, state_width:],
        r_cv,
        r_cvb,
        r_cs,
        r_csb,
        r_sb,
        r_dl,
        r_sg,
        r_gg,
        early[1],
    )


def solution(mesh):
    in_specs = (
        P("dp", None, None),
        P("dp", None),
        P(),
        P(None, "tensor"),
        P(None, "tensor"),
        P(),
        P(None, "tensor"),
        P(None, "tensor"),
        P("tensor"),
        P(),
        P(),
        P("tensor"),
        P("tensor"),
        P("tensor"),
        P("tensor"),
        P(None, "tensor"),
        P("dp", None, None),
    )
    out_specs = (
        P("dp", None, None),
        P("dp", None, None),
        P(),
        P("dp", "tensor"),
        P("dp", "tensor"),
        P("dp", None),
        P("dp", "tensor"),
        P(None, "tensor"),
        P("tensor"),
        P(),
        P(),
        P("tensor"),
        P("tensor"),
        P("tensor"),
        P("tensor"),
        P("dp", "tensor"),
    )
    return jax.shard_map(local, mesh=mesh, in_specs=in_specs, out_specs=out_specs, check_vma=False)
```

time: 806 us -> 628 us (0.78); the launches traced: 795 us -> 627 us
  other arithmetic: 237 us -> 99.7 us
  Pallas kernels: 0 us -> 136 us
  matrix products: 220 us -> 97.6 us
  local copies, waits for them, and re-layouts: 142 us -> 37 us
  waiting for transfers between devices: 125 us -> 194 us
  blocking collectives: 50.2 us -> 40.1 us
    pallas_call x0 -> x4, Pallas kernels: none -> 136 us  [the longest x2 82.2 us: mix_backward(): pl.pallas_call(back_kernel, grid=(seqs, chunks), in_specs=[slab, spec((ch...]
    ppermute x4 -> x6, waiting for transfers between devices: 111 us -> 182 us  [tensor_others(): return lax.ppermute(part, 'tensor', [(0, 1), (1, 0)])]
    dot_general x62 -> x24, matrix products: 158 us -> 91.3 us  [the longest x8 37.3 us: out_product(): lax.dot_general(left, weight, (((0,), (1,)), ((), ())), preferred_element...]
    reshape x10 -> x2, local copies, waits for them, and re-layouts: 38 us -> 0.65 us  [local(): sums = sums[:, :2].transpose(1, 0, 2).reshape(2, length)]
    dot_general x6 -> x2, matrix products: 37.4 us -> 1.52 us  [right_product(): lax.dot_general(left, weight, (((1,), (1,)), ((), ())), preferred_element...]
    convert_element_type x4 -> x0, local copies, waits for them, and re-layouts: 29.8 us -> none  [head_mix(): values.astype(jnp.bfloat16).reshape(chunks, CHUNK, heads, HEAD_DIM)]
    concatenate x5 -> x3, other arithmetic: 31.9 us -> 4.88 us  [the longest x1 4.76 us: local(): jnp.concatenate(d_values, axis=1)]
    reduce_sum x10 -> x6, other arithmetic: 32.7 us -> 7.9 us  [the longest x2 5.71 us: local(): d_conv = jnp.sum(d_conv, axis=-1)]
  transfers between devices with their start and end apart: 7 -> 10, of which waited for: 3 -> 6; matrix products, arithmetic and copies ran while one was open for 50% -> 22% of each run, Pallas kernels for 0% -> 17%
where the time goes in v1:
time: 628 us; the launch traced here: 627 us
  waiting for transfers between devices  194 us (31%)
  Pallas kernels  136 us (22%)
  other arithmetic  99.7 us (16%)
  matrix products  97.6 us (16%)
  blocking collectives  40.1 us (6%)
  local copies, waits for them, and re-layouts  37 us (6%)
  between operations  15.6 us (2%)
  starting transfers between devices  7.66 us (1%)
    ppermute x6, waiting for transfers between devices, tensor_others(): return lax.ppermute(part, 'tensor', [(0, 1), (1, 0)])  182 us
    pallas_call x2, Pallas kernels, mix_backward(): pl.pallas_call(back_kernel, grid=(seqs, chunks), in_specs=[slab, spec((ch...  82.2 us
    pallas_call x2, Pallas kernels, mix_forward(): pl.pallas_call(mix_kernel, grid=(seqs, chunks), in_specs=[slab, slab, sla...  53.5 us
    psum x1, blocking collectives, local(): lax.psum(after(jnp.concatenate([slots] + [g.reshape(-1) for g in shared])...  40.1 us
    dot_general x8, matrix products, out_product(): lax.dot_general(left, weight, (((0,), (1,)), ((), ())), preferred_element...  37.3 us
    dot_general x8, matrix products, in_product(): lax.dot_general(weight, tokens, (((0,), (1,)), ((), ())), preferred_eleme...  30.1 us
    convert_element_type x1, other arithmetic, local(): (d_gated * mixed * sigma * (1.0 + gate * (1.0 - sigma))).astype(jnp.bfloa...  24.5 us
    dot_general x4, matrix products, grad_product(): lax.dot_general(tokens, channels, (((0,), (1,)), ((), ())), preferred_ele...  20.9 us
  transfers between devices with their start and end apart: 10, of which 6 were waited for; matrix products, arithmetic and copies ran while one was open for 22% of the time, Pallas kernels for 17%

profile of v1, /device:TPU:0, one launch (start us, length us, event | category | flops | bytes accessed | tf_op | source)
XLA Modules:
  0.0 627.1 jit_solution(9082553084799978311)
XLA Ops:
  7.3 3.3 fusion
  11.2 1.3 fusion.2
  13.9 1.7 fusion.114
  15.7 1.8 fusion.116
  28.3 7.2 %multiply_convert_fusion.7 = (bf16[1024,256]{0,1:T(8,128)(2,1)}, f32[1024,256]{0,1:T(8,128)}, bf16[1024,256]{0,1:T(8,128)(2,1)S(1)}, f32[1024,256]{0,1:T(8,128)}) fusion(f32[1024]{0:T(1024)S(1)} %get-tuple-element.254, f32[1021,256]{0,1:T(8,128)} %bitcast.288, f32[256]{0:T(256)S(1)} %bitcast.335, f32[1024]{0:T(1024)S(1)} %get-tuple-element.253, ...), kind=kLoop, calls=%fused_computation.119 | loop fusion | flops 8388608 | bytes 11551744 | tf_op jit(solution)/shard_map/convert_element_type | solution.py:506
  35.6 1.0 fusion.106
  36.7 6.8 %convolution_bitcast_fusion.gate_ref = f32[1024,1024]{1,0:T(8,128)} fusion(bf16[1024,1024]{1,0:T(8,128)(2,1)} %copy-done.26, bf16[1024,1024]{1,0:T(8,128)(2,1)} %param.20), kind=kOutput, calls=%fused_computation.67 | convolution fusion | flops 2147483648 | bytes 8388608 | tf_op jit(solution)/shard_map/dot_general | solution.py:419
  43.5 4.4 convolution_bitcast_fusion.1.raw_ref.before_ref
  48.0 4.4 fusion.38.dout_ref
  52.6 1.9 broadcast_in_dim.20.conv_ref
  54.7 26.9 %mix_forward.3 = (f32[1024,1024]{1,0:T(8,128)}, bf16[8,1024,128]{2,1,0:T(8,128)(2,1)S(1)}, f32[8,8,128]{2,1,0:T(8,128)S(1)}) custom-call(f32[1024,1024]{1,0:T(8,128)} %convolution_bitcast_fusion.1.raw_ref.before_ref, f32[1024,1024]{1,0:T(8,128)} %convolution_bitcast_fusion.gate_ref, f32[1024,1024]{1,0:T(8,128)} %fusion.38.dout_ref, ...), custom_call_target="tpu_custom_call" | custom-call | flops 1073741824 | bytes 18874368 | tf_op jit(solution)/shard_map/mix_forward/pallas_call | solution.py:252
  82.3 3.0 collective-permute-start.2
  85.2 4.4 convolution_bitcast_fusion.2.gate_ref
  89.6 4.4 convolution_bitcast_fusion.3.raw_ref.before_ref
  94.0 4.5 fusion.40.dout_ref
  99.2 1.0 fusion.107
  100.3 1.8 copy.148.into_ref
  102.0 1.0 copy-done.3
  103.1 0.9 copy-done.5
  104.0 0.9 copy-done.9
  105.0 26.6 %mix_forward.2 = (f32[1024,1024]{1,0:T(8,128)}, bf16[8,1024,128]{2,1,0:T(8,128)(2,1)S(1)}, f32[8,8,128]{2,1,0:T(8,128)S(1)}) custom-call(f32[1024,1024]{1,0:T(8,128)} %convolution_bitcast_fusion.3.raw_ref.before_ref, f32[1024,1024]{1,0:T(8,128)} %convolution_bitcast_fusion.2.gate_ref, f32[1024,1024]{1,0:T(8,128)} %fusion.40.dout_ref, ...), custom_call_target="tpu_custom_call" | custom-call | flops 1073741824 | bytes 18874368 | tf_op jit(solution)/shard_map/mix_forward/pallas_call | solution.py:252
  132.4 2.9 collective-permute-done
  135.4 24.5 %multiply_convert_fusion.3 = (bf16[1024,1024]{1,0:T(8,128)(2,1)S(1)}, bf16[1024,1024]{1,0:T(8,128)(2,1)}, f32[1024]{0:T(1024)}, bf16[1024,1024]{1,0:T(8,128)(2,1...) fusion(f32[1024,1024]{1,0:T(8,128)} %convolution_bitcast_fusion, ...), kind=kLoop, calls=%fused_computation.57 | loop fusion | flops 56621056 | bytes 37785600 | tf_op jit(solution)/shard_map/convert_element_type | solution.py:536
  159.9 4.6 fusion.33
  164.5 6.4 %fusion.30 = f32[1,1024,1024]{2,1,0:T(8,128)S(1)} fusion(bf16[2048,1024]{1,0:T(8,128)(2,1)S(1)} %bitcast.294, bf16[1024,1024]{1,0:T(8,128)(2,1)S(1)} %get-tuple-element.214, bf16[1024,1024]{1,0:T(8,128)(2,1)} %get-tuple-element.152), kind=kOutput, calls=%fused_computation.65 | convolution fusion | flops 4303355904 | bytes 12582912 | tf_op jit(solution)/shard_map/dot_general | solution.py:423
  170.9 4.2 pad_maximum_fusion
  176.3 1.1 copy.175.out_ref
  178.0 6.1 fusion.115
  184.2 4.5 fusion.117
  188.7 2.0 collective-permute-start.3
  190.7 41.5 %mix_backward.2 = (bf16[1024,1024]{1,0:T(8,128)(2,1)}, f32[8,8,16,128]{3,2,1,0:T(8,128)S(1)}, f32[1024,256]{1,0:T(8,128)S(1)}, f32[5,1024,128]{2,1,0:T(8,128)}) custom-call(f32[1024,1024]{1,0:T(8,128)} %convolution_bitcast_fusion.3.raw_ref.before_ref, f32[1024,1024]{1,0:T(8,128)} %convolution_bitcast_fusion.3.raw_ref.before_ref, ...), custom_call_target="tpu_custom_call" | custom-call | flops 2147483648 | bytes 16777216 | tf_op jit(solution)/shard_map/mix_backward/pallas_call | solution.py:294
  233.1 1.0 copy.170
  234.9 3.8 multiply_reduce_fusion.9
  239.4 3.2 reduce_sum.265
  243.2 1.4 multiply_reduce_fusion.8
  245.8 1.1 fusion.99
  248.3 2.4 fusion.118
  250.7 4.5 fusion.121
  255.2 2.6 fusion.119
  257.8 2.8 add_add_fusion.1
  260.5 17.5 %collective-permute-done.1 = f32[1024,1024]{1,0:T(8,128)} collective-permute-done((f32[1024,1024]{1,0:T(8,128)}, f32[1024,1024]{1,0:T(8,128)}, u32[]{:S(2)}, u32[]{:S(2)}) %collective-permute-start.1) | collective-permute-done | bytes 4194336 | tf_op jit(solution)/shard_map/ppermute | solution.py:443
  278.0 40.7 %mix_backward.3 = (bf16[1024,1024]{1,0:T(8,128)(2,1)}, f32[8,8,16,128]{3,2,1,0:T(8,128)S(1)}, f32[1024,256]{1,0:T(8,128)S(1)}, f32[5,1024,128]{2,1,0:T(8,128)}) custom-call(f32[1024,1024]{1,0:T(8,128)} %convolution_bitcast_fusion.1.raw_ref.before_ref, f32[1024,1024]{1,0:T(8,128)} %convolution_bitcast_fusion.1.raw_ref.before_ref, ...), custom_call_target="tpu_custom_call" | custom-call | flops 2147483648 | bytes 16777216 | tf_op jit(solution)/shard_map/mix_backward/pallas_call | solution.py:294
  319.9 1.8 fusion.57
  321.8 2.2 multiply_reduce_fusion.5
  328.2 1.3 fusion.50
  330.3 1.6 copy.196
  332.0 2.5 reduce_sum.304
  334.8 6.7 %fusion.122 = f32[1024,1024]{1,0:T(8,128)} fusion(bf16[1024,1024]{1,0:T(8,128)(2,1)} %get-tuple-element.48, bf16[1024,1024]{1,0:T(8,128)(2,1)} %param.21), kind=kOutput, calls=%fused_computation.278 | convolution fusion | flops 2147483648 | bytes 8388608 | tf_op jit(solution)/shard_map/dot_general | solution.py:415
  342.6 1.5 copy-done.16
  344.1 7.8 %fusion.16 = (f32[1024]{0:T(1024)S(1)}, f32[1024]{0:T(1024)S(1)}, f32[1024,1024]{1,0:T(8,128)}) fusion(f32[1024]{0:T(1024)S(1)} %copy-done.64, bf16[2,1024,1024]{2,1,0:T(8,128)(2,1)S(1)} %copy-done.16, f32[1024]{0:T(1024)S(1)} %copy-done.66, f32[1024,1024]{1,0:T(8,128)} %add_add_fusion.1, bf16[16,1024]{1,0:T(8,128)(2,1)S(1)} %get-tuple-element.135, ...), kind=kOutput, calls=%fused_computation.30 | convolution fusion | flops 45086720 | bytes 25247744 | tf_op jit(solution)/shard_map/dot_general | solution.py:415
  352.0 15.9 %collective-permute-done.3 = f32[1024,1024]{1,0:T(8,128)} collective-permute-done((f32[1024,1024]{1,0:T(8,128)}, f32[1024,1024]{1,0:T(8,128)}, u32[]{:S(2)}, u32[]{:S(2)}) %collective-permute-start.3) | collective-permute-done | bytes 4194336 | tf_op jit(solution)/shard_map/ppermute | solution.py:443
  367.9 87.3 %collective-permute-done.4 = f32[1024,1024]{1,0:T(8,128)} collective-permute-done((f32[1024,1024]{1,0:T(8,128)}, f32[1024,1024]{1,0:T(8,128)}, u32[]{:S(2)}, u32[]{:S(2)}) %collective-permute-start.4) | collective-permute-done | bytes 4194336 | tf_op jit(solution)/shard_map/ppermute | solution.py:443
  455.2 40.1 %psum.14 = f32[14688]{0:T(1024)S(1)} all-reduce(f32[14688]{0:T(1024)S(1)} %concatenate.155), channel_id=1, replica_groups=mesh['dp'=16,'tensor'=2] {'dp','tensor'}, use_global_device_ids=true, to_apply=%region_28.29 | all-reduce | flops 14688 | bytes 117504 | tf_op jit(solution)/shard_map/psum | solution.py:588
  495.3 2.3 collective-permute-start.5
  497.6 4.8 pad_maximum_fusion.4
  504.1 9.3 %fusion.97 = f32[1024,1024]{1,0:T(8,128)} fusion(bf16[1024,2048]{1,0:T(8,128)(2,1)} %pad_maximum_fusion.4, bf16[1024,1024]{1,0:T(8,128)(2,1)} %copy-done.26, bf16[1024,1024]{1,0:T(8,128)(2,1)S(1)} %copy-done.25), kind=kOutput, calls=%fused_computation.257 | convolution fusion | flops 4303355904 | bytes 12582912 | tf_op jit(solution)/shard_map/dot_general | solution.py:423
  514.8 11.7 %all-reduce.26.cloned.1.call-done = f32[64,256]{0,1:T(8,128)} async-done(((f32[64,256]{0,1:T(8,128)}), f32[64,256]{0,1:T(8,128)}) %all-reduce.26.cloned.1.call-update) | async-done | bytes 65552 | tf_op jit(solution)/shard_map/psum | solution.py:633
  526.5 1.6 copy.184
  532.2 58.4 %collective-permute-done.5 = f32[1024,1024]{1,0:T(8,128)} collective-permute-done((f32[1024,1024]{1,0:T(8,128)}, f32[1024,1024]{1,0:T(8,128)}, u32[]{:S(2)}, u32[]{:S(2)}) %collective-permute-start.5) | collective-permute-done | bytes 4194336 | tf_op jit(solution)/shard_map/ppermute | solution.py:443
  590.6 10.6 %fusion.8 = (f32[1024]{0:T(1024)S(1)}, f32[1024]{0:T(1024)S(1)}, bf16[1,1024,1024]{2,1,0:T(8,128)(2,1)S(1)}) fusion(f32[1024]{0:T(1024)S(1)} %copy-done.72, f32[1024,1024]{1,0:T(8,128)} %add_add_fusion.1, f32[1024,1024]{1,0:T(8,128)} %collective-permute-done.4, bf16[2,1024,1024]{2,1,0:T(8,128)(2,1)} %param.17, f32[1024,1024]{1,0:T(8,128)} %get-tuple-element.54, ...), kind=kLoop, calls=%fused_computation.22 | loop fusion | flops 13629440 | bytes 31469568 | tf_op jit(solution)/shard_map/reduce_sum | solution.py:625
  601.3 11.1 %fusion.7 = (f32[1,1024,1024]{2,1,0:T(8,128)S(1)}, f32[1,1024,1024]{2,1,0:T(8,128)}, bf16[1,1024,1024]{2,1,0:T(8,128)(2,1)S(1)}) fusion(f32[1024]{0:T(1024)S(1)} %get-tuple-element.104, f32[1024]{0:T(1024)S(1)} %copy-done.91, f32[1024]{0:T(1024)S(1)} %copy-done.66, bf16[2,1024,1024]{2,1,0:T(8,128)(2,1)} %param.33, f32[1024]{0:T(1024)S(1)} %copy-done.72, ...), kind=kLoop, calls=%fused_computation.21 | loop fusion | flops 24117248 | bytes 44068864 | tf_op jit(solution)/shard_map/stack | solution.py:646
  612.4 2.5 pad_maximum_fusion.2
  614.8 1.2 copy-done.30
  616.1 4.2 pad_maximum_fusion.1
  (358 shorter events, 37.3 us)
Async XLA Ops:
  7.2 40.8 %copy-start = (bf16[1024,1024]{1,0:T(8,128)(2,1)S(1)}, bf16[1024,1024]{1,0:T(8,128)(2,1)}, u32[]{:S(2)}) copy-start(bf16[1024,1024]{1,0:T(8,128)(2,1)} %param.32) | copy-start | bytes 6291460
  7.2 447.9 %reduce-scatter.6.cloned.1.call-start = ((), (), s32[]{:S(2)}) async-start(), calls=%async_computation.3 | async-start | bytes 8912896 | tf_op jit(solution)/shard_map/reduce_scatter | solution.py:549
  13.9 9.9 %copy-start.110 = (f32[16]{0:T(128)S(1)}, f32[16]{0:T(128)}, u32[]{:S(2)}) copy-start(f32[16]{0:T(128)} %param.30) | copy-start | bytes 196
  15.7 11.6 %copy-start.103 = (f32[4,256]{1,0:T(4,128)S(1)}, f32[4,256]{1,0:T(4,128)}, u32[]{:S(2)}) copy-start(f32[4,256]{1,0:T(4,128)} %param.26) | copy-start | bytes 12292
  19.4 16.1 %copy-start.50 = (f32[2,8,8,128]{3,2,1,0:T(8,128)}, f32[2,8,8,128]{3,2,1,0:T(8,128)S(1)}, u32[]{:S(2)}) copy-start(f32[2,8,8,128]{3,2,1,0:T(8,128)S(1)} %copy.202) | copy-start | bytes 196612
  19.4 16.0 %copy-start.52 = (f32[2,8,8,128]{3,2,1,0:T(8,128)}, f32[2,8,8,128]{3,2,1,0:T(8,128)S(1)}, u32[]{:S(2)}) copy-start(f32[2,8,8,128]{3,2,1,0:T(8,128)S(1)} %copy.204) | copy-start | bytes 196612
  27.2 8.3 %copy-start.2 = (f32[8,8,2,8,128]{4,2,0,1,3:T(2,128)}, f32[8,8,2,8,128]{4,2,0,1,3:T(2,128)S(1)}, u32[]{:S(2)}) copy-start(f32[8,8,2,8,128]{4,2,0,1,3:T(2,128)S(1)} %get-tuple-element.225) | copy-start | bytes 1572868
  27.3 8.2 %copy-start.75 = (f32[1,256]{1,0:T(1,128)}, f32[1,256]{1,0:T(1,128)S(1)}, u32[]{:S(2)}) copy-start(f32[1,256]{1,0:T(1,128)S(1)} %get-tuple-element.229) | copy-start | bytes 3076
  27.3 8.2 %copy-start.77 = (f32[1,256]{1,0:T(1,128)}, f32[1,256]{1,0:T(1,128)S(1)}, u32[]{:S(2)}) copy-start(f32[1,256]{1,0:T(1,128)S(1)} %get-tuple-element.231) | copy-start | bytes 3076
  27.3 8.2 %copy-start.80 = (f32[1,256]{1,0:T(1,128)}, f32[1,256]{1,0:T(1,128)S(1)}, u32[]{:S(2)}) copy-start(f32[1,256]{1,0:T(1,128)S(1)} %get-tuple-element.230) | copy-start | bytes 3076
  27.3 8.2 %copy-start.83 = (f32[1,256]{1,0:T(1,128)}, f32[1,256]{1,0:T(1,128)S(1)}, u32[]{:S(2)}) copy-start(f32[1,256]{1,0:T(1,128)S(1)} %get-tuple-element.232) | copy-start | bytes 3076
  28.3 7.3 %copy-start.67 = (f32[1024]{0:T(1024)}, f32[1024]{0:T(1024)S(1)}, u32[]{:S(2)}) copy-start(f32[1024]{0:T(1024)S(1)} %get-tuple-element.233) | copy-start | bytes 12292
  28.3 7.3 %copy-start.69 = (f32[1024]{0:T(1024)}, f32[1024]{0:T(1024)S(1)}, u32[]{:S(2)}) copy-start(f32[1024]{0:T(1024)S(1)} %get-tuple-element.255) | copy-start | bytes 12292
  36.7 6.8 %copy-start.27 = (bf16[1024,1024]{1,0:T(8,128)(2,1)S(1)}, bf16[1024,1024]{1,0:T(8,128)(2,1)}, u32[]{:S(2)}) copy-start(bf16[1024,1024]{1,0:T(8,128)(2,1)} %copy-done.26) | copy-start | bytes 6291460
  36.7 6.8 %copy-start.113 = (bf16[1024,1024]{1,0:T(8,128)(2,1)S(1)}, bf16[1024,1024]{1,0:T(8,128)(2,1)}, u32[]{:S(2)}) copy-start(bf16[1024,1024]{1,0:T(8,128)(2,1)} %param.21) | copy-start | bytes 6291460
  48.0 6.6 %copy-start.7 = (bf16[128,1024]{1,0:T(8,128)(2,1)S(1)}, bf16[128,1024]{1,0:T(8,128)(2,1)}, u32[]{:S(2)}) copy-start(bf16[128,1024]{1,0:T(8,128)(2,1)} %get-tuple-element.172.outt_ref) | copy-start | bytes 786436
  54.7 30.6 %copy-start.23 = (bf16[1024,1024]{1,0:T(8,128)(2,1)S(1)}, bf16[1024,1024]{1,0:T(8,128)(2,1)}, u32[]{:S(2)}) copy-start(bf16[1024,1024]{1,0:T(8,128)(2,1)} %copy-done.22) | copy-start | bytes 6291460
  54.7 30.6 %copy-start.111 = (bf16[1024,1024]{1,0:T(8,128)(2,1)S(1)}, bf16[1024,1024]{1,0:T(8,128)(2,1)}, u32[]{:S(2)}) copy-start(bf16[1024,1024]{1,0:T(8,128)(2,1)} %param.20) | copy-start | bytes 6291460
  81.6 8.0 %copy-start.11 = (bf16[8,1024,128]{2,1,0:T(8,128)(2,1)}, bf16[8,1024,128]{2,1,0:T(8,128)(2,1)S(1)}, u32[]{:S(2)}) copy-start(bf16[8,1024,128]{2,1,0:T(8,128)(2,1)S(1)} %get-tuple-element.47.entry_ref) | copy-start | bytes 6291460
  82.3 7.4 %copy-start.114 = (bf16[1024,1024]{1,0:T(8,128)(2,1)S(1)}, bf16[1024,1024]{1,0:T(8,128)(2,1)}, u32[]{:S(2)}) copy-start(bf16[1024,1024]{1,0:T(8,128)(2,1)} %param.21) | copy-start | bytes 6291460
  82.3 49.4 %collective-permute-start.2 = (f32[2,1024]{1,0:T(2,128)}, f32[2,1024]{1,0:T(2,128)}, u32[]{:S(2)}, u32[]{:S(2)}) collective-permute-start(f32[2,1024]{1,0:T(2,128)} %slice_bitcast_fusion.2), channel_id=1, source_target_pairs={{0,1},{1,0},{2,3},{3,2},{4,5},{5,4},{6,7},{7,6},{8,9},{9,8},{10,11... | collective-permute-start | bytes 24584 | tf_op jit(solution)/shard_map/ppermute | solution.py:443
  105.0 30.3 %copy-start.31 = (f32[1024,1024]{1,0:T(8,128)S(1)}, f32[1024,1024]{1,0:T(8,128)}, u32[]{:S(2)}) copy-start(f32[1024,1024]{1,0:T(8,128)} %get-tuple-element.38.mixed_ref) | copy-start | bytes 12582916
  105.0 30.3 %copy-start.74 = (f32[1024]{0:T(1024)S(1)}, f32[1024]{0:T(1024)}, u32[]{:S(2)}) copy-start(f32[1024]{0:T(1024)} %param.31) | copy-start | bytes 12292
  131.6 28.3 %copy-start.12 = (bf16[8,1024,128]{2,1,0:T(8,128)(2,1)}, bf16[8,1024,128]{2,1,0:T(8,128)(2,1)S(1)}, u32[]{:S(2)}) copy-start(bf16[8,1024,128]{2,1,0:T(8,128)(2,1)S(1)} %get-tuple-element.41.entry_ref) | copy-start | bytes 6291460
  131.6 3.7 collective-permute-start
  135.3 24.5 %copy-start.24 = (bf16[1024,1024]{1,0:T(8,128)(2,1)S(1)}, bf16[1024,1024]{1,0:T(8,128)(2,1)}, u32[]{:S(2)}) copy-start(bf16[1024,1024]{1,0:T(8,128)(2,1)} %copy-done.22) | copy-start | bytes 6291460
  135.4 24.5 %copy-start.28 = (bf16[1024,1024]{1,0:T(8,128)(2,1)S(1)}, bf16[1024,1024]{1,0:T(8,128)(2,1)}, u32[]{:S(2)}) copy-start(bf16[1024,1024]{1,0:T(8,128)(2,1)} %copy-done.26) | copy-start | bytes 6291460
  175.2 327.2 %reduce-scatter.10.cloned.1.call-start = ((), (), s32[]{:S(2)}) async-start(), calls=%async_computation.6 | async-start | bytes 1671168
  184.1 6.6 %copy-start.4 = (f32[8,8,2,8,128]{4,2,0,1,3:T(2,128)S(1)}, f32[8,8,2,8,128]{4,2,0,1,3:T(2,128)}, u32[]{:S(2)}) copy-start(f32[8,8,2,8,128]{4,2,0,1,3:T(2,128)} %broadcast_dynamic-update-slice_fusion.1) | copy-start | bytes 1572868
  184.1 6.6 %copy-start.6 = (bf16[1024,128]{1,0:T(8,128)(2,1)S(1)}, bf16[1024,128]{1,0:T(8,128)(2,1)}, u32[]{:S(2)}) copy-start(bf16[1024,128]{1,0:T(8,128)(2,1)} %copy.148.into_ref) | copy-start | bytes 786436
  184.1 6.6 %copy-start.10 = (bf16[128,1024]{1,0:T(8,128)(2,1)S(1)}, bf16[128,1024]{1,0:T(8,128)(2,1)}, u32[]{:S(2)}) copy-start(bf16[128,1024]{1,0:T(8,128)(2,1)} %get-tuple-element.178.outt_ref) | copy-start | bytes 786436
  184.1 6.6 %copy-start.14 = (bf16[128,1024]{1,0:T(8,128)(2,1)S(1)}, bf16[128,1024]{1,0:T(8,128)(2,1)}, u32[]{:S(2)}) copy-start(bf16[128,1024]{1,0:T(8,128)(2,1)} %get-tuple-element.177.intot_ref) | copy-start | bytes 786436
  184.1 93.9 %collective-permute-start.1 = (f32[1024,1024]{1,0:T(8,128)}, f32[1024,1024]{1,0:T(8,128)}, u32[]{:S(2)}, u32[]{:S(2)}) collective-permute-start(f32[1024,1024]{1,0:T(8,128)} %fusion.115), channel_id=1, source_target_pairs={{0,1},{1,0},{2,3},{3,2},{4,5},{5,4},{6,7},{7,6},{8,9},{9,8},{10,11... | collective-permute-start | bytes 12582920 | tf_op jit(solution)/shard_map/ppermute | solution.py:443
  188.7 179.2 %collective-permute-start.3 = (f32[1024,1024]{1,0:T(8,128)}, f32[1024,1024]{1,0:T(8,128)}, u32[]{:S(2)}, u32[]{:S(2)}) collective-permute-start(f32[1024,1024]{1,0:T(8,128)} %fusion.117), channel_id=1, source_target_pairs={{0,1},{1,0},{2,3},{3,2},{4,5},{5,4},{6,7},{7,6},{8,9},{9,8},{10,11... | collective-permute-start | bytes 12582920 | tf_op jit(solution)/shard_map/ppermute | solution.py:443
  190.7 43.4 %copy-start.97 = (f32[16]{0:T(128)S(1)}, f32[16]{0:T(128)}, u32[]{:S(2)}) copy-start(f32[16]{0:T(128)} %copy-done.96) | copy-start | bytes 196
  232.2 6.5 %copy-start.58 = (f32[16,1024]{1,0:T(8,128)S(1)}, f32[16,1024]{1,0:T(8,128)}, u32[]{:S(2)}) copy-start(f32[16,1024]{1,0:T(8,128)} %copy-done.57) | copy-start | bytes 196612
  234.1 8.5 %copy-start.87 = (f32[1024]{0:T(1024)S(1)}, f32[1024]{0:T(1024)}, u32[]{:S(2)}) copy-start(f32[1024]{0:T(1024)} %get-tuple-element.151) | copy-start | bytes 12292
  234.1 8.5 %copy-start.88 = (f32[1024]{0:T(1024)S(1)}, f32[1024]{0:T(1024)}, u32[]{:S(2)}) copy-start(f32[1024]{0:T(1024)} %get-tuple-element.215) | copy-start | bytes 12292
  234.1 9.1 %copy-start.19 = (f32[1024,256]{0,1:T(8,128)S(1)}, f32[1024,256]{0,1:T(8,128)}, u32[]{:S(2)}) copy-start(f32[1024,256]{0,1:T(8,128)} %fusion.114) | copy-start | bytes 3145732
  234.1 9.1 %copy-start.70 = (f32[1024]{0:T(1024)S(1)}, f32[1024]{0:T(1024)}, u32[]{:S(2)}) copy-start(f32[1024]{0:T(1024)} %copy-done.69) | copy-start | bytes 12292
  257.8 20.2 %copy-start.8 = (bf16[128,1024]{1,0:T(8,128)(2,1)S(1)}, bf16[128,1024]{1,0:T(8,128)(2,1)}, u32[]{:S(2)}) copy-start(bf16[128,1024]{1,0:T(8,128)(2,1)} %get-tuple-element.172.outt_ref) | copy-start | bytes 786436
  257.8 20.2 %copy-start.13 = (bf16[128,1024]{1,0:T(8,128)(2,1)S(1)}, bf16[128,1024]{1,0:T(8,128)(2,1)}, u32[]{:S(2)}) copy-start(bf16[128,1024]{1,0:T(8,128)(2,1)} %get-tuple-element.171.intot_ref) | copy-start | bytes 786436
  278.0 41.9 %copy-start.51 = (f32[2,8,8,128]{3,2,1,0:T(8,128)S(1)}, f32[2,8,8,128]{3,2,1,0:T(8,128)}, u32[]{:S(2)}) copy-start(f32[2,8,8,128]{3,2,1,0:T(8,128)} %copy-done.50) | copy-start | bytes 196612
  278.0 41.9 %copy-start.53 = (f32[2,8,8,128]{3,2,1,0:T(8,128)S(1)}, f32[2,8,8,128]{3,2,1,0:T(8,128)}, u32[]{:S(2)}) copy-start(f32[2,8,8,128]{3,2,1,0:T(8,128)} %copy-done.52) | copy-start | bytes 196612
  278.0 43.7 %copy-start.56 = (f32[16,1024]{1,0:T(8,128)S(1)}, f32[16,1024]{1,0:T(8,128)}, u32[]{:S(2)}) copy-start(f32[16,1024]{1,0:T(8,128)} %copy-done.55) | copy-start | bytes 196612
  319.8 135.3 %collective-permute-start.4 = (f32[1024,1024]{1,0:T(8,128)}, f32[1024,1024]{1,0:T(8,128)}, u32[]{:S(2)}, u32[]{:S(2)}) collective-permute-start(f32[1024,1024]{1,0:T(8,128)} %add_add_fusion.1), channel_id=1, source_target_pairs={{0,1},{1,0},{2,3},{3,2},{4,5},{5,4},{6,7},{7,6},{8,9},{9,8},{10,11... | collective-permute-start | bytes 12582920 | tf_op jit(solution)/shard_map/ppermute | solution.py:443
  334.6 192.0 %all-reduce.26.cloned.1.call-start = ((), (), s32[]{:S(2)}) async-start(), calls=%async_computation.5 | async-start | bytes 262144 | tf_op jit(solution)/shard_map/psum | solution.py:633
  334.8 6.8 %copy-start.106 = (pred[2]{0:T(512)(128)(4,1)S(1)}, pred[2]{0:T(512)(128)(4,1)}, u32[]{:S(2)}) copy-start(pred[2]{0:T(512)(128)(4,1)} %iota_compare_fusion.2) | copy-start | bytes 10
  334.8 6.9 %copy-start.98 = (f32[256]{0:T(256)S(1)}, f32[256]{0:T(256)}, u32[]{:S(2)}) copy-start(f32[256]{0:T(256)} %get-tuple-element.120) | copy-start | bytes 3076
  334.8 6.9 %copy-start.100 = (f32[256]{0:T(256)S(1)}, f32[256]{0:T(256)}, u32[]{:S(2)}) copy-start(f32[256]{0:T(256)} %get-tuple-element.123) | copy-start | bytes 3076
  334.8 6.9 %copy-start.101 = (f32[256]{0:T(256)S(1)}, f32[256]{0:T(256)}, u32[]{:S(2)}) copy-start(f32[256]{0:T(256)} %get-tuple-element.164) | copy-start | bytes 3076
  334.8 6.9 %copy-start.102 = (f32[256]{0:T(256)S(1)}, f32[256]{0:T(256)}, u32[]{:S(2)}) copy-start(f32[256]{0:T(256)} %get-tuple-element.113) | copy-start | bytes 3076
  334.8 7.0 %copy-start.34 = (bf16[1024,256]{1,0:T(8,128)(2,1)S(1)}, bf16[1024,256]{1,0:T(8,128)(2,1)}, u32[]{:S(2)}) copy-start(bf16[1024,256]{1,0:T(8,128)(2,1)} %param.22) | copy-start | bytes 1572868
  334.8 7.0 %copy-start.47 = (bf16[1024,256]{0,1:T(8,128)(2,1)S(1)}, bf16[1024,256]{0,1:T(8,128)(2,1)}, u32[]{:S(2)}) copy-start(bf16[1024,256]{0,1:T(8,128)(2,1)} %copy-done.46) | copy-start | bytes 1572868
  344.1 7.8 %copy-start.99 = (f32[256]{0:T(256)S(1)}, f32[256]{0:T(256)}, u32[]{:S(2)}) copy-start(f32[256]{0:T(256)} %get-tuple-element.112) | copy-start | bytes 3076
  495.3 95.2 %collective-permute-start.5 = (f32[1024,1024]{1,0:T(8,128)}, f32[1024,1024]{1,0:T(8,128)}, u32[]{:S(2)}, u32[]{:S(2)}) collective-permute-start(f32[1024,1024]{1,0:T(8,128)} %get-tuple-element.54), channel_id=1, source_target_pairs={{0,1},{1,0},{2,3},{3,2},{4,5},{5,4},{6,7},{7,6},{8,9},{9,8},{10,11... | collective-permute-start | bytes 12582920 | tf_op jit(solution)/shard_map/ppermute | solution.py:443
  504.0 116.3 %reduce-scatter.8.cloned.1.call-start = ((), (), s32[]{:S(2)}) async-start(), calls=%async_computation.4 | async-start | bytes 4456448 | tf_op jit(solution)/shard_map/reduce_scatter | solution.py:600
  513.4 17.9 %copy-start.60 = (f32[2,64,1024]{2,1,0:T(8,128)S(1)}, f32[2,64,1024]{2,1,0:T(8,128)}, u32[]{:S(2)}) copy-start(f32[2,64,1024]{2,1,0:T(8,128)} %reduce-scatter.6.cloned.1.call-done) | copy-start | bytes 1572868
  513.4 77.2 %copy-start.72 = (f32[1024]{0:T(1024)S(1)}, f32[1024]{0:T(1024)}, u32[]{:S(2)}) copy-start(f32[1024]{0:T(1024)} %param.19) | copy-start | bytes 12292
  532.2 69.0 %copy-start.17 = (bf16[2,1024,1024]{2,1,0:T(8,128)(2,1)S(1)}, bf16[2,1024,1024]{2,1,0:T(8,128)(2,1)}, u32[]{:S(2)}) copy-start(bf16[2,1024,1024]{2,1,0:T(8,128)(2,1)} %param.17) | copy-start | bytes 12582916
  532.2 69.0 %copy-start.20 = (f32[1024,1024]{1,0:T(8,128)S(1)}, f32[1024,1024]{1,0:T(8,128)}, u32[]{:S(2)}) copy-start(f32[1024,1024]{1,0:T(8,128)} %add_add_fusion.1) | copy-start | bytes 12582916
  532.2 69.0 %copy-start.21 = (f32[1024,1024]{1,0:T(8,128)S(1)}, f32[1024,1024]{1,0:T(8,128)}, u32[]{:S(2)}) copy-start(f32[1024,1024]{1,0:T(8,128)} %get-tuple-element.54) | copy-start | bytes 12582916
  532.2 69.1 %copy-start.90 = (f32[1024]{0:T(1024)S(1)}, f32[1024]{0:T(1024)}, u32[]{:S(2)}) copy-start(f32[1024]{0:T(1024)} %get-tuple-element.220) | copy-start | bytes 12292
  532.2 69.1 %copy-start.91 = (f32[1024]{0:T(1024)S(1)}, f32[1024]{0:T(1024)}, u32[]{:S(2)}) copy-start(f32[1024]{0:T(1024)} %get-tuple-element.250) | copy-start | bytes 12292
  (64 other events, 209.4 us)
Sparse Core Ops, SparseCore 0:
  175.3 104.9 reduce-scatter.5
  334.7 61.1 reduce-scatter.9
  504.2 22.3 all-reduce.25
  531.3 72.3 reduce-scatter.7

commit v2 on v1

--- a/solution.py
+++ b/solution.py
@@ -411,6 +411,47 @@
     )
 
 
+def finish_kernel(
+    part_ref, other_ref, branch_ref, received_ref, hidden_ref, cotangent_ref, gain_ref, *rest
+):
+    out_ref, grad_ref = rest[-2:]
+    wide = hidden_ref[0].astype(jnp.float32)
+    width = wide.shape[1]
+    row_scale = lax.rsqrt(jnp.mean(wide * wide, axis=-1, keepdims=True) + epsilon)
+    scaled = (part_ref[...] + other_ref[...]) * gain_ref[...]
+    inner = jnp.sum(scaled * wide, axis=-1, keepdims=True)
+    grad_ref[0] = (
+        cotangent_ref[0].astype(jnp.float32)
+        + row_scale * scaled
+        - wide * (row_scale * row_scale * row_scale * inner / width)
+    )
+    out_ref[0] = (wide + (branch_ref[...] + received_ref[...])).astype(bf16)
+
+
+def finish(s, part, other, branch, received, hidden, out_grad, norm_gain, earlier):
+    seqs, length, width = hidden.shape
+    tile = 256
+    flat = spec((tile, width), lambda i: (i, 0))
+    deep = spec((1, tile, width), lambda i: (s, i, 0))
+    held = [pl.BlockSpec(memory_space=pl.ANY)] * len(earlier)
+    return pl.pallas_call(
+        finish_kernel,
+        grid=(length // tile,),
+        in_specs=[flat] * 4 + [deep, deep, spec((1, width), lambda i: (0, 0))] + held,
+        out_specs=[deep, deep],
+        out_shape=[
+            jax.ShapeDtypeStruct((seqs, length, width), bf16),
+            jax.ShapeDtypeStruct((seqs, length, width), jnp.float32),
+        ],
+        input_output_aliases={7 + i: i for i in range(len(earlier))},
+        compiler_params=pltpu.CompilerParams(vmem_limit_bytes=VMEM_BYTES),
+        cost_estimate=pl.CostEstimate(
+            flops=length * width * 20, bytes_accessed=length * width * 26, transcendentals=0
+        ),
+        name="finish",
+    )(part, other, branch, received, hidden, out_grad, norm_gain[None, :], *earlier)
+
+
 def out_product(left, weight):
     return lax.dot_general(left, weight, (((0,), (1,)), ((), ())), preferred_element_type=jnp.float32)
 
@@ -448,8 +489,117 @@
     return part + others if lax.axis_size("tensor") == 2 else others
 
 
+def only_others(part, others):
+    return others if lax.axis_size("tensor") == 2 else others - part
+
+
 def after(value, *earlier):
     return lax.optimization_barrier((value, *earlier))[0]
+
+
+def assemble_kernel(quarter_ref, first_ref, second_ref, third_ref, fourth_ref, whole_ref):
+    rows = first_ref.shape[0]
+    pieces = (first_ref, second_ref, third_ref, fourth_ref)
+    for piece_ref, flip in zip(pieces, (0, 2, 1, 3)):
+        place = jnp.bitwise_xor(quarter_ref[0], flip)
+        part = pl.ds(pl.multiple_of(place * rows, rows), rows)
+        whole_ref[part, :] = piece_ref[...].astype(whole_ref.dtype)
+
+
+def gather_first(weight):
+    rows, columns = weight.shape[0] // 4, weight.shape[1]
+    quarter = lax.rem(lax.axis_index("dp"), 4)
+    mine = lax.dynamic_slice(weight, (quarter * rows, 0), (rows, columns))
+    mine = lax.optimization_barrier(mine.astype(jnp.float32))
+    return lax.ppermute(mine, "tensor", [(0, 1), (1, 0)])
+
+
+def along_dp(piece, flip):
+    return lax.ppermute(piece, "dp", [(j, j ^ flip) for j in range(lax.axis_size("dp"))])
+
+
+def assemble(weight, *pieces):
+    quarter = lax.rem(lax.axis_index("dp"), 4)
+    return pl.pallas_call(
+        assemble_kernel,
+        in_specs=[pl.BlockSpec(memory_space=pltpu.SMEM)]
+        + [pl.BlockSpec(memory_space=pltpu.VMEM)] * 4,
+        out_specs=pl.BlockSpec(memory_space=pltpu.VMEM),
+        out_shape=jax.ShapeDtypeStruct(weight.shape, weight.dtype),
+        compiler_params=pltpu.CompilerParams(vmem_limit_bytes=VMEM_BYTES),
+        cost_estimate=pl.CostEstimate(
+            flops=weight.size, bytes_accessed=6 * weight.size, transcendentals=0
+        ),
+        name="assemble",
+    )(quarter.reshape(1), *pieces)
+
+
+def swap_small(arrays):
+    flat = jnp.concatenate([a.astype(jnp.float32).reshape(-1) for a in arrays])
+    flat = lax.ppermute(lax.optimization_barrier(flat), "tensor", [(0, 1), (1, 0)])
+    flat = lax.optimization_barrier(flat)
+    result, edge = [], 0
+    for a in arrays:
+        result.append(flat[edge : edge + a.size].reshape(a.shape).astype(a.dtype))
+        edge += a.size
+    return result
+
+
+def unit_forward(weights, normed, cotangent, segments, states):
+    step = in_product(weights["step"], normed)
+    gate = in_product(weights["gate"], normed)
+    raw = in_product(weights["value"], normed)
+    dout = in_product(weights["out"], cotangent)
+    rows, masks = step_rows(
+        step, weights["step_bias"], weights["decay_log"], weights["skip_gain"], segments
+    )
+    into, _, _, outt = states
+    mixed, entry, sums = mix_forward(
+        1, raw, gate, dout, rows, masks, into, outt, weights["conv"], weights["gain_wide"]
+    )
+    sums = sums[:, :2].transpose(1, 0, 2).reshape(2, normed.shape[0])
+    return dict(
+        step=step, gate=gate, raw=raw, dout=dout, rows=rows, masks=masks, mixed=mixed,
+        entry=entry, sums=sums, states=states,
+    )
+
+
+def unit_middle(unit, weights, both, inner_total):
+    gate, mixed, dout = unit["gate"], unit["mixed"], unit["dout"]
+    gain = weights["gate_gain"][:, None]
+    sigma = sigmoid(gate)
+    gated = mixed * gate * sigma
+    gated_scale = lax.rsqrt(both[0:1] / inner_total + epsilon)
+    output_in = (gated * gated_scale * gain).astype(bf16)
+    d_gated = gated_scale * (dout * gain) - gated * (
+        gated_scale**3 * both[1:2] / inner_total
+    )
+    d_mixed = (d_gated * gate * sigma).astype(bf16)
+    d_gate = (d_gated * mixed * sigma * (1.0 + gate * (1.0 - sigma))).astype(bf16)
+    grad_gain = jnp.sum(dout * gated * gated_scale, axis=1)
+    return output_in, d_gate, d_mixed, grad_gain
+
+
+def unit_backward(unit, weights, d_gate, d_mixed, state_back):
+    d_value, d_rows, d_state, d_conv = mix_backward(
+        1, unit["raw"], unit["mixed"], d_mixed, unit["entry"], unit["rows"], unit["masks"],
+        *unit["states"], weights["conv"],
+    )
+    d_step, *step_params = step_grads(
+        d_rows, unit["step"], weights["step_bias"], weights["decay_log"], 1
+    )
+    d_state, g_cs, g_csb = state_back(d_state.astype(bf16).astype(jnp.float32))
+    d_state, d_step = d_state.astype(bf16), d_step.astype(bf16)
+    return d_value, d_state, d_step, (d_conv, g_cs, g_csb, *step_params)
+
+
+def normed_part(weights, d_gate, d_value, d_state, d_step):
+    return (
+        out_product(d_gate, weights["gate"])
+        + out_product(d_value, weights["value"])
+        + right_product(d_state, weights["state"])
+        + out_product(d_step, weights["step"])
+    )
 
 
 def local(
@@ -477,24 +627,33 @@
     tensor_count = lax.axis_size("tensor")
     inner_total = local_inner * tensor_count
     every = range(seq_count)
-
-    wides = [hidden[s].astype(jnp.float32) for s in every]
-    row_scales = [
-        lax.rsqrt(jnp.mean(w * w, axis=-1, keepdims=True) + epsilon) for w in wides
-    ]
-    normeds = [
-        (w * r * norm_gain[None, :]).astype(jnp.bfloat16) for w, r in zip(wides, row_scales)
-    ]
-    conv_wide = wide_lanes(jnp.concatenate([conv_value, conv_value_bias[None, :]], axis=0))
-    gain_wide = wide_lanes(gate_gain)
-
-    gates, douts, raws, steps, rows, masks, states = [], [], [], [], [], [], []
-    state_backs, mixeds, entries, boths = [], [], [], []
+    whole_from = seq_count
+    if tensor_count == 2 and lax.axis_size("dp") % 4 == 0 and seq_count > 1:
+        whole_from = seq_count - 1
+
+    own = dict(
+        gate=proj_gate, value=proj_value, out=proj_out, state=proj_state, step=proj_step,
+        step_bias=step_bias, decay_log=decay_log, skip_gain=skip_gain, gate_gain=gate_gain,
+    )
+    own["conv"] = wide_lanes(jnp.concatenate([conv_value, conv_value_bias[None, :]], axis=0))
+    own["gain_wide"] = wide_lanes(gate_gain)
+    if whole_from < seq_count:
+        c_w, c_b, step, s_b, d_l, s_g, g_g = swap_small(
+            [conv_value, conv_value_bias, proj_step, step_bias, decay_log, skip_gain, gate_gain]
+        )
+        other = dict(
+            state=proj_state, step=step, step_bias=s_b, decay_log=d_l, skip_gain=s_g, gate_gain=g_g
+        )
+        sent = dict(value=proj_value, gate=proj_gate, out=proj_out)
+        first = {k: gather_first(w) for k, w in sent.items()}
+        other["conv"] = wide_lanes(jnp.concatenate([c_w, c_b[None, :]], axis=0))
+        other["gain_wide"] = wide_lanes(g_g)
+
+    normeds, states, state_backs, units, boths = [], [], [], [], []
     for s in every:
-        gates.append(in_product(proj_gate, normeds[s]))
-        raws.append(in_product(proj_value, normeds[s]))
-        steps.append(in_product(proj_step, normeds[s]))
-        douts.append(in_product(proj_out, out_grad[s]))
+        wide = hidden[s].astype(jnp.float32)
+        row_scale = lax.rsqrt(jnp.mean(wide * wide, axis=-1, keepdims=True) + epsilon)
+        normeds.append((wide * row_scale * norm_gain[None, :]).astype(bf16))
         state_raw = jnp.dot(normeds[s], proj_state, preferred_element_type=jnp.float32)
         state_conv, back = jax.vjp(
             functools.partial(causal_conv, doc_masks=lag_masks(segment_ids[s])),
@@ -503,39 +662,42 @@
             conv_state_bias,
         )
         state_backs.append(back)
-        low = state_conv.astype(jnp.bfloat16)
+        low = state_conv.astype(bf16)
         into, out = low[:, :STATE], low[:, STATE:]
         states.append((into, into.T, out, out.T))
-        row, mask = step_rows(steps[s], step_bias, decay_log, skip_gain, segment_ids[s : s + 1])
-        rows.append(row)
-        masks.append(mask)
-        mixed, entry, sums = mix_forward(
-            1, raws[s], gates[s], douts[s], row, mask, into, out.T, conv_wide, gain_wide
-        )
-        mixeds.append(mixed)
-        entries.append(entry)
-        sums = sums[:, :2].transpose(1, 0, 2).reshape(2, length)
-        boths.append(tensor_join(sums, tensor_others(sums)))
-
+        units.append(unit_forward(own, normeds[s], out_grad[s], segment_ids[s : s + 1], states[s]))
+        if s < whole_from:
+            sums = units[s]["sums"]
+            boths.append(tensor_join(sums, tensor_others(sums)))
     branches, received, output_ins, d_gates, d_mixeds = [], [], [], [], []
     grad_gate_gain = jnp.zeros((local_inner,), jnp.float32)
+    extras, middles = {}, {}
+    if whole_from < seq_count:
+        second = {k: along_dp(after(first[k], units[0]["mixed"]), 2) for k in sent}
+        third = {k: along_dp(first[k], 1) for k in sent}
+        fourth = {k: along_dp(after(second[k], units[-1]["mixed"]), 1) for k in sent}
     for s in every:
-        gate, mixed, dout = gates[s], mixeds[s], douts[s]
-        sigma = jax.nn.sigmoid(gate)
-        gated = mixed * gate * sigma
-        gated_scale = lax.rsqrt(boths[s][0:1] / inner_total + epsilon)
-        gate_inner = boths[s][1:2]
-        output_in = (gated * gated_scale * gate_gain[:, None]).astype(jnp.bfloat16)
-        branches.append(out_product(output_in, proj_out))
-        received.append(tensor_others(branches[s]))
-        grad_gate_gain = grad_gate_gain + jnp.sum(dout * gated * gated_scale, axis=1)
-        weighted = dout * gate_gain[:, None]
-        d_gated = gated_scale * weighted - gated_scale**3 * gated * gate_inner / inner_total
-        d_mixeds.append((d_gated * gate * sigma).astype(jnp.bfloat16))
-        d_gates.append(
-            (d_gated * mixed * sigma * (1.0 + gate * (1.0 - sigma))).astype(jnp.bfloat16)
-        )
+        if s == whole_from:
+            for k in sent:
+                pieces = (first[k], second[k], third[k], fourth[k])
+                pieces = lax.optimization_barrier((*pieces, branches[0]))[:4]
+                other[k] = assemble(sent[k], *pieces)
+        if s >= whole_from:
+            extras[s] = unit_forward(
+                other, normeds[s], out_grad[s], segment_ids[s : s + 1], states[s]
+            )
+            boths.append(units[s]["sums"] + extras[s]["sums"])
+            middles[s] = unit_middle(extras[s], other, boths[s], inner_total)
+        output_in, d_gate, d_mixed, grad_gain = unit_middle(units[s], own, boths[s], inner_total)
+        grad_gate_gain = grad_gate_gain + grad_gain
         output_ins.append(output_in)
+        d_gates.append(d_gate)
+        d_mixeds.append(d_mixed)
+        branches.append(lax.optimization_barrier(out_product(output_in, proj_out)))
+        if s < whole_from:
+            received.append(tensor_others(branches[s]))
+        else:
+            received.append(lax.optimization_barrier(out_product(middles[s][0], other["out"])))
 
     normed_all = jnp.concatenate(normeds, axis=0)
     early_part = jnp.stack(
@@ -548,89 +710,60 @@
     )
     early = lax.psum_scatter(early_part, "dp", scatter_dimension=1, tiled=True)
 
-    param_grads, d_values, d_states, d_steps = None, [], [], []
-    parts, others, grad_hiddens = [], [], []
+    backs, parts, others = [], [], []
     waits = (early_part, *branches)
+    for s in every:
+        back = unit_backward(units[s], own, d_gates[s], after(d_mixeds[s], *waits), state_backs[s])
+        backs.append(back)
+        parts.append(lax.optimization_barrier(normed_part(own, d_gates[s], *back[:3])))
+        if s < whole_from:
+            others.append(tensor_others(after(parts[s], received[s])))
+            waits = (parts[s],)
+    later_part = jnp.concatenate(
+        [
+            grad_product(normed_all, jnp.concatenate([b[0] for b in backs], axis=1)),
+            token_product(normed_all, jnp.concatenate([b[1] for b in backs], axis=0)),
+            grad_product(normed_all, jnp.concatenate([b[2] for b in backs], axis=1)),
+        ],
+        axis=1,
+    )
+    later_part = after(later_part, early)
+    later = lax.psum_scatter(later_part, "dp", scatter_dimension=0, tiled=True)
+    later_value = later[:, :local_inner]
+    edge = local_inner + state_width
+    state_part = later[:, local_inner:edge]
+    grad_proj_state = tensor_join(state_part, tensor_others(state_part))
+    waits = (later_part,)
     grad_norm_gain = jnp.zeros((width,), jnp.float32)
     for s in every:
-        d_value, d_rows, d_state, d_conv = mix_backward(
-            1, raws[s], mixeds[s], after(d_mixeds[s], *waits), entries[s], rows[s], masks[s],
-            *states[s], conv_wide,
+        wide = hidden[s].astype(jnp.float32)
+        row_scale = lax.rsqrt(jnp.mean(wide * wide, axis=-1, keepdims=True) + epsilon)
+        grad_norm_gain = grad_norm_gain + jnp.sum(parts[s] * wide * row_scale, axis=0)
+    for s in range(whole_from, seq_count):
+        d_gate = middles[s][1]
+        back = unit_backward(extras[s], other, d_gate, after(middles[s][2], *waits), state_backs[s])
+        others.append(lax.optimization_barrier(normed_part(other, d_gate, *back[:3])))
+
+    stacked = ()
+    for s in reversed(every):
+        stacked = finish(
+            s, parts[s], only_others(parts[s], others[s]), branches[s],
+            only_others(branches[s], received[s]), hidden, out_grad, norm_gain, stacked
         )
-        d_step, g_sb, g_dl, g_sg = step_grads(d_rows, steps[s], step_bias, decay_log, 1)
-        d_state = d_state.astype(jnp.bfloat16).astype(jnp.float32)
-        d_state, g_cs, g_csb = state_backs[s](d_state)
-        d_conv = jnp.sum(d_conv, axis=-1)
-        grads = (d_conv[:KERNEL], d_conv[KERNEL], g_cs, g_csb, g_sb, g_dl, g_sg)
-        param_grads = grads if s == 0 else [a + b for a, b in zip(param_grads, grads)]
-        d_values.append(d_value)
-        d_states.append(d_state.astype(jnp.bfloat16))
-        d_steps.append(d_step.astype(jnp.bfloat16))
-        part = (
-            out_product(d_gates[s], proj_gate)
-            + out_product(d_value, proj_value)
-            + right_product(d_states[s], proj_state)
-            + out_product(d_steps[s], proj_step)
-        )
-        grad_norm_gain = grad_norm_gain + jnp.sum(part * wides[s] * row_scales[s], axis=0)
-        parts.append(part)
-        if s < seq_count - 1:
-            parts[s] = after(part, received[s])
-            others.append(tensor_others(parts[s]))
-            waits = (part, received[s])
-    g_cv, g_cvb, g_cs, g_csb, g_sb, g_dl, g_sg = param_grads
-    own = [g_cv, g_cvb, g_sb, g_dl, g_sg, grad_gate_gain]
+    param_grads = [sum(grads) for grads in zip(*[b[3] for b in backs])]
+    d_conv, g_cs, g_csb, g_sb, g_dl, g_sg = param_grads
+    d_conv = jnp.sum(d_conv, axis=-1)
+    own_grads = [d_conv[:KERNEL], d_conv[KERNEL], g_sb, g_dl, g_sg, grad_gate_gain]
     shared = [g_cs, g_csb, grad_norm_gain]
-    own_flat = jnp.concatenate([g.reshape(-1) for g in own])
+    own_flat = jnp.concatenate([g.reshape(-1) for g in own_grads])
     place = lax.axis_index("tensor")
     mine = (jnp.arange(tensor_count) == place)[:, None]
     slots = jnp.where(mine, own_flat[None, :], 0.0).reshape(-1)
-    packed = lax.psum(
-        after(
-            jnp.concatenate([slots] + [g.reshape(-1) for g in shared]),
-            early,
-            received[-1],
-            *others,
-        ),
-        ("dp", "tensor"),
-    )
+    packed = jnp.concatenate([slots] + [g.reshape(-1) for g in shared])
+    packed = jnp.pad(packed, (0, -packed.shape[0] % 16384))
+    packed = lax.psum(after(packed, later), ("dp", "tensor"))
     own_sum = lax.dynamic_slice(packed, (place * own_flat.shape[0],), (own_flat.shape[0],))
     shared_sum = packed[slots.shape[0] :]
-
-    later_value = lax.psum_scatter(
-        grad_product(normed_all, after(jnp.concatenate(d_values, axis=1), packed)),
-        "dp",
-        scatter_dimension=0,
-        tiled=True,
-    )
-    later_rest = lax.psum_scatter(
-        jnp.concatenate(
-            [
-                token_product(normed_all, jnp.concatenate(d_states, axis=0)),
-                grad_product(normed_all, jnp.concatenate(d_steps, axis=1)),
-            ],
-            axis=1,
-        ),
-        "dp",
-        scatter_dimension=0,
-        tiled=True,
-    )
-    block_outs = []
-    for s in every:
-        if s == seq_count - 1:
-            parts[s] = after(parts[s], packed)
-            others.append(tensor_others(parts[s]))
-        d_scaled = tensor_join(parts[s], others[s]) * norm_gain[None, :]
-        row_scale, wide = row_scales[s], wides[s]
-        norm_inner = jnp.sum(d_scaled * wide, axis=-1, keepdims=True)
-        grad_hiddens.append(
-            out_grad[s].astype(jnp.float32)
-            + row_scale * d_scaled
-            - row_scale**3 * wide * norm_inner / width
-        )
-        branch = tensor_join(branches[s], received[s])
-        block_outs.append((wide + branch).astype(jnp.bfloat16))
-    grad_proj_state = lax.psum(later_rest[:, :state_width], "tensor")
 
     def split(flat, like):
         result, edge = [], 0
@@ -639,16 +772,15 @@
             edge += g.size
         return result
 
-    r_cv, r_cvb, r_sb, r_dl, r_sg, r_gg = split(own_sum, own)
+    r_cv, r_cvb, r_sb, r_dl, r_sg, r_gg = split(own_sum, own_grads)
     r_cs, r_csb, r_ng = split(shared_sum, shared)
     return (
-        jnp.stack(block_outs),
-        jnp.stack(grad_hiddens),
+        *stacked,
         r_ng,
         early[0],
         later_value,
         grad_proj_state,
-        later_rest[:, state_width:],
+        later[:, edge:],
         r_cv,
         r_cvb,
         r_cs,

time: 628 us -> 661 us (1.053)
  Pallas kernels: 136 us -> 233 us
  waiting for transfers between devices: 194 us -> 116 us
  blocking collectives: 40.1 us -> 0 us
  matrix products: 97.6 us -> 130 us
  local copies, waits for them, and re-layouts: 37 us -> 63.2 us
  other arithmetic: 99.7 us -> 82.9 us
  starting transfers between devices: 7.66 us -> 15.2 us
    ppermute x6 -> x4, waiting for transfers between devices: 182 us -> 17.7 us  [tensor_others(): return lax.ppermute(part, 'tensor', [(0, 1), (1, 0)])]
    psum x1, waiting for transfers between devices: 11.7 us -> 77.2 us  [local(): packed = lax.psum(after(packed, later), ('dp', 'tensor'))]
    pallas_call x2 -> x3, Pallas kernels: 82.2 us -> 124 us  [mix_backward(): pl.pallas_call(back_kernel, grid=(seqs, chunks), in_specs=[slab, spec((ch...]
    psum x1 -> x0, blocking collectives: 40.1 us -> none  [local(): lax.psum(after(jnp.concatenate([slots] + [g.reshape(-1) for g in shared])...]
    pallas_call x0 -> x5, Pallas kernels: none -> 30.2 us  [the longest x2 20.2 us: finish(): pl.pallas_call(finish_kernel, grid=(length // tile,), in_specs=[flat] * 4...]
    pallas_call x2 -> x3, Pallas kernels: 53.5 us -> 79.5 us  [mix_forward(): pl.pallas_call(mix_kernel, grid=(seqs, chunks), in_specs=[slab, slab, sla...]
    ppermute x0 -> x13, waiting for transfers between devices: none -> 20.8 us  [the longest x9 20.8 us: along_dp(): lax.ppermute(piece, 'dp', [(j, j ^ flip) for j in range(lax.axis_size('dp...]
    another operation x3 -> x0, other arithmetic: 17.8 us -> none  [the longest x2 15.3 us: local(): jnp.stack(grad_hiddens)]
  transfers between devices with their start and end apart: 10 -> 20, of which waited for: 6 -> 4; matrix products, arithmetic and copies ran while one was open for 22% -> 33% of each run, Pallas kernels for 17% -> 31%
where the time goes in v2:
time: 661 us; the launch traced here: 656 us
  Pallas kernels  233 us (35%)
  matrix products  130 us (20%)
  waiting for transfers between devices  116 us (18%)
  other arithmetic  82.9 us (13%)
  local copies, waits for them, and re-layouts  63.2 us (10%)
  between operations  15.9 us (2%)
  starting transfers between devices  15.2 us (2%)
    pallas_call x3, Pallas kernels, mix_backward(): pl.pallas_call(back_kernel, grid=(seqs, chunks), in_specs=[slab, spec((ch...  124 us
    pallas_call x3, Pallas kernels, mix_forward(): pl.pallas_call(mix_kernel, grid=(seqs, chunks), in_specs=[slab, slab, sla...  79.5 us
    psum x1, waiting for transfers between devices, local(): packed = lax.psum(after(packed, later), ('dp', 'tensor'))  77.2 us
    dot_general x12, matrix products, out_product(): lax.dot_general(left, weight, (((0,), (1,)), ((), ())), preferred_element...  51.2 us
    dot_general x12, matrix products, in_product(): lax.dot_general(weight, tokens, (((0,), (1,)), ((), ())), preferred_eleme...  47.4 us
    unnamed x308, local copies, waits for them, and re-layouts  28.7 us
    dot_general x4, matrix products, grad_product(): lax.dot_general(tokens, channels, (((0,), (1,)), ((), ())), preferred_ele...  20.9 us
    ppermute x9, waiting for transfers between devices, along_dp(): lax.ppermute(piece, 'dp', [(j, j ^ flip) for j in range(lax.axis_size('dp...  20.8 us
  transfers between devices with their start and end apart: 20, of which 4 were waited for; matrix products, arithmetic and copies ran while one was open for 33% of the time, Pallas kernels for 31%

profile of v2, /device:TPU:0, one launch (start us, length us, event | category | flops | bytes accessed | tf_op | source)
XLA Modules:
  0.0 655.8 jit_solution(3372012930837436550)
XLA Ops:
  10.0 3.0 collective-permute-start.13
  12.9 2.1 dynamic-slice_convert_fusion
  15.1 2.1 dynamic-slice_convert_fusion.1
  17.2 2.0 collective-permute-start.5
  19.2 2.1 dynamic-slice_convert_fusion.2
  22.7 3.4 fusion.3
  29.9 1.8 fusion.159
  31.6 4.5 convolution_bitcast_fusion.gate_ref
  36.1 4.5 convolution_bitcast_fusion.1.raw_ref.before_ref
  40.6 4.5 convolution_bitcast_fusion.2.gate_ref
  45.1 4.5 convolution_bitcast_fusion.3.raw_ref.before_ref
  49.5 4.9 fusion.43.dout_ref
  54.4 4.4 fusion.45.dout_ref
  62.5 5.6 multiply_convert_fusion.11
  69.3 1.9 fusion.150
  73.6 2.4 fusion.61
  81.0 1.9 broadcast_in_dim.28.conv_ref
  83.1 26.5 %mix_forward.3 = (f32[1024,1024]{1,0:T(8,128)}, bf16[8,1024,128]{2,1,0:T(8,128)(2,1)S(1)}, f32[8,8,128]{2,1,0:T(8,128)S(1)}) custom-call(f32[1024,1024]{1,0:T(8,128)} %convolution_bitcast_fusion.3.raw_ref.before_ref, f32[1024,1024]{1,0:T(8,128)} %convolution_bitcast_fusion.2.gate_ref, f32[1024,1024]{1,0:T(8,128)} %fusion.45.dout_ref, ...), custom_call_target="tpu_custom_call" | custom-call | flops 1073741824 | bytes 18874368 | tf_op jit(solution)/shard_map/mix_forward/pallas_call | solution.py:252
  111.6 2.0 collective-permute-start
  127.1 26.6 %mix_forward.4 = (f32[1024,1024]{1,0:T(8,128)}, bf16[8,1024,128]{2,1,0:T(8,128)(2,1)S(1)}, f32[8,8,128]{2,1,0:T(8,128)S(1)}) custom-call(f32[1024,1024]{1,0:T(8,128)} %convolution_bitcast_fusion.1.raw_ref.before_ref, f32[1024,1024]{1,0:T(8,128)} %convolution_bitcast_fusion.gate_ref, f32[1024,1024]{1,0:T(8,128)} %fusion.43.dout_ref, ...), custom_call_target="tpu_custom_call" | custom-call | flops 1073741824 | bytes 18874368 | tf_op jit(solution)/shard_map/mix_forward/pallas_call | solution.py:252
  156.5 13.8 %collective-permute-done.6.second_ref = f32[256,1024]{1,0:T(8,128)} collective-permute-done((f32[256,1024]{1,0:T(8,128)}, f32[256,1024]{1,0:T(8,128)}, u32[]{:S(2)}, u32[]{:S(2)}) %collective-permute-start.6) | collective-permute-done | bytes 1048608 | tf_op jit(solution)/shard_map/ppermute | solution.py:518
  170.4 8.3 %multiply_convert_fusion.8 = (bf16[1024,1024]{1,0:T(8,128)(2,1)}, bf16[1024,1024]{1,0:T(8,128)(2,1)}, f32[1024]{0:T(1024)}, bf16[1024,1024]{1,0:T(8,128)(2,1)S(1)}) fusion(f32[1024,1024]{1,0:T(8,128)} %convolution_bitcast_fusion.2.gate_ref, f32[1024,1024]{1,0:T(8,128)S(1)} %copy-done.26, f32[1024]{0:T(1024)S(1)} %bitcast.439, ...), kind=kLoop, calls=%fused_computation.54 | loop fusion | flops 26213376 | bytes 18890752 | tf_op jit(solution)/shard_map/convert_element_type | solution.py:578
  178.6 4.5 fusion.162.branch_ref
  183.1 7.0 %collective-permute-done.2.second_ref = f32[256,1024]{1,0:T(8,128)S(1)} collective-permute-done((f32[256,1024]{1,0:T(8,128)}, f32[256,1024]{1,0:T(8,128)S(1)}, u32[]{:S(2)}, u32[]{:S(2)}) %collective-permute-start.2) | collective-permute-done | bytes 1048608 | tf_op jit(solution)/shard_map/ppermute | solution.py:518
  191.6 3.4 assemble.5
  195.0 3.5 assemble.4
  198.6 6.1 fusion.41.dout_ref
  204.6 4.5 fusion.164.gate_ref
  209.1 3.1 assemble.3
  212.2 5.9 fusion.163.raw_ref.before_ref
  218.2 1.9 broadcast_in_dim.31.conv_ref
  220.3 26.5 %mix_forward.5 = (f32[1024,1024]{1,0:T(8,128)}, bf16[8,1024,128]{2,1,0:T(8,128)(2,1)S(1)}, f32[8,8,128]{2,1,0:T(8,128)S(1)}) custom-call(f32[1024,1024]{1,0:T(8,128)} %fusion.163.raw_ref.before_ref, f32[1024,1024]{1,0:T(8,128)} %fusion.164.gate_ref, f32[1024,1024]{1,0:T(8,128)} %fusion.41.dout_ref, f32[8,8,16,128]{3,2,1,0:T(8,128)S(1)} %bitcast.340, ...), custom_call_target="tpu_custom_call" | custom-call | flops 1073741824 | bytes 18874368 | tf_op jit(solution)/shard_map/mix_forward/pallas_call | solution.py:252
  246.8 14.5 %multiply_convert_fusion.3 = (bf16[1024,1024]{1,0:T(8,128)(2,1)}, bf16[1024,1024]{1,0:T(8,128)(2,1)S(1)}, f32[1024]{0:T(1024)}, bf16[1024,1024]{1,0:T(8,128)(2,1)}, bf16[1024,1024]{1,0:T(8,128)(2,1)}) fusion(f32[1024,1024]{1,0:T(8,128)} %convolution_bitcast_fusion.gate_ref, f32[1024]{0:T(1024)S(1)} %bitcast.429, f32[1024,1024]{1,0:T(8,128)} %fusion.43.dout_ref, ...), kind=kLoop, calls=%fused_computation.45 | loop fusion | flops 38796288 | bytes 33574912 | tf_op jit(solution)/shard_map/convert_element_type | solution.py:577
  261.4 6.9 %fusion.33 = f32[1,1024,1024]{2,1,0:T(8,128)S(1)} fusion(bf16[1024,1024]{1,0:T(8,128)(2,1)S(1)} %get-tuple-element.203, bf16[1024,1024]{1,0:T(8,128)(2,1)} %get-tuple-element.204, bf16[1024,1024]{1,0:T(8,128)(2,1)S(1)} %copy-done.19, bf16[1024,1024]{1,0:T(8,128)(2,1)S(1)} %copy-done.22), kind=kOutput, calls=%fused_computation.60 | convolution fusion | flops 4311744512 | bytes 12582912 | tf_op jit(solution)/shard_map/dot_general | solution.py:464
  268.3 6.4 fusion.30
  274.7 4.2 pad_maximum_fusion
  283.1 7.1 %fusion.160 = f32[1024,1024]{1,0:T(8,128)} fusion(bf16[1024,1024]{1,0:T(8,128)(2,1)} %get-tuple-element.204, bf16[1024,1024]{1,0:T(8,128)(2,1)} %param.20), kind=kOutput, calls=%fused_computation.330 | convolution fusion | flops 2147483648 | bytes 8388608 | tf_op jit(solution)/shard_map/dot_general | solution.py:456
  290.3 4.4 fusion.165.branch_ref
  294.7 41.2 %mix_backward.3 = (bf16[1024,1024]{1,0:T(8,128)(2,1)}, f32[8,8,16,128]{3,2,1,0:T(8,128)S(1)}, f32[1024,256]{1,0:T(8,128)S(1)}, f32[5,1024,128]{2,1,0:T(8,128)}) custom-call(f32[1024,1024]{1,0:T(8,128)} %convolution_bitcast_fusion.3.raw_ref.before_ref, f32[1024,1024]{1,0:T(8,128)} %convolution_bitcast_fusion.3.raw_ref.before_ref, ...), custom_call_target="tpu_custom_call" | custom-call | flops 2147483648 | bytes 16777216 | tf_op jit(solution)/shard_map/mix_backward/pallas_call | solution.py:294
  340.6 2.9 multiply_reduce_fusion.9
  343.5 3.1 multiply_reduce_fusion.8
  350.4 2.4 fusion.166
  352.8 2.7 add_add_fusion.2.part_ref
  355.6 41.2 %mix_backward.4 = (bf16[1024,1024]{1,0:T(8,128)(2,1)}, f32[8,8,16,128]{3,2,1,0:T(8,128)S(1)}, f32[1024,256]{1,0:T(8,128)S(1)}, f32[5,1024,128]{2,1,0:T(8,128)}) custom-call(f32[1024,1024]{1,0:T(8,128)} %convolution_bitcast_fusion.1.raw_ref.before_ref, f32[1024,1024]{1,0:T(8,128)} %convolution_bitcast_fusion.1.raw_ref.before_ref, ...), custom_call_target="tpu_custom_call" | custom-call | flops 2147483648 | bytes 16777216 | tf_op jit(solution)/shard_map/mix_backward/pallas_call | solution.py:294
  397.7 2.2 copy.216
  402.0 1.9 fusion.85
  404.1 2.9 fusion.88
  415.2 2.4 fusion.168
  417.7 2.4 fusion.169
  420.1 2.7 add_add_fusion.1.part_ref
  422.8 4.7 fusion.23
  427.5 2.9 pad_maximum_fusion.1
  430.4 6.1 copy.244
  436.7 3.3 add_reduce_fusion
  440.6 5.8 fusion.7
  447.2 12.5 %fusion.36 = f32[1024,1024]{1,0:T(8,128)} fusion(bf16[1024,1024]{1,0:T(8,128)(2,1)} %assemble.4, f32[1024,1024]{1,0:T(8,128)} %fusion.164.gate_ref, f32[1024,1024]{1,0:T(8,128)} %get-tuple-element.98.mixed_ref, f32[1024,1024]{1,0:T(8,128)} %fusion.41.dout_ref, f32[1024]{0:T(1024)S(1)} %copy-done.85, f32[1024]{0:T(1024)S(1)} %bitcast.430, f32[1024]{0:T(1024)S(1)} %bitcast.427), kind=kOutput, calls=%fused_computation.65 | convolution fusion | flops 2164260864 | bytes 18886656 | tf_op jit(solution)/shard_map/dot_general | solution.py:456
  461.1 4.8 fusion.37.received_ref
  465.8 41.4 %mix_backward.5 = (bf16[1024,1024]{1,0:T(8,128)(2,1)}, f32[8,8,16,128]{3,2,1,0:T(8,128)S(1)}, f32[1024,256]{1,0:T(8,128)S(1)}, f32[5,1024,128]{2,1,0:T(8,128)}) custom-call(f32[1024,1024]{1,0:T(8,128)} %fusion.163.raw_ref.before_ref, f32[1024,1024]{1,0:T(8,128)} %fusion.163.raw_ref.before_ref, f32[1024,1024]{1,0:T(8,128)} %get-tuple-element.98.mixed_ref, ...), custom_call_target="tpu_custom_call" | custom-call | flops 2147483648 | bytes 16777216 | tf_op jit(solution)/shard_map/mix_backward/pallas_call | solution.py:294
  508.2 1.8 add_reduce_fusion.1
  517.5 4.5 add_add_fusion.other_ref
  524.2 10.1 %finish.2 = (bf16[2,1024,1024]{2,1,0:T(8,128)(2,1)}, f32[2,1024,1024]{2,1,0:T(8,128)}) custom-call(f32[1024,1024]{1,0:T(8,128)} %add_add_fusion.1.part_ref, f32[1024,1024]{1,0:T(8,128)} %add_add_fusion.other_ref, f32[1024,1024]{1,0:T(8,128)} %fusion.165.branch_ref, f32[1024,1024]{1,0:T(8,128)} %fusion.37.received_ref, bf16[2,1024,1024]{2,1,0:T(8,128)(2,1)} %hidden_ref.3, ...), custom_call_target="tpu_custom_call" | custom-call | flops 20971520 | bytes 27262976 | tf_op jit(solution)/shard_map/finish/pallas_call | solution.py:437
  534.3 17.6 %collective-permute-done.15.other_ref = f32[1024,1024]{1,0:T(8,128)} collective-permute-done((f32[1024,1024]{1,0:T(8,128)}, f32[1024,1024]{1,0:T(8,128)}, u32[]{:S(2)}, u32[]{:S(2)}) %collective-permute-start.15) | collective-permute-done | bytes 4194336 | tf_op jit(solution)/shard_map/ppermute | solution.py:484
  551.9 10.1 %finish.3 = (bf16[2,1024,1024]{2,1,0:T(8,128)(2,1)}, f32[2,1024,1024]{2,1,0:T(8,128)}) custom-call(f32[1024,1024]{1,0:T(8,128)} %add_add_fusion.2.part_ref, f32[1024,1024]{1,0:T(8,128)} %collective-permute-done.15.other_ref, f32[1024,1024]{1,0:T(8,128)} %fusion.162.branch_ref, ...), custom_call_target="tpu_custom_call", output_to_operand_aliasing={{0}: (7, {}), {1}: (8, {})} | custom-call | flops 20971520 | bytes 27262976 | tf_op jit(solution)/shard_map/finish/pallas_call | solution.py:437
  565.0 77.2 %all-reduce.30.cloned.1.call-done = f32[16384]{0:T(1024)} async-done(((f32[16384]{0:T(1024)}), f32[16384]{0:T(1024)}) %all-reduce.30.cloned.1.call-update) | async-done | bytes 65552 | tf_op jit(solution)/shard_map/psum | solution.py:764
  (475 shorter events, 86.6 us)
Async XLA Ops:
  7.2 21.9 %copy-start = (bf16[1024,256]{1,0:T(8,128)(2,1)S(1)}, bf16[1024,256]{1,0:T(8,128)(2,1)}, u32[]{:S(2)}) copy-start(bf16[1024,256]{1,0:T(8,128)(2,1)} %param.22) | copy-start | bytes 1572868
  7.2 14.2 %copy-start.131 = (f32[16]{0:T(128)S(1)}, f32[16]{0:T(128)}, u32[]{:S(2)}) copy-start(f32[16]{0:T(128)} %param.29) | copy-start | bytes 196
  7.2 14.2 %copy-start.127 = (f32[16]{0:T(128)S(1)}, f32[16]{0:T(128)}, u32[]{:S(2)}) copy-start(f32[16]{0:T(128)} %param.30) | copy-start | bytes 196
  7.2 14.9 %copy-start.63 = (s32[2,1024]{1,0:T(2,128)S(1)}, s32[2,1024]{1,0:T(2,128)}, u32[]{:S(2)}) copy-start(s32[2,1024]{1,0:T(2,128)} %param.18) | copy-start | bytes 24580
  7.2 423.2 %reduce-scatter.5.cloned.1.call-start = ((), (), s32[]{:S(2)}) async-start(), calls=%async_computation.2 | async-start | bytes 8912896 | tf_op jit(solution)/shard_map/reduce_scatter | solution.py:711
  10.0 62.2 %collective-permute-start.13 = (f32[22576]{0:T(1024)S(1)}, f32[22576]{0:T(1024)S(1)}, u32[]{:S(2)}, u32[]{:S(2)}) collective-permute-start(f32[22576]{0:T(1024)S(1)} %concatenate.164), channel_id=1, source_target_pairs={{0,1},{1,0},{2,3},{3,2},{4,5},{5,4},{6,7},{7,6},{8,9},{9,8},{10,11... | collective-permute-start | bytes 270920 | tf_op jit(solution)/shard_map/ppermute | solution.py:539
  12.9 13.3 %copy-start.12 = (f32[1024]{0:T(1024)S(1)}, f32[1024]{0:T(1024)}, u32[]{:S(2)}) copy-start(f32[1024]{0:T(1024)} %param.19) | copy-start | bytes 12292
  15.1 106.3 %collective-permute-start.9 = (f32[256,1024]{1,0:T(8,128)}, f32[256,1024]{1,0:T(8,128)}, u32[]{:S(2)}, u32[]{:S(2)}) collective-permute-start(f32[256,1024]{1,0:T(8,128)} %dynamic-slice_convert_fusion), channel_id=1, source_target_pairs={{0,1},{1,0},{2,3},{3,2},{4,5},{5,4},{6,7},{7,6},{8,9},{9,8},{10,11... | collective-permute-start | bytes 3145736 | tf_op jit(solution)/shard_map/ppermute | solution.py:514
  17.2 105.7 %collective-permute-start.5 = (f32[256,1024]{1,0:T(8,128)}, f32[256,1024]{1,0:T(8,128)}, u32[]{:S(2)}, u32[]{:S(2)}) collective-permute-start(f32[256,1024]{1,0:T(8,128)} %dynamic-slice_convert_fusion.1), channel_id=1, source_target_pairs={{0,1},{1,0},{2,3},{3,2},{4,5},{5,4},{6,7},{7,6},{8,9},{9,8},{10,11... | collective-permute-start | bytes 3145736 | tf_op jit(solution)/shard_map/ppermute | solution.py:514
  21.3 133.1 %collective-permute-start.1 = (f32[256,1024]{1,0:T(8,128)}, f32[256,1024]{1,0:T(8,128)}, u32[]{:S(2)}, u32[]{:S(2)}) collective-permute-start(f32[256,1024]{1,0:T(8,128)} %dynamic-slice_convert_fusion.2), channel_id=1, source_target_pairs={{0,1},{1,0},{2,3},{3,2},{4,5},{5,4},{6,7},{7,6},{8,9},{9,8},{10,11... | collective-permute-start | bytes 3145736 | tf_op jit(solution)/shard_map/ppermute | solution.py:514
  21.4 37.6 %copy-start.115 = (f32[16]{0:T(128)}, f32[16]{0:T(128)S(1)}, u32[]{:S(2)}) copy-start(f32[16]{0:T(128)S(1)} %exponential_negate_fusion) | copy-start | bytes 196
  26.2 47.4 %copy-start.80 = (f32[1024]{0:T(1024)}, f32[1024]{0:T(1024)S(1)}, u32[]{:S(2)}) copy-start(f32[1024]{0:T(1024)S(1)} %add_rsqrt_fusion) | copy-start | bytes 12292
  27.7 8.4 %copy-start.18 = (bf16[1024,1024]{1,0:T(8,128)(2,1)}, bf16[1024,1024]{1,0:T(8,128)(2,1)S(1)}, u32[]{:S(2)}) copy-start(bf16[1024,1024]{1,0:T(8,128)(2,1)S(1)} %get-tuple-element.210) | copy-start | bytes 6291460
  27.7 17.4 %copy-start.21 = (bf16[1024,1024]{1,0:T(8,128)(2,1)}, bf16[1024,1024]{1,0:T(8,128)(2,1)S(1)}, u32[]{:S(2)}) copy-start(bf16[1024,1024]{1,0:T(8,128)(2,1)S(1)} %get-tuple-element.211) | copy-start | bytes 6291460
  28.4 30.4 %copy-start.54 = (f32[16,1024]{1,0:T(8,128)}, f32[16,1024]{1,0:T(8,128)S(1)}, u32[]{:S(2)}) copy-start(f32[16,1024]{1,0:T(8,128)S(1)} %fusion.59) | copy-start | bytes 196612
  29.1 29.8 %copy-start.56 = (f32[16,1024]{1,0:T(8,128)}, f32[16,1024]{1,0:T(8,128)S(1)}, u32[]{:S(2)}) copy-start(f32[16,1024]{1,0:T(8,128)S(1)} %fusion.60) | copy-start | bytes 196612
  29.8 32.6 %copy-start.15 = (f32[1024,256]{0,1:T(8,128)}, f32[1024,256]{0,1:T(8,128)S(1)}, u32[]{:S(2)}) copy-start(f32[1024,256]{0,1:T(8,128)S(1)} %fusion.161) | copy-start | bytes 3145732
  54.4 7.2 %copy-start.126 = (f32[4,256]{1,0:T(4,128)S(1)}, f32[4,256]{1,0:T(4,128)}, u32[]{:S(2)}) copy-start(f32[4,256]{1,0:T(4,128)} %param.26) | copy-start | bytes 12292
  54.4 8.0 %copy-start.130 = (f32[256]{0:T(256)S(1)}, f32[256]{0:T(256)}, u32[]{:S(2)}) copy-start(f32[256]{0:T(256)} %param.27) | copy-start | bytes 3076
  58.9 20.8 %copy-start.47 = (f32[2,8,8,128]{3,2,1,0:T(8,128)}, f32[2,8,8,128]{3,2,1,0:T(8,128)S(1)}, u32[]{:S(2)}) copy-start(f32[2,8,8,128]{3,2,1,0:T(8,128)S(1)} %copy.250) | copy-start | bytes 196612
  59.0 12.4 %copy-start.49 = (f32[2,8,8,128]{3,2,1,0:T(8,128)}, f32[2,8,8,128]{3,2,1,0:T(8,128)S(1)}, u32[]{:S(2)}) copy-start(f32[2,8,8,128]{3,2,1,0:T(8,128)S(1)} %copy.248) | copy-start | bytes 196612
  62.5 9.5 %copy-start.73 = (f32[1024]{0:T(1024)}, f32[1024]{0:T(1024)S(1)}, u32[]{:S(2)}) copy-start(f32[1024]{0:T(1024)S(1)} %get-tuple-element.310) | copy-start | bytes 12292
  69.1 8.5 %copy-start.128 = (f32[8]{0:T(128)S(1)}, f32[8]{0:T(128)}, u32[]{:S(2)}) copy-start(f32[8]{0:T(128)} %get-tuple-element.307) | copy-start | bytes 100
  71.2 11.9 %copy-start.2 = (bf16[128,1024]{1,0:T(8,128)(2,1)}, bf16[128,1024]{1,0:T(8,128)(2,1)S(1)}, u32[]{:S(2)}) copy-start(bf16[128,1024]{1,0:T(8,128)(2,1)S(1)} %get-tuple-element.233.outt_ref) | copy-start | bytes 786436
  73.6 9.3 %copy-start.76 = (f32[1024]{0:T(1024)S(1)}, f32[1024]{0:T(1024)}, u32[]{:S(2)}) copy-start(f32[1024]{0:T(1024)} %param.31) | copy-start | bytes 12292
  83.1 30.4 %copy-start.62 = (f32[16,8,128]{2,1,0:T(8,128)S(1)}, f32[16,8,128]{2,1,0:T(8,128)}, u32[]{:S(2)}) copy-start(f32[16,8,128]{2,1,0:T(8,128)} %get-tuple-element.261) | copy-start | bytes 196612
  111.6 42.1 %collective-permute-start = (f32[2,1024]{1,0:T(2,128)}, f32[2,1024]{1,0:T(2,128)}, u32[]{:S(2)}, u32[]{:S(2)}) collective-permute-start(f32[2,1024]{1,0:T(2,128)} %slice_bitcast_fusion.3), channel_id=1, source_target_pairs={{0,1},{1,0},{2,3},{3,2},{4,5},{5,4},{6,7},{7,6},{8,9},{9,8},{10,11... | collective-permute-start | bytes 24584 | tf_op jit(solution)/shard_map/ppermute | solution.py:484
  121.4 35.1 %collective-permute-start.10 = (f32[256,1024]{1,0:T(8,128)}, f32[256,1024]{1,0:T(8,128)}, u32[]{:S(2)}, u32[]{:S(2)}) collective-permute-start(f32[256,1024]{1,0:T(8,128)} %collective-permute-done.9.first_ref), channel_id=1, source_target_pairs={{0,4},{2,6},{4,0},{6,2},{8,12},{10,14},{12,8},{14,10},{16,20},{18,... | collective-permute-start | bytes 3145736 | tf_op jit(solution)/shard_map/ppermute | solution.py:518
  122.9 47.4 %collective-permute-start.6 = (f32[256,1024]{1,0:T(8,128)}, f32[256,1024]{1,0:T(8,128)}, u32[]{:S(2)}, u32[]{:S(2)}) collective-permute-start(f32[256,1024]{1,0:T(8,128)} %collective-permute-done.5.first_ref), channel_id=1, source_target_pairs={{0,4},{2,6},{4,0},{6,2},{8,12},{10,14},{12,8},{14,10},{16,20},{18,... | collective-permute-start | bytes 3145736 | tf_op jit(solution)/shard_map/ppermute | solution.py:518
  127.1 43.3 %copy-start.26 = (f32[1024,1024]{1,0:T(8,128)S(1)}, f32[1024,1024]{1,0:T(8,128)}, u32[]{:S(2)}) copy-start(f32[1024,1024]{1,0:T(8,128)} %get-tuple-element.65.mixed_ref) | copy-start | bytes 12582916
  127.1 43.3 %copy-start.77 = (f32[1024]{0:T(1024)S(1)}, f32[1024]{0:T(1024)}, u32[]{:S(2)}) copy-start(f32[1024]{0:T(1024)} %param.31) | copy-start | bytes 12292
  153.7 24.9 %copy-start.5 = (bf16[8,1024,128]{2,1,0:T(8,128)(2,1)}, bf16[8,1024,128]{2,1,0:T(8,128)(2,1)S(1)}, u32[]{:S(2)}) copy-start(bf16[8,1024,128]{2,1,0:T(8,128)(2,1)S(1)} %get-tuple-element.94.entry_ref) | copy-start | bytes 6291460
  154.4 35.7 %collective-permute-start.2 = (f32[256,1024]{1,0:T(8,128)}, f32[256,1024]{1,0:T(8,128)S(1)}, u32[]{:S(2)}, u32[]{:S(2)}) collective-permute-start(f32[256,1024]{1,0:T(8,128)} %collective-permute-done.1.first_ref), channel_id=1, source_target_pairs={{0,4},{2,6},{4,0},{6,2},{8,12},{10,14},{12,8},{14,10},{16,20},{18,... | collective-permute-start | bytes 3145736 | tf_op jit(solution)/shard_map/ppermute | solution.py:518
  156.0 34.1 %collective-permute-start.11 = (f32[256,1024]{1,0:T(8,128)}, f32[256,1024]{1,0:T(8,128)S(1)}, u32[]{:S(2)}, u32[]{:S(2)}) collective-permute-start(f32[256,1024]{1,0:T(8,128)} %collective-permute-done.9.first_ref), channel_id=1, source_target_pairs={{0,2},{2,0},{4,6},{6,4},{8,10},{10,8},{12,14},{14,12},{16,18},{18,... | collective-permute-start | bytes 3145736 | tf_op jit(solution)/shard_map/ppermute | solution.py:518
  156.0 34.6 %collective-permute-start.7 = (f32[256,1024]{1,0:T(8,128)}, f32[256,1024]{1,0:T(8,128)S(1)}, u32[]{:S(2)}, u32[]{:S(2)}) collective-permute-start(f32[256,1024]{1,0:T(8,128)} %collective-permute-done.5.first_ref), channel_id=1, source_target_pairs={{0,2},{2,0},{4,6},{6,4},{8,10},{10,8},{12,14},{14,12},{16,18},{18,... | collective-permute-start | bytes 3145736 | tf_op jit(solution)/shard_map/ppermute | solution.py:518
  156.5 34.1 %collective-permute-start.12 = (f32[256,1024]{1,0:T(8,128)}, f32[256,1024]{1,0:T(8,128)S(1)}, u32[]{:S(2)}, u32[]{:S(2)}) collective-permute-start(f32[256,1024]{1,0:T(8,128)} %collective-permute-done.10.second_ref), channel_id=1, source_target_pairs={{0,2},{2,0},{4,6},{6,4},{8,10},{10,8},{12,14},{14,12},{16,18},{18,... | collective-permute-start | bytes 3145736 | tf_op jit(solution)/shard_map/ppermute | solution.py:518
  170.3 20.3 %collective-permute-start.8 = (f32[256,1024]{1,0:T(8,128)}, f32[256,1024]{1,0:T(8,128)}, u32[]{:S(2)}, u32[]{:S(2)}) collective-permute-start(f32[256,1024]{1,0:T(8,128)} %collective-permute-done.6.second_ref), channel_id=1, source_target_pairs={{0,2},{2,0},{4,6},{6,4},{8,10},{10,8},{12,14},{14,12},{16,18},{18,... | collective-permute-start | bytes 3145736 | tf_op jit(solution)/shard_map/ppermute | solution.py:518
  170.3 8.3 %copy-start.65 = (bf16[1024,1024]{1,0:T(8,128)(2,1)S(1)}, bf16[1024,1024]{1,0:T(8,128)(2,1)}, u32[]{:S(2)}) copy-start(bf16[1024,1024]{1,0:T(8,128)(2,1)} %param.32) | copy-start | bytes 6291460
  190.1 19.0 %collective-permute-start.3 = (f32[256,1024]{1,0:T(8,128)}, f32[256,1024]{1,0:T(8,128)S(1)}, u32[]{:S(2)}, u32[]{:S(2)}) collective-permute-start(f32[256,1024]{1,0:T(8,128)} %collective-permute-done.1.first_ref), channel_id=1, source_target_pairs={{0,2},{2,0},{4,6},{6,4},{8,10},{10,8},{12,14},{14,12},{16,18},{18,... | collective-permute-start | bytes 3145736 | tf_op jit(solution)/shard_map/ppermute | solution.py:518
  190.1 19.0 %collective-permute-start.4 = (f32[256,1024]{1,0:T(8,128)S(1)}, f32[256,1024]{1,0:T(8,128)}, u32[]{:S(2)}, u32[]{:S(2)}) collective-permute-start(f32[256,1024]{1,0:T(8,128)S(1)} %collective-permute-done.2.second_ref), channel_id=1, source_target_pairs={{0,2},{2,0},{4,6},{6,4},{8,10},{10,8},{12,14},{14,12},{16,18},{18,... | collective-permute-start | bytes 3145736 | tf_op jit(solution)/shard_map/ppermute | solution.py:518
  212.2 7.8 %copy-start.84 = (f32[1024]{0:T(1024)S(1)}, f32[1024]{0:T(1024)}, u32[]{:S(2)}) copy-start(f32[1024]{0:T(1024)} %get-tuple-element.235) | copy-start | bytes 12292
  246.7 14.6 %copy-start.4 = (bf16[8,1024,128]{2,1,0:T(8,128)(2,1)}, bf16[8,1024,128]{2,1,0:T(8,128)(2,1)S(1)}, u32[]{:S(2)}) copy-start(bf16[8,1024,128]{2,1,0:T(8,128)(2,1)S(1)} %get-tuple-element.101.entry_ref) | copy-start | bytes 6291460
  246.8 14.6 %copy-start.104 = (f32[1,8,128]{2,0,1:T(1,128)}, f32[1,8,128]{2,0,1:T(1,128)S(1)}, u32[]{:S(2)}) copy-start(f32[1,8,128]{2,0,1:T(1,128)S(1)} %get-tuple-element.195) | copy-start | bytes 12292
  246.8 14.5 %copy-start.106 = (f32[1,1024]{1,0:T(1,128)}, f32[1,1024]{1,0:T(1,128)S(1)}, u32[]{:S(2)}) copy-start(f32[1,1024]{1,0:T(1,128)S(1)} %get-tuple-element.194) | copy-start | bytes 12292
  246.8 14.5 %copy-start.22 = (bf16[1024,1024]{1,0:T(8,128)(2,1)S(1)}, bf16[1024,1024]{1,0:T(8,128)(2,1)}, u32[]{:S(2)}) copy-start(bf16[1024,1024]{1,0:T(8,128)(2,1)} %copy-done.21) | copy-start | bytes 6291460
  261.3 7.0 %copy-start.35 = (bf16[1024,1024]{1,0:T(8,128)(2,1)}, bf16[1024,1024]{1,0:T(8,128)(2,1)S(1)}, u32[]{:S(2)}) copy-start(bf16[1024,1024]{1,0:T(8,128)(2,1)S(1)} %get-tuple-element.203) | copy-start | bytes 6291460
  261.3 7.0 %copy-start.37 = (bf16[1024,1024]{1,0:T(8,128)(2,1)S(1)}, bf16[1024,1024]{1,0:T(8,128)(2,1)}, u32[]{:S(2)}) copy-start(bf16[1024,1024]{1,0:T(8,128)(2,1)} %get-tuple-element.209) | copy-start | bytes 6291460
  279.0 243.1 %reduce-scatter.7.cloned.1.call-start = ((), (), s32[]{:S(2)}) async-start(), calls=%async_computation.4 | async-start | bytes 6127616
  282.8 7.4 %copy-start.38 = (bf16[1024,1024]{1,0:T(8,128)(2,1)S(1)}, bf16[1024,1024]{1,0:T(8,128)(2,1)}, u32[]{:S(2)}) copy-start(bf16[1024,1024]{1,0:T(8,128)(2,1)} %get-tuple-element.209) | copy-start | bytes 6291460
  282.8 7.4 %copy-start.66 = (bf16[1024,1024]{1,0:T(8,128)(2,1)S(1)}, bf16[1024,1024]{1,0:T(8,128)(2,1)}, u32[]{:S(2)}) copy-start(bf16[1024,1024]{1,0:T(8,128)(2,1)} %param.32) | copy-start | bytes 6291460
  282.8 176.9 %collective-permute-start.14 = (f32[1024,1024]{1,0:T(8,128)}, f32[1024,1024]{1,0:T(8,128)}, u32[]{:S(2)}, u32[]{:S(2)}) collective-permute-start(f32[1024,1024]{1,0:T(8,128)} %fusion.162.branch_ref), channel_id=1, source_target_pairs={{0,1},{1,0},{2,3},{3,2},{4,5},{5,4},{6,7},{7,6},{8,9},{9,8},{10,11... | collective-permute-start | bytes 12582920 | tf_op jit(solution)/shard_map/ppermute | solution.py:484
  294.7 44.4 %copy-start.116 = (f32[16]{0:T(128)S(1)}, f32[16]{0:T(128)}, u32[]{:S(2)}) copy-start(f32[16]{0:T(128)} %copy-done.115) | copy-start | bytes 196
  294.7 45.3 %copy-start.57 = (f32[16,1024]{1,0:T(8,128)S(1)}, f32[16,1024]{1,0:T(8,128)}, u32[]{:S(2)}) copy-start(f32[16,1024]{1,0:T(8,128)} %copy-done.56) | copy-start | bytes 196612
  294.7 45.9 %copy-start.74 = (f32[1024]{0:T(1024)S(1)}, f32[1024]{0:T(1024)}, u32[]{:S(2)}) copy-start(f32[1024]{0:T(1024)} %copy-done.73) | copy-start | bytes 12292
  355.5 46.5 %copy-start.48 = (f32[2,8,8,128]{3,2,1,0:T(8,128)S(1)}, f32[2,8,8,128]{3,2,1,0:T(8,128)}, u32[]{:S(2)}) copy-start(f32[2,8,8,128]{3,2,1,0:T(8,128)} %copy-done.47) | copy-start | bytes 196612
  355.5 46.5 %copy-start.50 = (f32[2,8,8,128]{3,2,1,0:T(8,128)S(1)}, f32[2,8,8,128]{3,2,1,0:T(8,128)}, u32[]{:S(2)}) copy-start(f32[2,8,8,128]{3,2,1,0:T(8,128)} %copy-done.49) | copy-start | bytes 196612
  355.5 48.4 %copy-start.55 = (f32[16,1024]{1,0:T(8,128)S(1)}, f32[16,1024]{1,0:T(8,128)}, u32[]{:S(2)}) copy-start(f32[16,1024]{1,0:T(8,128)} %copy-done.54) | copy-start | bytes 196612
  436.6 205.6 %all-reduce.30.cloned.1.call-start = ((), (), s32[]{:S(2)}) async-start(), calls=%async_computation.3 | async-start | bytes 131072 | tf_op jit(solution)/shard_map/psum | solution.py:764
  447.1 14.0 %copy-start.27 = (f32[1024,1024]{1,0:T(8,128)S(1)}, f32[1024,1024]{1,0:T(8,128)}, u32[]{:S(2)}) copy-start(f32[1024,1024]{1,0:T(8,128)} %get-tuple-element.98.mixed_ref) | copy-start | bytes 12582916
  447.1 14.0 %copy-start.28 = (f32[1024,1024]{1,0:T(8,128)S(1)}, f32[1024,1024]{1,0:T(8,128)}, u32[]{:S(2)}) copy-start(f32[1024,1024]{1,0:T(8,128)} %fusion.164.gate_ref) | copy-start | bytes 12582916
  447.1 13.9 %copy-start.33 = (bf16[1024,1024]{1,0:T(8,128)(2,1)S(1)}, bf16[1024,1024]{1,0:T(8,128)(2,1)}, u32[]{:S(2)}) copy-start(bf16[1024,1024]{1,0:T(8,128)(2,1)} %assemble.5) | copy-start | bytes 6291460
  459.7 92.2 %collective-permute-start.15 = (f32[1024,1024]{1,0:T(8,128)}, f32[1024,1024]{1,0:T(8,128)}, u32[]{:S(2)}, u32[]{:S(2)}) collective-permute-start(f32[1024,1024]{1,0:T(8,128)} %add_add_fusion.2.part_ref), channel_id=1, source_target_pairs={{0,1},{1,0},{2,3},{3,2},{4,5},{5,4},{6,7},{7,6},{8,9},{9,8},{10,11... | collective-permute-start | bytes 12582920 | tf_op jit(solution)/shard_map/ppermute | solution.py:484
  465.8 44.3 %copy-start.118 = (f32[16]{0:T(128)S(1)}, f32[16]{0:T(128)}, u32[]{:S(2)}) copy-start(f32[16]{0:T(128)} %copy-done.117) | copy-start | bytes 196
  562.7 85.7 %collective-permute-start.16 = (f32[64,256]{0,1:T(8,128)S(1)}, f32[64,256]{0,1:T(8,128)S(1)}, u32[]{:S(2)}, u32[]{:S(2)}) collective-permute-start(f32[64,256]{0,1:T(8,128)S(1)} %slice.415), channel_id=1, source_target_pairs={{0,1},{1,0},{2,3},{3,2},{4,5},{5,4},{6,7},{7,6},{8,9},{9,8},{10,11... | collective-permute-start | bytes 196616 | tf_op jit(solution)/shard_map/ppermute | solution.py:484
  (95 other events, 340.7 us)
Sparse Core Ops, SparseCore 0:
  279.1 104.9 reduce-scatter.4
  436.7 82.5 reduce-scatter.6
  525.5 116.6 all-reduce.29

commit v3 on v2

--- a/solution.py
+++ b/solution.py
@@ -130,7 +130,8 @@
         return sums[0] + square, sums[1] + jnp.sum(inner, axis=0, keepdims=True)
 
     zero = jnp.zeros((1, CHUNK), jnp.float32)
-    square, inner = lax.fori_loop(0, raw_ref.shape[0] // PAIR, body, (zero, zero))
+    pairs = raw_ref.shape[0] // PAIR
+    square, inner = lax.fori_loop(0, pairs, body, (zero, zero), unroll=min(8, pairs))
     sums_ref[0, 0:1, :] = square
     sums_ref[0, 1:2, :] = inner
 
@@ -230,9 +231,8 @@
         draw_ref[part, :] = draw.astype(bf16)
         return daffinity
 
-    daffinity = lax.fori_loop(
-        0, raw_ref.shape[0] // PAIR, body, jnp.zeros((CHUNK, CHUNK), jnp.float32)
-    )
+    zero = jnp.zeros((CHUNK, CHUNK), jnp.float32)
+    daffinity = lax.fori_loop(0, raw_ref.shape[0] // PAIR, body, zero, unroll=2)
     daffinity = (daffinity * allowed).astype(bf16)
     dstate_ref[:, :STATE] = dfar_ref[:, :STATE] + mxu(daffinity, out)
     dstate_ref[:, STATE:] = dfar_ref[:, STATE:] + mxu(daffinity, into, TN)
@@ -327,7 +327,7 @@
         ],
         compiler_params=pltpu.CompilerParams(vmem_limit_bytes=VMEM_BYTES),
         cost_estimate=pl.CostEstimate(
-            flops=tokens * ch * 2048, bytes_accessed=tokens * ch * 16, transcendentals=tokens * ch * 4
+            flops=tokens, bytes_accessed=tokens, transcendentals=0
         ),
         name="mix_backward",
     )(raw, raw, mixed, dmix, entry, rows, masks, into, intot, out, outt, conv)
@@ -446,7 +446,7 @@
         input_output_aliases={7 + i: i for i in range(len(earlier))},
         compiler_params=pltpu.CompilerParams(vmem_limit_bytes=VMEM_BYTES),
         cost_estimate=pl.CostEstimate(
-            flops=length * width * 20, bytes_accessed=length * width * 26, transcendentals=0
+            flops=length, bytes_accessed=length, transcendentals=0
         ),
         name="finish",
     )(part, other, branch, received, hidden, out_grad, norm_gain[None, :], *earlier)
@@ -532,6 +532,20 @@
         ),
         name="assemble",
     )(quarter.reshape(1), *pieces)
+
+
+def sum_dp(value, *between):
+    count = lax.axis_size("dp")
+    if count & (count - 1) or not between:
+        return lax.psum(value, "dp")
+    flip, between = 1, list(between)
+    while flip < count:
+        arrived = along_dp(value, flip)
+        if between:
+            arrived = after(arrived, between.pop(0))
+        value = value + arrived
+        flip *= 2
+    return value
 
 
 def swap_small(arrays):
@@ -711,13 +725,13 @@
     early = lax.psum_scatter(early_part, "dp", scatter_dimension=1, tiled=True)
 
     backs, parts, others = [], [], []
-    waits = (early_part, *branches)
+    waits = (early_part, *branches, received[0])
     for s in every:
         back = unit_backward(units[s], own, d_gates[s], after(d_mixeds[s], *waits), state_backs[s])
         backs.append(back)
         parts.append(lax.optimization_barrier(normed_part(own, d_gates[s], *back[:3])))
         if s < whole_from:
-            others.append(tensor_others(after(parts[s], received[s])))
+            others.append(tensor_others(parts[s]))
             waits = (parts[s],)
     later_part = jnp.concatenate(
         [
@@ -732,8 +746,7 @@
     later_value = later[:, :local_inner]
     edge = local_inner + state_width
     state_part = later[:, local_inner:edge]
-    grad_proj_state = tensor_join(state_part, tensor_others(state_part))
-    waits = (later_part,)
+    waits, extra_backs = (later_part, *others), []
     grad_norm_gain = jnp.zeros((width,), jnp.float32)
     for s in every:
         wide = hidden[s].astype(jnp.float32)
@@ -742,28 +755,35 @@
     for s in range(whole_from, seq_count):
         d_gate = middles[s][1]
         back = unit_backward(extras[s], other, d_gate, after(middles[s][2], *waits), state_backs[s])
+        extra_backs.append(back)
         others.append(lax.optimization_barrier(normed_part(other, d_gate, *back[:3])))
 
-    stacked = ()
-    for s in reversed(every):
-        stacked = finish(
-            s, parts[s], only_others(parts[s], others[s]), branches[s],
-            only_others(branches[s], received[s]), hidden, out_grad, norm_gain, stacked
-        )
     param_grads = [sum(grads) for grads in zip(*[b[3] for b in backs])]
     d_conv, g_cs, g_csb, g_sb, g_dl, g_sg = param_grads
     d_conv = jnp.sum(d_conv, axis=-1)
     own_grads = [d_conv[:KERNEL], d_conv[KERNEL], g_sb, g_dl, g_sg, grad_gate_gain]
     shared = [g_cs, g_csb, grad_norm_gain]
     own_flat = jnp.concatenate([g.reshape(-1) for g in own_grads])
-    place = lax.axis_index("tensor")
-    mine = (jnp.arange(tensor_count) == place)[:, None]
-    slots = jnp.where(mine, own_flat[None, :], 0.0).reshape(-1)
-    packed = jnp.concatenate([slots] + [g.reshape(-1) for g in shared])
-    packed = jnp.pad(packed, (0, -packed.shape[0] % 16384))
-    packed = lax.psum(after(packed, later), ("dp", "tensor"))
-    own_sum = lax.dynamic_slice(packed, (place * own_flat.shape[0],), (own_flat.shape[0],))
-    shared_sum = packed[slots.shape[0] :]
+    shared_flat = jnp.concatenate([g.reshape(-1) for g in shared])
+    arrived = tensor_others(shared_flat)
+    between = []
+    if whole_from < seq_count:
+        arrived = after(arrived, *waits)
+        between = [others[0], others[0], others[-1]]
+    shared_flat = tensor_join(shared_flat, arrived)
+    stacked = ()
+    parts[0] = after(parts[0], later)
+    for s in reversed(every):
+        stacked = finish(
+            s, parts[s], only_others(parts[s], others[s]), branches[s],
+            only_others(branches[s], received[s]), hidden, out_grad, norm_gain, stacked
+        )
+        if between and s == every[-1]:
+            between.append(stacked[0])
+    packed = sum_dp(jnp.concatenate([own_flat, shared_flat]), *between)
+    own_sum, shared_sum = packed[: own_flat.shape[0]], packed[own_flat.shape[0] :]
+
+    grad_proj_state = tensor_join(state_part, tensor_others(state_part))
 
     def split(flat, like):
         result, edge = [], 0

time: 661 us -> 598 us (0.905)
  Pallas kernels: 233 us -> 170 us
  other arithmetic: 82.9 us -> 70.8 us
    psum x1 -> x0, waiting for transfers between devices: 77.2 us -> none  [local(): packed = lax.psum(after(packed, later), ('dp', 'tensor'))]
    ppermute x4 -> x5, waiting for transfers between devices: 17.7 us -> 68.6 us  [tensor_others(): return lax.ppermute(part, 'tensor', [(0, 1), (1, 0)])]
    pallas_call x3, Pallas kernels: 79.5 us -> 43.5 us  [mix_forward(): pl.pallas_call(mix_kernel, grid=(seqs, chunks), in_specs=[slab, slab, sla...]
    pallas_call x3, Pallas kernels: 124 us -> 95.2 us  [mix_backward(): pl.pallas_call(back_kernel, grid=(seqs, chunks), in_specs=[slab, spec((ch...]
    ppermute x9 -> x13, waiting for transfers between devices: 20.8 us -> 49.1 us  [along_dp(): lax.ppermute(piece, 'dp', [(j, j ^ flip) for j in range(lax.axis_size('dp...]
    unnamed x308 -> x312, local copies, waits for them, and re-layouts: 28.7 us -> 30.5 us
  transfers between devices with their start and end apart: 20 -> 24, of which waited for: 4 -> 6; matrix products, arithmetic and copies ran while one was open for 33% -> 32% of each run, Pallas kernels for 31% -> 24%
where the time goes in v3:
time: 598 us; the launch traced here: 591 us
  Pallas kernels  170 us (28%)
  matrix products  131 us (22%)
  waiting for transfers between devices  118 us (20%)
  other arithmetic  70.8 us (12%)
  local copies, waits for them, and re-layouts  63.5 us (11%)
  starting transfers between devices  21.2 us (4%)
  between operations  16.5 us (3%)
    pallas_call x3, Pallas kernels, mix_backward(): pl.pallas_call(back_kernel, grid=(seqs, chunks), in_specs=[slab, spec((ch...  95.2 us
    ppermute x5, waiting for transfers between devices, tensor_others(): return lax.ppermute(part, 'tensor', [(0, 1), (1, 0)])  68.6 us
    dot_general x12, matrix products, in_product(): lax.dot_general(weight, tokens, (((0,), (1,)), ((), ())), preferred_eleme...  50.2 us
    dot_general x12, matrix products, out_product(): lax.dot_general(left, weight, (((0,), (1,)), ((), ())), preferred_element...  50.2 us
    ppermute x13, waiting for transfers between devices, along_dp(): lax.ppermute(piece, 'dp', [(j, j ^ flip) for j in range(lax.axis_size('dp...  49.1 us
    pallas_call x3, Pallas kernels, mix_forward(): pl.pallas_call(mix_kernel, grid=(seqs, chunks), in_specs=[slab, slab, sla...  43.5 us
    unnamed x312, local copies, waits for them, and re-layouts  30.5 us
    dot_general x4, matrix products, grad_product(): lax.dot_general(tokens, channels, (((0,), (1,)), ((), ())), preferred_ele...  20.8 us
  transfers between devices with their start and end apart: 24, of which 6 were waited for; matrix products, arithmetic and copies ran while one was open for 32% of the time, Pallas kernels for 24%

profile of v3, /device:TPU:0, one launch (start us, length us, event | category | flops | bytes accessed | tf_op | source)
XLA Modules:
  0.0 590.7 jit_solution(9969198097131845870)
XLA Ops:
  10.1 3.0 collective-permute-start.13
  13.1 2.1 dynamic-slice_convert_fusion
  15.2 2.1 dynamic-slice_convert_fusion.2
  17.4 2.0 collective-permute-start.1
  19.4 2.2 dynamic-slice_convert_fusion.1
  22.9 6.1 %fusion.43.dout_ref = f32[1024,1024]{1,0:T(8,128)} fusion(bf16[1024,1024]{1,0:T(8,128)(2,1)S(1)} %copy-done.72, bf16[2,1024,1024]{2,1,0:T(8,128)(2,1)} %cotangent_ref.3), kind=kOutput, calls=%fused_computation.71 | convolution fusion | flops 2147483648 | bytes 8388608 | tf_op jit(solution)/shard_map/dot_general | solution.py:460
  29.0 4.5 fusion.45.dout_ref
  39.8 4.5 convolution_bitcast_fusion.2.gate_ref
  44.3 4.5 convolution_bitcast_fusion.3.raw_ref.before_ref
  48.8 4.5 convolution_bitcast_fusion.gate_ref
  53.3 4.5 convolution_bitcast_fusion.1.raw_ref.before_ref
  60.0 5.7 multiply_convert_fusion.11
  66.9 2.0 fusion.149
  73.5 2.4 fusion.61
  80.6 1.9 broadcast_in_dim.15.conv_ref
  83.5 14.5 %mix_forward.3 = (f32[1024,1024]{1,0:T(8,128)}, bf16[8,1024,128]{2,1,0:T(8,128)(2,1)S(1)}, f32[8,8,128]{2,1,0:T(8,128)S(1)}) custom-call(f32[1024,1024]{1,0:T(8,128)} %convolution_bitcast_fusion.3.raw_ref.before_ref, f32[1024,1024]{1,0:T(8,128)} %convolution_bitcast_fusion.2.gate_ref, f32[1024,1024]{1,0:T(8,128)} %fusion.45.dout_ref, ...), custom_call_target="tpu_custom_call" | custom-call | flops 1073741824 | bytes 18874368 | tf_op jit(solution)/shard_map/mix_forward/pallas_call | solution.py:252
  99.9 2.0 collective-permute-start
  110.2 14.6 %mix_forward.4 = (f32[1024,1024]{1,0:T(8,128)}, bf16[8,1024,128]{2,1,0:T(8,128)(2,1)S(1)}, f32[8,8,128]{2,1,0:T(8,128)S(1)}) custom-call(f32[1024,1024]{1,0:T(8,128)} %convolution_bitcast_fusion.1.raw_ref.before_ref, f32[1024,1024]{1,0:T(8,128)} %convolution_bitcast_fusion.gate_ref, f32[1024,1024]{1,0:T(8,128)} %fusion.43.dout_ref, ...), custom_call_target="tpu_custom_call" | custom-call | flops 1073741824 | bytes 18874368 | tf_op jit(solution)/shard_map/mix_forward/pallas_call | solution.py:252
  126.1 4.1 collective-permute-done.2.second_ref
  130.2 22.5 %collective-permute-done.6.second_ref = f32[256,1024]{1,0:T(8,128)} collective-permute-done((f32[256,1024]{1,0:T(8,128)}, f32[256,1024]{1,0:T(8,128)}, u32[]{:S(2)}, u32[]{:S(2)}) %collective-permute-start.6) | collective-permute-done | bytes 1048608 | tf_op jit(solution)/shard_map/ppermute | solution.py:518
  152.6 19.9 %collective-permute-done.10.second_ref = f32[256,1024]{1,0:T(8,128)} collective-permute-done((f32[256,1024]{1,0:T(8,128)}, f32[256,1024]{1,0:T(8,128)}, u32[]{:S(2)}, u32[]{:S(2)}) %collective-permute-start.10) | collective-permute-done | bytes 1048608 | tf_op jit(solution)/shard_map/ppermute | solution.py:518
  173.0 7.9 %multiply_convert_fusion.8 = (bf16[1024,1024]{1,0:T(8,128)(2,1)}, bf16[1024,1024]{1,0:T(8,128)(2,1)}, f32[1024]{0:T(1024)S(1)}, bf16[1024,1024]{1,0:T(8,128)(2,1)S(1)}) fusion(f32[1024,1024]{1,0:T(8,128)} %convolution_bitcast_fusion.2.gate_ref, f32[1024,1024]{1,0:T(8,128)S(1)} %copy-done.29, f32[1024]{0:T(1024)S(1)} %bitcast.440, ...), kind=kLoop, calls=%fused_computation.54 | loop fusion | flops 26213376 | bytes 18890752 | tf_op jit(solution)/shard_map/convert_element_type | solution.py:592
  181.0 4.4 fusion.161.branch_ref
  186.7 3.4 assemble.4
  190.1 6.0 %fusion.163.gate_ref = f32[1024,1024]{1,0:T(8,128)} fusion(bf16[1024,1024]{1,0:T(8,128)(2,1)} %assemble.4, bf16[1024,1024]{1,0:T(8,128)(2,1)S(1)} %copy-done.22), kind=kOutput, calls=%fused_computation.332 | convolution fusion | flops 2147483648 | bytes 8388608 | tf_op jit(solution)/shard_map/dot_general | solution.py:460
  196.1 3.9 assemble.5
  199.9 6.0 %fusion.41.dout_ref = f32[1024,1024]{1,0:T(8,128)} fusion(bf16[1024,1024]{1,0:T(8,128)(2,1)} %assemble.5, bf16[2,1024,1024]{2,1,0:T(8,128)(2,1)S(1)} %copy-done.28), kind=kOutput, calls=%fused_computation.69 | convolution fusion | flops 2147483648 | bytes 8388608 | tf_op jit(solution)/shard_map/dot_general | solution.py:460
  205.9 3.4 assemble.3
  209.4 6.0 %fusion.162.raw_ref.before_ref = f32[1024,1024]{1,0:T(8,128)} fusion(bf16[1024,1024]{1,0:T(8,128)(2,1)} %assemble.3, bf16[1024,1024]{1,0:T(8,128)(2,1)S(1)} %copy-done.22), kind=kOutput, calls=%fused_computation.331 | convolution fusion | flops 2147483648 | bytes 8388608 | tf_op jit(solution)/shard_map/dot_general | solution.py:460
  215.6 2.0 broadcast_in_dim.18.conv_ref
  217.6 14.4 %mix_forward.5 = (f32[1024,1024]{1,0:T(8,128)}, bf16[8,1024,128]{2,1,0:T(8,128)(2,1)S(1)}, f32[8,8,128]{2,1,0:T(8,128)S(1)}) custom-call(f32[1024,1024]{1,0:T(8,128)} %fusion.162.raw_ref.before_ref, f32[1024,1024]{1,0:T(8,128)} %fusion.163.gate_ref, f32[1024,1024]{1,0:T(8,128)} %fusion.41.dout_ref, f32[8,8,16,128]{3,2,1,0:T(8,128)S(1)} %bitcast.340, ...), custom_call_target="tpu_custom_call" | custom-call | flops 1073741824 | bytes 18874368 | tf_op jit(solution)/shard_map/mix_forward/pallas_call | solution.py:252
  232.0 13.5 %multiply_convert_fusion.3 = (bf16[1024,1024]{1,0:T(8,128)(2,1)}, bf16[1024,1024]{1,0:T(8,128)(2,1)S(1)}, f32[1024]{0:T(1024)S(1)}, bf16[1024,1024]{1,0:T(8,128)(2,1)}, bf16[1024,1024]{1,0:T(8,128)(2,1)}) fusion(f32[1024,1024]{1,0:T(8,128)} %convolution_bitcast_fusion.gate_ref, f32[1024]{0:T(1024)S(1)} %bitcast.428, f32[1024,1024]{1,0:T(8,128)} %fusion.43.dout_ref, ...), kind=kLoop, calls=%fused_computation.45 | loop fusion | flops 38796288 | bytes 33574912 | tf_op jit(solution)/shard_map/convert_element_type | solution.py:591
  245.6 6.9 %fusion.33 = f32[1,1024,1024]{2,1,0:T(8,128)S(1)} fusion(bf16[1024,1024]{1,0:T(8,128)(2,1)S(1)} %get-tuple-element.211, bf16[1024,1024]{1,0:T(8,128)(2,1)} %get-tuple-element.212, bf16[1024,1024]{1,0:T(8,128)(2,1)S(1)} %copy-done.22, bf16[1024,1024]{1,0:T(8,128)(2,1)S(1)} %copy-done.25), kind=kOutput, calls=%fused_computation.60 | convolution fusion | flops 4311744512 | bytes 12582912 | tf_op jit(solution)/shard_map/dot_general | solution.py:464
  252.6 6.4 %fusion.30 = f32[1,1024,1024]{2,1,0:T(8,128)S(1)} fusion(bf16[2048,1024]{1,0:T(8,128)(2,1)S(1)} %bitcast.358, bf16[1024,1024]{1,0:T(8,128)(2,1)S(1)} %copy-done.43, bf16[1024,1024]{1,0:T(8,128)(2,1)} %copy-done.50), kind=kOutput, calls=%fused_computation.59 | convolution fusion | flops 4303355904 | bytes 12582912 | tf_op jit(solution)/shard_map/dot_general | solution.py:464
  259.0 4.2 pad_maximum_fusion
  267.8 7.2 %fusion.159 = f32[1024,1024]{1,0:T(8,128)} fusion(bf16[1024,1024]{1,0:T(8,128)(2,1)} %get-tuple-element.212, bf16[1024,1024]{1,0:T(8,128)(2,1)} %param.20), kind=kOutput, calls=%fused_computation.328 | convolution fusion | flops 2147483648 | bytes 8388608 | tf_op jit(solution)/shard_map/dot_general | solution.py:456
  275.4 4.9 fusion.37.received_ref
  280.2 4.4 fusion.164.branch_ref
  285.2 4.4 fusion.167
  289.6 66.8 %collective-permute-done.14.received_ref = f32[1024,1024]{1,0:T(8,128)} collective-permute-done((f32[1024,1024]{1,0:T(8,128)}, f32[1024,1024]{1,0:T(8,128)}, u32[]{:S(2)}, u32[]{:S(2)}) %collective-permute-start.14) | collective-permute-done | bytes 4194336 | tf_op jit(solution)/shard_map/ppermute | solution.py:484
  356.4 31.9 %mix_backward.3 = (bf16[1024,1024]{1,0:T(8,128)(2,1)}, f32[8,8,16,128]{3,2,1,0:T(8,128)S(1)}, f32[1024,256]{1,0:T(8,128)S(1)}, f32[5,1024,128]{2,1,0:T(8,128)}) custom-call(f32[1024,1024]{1,0:T(8,128)} %convolution_bitcast_fusion.3.raw_ref.before_ref, f32[1024,1024]{1,0:T(8,128)} %convolution_bitcast_fusion.3.raw_ref.before_ref, ...), custom_call_target="tpu_custom_call" | custom-call | flops 1024 | bytes 1024 | tf_op jit(solution)/shard_map/mix_backward/pallas_call | solution.py:294
  391.6 2.2 slice_reduce_fusion.1
  395.4 2.8 multiply_reduce_fusion.9
  398.6 3.1 multiply_reduce_fusion.8
  405.0 2.4 fusion.165
  407.4 2.7 add_add_fusion.2.part_ref
  410.4 31.7 %mix_backward.4 = (bf16[1024,1024]{1,0:T(8,128)(2,1)}, f32[8,8,16,128]{3,2,1,0:T(8,128)S(1)}, f32[1024,256]{1,0:T(8,128)S(1)}, f32[5,1024,128]{2,1,0:T(8,128)}) custom-call(f32[1024,1024]{1,0:T(8,128)} %convolution_bitcast_fusion.1.raw_ref.before_ref, f32[1024,1024]{1,0:T(8,128)} %convolution_bitcast_fusion.1.raw_ref.before_ref, ...), custom_call_target="tpu_custom_call" | custom-call | flops 1024 | bytes 1024 | tf_op jit(solution)/shard_map/mix_backward/pallas_call | solution.py:294
  443.1 2.2 copy.216
  447.4 1.9 fusion.85
  449.5 2.9 fusion.88
  459.5 4.5 fusion.23
  464.0 2.9 pad_maximum_fusion.1
  466.9 6.3 %copy.244 = f32[1024,1296]{1,0:T(8,128)} copy(f32[1024,1296]{0,1:T(8,128)} %pad_maximum_fusion.1) | data formatting | bytes 10616832
  473.9 11.4 %fusion.36 = f32[1024,1024]{1,0:T(8,128)} fusion(bf16[1024,1024]{1,0:T(8,128)(2,1)} %assemble.4, f32[1024,1024]{1,0:T(8,128)} %fusion.163.gate_ref, f32[1024,1024]{1,0:T(8,128)} %get-tuple-element.103.mixed_ref, f32[1024,1024]{1,0:T(8,128)} %fusion.41.dout_ref, f32[1024]{0:T(1024)S(1)} %copy-done.92, f32[1024]{0:T(1024)S(1)} %bitcast.429, ...), kind=kOutput, calls=%fused_computation.65 | convolution fusion | flops 2164260864 | bytes 18886656 | tf_op jit(solution)/shard_map/dot_general | solution.py:456
  487.8 2.4 fusion.168
  491.1 3.2 copy-done.16
  494.4 3.2 fusion.7
  500.4 1.8 collective-permute-done.16
  502.3 31.7 %mix_backward.5 = (bf16[1024,1024]{1,0:T(8,128)(2,1)}, f32[8,8,16,128]{3,2,1,0:T(8,128)S(1)}, f32[1024,256]{1,0:T(8,128)S(1)}, f32[5,1024,128]{2,1,0:T(8,128)}) custom-call(f32[1024,1024]{1,0:T(8,128)} %fusion.162.raw_ref.before_ref, f32[1024,1024]{1,0:T(8,128)} %fusion.162.raw_ref.before_ref, f32[1024,1024]{1,0:T(8,128)} %get-tuple-element.103.mixed_ref, ...), custom_call_target="tpu_custom_call" | custom-call | flops 1024 | bytes 1024 | tf_op jit(solution)/shard_map/mix_backward/pallas_call | solution.py:294
  543.4 2.6 collective-permute-done.18
  547.6 4.5 add_add_fusion.other_ref
  552.1 2.7 collective-permute-start.20
  555.7 10.1 %finish.2 = (bf16[2,1024,1024]{2,1,0:T(8,128)(2,1)}, f32[2,1024,1024]{2,1,0:T(8,128)}) custom-call(f32[1024,1024]{1,0:T(8,128)} %copy-done.20, f32[1024,1024]{1,0:T(8,128)} %add_add_fusion.other_ref, f32[1024,1024]{1,0:T(8,128)} %fusion.164.branch_ref, f32[1024,1024]{1,0:T(8,128)} %fusion.37.received_ref, bf16[2,1024,1024]{2,1,0:T(8,128)(2,1)} %hidden_ref.3, ...), custom_call_target="tpu_custom_call" | custom-call | flops 1024 | bytes 1024 | tf_op jit(solution)/shard_map/finish/pallas_call | solution.py:437
  571.1 10.1 %finish.3 = (bf16[2,1024,1024]{2,1,0:T(8,128)(2,1)}, f32[2,1024,1024]{2,1,0:T(8,128)}) custom-call(f32[1024,1024]{1,0:T(8,128)} %add_add_fusion.2.part_ref, f32[1024,1024]{1,0:T(8,128)} %collective-permute-done.15.other_ref, f32[1024,1024]{1,0:T(8,128)} %fusion.161.branch_ref, ...), custom_call_target="tpu_custom_call", output_to_operand_aliasing={{0}: (7, {}), {1}: (8, {})} | custom-call | flops 1024 | bytes 1024 | tf_op jit(solution)/shard_map/finish/pallas_call | solution.py:437
  (487 shorter events, 87.5 us)
Async XLA Ops:
  7.2 30.1 %copy-start = (bf16[1024,256]{1,0:T(8,128)(2,1)S(1)}, bf16[1024,256]{1,0:T(8,128)(2,1)}, u32[]{:S(2)}) copy-start(bf16[1024,256]{1,0:T(8,128)(2,1)} %param.22) | copy-start | bytes 1572868
  7.2 14.4 %copy-start.131 = (f32[16]{0:T(128)S(1)}, f32[16]{0:T(128)}, u32[]{:S(2)}) copy-start(f32[16]{0:T(128)} %param.30) | copy-start | bytes 196
  7.2 14.3 %copy-start.133 = (f32[16]{0:T(128)S(1)}, f32[16]{0:T(128)}, u32[]{:S(2)}) copy-start(f32[16]{0:T(128)} %param.29) | copy-start | bytes 196
  7.2 15.7 %copy-start.72 = (bf16[1024,1024]{1,0:T(8,128)(2,1)S(1)}, bf16[1024,1024]{1,0:T(8,128)(2,1)}, u32[]{:S(2)}) copy-start(bf16[1024,1024]{1,0:T(8,128)(2,1)} %param.32) | copy-start | bytes 6291460
  7.2 15.0 %copy-start.70 = (s32[2,1024]{1,0:T(2,128)S(1)}, s32[2,1024]{1,0:T(2,128)}, u32[]{:S(2)}) copy-start(s32[2,1024]{1,0:T(2,128)} %param.18) | copy-start | bytes 24580
  7.2 459.7 %reduce-scatter.5.cloned.1.call-start = ((), (), s32[]{:S(2)}) async-start(), calls=%async_computation.2 | async-start | bytes 8912896 | tf_op jit(solution)/shard_map/reduce_scatter | solution.py:725
  10.1 59.6 %collective-permute-start.13 = (f32[22576]{0:T(1024)S(1)}, f32[22576]{0:T(1024)}, u32[]{:S(2)}, u32[]{:S(2)}) collective-permute-start(f32[22576]{0:T(1024)S(1)} %concatenate.164), channel_id=1, source_target_pairs={{0,1},{1,0},{2,3},{3,2},{4,5},{5,4},{6,7},{7,6},{8,9},{9,8},{10,11... | collective-permute-start | bytes 270920 | tf_op jit(solution)/shard_map/ppermute | solution.py:553
  15.2 88.5 %collective-permute-start.9 = (f32[256,1024]{1,0:T(8,128)}, f32[256,1024]{1,0:T(8,128)}, u32[]{:S(2)}, u32[]{:S(2)}) collective-permute-start(f32[256,1024]{1,0:T(8,128)} %dynamic-slice_convert_fusion), channel_id=1, source_target_pairs={{0,1},{1,0},{2,3},{3,2},{4,5},{5,4},{6,7},{7,6},{8,9},{9,8},{10,11... | collective-permute-start | bytes 3145736 | tf_op jit(solution)/shard_map/ppermute | solution.py:514
  17.4 86.3 %collective-permute-start.1 = (f32[256,1024]{1,0:T(8,128)}, f32[256,1024]{1,0:T(8,128)}, u32[]{:S(2)}, u32[]{:S(2)}) collective-permute-start(f32[256,1024]{1,0:T(8,128)} %dynamic-slice_convert_fusion.2), channel_id=1, source_target_pairs={{0,1},{1,0},{2,3},{3,2},{4,5},{5,4},{6,7},{7,6},{8,9},{9,8},{10,11... | collective-permute-start | bytes 3145736 | tf_op jit(solution)/shard_map/ppermute | solution.py:514
  21.5 82.2 %collective-permute-start.5 = (f32[256,1024]{1,0:T(8,128)}, f32[256,1024]{1,0:T(8,128)}, u32[]{:S(2)}, u32[]{:S(2)}) collective-permute-start(f32[256,1024]{1,0:T(8,128)} %dynamic-slice_convert_fusion.1), channel_id=1, source_target_pairs={{0,1},{1,0},{2,3},{3,2},{4,5},{5,4},{6,7},{7,6},{8,9},{9,8},{10,11... | collective-permute-start | bytes 3145736 | tf_op jit(solution)/shard_map/ppermute | solution.py:514
  21.6 36.7 %copy-start.120 = (f32[16]{0:T(128)}, f32[16]{0:T(128)S(1)}, u32[]{:S(2)}) copy-start(f32[16]{0:T(128)S(1)} %exponential_negate_fusion) | copy-start | bytes 196
  34.4 39.1 %copy-start.87 = (f32[1024]{0:T(1024)}, f32[1024]{0:T(1024)S(1)}, u32[]{:S(2)}) copy-start(f32[1024]{0:T(1024)S(1)} %add_rsqrt_fusion) | copy-start | bytes 12292
  35.9 8.4 %copy-start.24 = (bf16[1024,1024]{1,0:T(8,128)(2,1)}, bf16[1024,1024]{1,0:T(8,128)(2,1)S(1)}, u32[]{:S(2)}) copy-start(bf16[1024,1024]{1,0:T(8,128)(2,1)S(1)} %get-tuple-element.219) | copy-start | bytes 6291460
  35.9 17.3 %copy-start.21 = (bf16[1024,1024]{1,0:T(8,128)(2,1)}, bf16[1024,1024]{1,0:T(8,128)(2,1)S(1)}, u32[]{:S(2)}) copy-start(bf16[1024,1024]{1,0:T(8,128)(2,1)S(1)} %get-tuple-element.218) | copy-start | bytes 6291460
  36.6 21.6 %copy-start.63 = (f32[16,1024]{1,0:T(8,128)}, f32[16,1024]{1,0:T(8,128)S(1)}, u32[]{:S(2)}) copy-start(f32[16,1024]{1,0:T(8,128)S(1)} %fusion.60) | copy-start | bytes 196612
  37.2 20.9 %copy-start.61 = (f32[16,1024]{1,0:T(8,128)}, f32[16,1024]{1,0:T(8,128)S(1)}, u32[]{:S(2)}) copy-start(f32[16,1024]{1,0:T(8,128)S(1)} %fusion.59) | copy-start | bytes 196612
  39.8 20.2 %copy-start.17 = (f32[1024,256]{0,1:T(8,128)}, f32[1024,256]{0,1:T(8,128)S(1)}, u32[]{:S(2)}) copy-start(f32[1024,256]{0,1:T(8,128)S(1)} %fusion.160) | copy-start | bytes 3145732
  58.2 21.0 %copy-start.55 = (f32[2,8,8,128]{3,2,1,0:T(8,128)}, f32[2,8,8,128]{3,2,1,0:T(8,128)S(1)}, u32[]{:S(2)}) copy-start(f32[2,8,8,128]{3,2,1,0:T(8,128)S(1)} %copy.250) | copy-start | bytes 196612
  58.3 10.8 %copy-start.57 = (f32[2,8,8,128]{3,2,1,0:T(8,128)}, f32[2,8,8,128]{3,2,1,0:T(8,128)S(1)}, u32[]{:S(2)}) copy-start(f32[2,8,8,128]{3,2,1,0:T(8,128)S(1)} %copy.248) | copy-start | bytes 196612
  60.0 9.5 %copy-start.81 = (f32[1024]{0:T(1024)}, f32[1024]{0:T(1024)S(1)}, u32[]{:S(2)}) copy-start(f32[1024]{0:T(1024)S(1)} %get-tuple-element.318) | copy-start | bytes 12292
  68.8 10.7 %copy-start.115 = (f32[8,2]{1,0:T(8,128)S(1)}, f32[8,2]{1,0:T(8,128)}, u32[]{:S(2)}) copy-start(f32[8,2]{1,0:T(8,128)} %stack.117) | copy-start | bytes 196
  83.5 19.8 %copy-start.66 = (f32[2,8,8,128]{3,2,1,0:T(8,128)S(1)}, f32[2,8,8,128]{3,2,1,0:T(8,128)}, u32[]{:S(2)}) copy-start(f32[2,8,8,128]{3,2,1,0:T(8,128)} %copy-done.65) | copy-start | bytes 196612
  83.5 20.0 %copy-start.71 = (f32[8,2,8]{1,0,2:T(8,128)S(1)}, f32[8,2,8]{1,0,2:T(8,128)}, u32[]{:S(2)}) copy-start(f32[8,2,8]{1,0,2:T(8,128)} %copy.200) | copy-start | bytes 1540
  83.5 23.8 %copy-start.83 = (f32[4,1024]{1,0:T(4,128)S(1)}, f32[4,1024]{1,0:T(4,128)}, u32[]{:S(2)}) copy-start(f32[4,1024]{1,0:T(4,128)} %reshape.740) | copy-start | bytes 49156
  99.9 24.8 %collective-permute-start = (f32[2,1024]{1,0:T(2,128)}, f32[2,1024]{1,0:T(2,128)}, u32[]{:S(2)}, u32[]{:S(2)}) collective-permute-start(f32[2,1024]{1,0:T(2,128)} %slice_bitcast_fusion.3), channel_id=1, source_target_pairs={{0,1},{1,0},{2,3},{3,2},{4,5},{5,4},{6,7},{7,6},{8,9},{9,8},{10,11... | collective-permute-start | bytes 24584 | tf_op jit(solution)/shard_map/ppermute | solution.py:484
  103.7 26.5 %collective-permute-start.2 = (f32[256,1024]{1,0:T(8,128)}, f32[256,1024]{1,0:T(8,128)}, u32[]{:S(2)}, u32[]{:S(2)}) collective-permute-start(f32[256,1024]{1,0:T(8,128)} %collective-permute-done.1.first_ref), channel_id=1, source_target_pairs={{0,4},{2,6},{4,0},{6,2},{8,12},{10,14},{12,8},{14,10},{16,20},{18,... | collective-permute-start | bytes 3145736 | tf_op jit(solution)/shard_map/ppermute | solution.py:518
  105.2 47.4 %collective-permute-start.6 = (f32[256,1024]{1,0:T(8,128)}, f32[256,1024]{1,0:T(8,128)}, u32[]{:S(2)}, u32[]{:S(2)}) collective-permute-start(f32[256,1024]{1,0:T(8,128)} %collective-permute-done.5.first_ref), channel_id=1, source_target_pairs={{0,4},{2,6},{4,0},{6,2},{8,12},{10,14},{12,8},{14,10},{16,20},{18,... | collective-permute-start | bytes 3145736 | tf_op jit(solution)/shard_map/ppermute | solution.py:518
  105.8 66.7 %collective-permute-start.10 = (f32[256,1024]{1,0:T(8,128)}, f32[256,1024]{1,0:T(8,128)}, u32[]{:S(2)}, u32[]{:S(2)}) collective-permute-start(f32[256,1024]{1,0:T(8,128)} %collective-permute-done.9.first_ref), channel_id=1, source_target_pairs={{0,4},{2,6},{4,0},{6,2},{8,12},{10,14},{12,8},{14,10},{16,20},{18,... | collective-permute-start | bytes 3145736 | tf_op jit(solution)/shard_map/ppermute | solution.py:518
  107.3 65.2 %collective-permute-start.11 = (f32[256,1024]{1,0:T(8,128)}, f32[256,1024]{1,0:T(8,128)}, u32[]{:S(2)}, u32[]{:S(2)}) collective-permute-start(f32[256,1024]{1,0:T(8,128)} %collective-permute-done.9.first_ref), channel_id=1, source_target_pairs={{0,2},{2,0},{4,6},{6,4},{8,10},{10,8},{12,14},{14,12},{16,18},{18,... | collective-permute-start | bytes 3145736 | tf_op jit(solution)/shard_map/ppermute | solution.py:518
  110.2 62.9 %copy-start.29 = (f32[1024,1024]{1,0:T(8,128)S(1)}, f32[1024,1024]{1,0:T(8,128)}, u32[]{:S(2)}) copy-start(f32[1024,1024]{1,0:T(8,128)} %get-tuple-element.69.mixed_ref) | copy-start | bytes 12582916
  110.2 62.9 %copy-start.84 = (f32[1024]{0:T(1024)S(1)}, f32[1024]{0:T(1024)}, u32[]{:S(2)}) copy-start(f32[1024]{0:T(1024)} %param.31) | copy-start | bytes 12292
  124.7 56.2 %copy-start.5 = (bf16[8,1024,128]{2,1,0:T(8,128)(2,1)}, bf16[8,1024,128]{2,1,0:T(8,128)(2,1)S(1)}, u32[]{:S(2)}) copy-start(bf16[8,1024,128]{2,1,0:T(8,128)(2,1)S(1)} %get-tuple-element.97.entry_ref) | copy-start | bytes 6291460
  125.5 59.9 %collective-permute-start.3 = (f32[256,1024]{1,0:T(8,128)}, f32[256,1024]{1,0:T(8,128)S(1)}, u32[]{:S(2)}, u32[]{:S(2)}) collective-permute-start(f32[256,1024]{1,0:T(8,128)} %collective-permute-done.1.first_ref), channel_id=1, source_target_pairs={{0,2},{2,0},{4,6},{6,4},{8,10},{10,8},{12,14},{14,12},{16,18},{18,... | collective-permute-start | bytes 3145736 | tf_op jit(solution)/shard_map/ppermute | solution.py:518
  130.2 55.2 %collective-permute-start.7 = (f32[256,1024]{1,0:T(8,128)}, f32[256,1024]{1,0:T(8,128)S(1)}, u32[]{:S(2)}, u32[]{:S(2)}) collective-permute-start(f32[256,1024]{1,0:T(8,128)} %collective-permute-done.5.first_ref), channel_id=1, source_target_pairs={{0,2},{2,0},{4,6},{6,4},{8,10},{10,8},{12,14},{14,12},{16,18},{18,... | collective-permute-start | bytes 3145736 | tf_op jit(solution)/shard_map/ppermute | solution.py:518
  152.6 33.7 %collective-permute-start.4 = (f32[256,1024]{1,0:T(8,128)}, f32[256,1024]{1,0:T(8,128)}, u32[]{:S(2)}, u32[]{:S(2)}) collective-permute-start(f32[256,1024]{1,0:T(8,128)} %collective-permute-done.2.second_ref), channel_id=1, source_target_pairs={{0,2},{2,0},{4,6},{6,4},{8,10},{10,8},{12,14},{14,12},{16,18},{18,... | collective-permute-start | bytes 3145736 | tf_op jit(solution)/shard_map/ppermute | solution.py:518
  172.5 12.8 %collective-permute-start.8 = (f32[256,1024]{1,0:T(8,128)}, f32[256,1024]{1,0:T(8,128)S(1)}, u32[]{:S(2)}, u32[]{:S(2)}) collective-permute-start(f32[256,1024]{1,0:T(8,128)} %collective-permute-done.6.second_ref), channel_id=1, source_target_pairs={{0,2},{2,0},{4,6},{6,4},{8,10},{10,8},{12,14},{14,12},{16,18},{18,... | collective-permute-start | bytes 3145736 | tf_op jit(solution)/shard_map/ppermute | solution.py:518
  172.5 12.8 %collective-permute-start.12 = (f32[256,1024]{1,0:T(8,128)}, f32[256,1024]{1,0:T(8,128)S(1)}, u32[]{:S(2)}, u32[]{:S(2)}) collective-permute-start(f32[256,1024]{1,0:T(8,128)} %collective-permute-done.10.second_ref), channel_id=1, source_target_pairs={{0,2},{2,0},{4,6},{6,4},{8,10},{10,8},{12,14},{14,12},{16,18},{18,... | collective-permute-start | bytes 3145736 | tf_op jit(solution)/shard_map/ppermute | solution.py:518
  232.0 13.6 %copy-start.4 = (bf16[8,1024,128]{2,1,0:T(8,128)(2,1)}, bf16[8,1024,128]{2,1,0:T(8,128)(2,1)S(1)}, u32[]{:S(2)}) copy-start(bf16[8,1024,128]{2,1,0:T(8,128)(2,1)S(1)} %get-tuple-element.105.entry_ref) | copy-start | bytes 6291460
  232.0 13.5 %copy-start.110 = (f32[1,1024]{1,0:T(1,128)}, f32[1,1024]{1,0:T(1,128)S(1)}, u32[]{:S(2)}) copy-start(f32[1,1024]{1,0:T(1,128)S(1)} %get-tuple-element.202) | copy-start | bytes 12292
  232.0 43.1 %copy-start.112 = (f32[1,8,128]{2,0,1:T(1,128)}, f32[1,8,128]{2,0,1:T(1,128)S(1)}, u32[]{:S(2)}) copy-start(f32[1,8,128]{2,0,1:T(1,128)S(1)} %get-tuple-element.203) | copy-start | bytes 12292
  232.0 13.5 %copy-start.25 = (bf16[1024,1024]{1,0:T(8,128)(2,1)S(1)}, bf16[1024,1024]{1,0:T(8,128)(2,1)}, u32[]{:S(2)}) copy-start(bf16[1024,1024]{1,0:T(8,128)(2,1)} %copy-done.24) | copy-start | bytes 6291460
  263.3 303.2 %reduce-scatter.7.cloned.1.call-start = ((), (), s32[]{:S(2)}) async-start(), calls=%async_computation.3 | async-start | bytes 6127616
  263.5 92.9 %collective-permute-start.14 = (f32[1024,1024]{1,0:T(8,128)}, f32[1024,1024]{1,0:T(8,128)}, u32[]{:S(2)}, u32[]{:S(2)}) collective-permute-start(f32[1024,1024]{1,0:T(8,128)} %fusion.161.branch_ref), channel_id=1, source_target_pairs={{0,1},{1,0},{2,3},{3,2},{4,5},{5,4},{6,7},{7,6},{8,9},{9,8},{10,11... | collective-permute-start | bytes 12582920 | tf_op jit(solution)/shard_map/ppermute | solution.py:484
  285.2 71.2 %copy-start.3 = (bf16[128,1024]{1,0:T(8,128)(2,1)S(1)}, bf16[128,1024]{1,0:T(8,128)(2,1)}, u32[]{:S(2)}) copy-start(bf16[128,1024]{1,0:T(8,128)(2,1)} %get-tuple-element.241.outt_ref) | copy-start | bytes 786436
  285.2 71.2 %copy-start.7 = (bf16[1024,128]{1,0:T(8,128)(2,1)S(1)}, bf16[1024,128]{1,0:T(8,128)(2,1)}, u32[]{:S(2)}) copy-start(bf16[1024,128]{1,0:T(8,128)(2,1)} %copy.209.out_ref) | copy-start | bytes 786436
  285.2 71.2 %copy-start.8 = (bf16[128,1024]{1,0:T(8,128)(2,1)S(1)}, bf16[128,1024]{1,0:T(8,128)(2,1)}, u32[]{:S(2)}) copy-start(bf16[128,1024]{1,0:T(8,128)(2,1)} %get-tuple-element.240.intot_ref) | copy-start | bytes 786436
  356.4 37.5 %copy-start.121 = (f32[16]{0:T(128)S(1)}, f32[16]{0:T(128)}, u32[]{:S(2)}) copy-start(f32[16]{0:T(128)} %copy-done.120) | copy-start | bytes 196
  356.4 38.3 %copy-start.64 = (f32[16,1024]{1,0:T(8,128)S(1)}, f32[16,1024]{1,0:T(8,128)}, u32[]{:S(2)}) copy-start(f32[16,1024]{1,0:T(8,128)} %copy-done.63) | copy-start | bytes 196612
  410.1 92.1 %collective-permute-start.15 = (f32[1024,1024]{1,0:T(8,128)}, f32[1024,1024]{1,0:T(8,128)}, u32[]{:S(2)}, u32[]{:S(2)}) collective-permute-start(f32[1024,1024]{1,0:T(8,128)} %add_add_fusion.2.part_ref), channel_id=1, source_target_pairs={{0,1},{1,0},{2,3},{3,2},{4,5},{5,4},{6,7},{7,6},{8,9},{9,8},{10,11... | collective-permute-start | bytes 12582920 | tf_op jit(solution)/shard_map/ppermute | solution.py:484
  410.4 37.0 %copy-start.56 = (f32[2,8,8,128]{3,2,1,0:T(8,128)S(1)}, f32[2,8,8,128]{3,2,1,0:T(8,128)}, u32[]{:S(2)}) copy-start(f32[2,8,8,128]{3,2,1,0:T(8,128)} %copy-done.55) | copy-start | bytes 196612
  410.4 37.0 %copy-start.58 = (f32[2,8,8,128]{3,2,1,0:T(8,128)S(1)}, f32[2,8,8,128]{3,2,1,0:T(8,128)}, u32[]{:S(2)}) copy-start(f32[2,8,8,128]{3,2,1,0:T(8,128)} %copy-done.57) | copy-start | bytes 196612
  410.4 37.0 %copy-start.122 = (f32[16]{0:T(128)S(1)}, f32[16]{0:T(128)}, u32[]{:S(2)}) copy-start(f32[16]{0:T(128)} %copy-done.120) | copy-start | bytes 196
  410.4 38.9 %copy-start.62 = (f32[16,1024]{1,0:T(8,128)S(1)}, f32[16,1024]{1,0:T(8,128)}, u32[]{:S(2)}) copy-start(f32[16,1024]{1,0:T(8,128)} %copy-done.61) | copy-start | bytes 196612
  473.9 11.4 %copy-start.126 = (f32[256]{0:T(256)S(1)}, f32[256]{0:T(256)}, u32[]{:S(2)}) copy-start(f32[256]{0:T(256)} %get-tuple-element.184) | copy-start | bytes 3076
  473.9 11.4 %copy-start.127 = (f32[256]{0:T(256)S(1)}, f32[256]{0:T(256)}, u32[]{:S(2)}) copy-start(f32[256]{0:T(256)} %get-tuple-element.187) | copy-start | bytes 3076
  473.9 11.4 %copy-start.128 = (f32[256]{0:T(256)S(1)}, f32[256]{0:T(256)}, u32[]{:S(2)}) copy-start(f32[256]{0:T(256)} %get-tuple-element.224) | copy-start | bytes 3076
  473.9 11.5 %copy-start.129 = (f32[256]{0:T(256)S(1)}, f32[256]{0:T(256)}, u32[]{:S(2)}) copy-start(f32[256]{0:T(256)} %get-tuple-element.172) | copy-start | bytes 3076
  473.9 11.5 %copy-start.48 = (bf16[1024,256]{0,1:T(8,128)(2,1)S(1)}, bf16[1024,256]{0,1:T(8,128)(2,1)}, u32[]{:S(2)}) copy-start(bf16[1024,256]{0,1:T(8,128)(2,1)} %copy-done.47) | copy-start | bytes 1572868
  497.7 4.5 collective-permute-start.16
  502.3 38.7 %collective-permute-start.17 = (f32[8496]{0:T(1024)S(1)}, f32[8496]{0:T(1024)S(1)}, u32[]{:S(2)}, u32[]{:S(2)}) collective-permute-start(f32[8496]{0:T(1024)S(1)} %concatenate.173), channel_id=1, source_target_pairs={{0,2},{2,0},{4,6},{6,4},{8,10},{10,8},{12,14},{14,12},{16,18},{18,... | collective-permute-start | bytes 101960 | tf_op jit(solution)/shard_map/ppermute | solution.py:518
  541.0 5.0 collective-permute-start.18
  546.0 6.1 %collective-permute-start.19 = (f32[8496]{0:T(1024)S(1)}, f32[8496]{0:T(1024)S(1)}, u32[]{:S(2)}, u32[]{:S(2)}) collective-permute-start(f32[8496]{0:T(1024)S(1)} %add.428), channel_id=1, source_target_pairs={{0,8},{2,10},{4,12},{6,14},{8,0},{10,2},{12,4},{14,6},{16,24},{18,... | collective-permute-start | bytes 101960 | tf_op jit(solution)/shard_map/ppermute | solution.py:518
  552.1 13.7 %collective-permute-start.20 = (f32[8496]{0:T(1024)S(1)}, f32[8496]{0:T(1024)S(1)}, u32[]{:S(2)}, u32[]{:S(2)}) collective-permute-start(f32[8496]{0:T(1024)S(1)} %add.429), channel_id=1, source_target_pairs={{0,16},{2,18},{4,20},{6,22},{8,24},{10,26},{12,28},{14,30},{16,0},... | collective-permute-start | bytes 101960 | tf_op jit(solution)/shard_map/ppermute | solution.py:518
  567.7 15.0 %collective-permute-start.21 = (f32[64,256]{0,1:T(8,128)S(1)}, f32[64,256]{0,1:T(8,128)S(1)}, u32[]{:S(2)}, u32[]{:S(2)}) collective-permute-start(f32[64,256]{0,1:T(8,128)S(1)} %slice.422), channel_id=1, source_target_pairs={{0,1},{1,0},{2,3},{3,2},{4,5},{5,4},{6,7},{7,6},{8,9},{9,8},{10,11... | collective-permute-start | bytes 196616 | tf_op jit(solution)/shard_map/ppermute | solution.py:484
  (101 other events, 387.0 us)
Sparse Core Ops, SparseCore 0:
  263.4 104.8 reduce-scatter.4
  473.4 85.4 reduce-scatter.6

commit v4 on v3

--- a/solution.py
+++ b/solution.py
@@ -277,7 +277,7 @@
         ],
         compiler_params=pltpu.CompilerParams(vmem_limit_bytes=VMEM_BYTES),
         cost_estimate=pl.CostEstimate(
-            flops=tokens * ch * 1024, bytes_accessed=tokens * ch * 18, transcendentals=tokens * ch * 4
+            flops=tokens, bytes_accessed=tokens, transcendentals=0
         ),
         name="mix_forward",
     )(raw, gate, dout, rows, masks, into, outt, conv, gain)
@@ -559,15 +559,16 @@
     return result
 
 
-def unit_forward(weights, normed, cotangent, segments, states):
+def unit_forward(weights, normed, cotangent, segments, states, earlier=(), between=()):
     step = in_product(weights["step"], normed)
-    gate = in_product(weights["gate"], normed)
-    raw = in_product(weights["value"], normed)
-    dout = in_product(weights["out"], cotangent)
+    gate = in_product(weights["gate"], normed).astype(bf16)
+    dout = in_product(weights["out"], cotangent).astype(bf16)
+    raw = in_product(weights["value"], after(normed, *earlier)).astype(bf16)
     rows, masks = step_rows(
         step, weights["step_bias"], weights["decay_log"], weights["skip_gain"], segments
     )
     into, _, _, outt = states
+    rows = after(rows, *between)
     mixed, entry, sums = mix_forward(
         1, raw, gate, dout, rows, masks, into, outt, weights["conv"], weights["gain_wide"]
     )
@@ -580,6 +581,7 @@
 
 def unit_middle(unit, weights, both, inner_total):
     gate, mixed, dout = unit["gate"], unit["mixed"], unit["dout"]
+    gate, dout = gate.astype(jnp.float32), dout.astype(jnp.float32)
     gain = weights["gate_gain"][:, None]
     sigma = sigmoid(gate)
     gated = mixed * gate * sigma
@@ -660,6 +662,7 @@
         )
         sent = dict(value=proj_value, gate=proj_gate, out=proj_out)
         first = {k: gather_first(w) for k, w in sent.items()}
+        second = dict(value=along_dp(first["value"], 2))
         other["conv"] = wide_lanes(jnp.concatenate([c_w, c_b[None, :]], axis=0))
         other["gain_wide"] = wide_lanes(g_g)
 
@@ -679,39 +682,60 @@
         low = state_conv.astype(bf16)
         into, out = low[:, :STATE], low[:, STATE:]
         states.append((into, into.T, out, out.T))
-        units.append(unit_forward(own, normeds[s], out_grad[s], segment_ids[s : s + 1], states[s]))
+        between = (second["value"],) if 0 < s == whole_from else ()
+        units.append(
+            unit_forward(
+                own, normeds[s], out_grad[s], segment_ids[s : s + 1], states[s], between=between
+            )
+        )
         if s < whole_from:
             sums = units[s]["sums"]
             boths.append(tensor_join(sums, tensor_others(sums)))
     branches, received, output_ins, d_gates, d_mixeds = [], [], [], [], []
     grad_gate_gain = jnp.zeros((local_inner,), jnp.float32)
-    extras, middles = {}, {}
+    extras, middles, arrivals = {}, {}, ()
     if whole_from < seq_count:
-        second = {k: along_dp(after(first[k], units[0]["mixed"]), 2) for k in sent}
+        second["gate"] = along_dp(after(first["gate"], units[0]["mixed"]), 2)
+        second["out"] = along_dp(after(first["out"], units[-1]["mixed"]), 2)
         third = {k: along_dp(first[k], 1) for k in sent}
-        fourth = {k: along_dp(after(second[k], units[-1]["mixed"]), 1) for k in sent}
-    for s in every:
-        if s == whole_from:
-            for k in sent:
-                pieces = (first[k], second[k], third[k], fourth[k])
-                pieces = lax.optimization_barrier((*pieces, branches[0]))[:4]
-                other[k] = assemble(sent[k], *pieces)
-        if s >= whole_from:
-            extras[s] = unit_forward(
-                other, normeds[s], out_grad[s], segment_ids[s : s + 1], states[s]
-            )
-            boths.append(units[s]["sums"] + extras[s]["sums"])
-            middles[s] = unit_middle(extras[s], other, boths[s], inner_total)
+        fourth = {k: along_dp(second[k], 1) for k in sent}
+        arrivals = (second["out"],)
+
+    backs, parts, others = [], [], []
+
+    def own_middle(s):
         output_in, d_gate, d_mixed, grad_gain = unit_middle(units[s], own, boths[s], inner_total)
-        grad_gate_gain = grad_gate_gain + grad_gain
         output_ins.append(output_in)
         d_gates.append(d_gate)
         d_mixeds.append(d_mixed)
         branches.append(lax.optimization_barrier(out_product(output_in, proj_out)))
-        if s < whole_from:
-            received.append(tensor_others(branches[s]))
-        else:
-            received.append(lax.optimization_barrier(out_product(middles[s][0], other["out"])))
+        return grad_gain
+
+    def own_backward(s, earlier, between=()):
+        d_mixed = after(d_mixeds[s], *earlier)
+        d_value, *rest = unit_backward(units[s], own, d_gates[s], d_mixed, state_backs[s])
+        backs.append((after(d_value, *between), *rest))
+        parts.append(lax.optimization_barrier(normed_part(own, d_gates[s], *backs[s][:3])))
+
+    for s in range(whole_from):
+        grad_gate_gain = grad_gate_gain + own_middle(s)
+        received.append(tensor_others(branches[s]))
+        earlier = (second["gate"],) if arrivals else ()
+        own_backward(s, (branches[s], *earlier), arrivals)
+        others.append(tensor_others(parts[s]))
+    if whole_from < seq_count:
+        for k in sent:
+            pieces = (first[k], second[k], third[k], fourth[k])
+            pieces = lax.optimization_barrier((*pieces, parts[0]))[:4]
+            other[k] = assemble(sent[k], *pieces)
+    for s in range(whole_from, seq_count):
+        extras[s] = unit_forward(
+            other, normeds[s], out_grad[s], segment_ids[s : s + 1], states[s], (received[0],)
+        )
+        boths.append(units[s]["sums"] + extras[s]["sums"])
+        grad_gate_gain = grad_gate_gain + own_middle(s)
+        middles[s] = unit_middle(extras[s], other, boths[s], inner_total)
+        received.append(lax.optimization_barrier(out_product(middles[s][0], other["out"])))
 
     normed_all = jnp.concatenate(normeds, axis=0)
     early_part = jnp.stack(
@@ -724,15 +748,8 @@
     )
     early = lax.psum_scatter(early_part, "dp", scatter_dimension=1, tiled=True)
 
-    backs, parts, others = [], [], []
-    waits = (early_part, *branches, received[0])
-    for s in every:
-        back = unit_backward(units[s], own, d_gates[s], after(d_mixeds[s], *waits), state_backs[s])
-        backs.append(back)
-        parts.append(lax.optimization_barrier(normed_part(own, d_gates[s], *back[:3])))
-        if s < whole_from:
-            others.append(tensor_others(parts[s]))
-            waits = (parts[s],)
+    for s in range(whole_from, seq_count):
+        own_backward(s, (early_part, branches[s]))
     later_part = jnp.concatenate(
         [
             grad_product(normed_all, jnp.concatenate([b[0] for b in backs], axis=1)),

time: 598 us -> 537 us (0.90)
  waiting for transfers between devices: 118 us -> 65 us
  Pallas kernels: 170 us -> 162 us
  other arithmetic: 70.8 us -> 78.1 us
    ppermute x5, waiting for transfers between devices: 68.6 us -> 0.01 us  [tensor_others(): return lax.ppermute(part, 'tensor', [(0, 1), (1, 0)])]
    reduce_scatter x1, waiting for transfers between devices: 0.01 us -> 31.2 us  [local(): early = lax.psum_scatter(early_part, 'dp', scatter_dimension=1, tiled=True)]
    ppermute x13, waiting for transfers between devices: 49.1 us -> 33.7 us  [along_dp(): lax.ppermute(piece, 'dp', [(j, j ^ flip) for j in range(lax.axis_size('dp...]
    convert_element_type x1 -> x2, other arithmetic: 7.9 us -> 22.8 us  [unit_middle(): (d_gated * mixed * sigma * (1.0 + gate * (1.0 - sigma))).astype(bf16)]
    convert_element_type x1 -> x0, other arithmetic: 13.5 us -> none  [unit_middle(): d_mixed = (d_gated * gate * sigma).astype(bf16)]
    unnamed x312 -> x352, local copies, waits for them, and re-layouts: 30.5 us -> 33.7 us
  transfers between devices with their start and end apart: 24 -> 24, of which waited for: 6 -> 4; matrix products, arithmetic and copies ran while one was open for 32% -> 39% of each run, Pallas kernels for 24% -> 28%
where the time goes in v4:
time: 537 us; the launch traced here: 533 us
  Pallas kernels  162 us (30%)
  matrix products  127 us (24%)
  other arithmetic  78.1 us (15%)
  local copies, waits for them, and re-layouts  65.6 us (12%)
  waiting for transfers between devices  65 us (12%)
  starting transfers between devices  18.6 us (3%)
  between operations  16.4 us (3%)
    pallas_call x3, Pallas kernels, mix_backward(): pl.pallas_call(back_kernel, grid=(seqs, chunks), in_specs=[slab, spec((ch...  90.5 us
    dot_general x12, matrix products, out_product(): lax.dot_general(left, weight, (((0,), (1,)), ((), ())), preferred_element...  49.2 us
    dot_general x12, matrix products, in_product(): lax.dot_general(weight, tokens, (((0,), (1,)), ((), ())), preferred_eleme...  46 us
    pallas_call x3, Pallas kernels, mix_forward(): pl.pallas_call(mix_kernel, grid=(seqs, chunks), in_specs=[slab, slab, sla...  40.9 us
    unnamed x352, local copies, waits for them, and re-layouts  33.7 us
    ppermute x13, waiting for transfers between devices, along_dp(): lax.ppermute(piece, 'dp', [(j, j ^ flip) for j in range(lax.axis_size('dp...  33.7 us
    reduce_scatter x1, waiting for transfers between devices, local(): early = lax.psum_scatter(early_part, 'dp', scatter_dimension=1, tiled=True)  31.2 us
    convert_element_type x2, other arithmetic, unit_middle(): (d_gated * mixed * sigma * (1.0 + gate * (1.0 - sigma))).astype(bf16)  22.8 us
  transfers between devices with their start and end apart: 24, of which 4 were waited for; matrix products, arithmetic and copies ran while one was open for 39% of the time, Pallas kernels for 28%

profile of v4, /device:TPU:0, one launch (start us, length us, event | category | flops | bytes accessed | tf_op | source)
XLA Modules:
  0.0 533.1 jit_solution(3028104343586817470)
XLA Ops:
  10.6 3.0 collective-permute-start.14
  13.5 2.3 dynamic-slice_convert_fusion.2
  15.8 2.2 dynamic-slice_convert_fusion
  18.0 2.0 collective-permute-start.4
  20.0 2.2 dynamic-slice_convert_fusion.1
  23.1 2.3 fusion.13
  25.6 3.7 convert_bitcast_fusion.3.gate_ref
  31.3 2.2 fusion.106
  33.6 2.5 fusion.207
  36.9 3.7 convert_bitcast_fusion.1.gate_ref
  40.6 3.8 fusion.92.dout_ref
  44.4 3.8 fusion.95.dout_ref
  48.2 4.2 convert_bitcast_fusion.4.raw_ref.before_ref
  57.3 3.3 multiply_convert_fusion.4
  62.6 6.0 %convert_bitcast_fusion.2.raw_ref.before_ref = bf16[1024,1024]{1,0:T(8,128)(2,1)} fusion(bf16[1024,1024]{1,0:T(8,128)(2,1)} %get-tuple-element.84, bf16[1024,1024]{1,0:T(8,128)(2,1)} %param.21), kind=kOutput, calls=%fused_computation.116 | convolution fusion | flops 2148532224 | bytes 6291456 | tf_op jit(solution)/shard_map/dot_general | solution.py:460
  75.6 2.4 fusion.108
  82.3 1.9 broadcast_in_dim.15.conv_ref
  85.1 13.5 %mix_forward.3 = (f32[1024,1024]{1,0:T(8,128)}, bf16[8,1024,128]{2,1,0:T(8,128)(2,1)S(1)}, f32[8,8,128]{2,1,0:T(8,128)S(1)}) custom-call(bf16[1024,1024]{1,0:T(8,128)(2,1)} %convert_bitcast_fusion.4.raw_ref.before_ref, bf16[1024,1024]{1,0:T(8,128)(2,1)} %convert_bitcast_fusion.3.gate_ref, bf16[1024,1024]{1,0:T(8,128)(2,1)} %fusion.92.dout_ref, ...), custom_call_target="tpu_custom_call" | custom-call | flops 1024 | bytes 1024 | tf_op jit(solution)/shard_map/mix_forward/pallas_call | solution.py:252
  100.6 2.0 collective-permute-start
  111.4 9.2 %fusion.31 = (bf16[1024,1024]{1,0:T(8,128)(2,1)S(1)}, bf16[1024,1024]{1,0:T(8,128)(2,1)}, f32[1024]{0:T(1024)}, bf16[1024,1024]{1,0:T(8,128)(2,1)S(1)}) fusion(bf16[1024,1024]{1,0:T(8,128)(2,1)} %convert_bitcast_fusion.3.gate_ref, f32[1024,1024]{1,0:T(8,128)} %get-tuple-element.68.mixed_ref, bf16[1024,1024]{1,0:T(8,128)(2,1)} %fusion.92.dout_ref, ...), kind=kLoop, calls=%fused_computation.54 | loop fusion | flops 28310528 | bytes 14696448 | tf_op jit(solution)/shard_map/convert_element_type | solution.py:594
  122.1 4.3 fusion.206.branch_ref
  127.0 4.4 fusion.205
  131.5 15.6 %collective-permute-done.2.second_ref = f32[256,1024]{1,0:T(8,128)} collective-permute-done((f32[256,1024]{1,0:T(8,128)}, f32[256,1024]{1,0:T(8,128)}, u32[]{:S(2)}, u32[]{:S(2)}) %collective-permute-start.2) | collective-permute-done | bytes 1048608 | tf_op jit(solution)/shard_map/ppermute | solution.py:518
  147.1 29.9 %mix_backward.3 = (bf16[1024,1024]{1,0:T(8,128)(2,1)}, f32[8,8,16,128]{3,2,1,0:T(8,128)S(1)}, f32[1024,256]{1,0:T(8,128)S(1)}, f32[5,1024,128]{2,1,0:T(8,128)}) custom-call(bf16[1024,1024]{1,0:T(8,128)(2,1)} %convert_bitcast_fusion.4.raw_ref.before_ref, bf16[1024,1024]{1,0:T(8,128)(2,1)} %convert_bitcast_fusion.4.raw_ref.before_ref, ...), custom_call_target="tpu_custom_call" | custom-call | flops 1024 | bytes 1024 | tf_op jit(solution)/shard_map/mix_backward/pallas_call | solution.py:294
  180.2 3.8 multiply_reduce_fusion.7
  184.0 2.3 multiply_reduce_fusion.6
  189.0 13.7 %mix_forward.4 = (f32[1024,1024]{1,0:T(8,128)}, bf16[8,1024,128]{2,1,0:T(8,128)(2,1)S(1)}, f32[8,8,128]{2,1,0:T(8,128)S(1)}) custom-call(bf16[1024,1024]{1,0:T(8,128)(2,1)} %convert_bitcast_fusion.2.raw_ref.before_ref, bf16[1024,1024]{1,0:T(8,128)(2,1)} %convert_bitcast_fusion.1.gate_ref, bf16[1024,1024]{1,0:T(8,128)(2,1)} %fusion.95.dout_ref, ...), custom_call_target="tpu_custom_call" | custom-call | flops 1024 | bytes 1024 | tf_op jit(solution)/shard_map/mix_forward/pallas_call | solution.py:252
  210.7 2.8 multiply_reduce_fusion.4
  214.3 15.7 %collective-permute-done.6.second_ref = f32[256,1024]{1,0:T(8,128)S(1)} collective-permute-done((f32[256,1024]{1,0:T(8,128)}, f32[256,1024]{1,0:T(8,128)S(1)}, u32[]{:S(2)}, u32[]{:S(2)}) %collective-permute-start.6) | collective-permute-done | bytes 1048608 | tf_op jit(solution)/shard_map/ppermute | solution.py:518
  231.5 4.8 add_add_fusion.2.part_ref
  236.3 3.7 assemble.3
  240.0 3.9 assemble.4
  243.9 5.3 %convolution_convert_fusion.gate_ref = bf16[1024,1024]{1,0:T(8,128)(2,1)} fusion(bf16[1024,1024]{1,0:T(8,128)(2,1)} %assemble.4, bf16[1024,1024]{1,0:T(8,128)(2,1)S(1)} %copy-done.26), kind=kOutput, calls=%fused_computation.125 | convolution fusion | flops 2148532224 | bytes 6291456 | tf_op jit(solution)/shard_map/dot_general | solution.py:460
  249.2 3.1 assemble.5
  252.3 6.1 %fusion.98.dout_ref = bf16[1024,1024]{1,0:T(8,128)(2,1)} fusion(bf16[1024,1024]{1,0:T(8,128)(2,1)} %assemble.5, bf16[2,1024,1024]{2,1,0:T(8,128)(2,1)} %cotangent_ref.3), kind=kOutput, calls=%fused_computation.124 | convolution fusion | flops 2148532224 | bytes 6291456 | tf_op jit(solution)/shard_map/dot_general | solution.py:460
  258.4 4.1 convolution_convert_fusion.1.raw_ref.before_ref
  262.5 1.9 broadcast_in_dim.18.conv_ref
  264.7 13.7 %mix_forward.5 = (f32[1024,1024]{1,0:T(8,128)}, bf16[8,1024,128]{2,1,0:T(8,128)(2,1)S(1)}, f32[8,8,128]{2,1,0:T(8,128)S(1)}) custom-call(bf16[1024,1024]{1,0:T(8,128)(2,1)} %convolution_convert_fusion.1.raw_ref.before_ref, bf16[1024,1024]{1,0:T(8,128)(2,1)} %convolution_convert_fusion.gate_ref, bf16[1024,1024]{1,0:T(8,128)(2,1)} %fusion.98.dout_ref, ...), custom_call_target="tpu_custom_call" | custom-call | flops 1024 | bytes 1024 | tf_op jit(solution)/shard_map/mix_forward/pallas_call | solution.py:252
  278.4 13.6 %fusion.43 = (bf16[1024,1024]{1,0:T(8,128)(2,1)S(1)}, bf16[1024,1024]{1,0:T(8,128)(2,1)}, f32[1024]{0:T(1024)}, bf16[1024,1024]{1,0:T(8,128)(2,1)}, bf16[1024,1024]{1,0:T(8,128)(2,1)}) fusion(bf16[1024,1024]{1,0:T(8,128)(2,1)S(1)} %copy-done.37, f32[1024,1024]{1,0:T(8,128)} %get-tuple-element.74.mixed_ref, bf16[1024,1024]{1,0:T(8,128)(2,1)} %fusion.95.dout_ref, ...), kind=kLoop, calls=%fused_computation.66 | loop fusion | flops 42990592 | bytes 25186304 | tf_op jit(solution)/shard_map/convert_element_type | solution.py:594
  292.1 6.9 %fusion.71 = f32[1,1024,1024]{2,1,0:T(8,128)S(1)} fusion(bf16[1024,1024]{1,0:T(8,128)(2,1)S(1)} %get-tuple-element.208, bf16[1024,1024]{1,0:T(8,128)(2,1)} %copy-done.65, bf16[1024,1024]{1,0:T(8,128)(2,1)S(1)} %copy-done.26, bf16[1024,1024]{1,0:T(8,128)(2,1)S(1)} %copy-done.30), kind=kOutput, calls=%fused_computation.101 | convolution fusion | flops 4311744512 | bytes 12582912 | tf_op jit(solution)/shard_map/dot_general | solution.py:464
  299.1 6.1 %fusion.68 = f32[1,1024,1024]{2,1,0:T(8,128)S(1)} fusion(bf16[2048,1024]{1,0:T(8,128)(2,1)S(1)} %bitcast.364, bf16[1024,1024]{1,0:T(8,128)(2,1)S(1)} %copy-done.57, bf16[1024,1024]{1,0:T(8,128)(2,1)} %copy-done.64), kind=kOutput, calls=%fused_computation.100 | convolution fusion | flops 4303355904 | bytes 12582912 | tf_op jit(solution)/shard_map/dot_general | solution.py:464
  305.2 4.2 pad_maximum_fusion
  312.0 6.7 %fusion.210.branch_ref = f32[1024,1024]{1,0:T(8,128)} fusion(bf16[1024,1024]{1,0:T(8,128)(2,1)} %get-tuple-element.215, bf16[1024,1024]{1,0:T(8,128)(2,1)} %param.32), kind=kOutput, calls=%fused_computation.378 | convolution fusion | flops 2147483648 | bytes 8388608 | tf_op jit(solution)/shard_map/dot_general | solution.py:456
  318.7 30.6 %mix_backward.4 = (bf16[1024,1024]{1,0:T(8,128)(2,1)}, f32[8,8,16,128]{3,2,1,0:T(8,128)S(1)}, f32[1024,256]{1,0:T(8,128)S(1)}, f32[5,1024,128]{2,1,0:T(8,128)}) custom-call(bf16[1024,1024]{1,0:T(8,128)(2,1)} %convert_bitcast_fusion.2.raw_ref.before_ref, bf16[1024,1024]{1,0:T(8,128)(2,1)} %convert_bitcast_fusion.2.raw_ref.before_ref, ...), custom_call_target="tpu_custom_call" | custom-call | flops 1024 | bytes 1024 | tf_op jit(solution)/shard_map/mix_backward/pallas_call | solution.py:294
  351.8 2.4 copy.206
  356.7 3.0 fusion.134
  366.9 4.4 fusion.211
  371.3 4.4 fusion.212
  375.7 4.7 fusion.64
  380.4 2.9 pad_maximum_fusion.1
  383.3 31.2 %reduce-scatter.5.cloned.1.call-done = f32[2,64,1024]{2,1,0:T(8,128)} async-done(((f32[2,1024,1024]{2,1,0:T(8,128)}), f32[2,64,1024]{2,1,0:T(8,128)}) %reduce-scatter.5.cloned.1.call-update) | async-done | bytes 524304 | tf_op jit(solution)/shard_map/reduce_scatter | solution.py:749
  414.6 6.1 %copy.232 = f32[1024,1296]{1,0:T(8,128)} copy(f32[1024,1296]{0,1:T(8,128)} %pad_maximum_fusion.1) | data formatting | bytes 10616832
  424.0 3.3 add_add_fusion.1.part_ref
  427.7 3.1 copy-done.23
  435.1 1.7 copy-done.34
  436.9 4.7 fusion.74.received_ref
  441.6 6.3 %fusion.90 = f32[1024,1024]{1,0:T(8,128)} fusion(bf16[1024,1024]{1,0:T(8,128)(2,1)S(1)} %copy-done.52, bf16[1024,1024]{1,0:T(8,128)(2,1)S(1)} %copy-done.40, f32[1024,1024]{1,0:T(8,128)S(1)} %copy-done.34, bf16[1024,1024]{1,0:T(8,128)(2,1)S(1)} %copy-done.41, f32[1024]{0:T(1024)S(1)} %copy-done.110, f32[1024]{0:T(1024)S(1)} %bitcast.435, ...), kind=kOutput, calls=%fused_computation.121 | convolution fusion | flops 2166358016 | bytes 14692352 | tf_op jit(solution)/shard_map/dot_general | solution.py:456
  448.2 30.0 %mix_backward.5 = (bf16[1024,1024]{1,0:T(8,128)(2,1)}, f32[8,8,16,128]{3,2,1,0:T(8,128)S(1)}, f32[1024,256]{1,0:T(8,128)S(1)}, f32[5,1024,128]{2,1,0:T(8,128)}) custom-call(bf16[1024,1024]{1,0:T(8,128)(2,1)} %convolution_convert_fusion.1.raw_ref.before_ref, bf16[1024,1024]{1,0:T(8,128)(2,1)} %convolution_convert_fusion.1.raw_ref.before_ref, ...), custom_call_target="tpu_custom_call" | custom-call | flops 1024 | bytes 1024 | tf_op jit(solution)/shard_map/mix_backward/pallas_call | solution.py:294
  481.0 1.6 fusion.115
  487.5 2.4 collective-permute-done.18
  489.9 1.7 collective-permute-start.19
  491.6 4.5 add_add_fusion.other_ref
  497.5 10.3 %finish.2 = (bf16[2,1024,1024]{2,1,0:T(8,128)(2,1)}, f32[2,1024,1024]{2,1,0:T(8,128)}) custom-call(f32[1024,1024]{1,0:T(8,128)} %copy-done.24, f32[1024,1024]{1,0:T(8,128)} %add_add_fusion.other_ref, f32[1024,1024]{1,0:T(8,128)} %fusion.210.branch_ref, f32[1024,1024]{1,0:T(8,128)} %fusion.74.received_ref, bf16[2,1024,1024]{2,1,0:T(8,128)(2,1)} %hidden_ref.3, ...), custom_call_target="tpu_custom_call" | custom-call | flops 1024 | bytes 1024 | tf_op jit(solution)/shard_map/finish/pallas_call | solution.py:437
  513.7 10.1 %finish.3 = (bf16[2,1024,1024]{2,1,0:T(8,128)(2,1)}, f32[2,1024,1024]{2,1,0:T(8,128)}) custom-call(f32[1024,1024]{1,0:T(8,128)} %add_add_fusion.2.part_ref, f32[1024,1024]{1,0:T(8,128)} %collective-permute-done.15.other_ref, f32[1024,1024]{1,0:T(8,128)} %fusion.206.branch_ref, ...), custom_call_target="tpu_custom_call", output_to_operand_aliasing={{0}: (7, {}), {1}: (8, {})} | custom-call | flops 1024 | bytes 1024 | tf_op jit(solution)/shard_map/finish/pallas_call | solution.py:437
  (527 shorter events, 94.4 us)
Async XLA Ops:
  7.2 26.4 %copy-start = (bf16[1024,256]{1,0:T(8,128)(2,1)S(1)}, bf16[1024,256]{1,0:T(8,128)(2,1)}, u32[]{:S(2)}) copy-start(bf16[1024,256]{1,0:T(8,128)(2,1)} %param.22) | copy-start | bytes 1572868
  7.2 407.4 %reduce-scatter.5.cloned.1.call-start = ((), (), s32[]{:S(2)}) async-start(), calls=%async_computation.2 | async-start | bytes 8912896 | tf_op jit(solution)/shard_map/reduce_scatter | solution.py:749
  10.6 59.9 %collective-permute-start.14 = (f32[22576]{0:T(1024)}, f32[22576]{0:T(1024)}, u32[]{:S(2)}, u32[]{:S(2)}) collective-permute-start(f32[22576]{0:T(1024)} %concatenate.164), channel_id=1, source_target_pairs={{0,1},{1,0},{2,3},{3,2},{4,5},{5,4},{6,7},{7,6},{8,9},{9,8},{10,11... | collective-permute-start | bytes 270920 | tf_op jit(solution)/shard_map/ppermute | solution.py:553
  13.5 9.6 %copy-start.15 = (f32[1024]{0:T(1024)S(1)}, f32[1024]{0:T(1024)}, u32[]{:S(2)}) copy-start(f32[1024]{0:T(1024)} %param.19) | copy-start | bytes 12292
  15.8 104.8 %collective-permute-start.1 = (f32[256,1024]{1,0:T(8,128)}, f32[256,1024]{1,0:T(8,128)}, u32[]{:S(2)}, u32[]{:S(2)}) collective-permute-start(f32[256,1024]{1,0:T(8,128)} %dynamic-slice_convert_fusion.2), channel_id=1, source_target_pairs={{0,1},{1,0},{2,3},{3,2},{4,5},{5,4},{6,7},{7,6},{8,9},{9,8},{10,11... | collective-permute-start | bytes 3145736 | tf_op jit(solution)/shard_map/ppermute | solution.py:514
  18.0 113.4 %collective-permute-start.4 = (f32[256,1024]{1,0:T(8,128)}, f32[256,1024]{1,0:T(8,128)}, u32[]{:S(2)}, u32[]{:S(2)}) collective-permute-start(f32[256,1024]{1,0:T(8,128)} %dynamic-slice_convert_fusion), channel_id=1, source_target_pairs={{0,1},{1,0},{2,3},{3,2},{4,5},{5,4},{6,7},{7,6},{8,9},{9,8},{10,11... | collective-permute-start | bytes 3145736 | tf_op jit(solution)/shard_map/ppermute | solution.py:514
  22.2 182.1 %collective-permute-start.3 = (f32[256,1024]{1,0:T(8,128)}, f32[256,1024]{1,0:T(8,128)}, u32[]{:S(2)}, u32[]{:S(2)}) collective-permute-start(f32[256,1024]{1,0:T(8,128)} %dynamic-slice_convert_fusion.1), channel_id=1, source_target_pairs={{0,1},{1,0},{2,3},{3,2},{4,5},{5,4},{6,7},{7,6},{8,9},{9,8},{10,11... | collective-permute-start | bytes 3145736 | tf_op jit(solution)/shard_map/ppermute | solution.py:514
  29.3 23.2 %copy-start.141 = (f32[16]{0:T(128)}, f32[16]{0:T(128)S(1)}, u32[]{:S(2)}) copy-start(f32[16]{0:T(128)S(1)} %exponential_negate_fusion) | copy-start | bytes 196
  30.0 22.5 %copy-start.78 = (f32[16,1024]{1,0:T(8,128)}, f32[16,1024]{1,0:T(8,128)S(1)}, u32[]{:S(2)}) copy-start(f32[16,1024]{1,0:T(8,128)S(1)} %fusion.107) | copy-start | bytes 196612
  33.6 18.8 %copy-start.77 = (f32[16,1024]{1,0:T(8,128)}, f32[16,1024]{1,0:T(8,128)S(1)}, u32[]{:S(2)}) copy-start(f32[16,1024]{1,0:T(8,128)S(1)} %fusion.106) | copy-start | bytes 196612
  36.1 21.2 %copy-start.19 = (f32[1024,256]{0,1:T(8,128)}, f32[1024,256]{0,1:T(8,128)S(1)}, u32[]{:S(2)}) copy-start(f32[1024,256]{0,1:T(8,128)S(1)} %fusion.207) | copy-start | bytes 3145732
  36.9 20.4 %copy-start.21 = (f32[1024,256]{0,1:T(8,128)}, f32[1024,256]{0,1:T(8,128)S(1)}, u32[]{:S(2)}) copy-start(f32[1024,256]{0,1:T(8,128)S(1)} %fusion.204) | copy-start | bytes 3145732
  48.2 9.1 %copy-start.157 = (f32[256]{0:T(256)S(1)}, f32[256]{0:T(256)}, u32[]{:S(2)}) copy-start(f32[256]{0:T(256)} %param.27) | copy-start | bytes 3076
  52.5 29.2 %copy-start.69 = (f32[2,8,8,128]{3,2,1,0:T(8,128)}, f32[2,8,8,128]{3,2,1,0:T(8,128)S(1)}, u32[]{:S(2)}) copy-start(f32[2,8,8,128]{3,2,1,0:T(8,128)S(1)} %copy.238) | copy-start | bytes 196612
  57.3 13.0 %copy-start.98 = (f32[1024]{0:T(1024)}, f32[1024]{0:T(1024)S(1)}, u32[]{:S(2)}) copy-start(f32[1024]{0:T(1024)S(1)} %get-tuple-element.316) | copy-start | bytes 12292
  61.5 23.6 %copy-start.3 = (bf16[128,1024]{1,0:T(8,128)(2,1)}, bf16[128,1024]{1,0:T(8,128)(2,1)S(1)}, u32[]{:S(2)}) copy-start(bf16[128,1024]{1,0:T(8,128)(2,1)S(1)} %get-tuple-element.239.outt_ref) | copy-start | bytes 786436
  61.6 23.5 %copy-start.1 = (bf16[1024,128]{1,0:T(8,128)(2,1)}, bf16[1024,128]{1,0:T(8,128)(2,1)S(1)}, u32[]{:S(2)}) copy-start(bf16[1024,128]{1,0:T(8,128)(2,1)S(1)} %copy.171.into_ref) | copy-start | bytes 786436
  62.6 13.0 %copy-start.105 = (f32[1024]{0:T(1024)S(1)}, f32[1024]{0:T(1024)}, u32[]{:S(2)}) copy-start(f32[1024]{0:T(1024)} %copy-done.104) | copy-start | bytes 12292
  68.7 11.0 %copy-start.76 = (f32[16,8,128]{2,1,0:T(8,128)S(1)}, f32[16,8,128]{2,1,0:T(8,128)}, u32[]{:S(2)}) copy-start(f32[16,8,128]{2,1,0:T(8,128)} %fusion.144) | copy-start | bytes 196612
  68.7 11.0 %copy-start.155 = (f32[8]{0:T(128)S(1)}, f32[8]{0:T(128)}, u32[]{:S(2)}) copy-start(f32[8]{0:T(128)} %get-tuple-element.313) | copy-start | bytes 100
  69.5 12.6 %copy-start.136 = (f32[8,2]{1,0:T(8,128)S(1)}, f32[8,2]{1,0:T(8,128)}, u32[]{:S(2)}) copy-start(f32[8,2]{1,0:T(8,128)} %stack.117) | copy-start | bytes 196
  85.1 17.6 %copy-start.86 = (f32[16,8,128]{2,1,0:T(8,128)S(1)}, f32[16,8,128]{2,1,0:T(8,128)}, u32[]{:S(2)}) copy-start(f32[16,8,128]{2,1,0:T(8,128)} %get-tuple-element.267) | copy-start | bytes 196612
  100.6 10.1 %collective-permute-start = (f32[2,1024]{1,0:T(2,128)}, f32[2,1024]{1,0:T(2,128)}, u32[]{:S(2)}, u32[]{:S(2)}) collective-permute-start(f32[2,1024]{1,0:T(2,128)} %slice_bitcast_fusion.3), channel_id=1, source_target_pairs={{0,1},{1,0},{2,3},{3,2},{4,5},{5,4},{6,7},{7,6},{8,9},{9,8},{10,11... | collective-permute-start | bytes 24584 | tf_op jit(solution)/shard_map/ppermute | solution.py:484
  111.4 10.7 %copy-start.91 = (bf16[1024,1024]{1,0:T(8,128)(2,1)S(1)}, bf16[1024,1024]{1,0:T(8,128)(2,1)}, u32[]{:S(2)}) copy-start(bf16[1024,1024]{1,0:T(8,128)(2,1)} %param.32) | copy-start | bytes 6291460
  120.6 26.4 %collective-permute-start.2 = (f32[256,1024]{1,0:T(8,128)}, f32[256,1024]{1,0:T(8,128)}, u32[]{:S(2)}, u32[]{:S(2)}) collective-permute-start(f32[256,1024]{1,0:T(8,128)} %collective-permute-done.1.first_ref), channel_id=1, source_target_pairs={{0,4},{2,6},{4,0},{6,2},{8,12},{10,14},{12,8},{14,10},{16,20},{18,... | collective-permute-start | bytes 3145736 | tf_op jit(solution)/shard_map/ppermute | solution.py:518
  126.5 131.9 %collective-permute-start.9 = (f32[1024,1024]{1,0:T(8,128)}, f32[1024,1024]{1,0:T(8,128)}, u32[]{:S(2)}, u32[]{:S(2)}) collective-permute-start(f32[1024,1024]{1,0:T(8,128)} %fusion.206.branch_ref), channel_id=1, source_target_pairs={{0,1},{1,0},{2,3},{3,2},{4,5},{5,4},{6,7},{7,6},{8,9},{9,8},{10,11... | collective-permute-start | bytes 12582920 | tf_op jit(solution)/shard_map/ppermute | solution.py:484
  127.0 20.1 %copy-start.2 = (bf16[1024,128]{1,0:T(8,128)(2,1)S(1)}, bf16[1024,128]{1,0:T(8,128)(2,1)}, u32[]{:S(2)}) copy-start(bf16[1024,128]{1,0:T(8,128)(2,1)} %copy-done.1) | copy-start | bytes 786436
  127.0 20.1 %copy-start.4 = (bf16[128,1024]{1,0:T(8,128)(2,1)S(1)}, bf16[128,1024]{1,0:T(8,128)(2,1)}, u32[]{:S(2)}) copy-start(bf16[128,1024]{1,0:T(8,128)(2,1)} %copy-done.3) | copy-start | bytes 786436
  127.0 20.1 %copy-start.8 = (bf16[1024,128]{1,0:T(8,128)(2,1)S(1)}, bf16[1024,128]{1,0:T(8,128)(2,1)}, u32[]{:S(2)}) copy-start(bf16[1024,128]{1,0:T(8,128)(2,1)} %copy.173.out_ref) | copy-start | bytes 786436
  127.0 20.1 %copy-start.9 = (bf16[128,1024]{1,0:T(8,128)(2,1)S(1)}, bf16[128,1024]{1,0:T(8,128)(2,1)}, u32[]{:S(2)}) copy-start(bf16[128,1024]{1,0:T(8,128)(2,1)} %get-tuple-element.238.intot_ref) | copy-start | bytes 786436
  131.4 57.6 %collective-permute-start.5 = (f32[256,1024]{1,0:T(8,128)}, f32[256,1024]{1,0:T(8,128)}, u32[]{:S(2)}, u32[]{:S(2)}) collective-permute-start(f32[256,1024]{1,0:T(8,128)} %collective-permute-done.4.first_ref), channel_id=1, source_target_pairs={{0,4},{2,6},{4,0},{6,2},{8,12},{10,14},{12,8},{14,10},{16,20},{18,... | collective-permute-start | bytes 3145736 | tf_op jit(solution)/shard_map/ppermute | solution.py:518
  131.5 99.3 %collective-permute-start.7 = (f32[256,1024]{1,0:T(8,128)}, f32[256,1024]{1,0:T(8,128)}, u32[]{:S(2)}, u32[]{:S(2)}) collective-permute-start(f32[256,1024]{1,0:T(8,128)} %collective-permute-done.4.first_ref), channel_id=1, source_target_pairs={{0,2},{2,0},{4,6},{6,4},{8,10},{10,8},{12,14},{14,12},{16,18},{18,... | collective-permute-start | bytes 3145736 | tf_op jit(solution)/shard_map/ppermute | solution.py:518
  147.0 89.2 %collective-permute-start.10 = (f32[256,1024]{1,0:T(8,128)}, f32[256,1024]{1,0:T(8,128)}, u32[]{:S(2)}, u32[]{:S(2)}) collective-permute-start(f32[256,1024]{1,0:T(8,128)} %collective-permute-done.1.first_ref), channel_id=1, source_target_pairs={{0,2},{2,0},{4,6},{6,4},{8,10},{10,8},{12,14},{14,12},{16,18},{18,... | collective-permute-start | bytes 3145736 | tf_op jit(solution)/shard_map/ppermute | solution.py:518
  147.1 33.1 %copy-start.99 = (f32[1024]{0:T(1024)S(1)}, f32[1024]{0:T(1024)}, u32[]{:S(2)}) copy-start(f32[1024]{0:T(1024)} %copy-done.98) | copy-start | bytes 12292
  189.0 15.1 %copy-start.96 = (f32[8,8,2]{2,1,0:T(8,128)S(1)}, f32[8,8,2]{2,1,0:T(8,128)}, u32[]{:S(2)}) copy-start(f32[8,8,2]{2,1,0:T(8,128)} %get-tuple-element.177) | copy-start | bytes 1540
  189.0 17.0 %copy-start.118 = (f32[1,256]{1,0:T(1,128)S(1)}, f32[1,256]{1,0:T(1,128)}, u32[]{:S(2)}) copy-start(f32[1,256]{1,0:T(1,128)} %copy-done.117) | copy-start | bytes 3076
  189.0 18.6 %copy-start.115 = (f32[1,256]{1,0:T(1,128)S(1)}, f32[1,256]{1,0:T(1,128)}, u32[]{:S(2)}) copy-start(f32[1,256]{1,0:T(1,128)} %copy-done.114) | copy-start | bytes 3076
  204.3 25.8 %collective-permute-start.6 = (f32[256,1024]{1,0:T(8,128)}, f32[256,1024]{1,0:T(8,128)S(1)}, u32[]{:S(2)}, u32[]{:S(2)}) collective-permute-start(f32[256,1024]{1,0:T(8,128)} %collective-permute-done.3.first_ref), channel_id=1, source_target_pairs={{0,4},{2,6},{4,0},{6,2},{8,12},{10,14},{12,8},{14,10},{16,20},{18,... | collective-permute-start | bytes 3145736 | tf_op jit(solution)/shard_map/ppermute | solution.py:518
  205.8 25.6 %collective-permute-start.8 = (f32[256,1024]{1,0:T(8,128)}, f32[256,1024]{1,0:T(8,128)S(1)}, u32[]{:S(2)}, u32[]{:S(2)}) collective-permute-start(f32[256,1024]{1,0:T(8,128)} %collective-permute-done.5.second_ref), channel_id=1, source_target_pairs={{0,2},{2,0},{4,6},{6,4},{8,10},{10,8},{12,14},{14,12},{16,18},{18,... | collective-permute-start | bytes 3145736 | tf_op jit(solution)/shard_map/ppermute | solution.py:518
  210.7 19.4 %copy-start.89 = (bf16[16,1024]{1,0:T(8,128)(2,1)}, bf16[16,1024]{1,0:T(8,128)(2,1)S(1)}, u32[]{:S(2)}) copy-start(bf16[16,1024]{1,0:T(8,128)(2,1)S(1)} %get-tuple-element.199) | copy-start | bytes 98308
  210.7 19.4 %copy-start.75 = (bf16[1024,16]{0,1:T(8,128)(2,1)S(1)}, bf16[1024,16]{0,1:T(8,128)(2,1)}, u32[]{:S(2)}) copy-start(bf16[1024,16]{0,1:T(8,128)(2,1)} %param.23) | copy-start | bytes 98308
  213.6 17.2 %copy-start.58 = (bf16[1024,256]{0,1:T(8,128)(2,1)}, bf16[1024,256]{0,1:T(8,128)(2,1)S(1)}, u32[]{:S(2)}) copy-start(bf16[1024,256]{0,1:T(8,128)(2,1)S(1)} %get-tuple-element.219) | copy-start | bytes 1572868
  213.6 17.9 %copy-start.43 = (f32[1024,1024]{1,0:T(8,128)S(1)}, f32[1024,1024]{1,0:T(8,128)}, u32[]{:S(2)}) copy-start(f32[1024,1024]{1,0:T(8,128)} %fusion.205) | copy-start | bytes 12582916
  213.6 17.9 %copy-start.46 = (bf16[1024,1024]{1,0:T(8,128)(2,1)S(1)}, bf16[1024,1024]{1,0:T(8,128)(2,1)}, u32[]{:S(2)}) copy-start(bf16[1024,1024]{1,0:T(8,128)(2,1)} %param.21) | copy-start | bytes 6291460
  213.6 17.9 %copy-start.50 = (bf16[1024,1024]{1,0:T(8,128)(2,1)S(1)}, bf16[1024,1024]{1,0:T(8,128)(2,1)}, u32[]{:S(2)}) copy-start(bf16[1024,1024]{1,0:T(8,128)(2,1)} %get-tuple-element.76) | copy-start | bytes 6291460
  230.1 6.2 %collective-permute-start.11 = (f32[256,1024]{1,0:T(8,128)}, f32[256,1024]{1,0:T(8,128)}, u32[]{:S(2)}, u32[]{:S(2)}) collective-permute-start(f32[256,1024]{1,0:T(8,128)} %collective-permute-done.2.second_ref), channel_id=1, source_target_pairs={{0,2},{2,0},{4,6},{6,4},{8,10},{10,8},{12,14},{14,12},{16,18},{18,... | collective-permute-start | bytes 3145736 | tf_op jit(solution)/shard_map/ppermute | solution.py:518
  230.8 18.4 %collective-permute-start.12 = (f32[256,1024]{1,0:T(8,128)}, f32[256,1024]{1,0:T(8,128)S(1)}, u32[]{:S(2)}, u32[]{:S(2)}) collective-permute-start(f32[256,1024]{1,0:T(8,128)} %collective-permute-done.3.first_ref), channel_id=1, source_target_pairs={{0,2},{2,0},{4,6},{6,4},{8,10},{10,8},{12,14},{14,12},{16,18},{18,... | collective-permute-start | bytes 3145736 | tf_op jit(solution)/shard_map/ppermute | solution.py:518
  231.4 17.8 %collective-permute-start.13 = (f32[256,1024]{1,0:T(8,128)S(1)}, f32[256,1024]{1,0:T(8,128)}, u32[]{:S(2)}, u32[]{:S(2)}) collective-permute-start(f32[256,1024]{1,0:T(8,128)S(1)} %collective-permute-done.6.second_ref), channel_id=1, source_target_pairs={{0,2},{2,0},{4,6},{6,4},{8,10},{10,8},{12,14},{14,12},{16,18},{18,... | collective-permute-start | bytes 3145736 | tf_op jit(solution)/shard_map/ppermute | solution.py:518
  264.6 13.8 %copy-start.37 = (bf16[1024,1024]{1,0:T(8,128)(2,1)S(1)}, bf16[1024,1024]{1,0:T(8,128)(2,1)}, u32[]{:S(2)}) copy-start(bf16[1024,1024]{1,0:T(8,128)(2,1)} %convert_bitcast_fusion.1.gate_ref) | copy-start | bytes 6291460
  264.6 13.8 %copy-start.100 = (f32[1024]{0:T(1024)S(1)}, f32[1024]{0:T(1024)}, u32[]{:S(2)}) copy-start(f32[1024]{0:T(1024)} %param.31) | copy-start | bytes 12292
  278.3 13.7 %copy-start.5 = (bf16[8,1024,128]{2,1,0:T(8,128)(2,1)}, bf16[8,1024,128]{2,1,0:T(8,128)(2,1)S(1)}, u32[]{:S(2)}) copy-start(bf16[8,1024,128]{2,1,0:T(8,128)(2,1)S(1)} %get-tuple-element.103.entry_ref) | copy-start | bytes 6291460
  278.4 13.7 %copy-start.130 = (f32[1,1024]{1,0:T(1,128)}, f32[1,1024]{1,0:T(1,128)S(1)}, u32[]{:S(2)}) copy-start(f32[1,1024]{1,0:T(1,128)S(1)} %get-tuple-element.200) | copy-start | bytes 12292
  278.4 13.7 %copy-start.132 = (f32[1,8,128]{2,0,1:T(1,128)}, f32[1,8,128]{2,0,1:T(1,128)S(1)}, u32[]{:S(2)}) copy-start(f32[1,8,128]{2,0,1:T(1,128)S(1)} %get-tuple-element.201) | copy-start | bytes 12292
  278.4 13.7 %copy-start.30 = (bf16[1024,1024]{1,0:T(8,128)(2,1)S(1)}, bf16[1024,1024]{1,0:T(8,128)(2,1)}, u32[]{:S(2)}) copy-start(bf16[1024,1024]{1,0:T(8,128)(2,1)} %copy-done.28) | copy-start | bytes 6291460
  309.5 199.0 %reduce-scatter.7.cloned.1.call-start = ((), (), s32[]{:S(2)}) async-start(), calls=%async_computation.3 | async-start | bytes 6127616
  311.7 136.4 %collective-permute-start.15 = (f32[1024,1024]{1,0:T(8,128)}, f32[1024,1024]{1,0:T(8,128)}, u32[]{:S(2)}, u32[]{:S(2)}) collective-permute-start(f32[1024,1024]{1,0:T(8,128)} %add_add_fusion.2.part_ref), channel_id=1, source_target_pairs={{0,1},{1,0},{2,3},{3,2},{4,5},{5,4},{6,7},{7,6},{8,9},{9,8},{10,11... | collective-permute-start | bytes 12582920 | tf_op jit(solution)/shard_map/ppermute | solution.py:484
  318.7 35.5 %copy-start.70 = (f32[2,8,8,128]{3,2,1,0:T(8,128)S(1)}, f32[2,8,8,128]{3,2,1,0:T(8,128)}, u32[]{:S(2)}) copy-start(f32[2,8,8,128]{3,2,1,0:T(8,128)} %copy-done.69) | copy-start | bytes 196612
  318.7 35.5 %copy-start.143 = (f32[16]{0:T(128)S(1)}, f32[16]{0:T(128)}, u32[]{:S(2)}) copy-start(f32[16]{0:T(128)} %copy-done.141) | copy-start | bytes 196
  432.2 15.9 %collective-permute-start.16 = (f32[2304]{0:T(1024)S(1)}, f32[2304]{0:T(1024)S(1)}, u32[]{:S(2)}, u32[]{:S(2)}) collective-permute-start(f32[2304]{0:T(1024)S(1)} %pad_maximum_fusion.5), channel_id=1, source_target_pairs={{0,1},{1,0},{2,3},{3,2},{4,5},{5,4},{6,7},{7,6},{8,9},{9,8},{10,11... | collective-permute-start | bytes 27656 | tf_op jit(solution)/shard_map/ppermute | solution.py:484
  448.2 37.0 %collective-permute-start.17 = (f32[8496]{0:T(1024)S(1)}, f32[8496]{0:T(1024)S(1)}, u32[]{:S(2)}, u32[]{:S(2)}) collective-permute-start(f32[8496]{0:T(1024)S(1)} %concatenate.173), channel_id=1, source_target_pairs={{0,2},{2,0},{4,6},{6,4},{8,10},{10,8},{12,14},{14,12},{16,18},{18,... | collective-permute-start | bytes 101960 | tf_op jit(solution)/shard_map/ppermute | solution.py:518
  485.3 4.6 collective-permute-start.18
  489.9 6.2 %collective-permute-start.19 = (f32[8496]{0:T(1024)S(1)}, f32[8496]{0:T(1024)S(1)}, u32[]{:S(2)}, u32[]{:S(2)}) collective-permute-start(f32[8496]{0:T(1024)S(1)} %add.428), channel_id=1, source_target_pairs={{0,8},{2,10},{4,12},{6,14},{8,0},{10,2},{12,4},{14,6},{16,24},{18,... | collective-permute-start | bytes 101960 | tf_op jit(solution)/shard_map/ppermute | solution.py:518
  496.1 11.7 %collective-permute-start.20 = (f32[8496]{0:T(1024)S(1)}, f32[8496]{0:T(1024)S(1)}, u32[]{:S(2)}, u32[]{:S(2)}) collective-permute-start(f32[8496]{0:T(1024)S(1)} %add.429), channel_id=1, source_target_pairs={{0,16},{2,18},{4,20},{6,22},{8,24},{10,26},{12,28},{14,30},{16,0},... | collective-permute-start | bytes 101960 | tf_op jit(solution)/shard_map/ppermute | solution.py:518
  509.7 15.5 %collective-permute-start.21 = (f32[64,256]{0,1:T(8,128)S(1)}, f32[64,256]{0,1:T(8,128)S(1)}, u32[]{:S(2)}, u32[]{:S(2)}) collective-permute-start(f32[64,256]{0,1:T(8,128)S(1)} %slice.422), channel_id=1, source_target_pairs={{0,1},{1,0},{2,3},{3,2},{4,5},{5,4},{6,7},{7,6},{8,9},{9,8},{10,11... | collective-permute-start | bytes 196616 | tf_op jit(solution)/shard_map/ppermute | solution.py:484
  (121 other events, 546.2 us)
Sparse Core Ops, SparseCore 0:
  309.6 104.9 reduce-scatter.4
  420.8 83.7 reduce-scatter.6

commit v5 on v4

--- a/solution.py
+++ b/solution.py
@@ -452,6 +452,55 @@
     )(part, other, branch, received, hidden, out_grad, norm_gain[None, :], *earlier)
 
 
+def middle_kernel(scale, gate_ref, mixed_ref, dout_ref, both_ref, gain_ref, *out_refs):
+    in_ref, dgate_ref, dmix_ref, dgain_ref = out_refs
+
+    @pl.when(pl.program_id(0) == 0)
+    def _():
+        dgain_ref[...] = jnp.zeros_like(dgain_ref)
+
+    gated_scale = lax.rsqrt(both_ref[0:1, :] * scale + epsilon)
+    pull = gated_scale * gated_scale * gated_scale * both_ref[1:2, :] * scale
+
+    def body(p, carry):
+        part = pl.ds(pl.multiple_of(p * PAIR, PAIR), PAIR)
+        gate = gate_ref[part, :].astype(jnp.float32)
+        mixed = mixed_ref[part, :]
+        gain = gain_ref[part, :]
+        sigma = sigmoid(gate)
+        active = gate * sigma
+        gated = mixed * active
+        scaled = gated * gated_scale
+        dout = dout_ref[part, :].astype(jnp.float32)
+        in_ref[part, :] = (scaled * gain).astype(bf16)
+        dgain_ref[part, :] += dout * scaled
+        d_gated = gated_scale * (dout * gain) - gated * pull
+        dmix_ref[part, :] = (d_gated * active).astype(bf16)
+        dgate_ref[part, :] = (d_gated * mixed * (sigma + active * (1.0 - sigma))).astype(bf16)
+        return carry
+
+    pairs = gate_ref.shape[0] // PAIR
+    lax.fori_loop(0, pairs, body, 0, unroll=min(4, pairs))
+
+
+def middle(gate, mixed, dout, both, gain_wide, inner_total):
+    ch, tokens = gate.shape
+    slab = spec((ch, CHUNK), lambda i: (0, i))
+    still = spec((ch, CHUNK), lambda i: (0, 0))
+    shape = jax.ShapeDtypeStruct((ch, tokens), bf16)
+    *result, gain_grad = pl.pallas_call(
+        functools.partial(middle_kernel, 1.0 / inner_total),
+        grid=(tokens // CHUNK,),
+        in_specs=[slab, slab, slab, spec((2, CHUNK), lambda i: (0, i)), still],
+        out_specs=[slab, slab, slab, still],
+        out_shape=[shape, shape, shape, jax.ShapeDtypeStruct((ch, CHUNK), jnp.float32)],
+        compiler_params=pltpu.CompilerParams(vmem_limit_bytes=VMEM_BYTES),
+        cost_estimate=pl.CostEstimate(flops=tokens, bytes_accessed=tokens, transcendentals=0),
+        name="gated_middle",
+    )(gate, mixed, dout, both, gain_wide)
+    return (*result, jnp.sum(gain_grad, axis=1))
+
+
 def out_product(left, weight):
     return lax.dot_general(left, weight, (((0,), (1,)), ((), ())), preferred_element_type=jnp.float32)
 
@@ -559,7 +608,7 @@
     return result
 
 
-def unit_forward(weights, normed, cotangent, segments, states, earlier=(), between=()):
+def unit_forward(weights, normed, cotangent, segments, states, earlier=()):
     step = in_product(weights["step"], normed)
     gate = in_product(weights["gate"], normed).astype(bf16)
     dout = in_product(weights["out"], cotangent).astype(bf16)
@@ -568,7 +617,6 @@
         step, weights["step_bias"], weights["decay_log"], weights["skip_gain"], segments
     )
     into, _, _, outt = states
-    rows = after(rows, *between)
     mixed, entry, sums = mix_forward(
         1, raw, gate, dout, rows, masks, into, outt, weights["conv"], weights["gain_wide"]
     )
@@ -580,27 +628,19 @@
 
 
 def unit_middle(unit, weights, both, inner_total):
-    gate, mixed, dout = unit["gate"], unit["mixed"], unit["dout"]
-    gate, dout = gate.astype(jnp.float32), dout.astype(jnp.float32)
-    gain = weights["gate_gain"][:, None]
-    sigma = sigmoid(gate)
-    gated = mixed * gate * sigma
-    gated_scale = lax.rsqrt(both[0:1] / inner_total + epsilon)
-    output_in = (gated * gated_scale * gain).astype(bf16)
-    d_gated = gated_scale * (dout * gain) - gated * (
-        gated_scale**3 * both[1:2] / inner_total
-    )
-    d_mixed = (d_gated * gate * sigma).astype(bf16)
-    d_gate = (d_gated * mixed * sigma * (1.0 + gate * (1.0 - sigma))).astype(bf16)
-    grad_gain = jnp.sum(dout * gated * gated_scale, axis=1)
-    return output_in, d_gate, d_mixed, grad_gain
-
-
-def unit_backward(unit, weights, d_gate, d_mixed, state_back):
+    return middle(
+        unit["gate"], unit["mixed"], unit["dout"], both, weights["gain_wide"], inner_total
+    )
+
+
+def unit_backward(unit, weights, d_gate, d_mixed, state_back, between=()):
     d_value, d_rows, d_state, d_conv = mix_backward(
         1, unit["raw"], unit["mixed"], d_mixed, unit["entry"], unit["rows"], unit["masks"],
         *unit["states"], weights["conv"],
     )
+    d_value, d_rows, d_state, d_conv = lax.optimization_barrier(
+        (d_value, d_rows, d_state, d_conv, *between)
+    )[:4]
     d_step, *step_params = step_grads(
         d_rows, unit["step"], weights["step_bias"], weights["decay_log"], 1
     )
@@ -662,7 +702,7 @@
         )
         sent = dict(value=proj_value, gate=proj_gate, out=proj_out)
         first = {k: gather_first(w) for k, w in sent.items()}
-        second = dict(value=along_dp(first["value"], 2))
+        second = {k: along_dp(first[k], 2) for k in ("value", "gate")}
         other["conv"] = wide_lanes(jnp.concatenate([c_w, c_b[None, :]], axis=0))
         other["gain_wide"] = wide_lanes(g_g)
 
@@ -682,24 +722,15 @@
         low = state_conv.astype(bf16)
         into, out = low[:, :STATE], low[:, STATE:]
         states.append((into, into.T, out, out.T))
-        between = (second["value"],) if 0 < s == whole_from else ()
-        units.append(
-            unit_forward(
-                own, normeds[s], out_grad[s], segment_ids[s : s + 1], states[s], between=between
-            )
-        )
+        units.append(unit_forward(own, normeds[s], out_grad[s], segment_ids[s : s + 1], states[s]))
         if s < whole_from:
             sums = units[s]["sums"]
             boths.append(tensor_join(sums, tensor_others(sums)))
     branches, received, output_ins, d_gates, d_mixeds = [], [], [], [], []
     grad_gate_gain = jnp.zeros((local_inner,), jnp.float32)
-    extras, middles, arrivals = {}, {}, ()
+    extras, middles = {}, {}
     if whole_from < seq_count:
-        second["gate"] = along_dp(after(first["gate"], units[0]["mixed"]), 2)
-        second["out"] = along_dp(after(first["out"], units[-1]["mixed"]), 2)
-        third = {k: along_dp(first[k], 1) for k in sent}
-        fourth = {k: along_dp(second[k], 1) for k in sent}
-        arrivals = (second["out"],)
+        third, fourth = {}, {}
 
     backs, parts, others = [], [], []
 
@@ -711,17 +742,26 @@
         branches.append(lax.optimization_barrier(out_product(output_in, proj_out)))
         return grad_gain
 
-    def own_backward(s, earlier, between=()):
+    def own_backward(s, earlier, last_hops=False):
         d_mixed = after(d_mixeds[s], *earlier)
-        d_value, *rest = unit_backward(units[s], own, d_gates[s], d_mixed, state_backs[s])
-        backs.append((after(d_value, *between), *rest))
+        between = tuple(second.values()) if last_hops else ()
+        d_value, *rest = unit_backward(
+            units[s], own, d_gates[s], d_mixed, state_backs[s], between
+        )
+        if last_hops:
+            second["out"] = along_dp(after(first["out"], d_value), 2)
+            for k in sent:
+                third[k] = along_dp(after(first[k], d_value), 1)
+                fourth[k] = along_dp(after(second[k], units[-1]["mixed"]), 1)
+            d_value = after(d_value, second["out"])
+        backs.append((d_value, *rest))
         parts.append(lax.optimization_barrier(normed_part(own, d_gates[s], *backs[s][:3])))
 
     for s in range(whole_from):
         grad_gate_gain = grad_gate_gain + own_middle(s)
         received.append(tensor_others(branches[s]))
-        earlier = (second["gate"],) if arrivals else ()
-        own_backward(s, (branches[s], *earlier), arrivals)
+        gathers = whole_from < seq_count and s == whole_from - 1
+        own_backward(s, (branches[s],), gathers)
         others.append(tensor_others(parts[s]))
     if whole_from < seq_count:
         for k in sent:
@@ -758,23 +798,26 @@
         ],
         axis=1,
     )
-    later_part = after(later_part, early)
+    waits, extra_backs = (later_part, *others), []
+    for s in range(whole_from, seq_count):
+        d_gate = middles[s][1]
+        back = unit_backward(extras[s], other, d_gate, after(middles[s][2], *waits), state_backs[s])
+        extra_backs.append(back)
+    later_part = after(later_part, early, *[back[0] for back in extra_backs])
     later = lax.psum_scatter(later_part, "dp", scatter_dimension=0, tiled=True)
     later_value = later[:, :local_inner]
     edge = local_inner + state_width
     state_part = later[:, local_inner:edge]
-    waits, extra_backs = (later_part, *others), []
+    for s, back in zip(range(whole_from, seq_count), extra_backs):
+        d_value = after(back[0], later_part)
+        others.append(
+            lax.optimization_barrier(normed_part(other, middles[s][1], d_value, *back[1:3]))
+        )
     grad_norm_gain = jnp.zeros((width,), jnp.float32)
     for s in every:
         wide = hidden[s].astype(jnp.float32)
         row_scale = lax.rsqrt(jnp.mean(wide * wide, axis=-1, keepdims=True) + epsilon)
         grad_norm_gain = grad_norm_gain + jnp.sum(parts[s] * wide * row_scale, axis=0)
-    for s in range(whole_from, seq_count):
-        d_gate = middles[s][1]
-        back = unit_backward(extras[s], other, d_gate, after(middles[s][2], *waits), state_backs[s])
-        extra_backs.append(back)
-        others.append(lax.optimization_barrier(normed_part(other, d_gate, *back[:3])))
-
     param_grads = [sum(grads) for grads in zip(*[b[3] for b in backs])]
     d_conv, g_cs, g_csb, g_sb, g_dl, g_sg = param_grads
     d_conv = jnp.sum(d_conv, axis=-1)
@@ -789,7 +832,6 @@
         between = [others[0], others[0], others[-1]]
     shared_flat = tensor_join(shared_flat, arrived)
     stacked = ()
-    parts[0] = after(parts[0], later)
     for s in reversed(every):
         stacked = finish(
             s, parts[s], only_others(parts[s], others[s]), branches[s],

time: 537 us -> 538 us (level)
  Pallas kernels: 162 us -> 191 us
  other arithmetic: 78.1 us -> 55.2 us
  matrix products: 127 us -> 115 us
  local copies, waits for them, and re-layouts: 65.6 us -> 71.3 us
    reduce_scatter x1, waiting for transfers between devices: 31.2 us -> 0.01 us  [local(): early = lax.psum_scatter(early_part, 'dp', scatter_dimension=1, tiled=True)]
    unnamed x3, waiting for transfers between devices: 0.03 us -> 29.9 us
    pallas_call x0 -> x3, Pallas kernels: none -> 29.4 us  [middle(): pl.pallas_call(functools.partial(middle_kernel, 1.0 / inner_total), grid=...]
    convert_element_type x2 -> x0, other arithmetic: 22.8 us -> none  [unit_middle(): (d_gated * mixed * sigma * (1.0 + gate * (1.0 - sigma))).astype(bf16)]
    ppermute x13, waiting for transfers between devices: 33.7 us -> 16.3 us  [along_dp(): lax.ppermute(piece, 'dp', [(j, j ^ flip) for j in range(lax.axis_size('dp...]
    ppermute x5, waiting for transfers between devices: 0.01 us -> 14.2 us  [tensor_others(): return lax.ppermute(part, 'tensor', [(0, 1), (1, 0)])]
    dot_general x12, matrix products: 49.2 us -> 38.6 us  [out_product(): lax.dot_general(left, weight, (((0,), (1,)), ((), ())), preferred_element...]
    unnamed x352 -> x364, local copies, waits for them, and re-layouts: 33.7 us -> 40.7 us
  transfers between devices with their start and end apart: 24 -> 24, of which waited for: 4 -> 4; matrix products, arithmetic and copies ran while one was open for 39% -> 34% of each run, Pallas kernels for 28% -> 31%
where the time goes in v5:
time: 538 us; the launch traced here: 533 us
  Pallas kernels  191 us (36%)
  matrix products  115 us (21%)
  local copies, waits for them, and re-layouts  71.3 us (13%)
  waiting for transfers between devices  60.4 us (11%)
  other arithmetic  55.2 us (10%)
  starting transfers between devices  23.5 us (4%)
  between operations  16.4 us (3%)
    pallas_call x3, Pallas kernels, mix_backward(): pl.pallas_call(back_kernel, grid=(seqs, chunks), in_specs=[slab, spec((ch...  90.1 us
    dot_general x12, matrix products, in_product(): lax.dot_general(weight, tokens, (((0,), (1,)), ((), ())), preferred_eleme...  44.2 us
    unnamed x364, local copies, waits for them, and re-layouts  40.7 us
    pallas_call x3, Pallas kernels, mix_forward(): pl.pallas_call(mix_kernel, grid=(seqs, chunks), in_specs=[slab, slab, sla...  40.6 us
    dot_general x12, matrix products, out_product(): lax.dot_general(left, weight, (((0,), (1,)), ((), ())), preferred_element...  38.6 us
    unnamed x3, waiting for transfers between devices  29.9 us
    pallas_call x3, Pallas kernels, middle(): pl.pallas_call(functools.partial(middle_kernel, 1.0 / inner_total), grid=...  29.4 us
    pallas_call x2, Pallas kernels, finish(): pl.pallas_call(finish_kernel, grid=(length // tile,), in_specs=[flat] * 4...  20.3 us
  transfers between devices with their start and end apart: 24, of which 4 were waited for; matrix products, arithmetic and copies ran while one was open for 34% of the time, Pallas kernels for 31%

profile of v5, /device:TPU:0, one launch (start us, length us, event | category | flops | bytes accessed | tf_op | source)
XLA Modules:
  0.0 533.1 jit_solution(10700551733690541417)
XLA Ops:
  10.6 3.0 collective-permute-start.15
  13.5 2.3 dynamic-slice_convert_fusion.2
  15.8 2.1 dynamic-slice_convert_fusion.1
  18.0 2.0 collective-permute-start.3
  20.0 2.1 dynamic-slice_convert_fusion
  24.7 3.8 convert_bitcast_fusion.4.gate_ref
  31.2 2.5 fusion.149
  33.8 1.7 fusion.144
  36.2 3.7 convert_bitcast_fusion.2.gate_ref
  39.9 3.7 fusion.45.dout_ref
  43.6 3.7 fusion.48.dout_ref
  47.3 4.1 convert_bitcast_fusion.3.raw_ref.before_ref
  57.0 5.6 %multiply_convert_fusion = (bf16[1024,256]{0,1:T(8,128)(2,1)S(1)}, f32[1024,256]{0,1:T(8,128)}, bf16[1024,256]{0,1:T(8,128)(2,1)S(1)}, f32[1024,256]{0,1:T(8,128)}) fusion(f32[1024]{0:T(1024)S(1)} %get-tuple-element.322, f32[1021,256]{0,1:T(8,128)S(1)} %bitcast.342, f32[256]{0:T(256)S(1)} %bitcast.412, f32[1024]{0:T(1024)S(1)} %get-tuple-element.323, ...), kind=kLoop, calls=%fused_computation.114 | loop fusion | flops 8388608 | bytes 11551744 | tf_op jit(solution)/shard_map/convert_element_type | solution.py:722
  64.4 6.0 %convert_bitcast_fusion.1.raw_ref.before_ref = bf16[1024,1024]{1,0:T(8,128)(2,1)} fusion(bf16[1024,1024]{1,0:T(8,128)(2,1)} %copy-done.34, bf16[1024,1024]{1,0:T(8,128)(2,1)} %param.21), kind=kOutput, calls=%fused_computation.51 | convolution fusion | flops 2148532224 | bytes 6291456 | tf_op jit(solution)/shard_map/dot_general | solution.py:509
  75.4 2.5 fusion.61
  82.1 2.0 broadcast_in_dim.15.conv_ref
  85.0 13.5 %mix_forward.3 = (f32[1024,1024]{1,0:T(8,128)}, bf16[8,1024,128]{2,1,0:T(8,128)(2,1)S(1)}, f32[8,8,128]{2,1,0:T(8,128)S(1)}) custom-call(bf16[1024,1024]{1,0:T(8,128)(2,1)} %convert_bitcast_fusion.3.raw_ref.before_ref, bf16[1024,1024]{1,0:T(8,128)(2,1)} %convert_bitcast_fusion.4.gate_ref, bf16[1024,1024]{1,0:T(8,128)(2,1)} %fusion.45.dout_ref, ...), custom_call_target="tpu_custom_call" | custom-call | flops 1024 | bytes 1024 | tf_op jit(solution)/shard_map/mix_forward/pallas_call | solution.py:252
  100.4 2.0 collective-permute-start
  114.0 13.6 %mix_forward.4 = (f32[1024,1024]{1,0:T(8,128)}, bf16[8,1024,128]{2,1,0:T(8,128)(2,1)S(1)}, f32[8,8,128]{2,1,0:T(8,128)S(1)}) custom-call(bf16[1024,1024]{1,0:T(8,128)(2,1)} %convert_bitcast_fusion.1.raw_ref.before_ref, bf16[1024,1024]{1,0:T(8,128)(2,1)} %convert_bitcast_fusion.2.gate_ref, bf16[1024,1024]{1,0:T(8,128)(2,1)} %fusion.48.dout_ref, ...), custom_call_target="tpu_custom_call" | custom-call | flops 1024 | bytes 1024 | tf_op jit(solution)/shard_map/mix_forward/pallas_call | solution.py:252
  129.6 9.6 %gated_middle.3 = (bf16[1024,1024]{1,0:T(8,128)(2,1)S(1)}, bf16[1024,1024]{1,0:T(8,128)(2,1)}, bf16[1024,1024]{1,0:T(8,128)(2,1)}, f32[1024,128]{1,0:T(8,128)S(1)}) custom-call(bf16[1024,1024]{1,0:T(8,128)(2,1)} %convert_bitcast_fusion.4.gate_ref, f32[1024,1024]{1,0:T(8,128)} %get-tuple-element.91.mixed_ref, bf16[1024,1024]{1,0:T(8,128)(2,1)} %fusion.45.dout_ref, ...), custom_call_target="tpu_custom_call" | custom-call | flops 1024 | bytes 1024 | tf_op jit(solution)/shard_map/gated_middle/pallas_call | solution.py:491
  139.2 4.3 fusion.145.branch_ref
  143.6 30.0 %mix_backward.3 = (bf16[1024,1024]{1,0:T(8,128)(2,1)}, f32[8,8,16,128]{3,2,1,0:T(8,128)S(1)}, f32[1024,256]{1,0:T(8,128)S(1)}, f32[5,1024,128]{2,1,0:T(8,128)}) custom-call(bf16[1024,1024]{1,0:T(8,128)(2,1)} %convert_bitcast_fusion.3.raw_ref.before_ref, bf16[1024,1024]{1,0:T(8,128)(2,1)} %convert_bitcast_fusion.3.raw_ref.before_ref, ...), custom_call_target="tpu_custom_call" | custom-call | flops 1024 | bytes 1024 | tf_op jit(solution)/shard_map/mix_backward/pallas_call | solution.py:294
  177.3 2.9 multiply_reduce_fusion.7
  188.1 2.0 collective-permute-start.6
  190.0 1.7 copy_add_fusion.1
  196.0 2.2 multiply_reduce_fusion.4
  199.0 14.6 %collective-permute-done.6.second_ref = f32[256,1024]{1,0:T(8,128)S(1)} collective-permute-done((f32[256,1024]{1,0:T(8,128)}, f32[256,1024]{1,0:T(8,128)S(1)}, u32[]{:S(2)}, u32[]{:S(2)}) %collective-permute-start.6) | collective-permute-done | bytes 1048608 | tf_op jit(solution)/shard_map/ppermute | solution.py:567
  213.7 2.4 fusion.146
  216.7 4.5 add_add_fusion.2.part_ref
  221.3 3.7 assemble.3
  225.0 3.5 assemble.4
  228.5 5.6 %convolution_convert_fusion.gate_ref = bf16[1024,1024]{1,0:T(8,128)(2,1)} fusion(bf16[1024,1024]{1,0:T(8,128)(2,1)} %assemble.4, bf16[1024,1024]{1,0:T(8,128)(2,1)S(1)} %copy-done.36), kind=kOutput, calls=%fused_computation.59 | convolution fusion | flops 2148532224 | bytes 6291456 | tf_op jit(solution)/shard_map/dot_general | solution.py:509
  234.1 3.1 assemble.5
  237.2 6.1 %fusion.51.dout_ref = bf16[1024,1024]{1,0:T(8,128)(2,1)} fusion(bf16[1024,1024]{1,0:T(8,128)(2,1)} %assemble.5, bf16[2,1024,1024]{2,1,0:T(8,128)(2,1)} %cotangent_ref.3), kind=kOutput, calls=%fused_computation.58 | convolution fusion | flops 2148532224 | bytes 6291456 | tf_op jit(solution)/shard_map/dot_general | solution.py:509
  243.3 3.8 convolution_convert_fusion.1.raw_ref.before_ref
  247.0 1.9 broadcast_in_dim.19.conv_ref
  249.1 13.5 %mix_forward.5 = (f32[1024,1024]{1,0:T(8,128)}, bf16[8,1024,128]{2,1,0:T(8,128)(2,1)S(1)}, f32[8,8,128]{2,1,0:T(8,128)S(1)}) custom-call(bf16[1024,1024]{1,0:T(8,128)(2,1)} %convolution_convert_fusion.1.raw_ref.before_ref, bf16[1024,1024]{1,0:T(8,128)(2,1)} %convolution_convert_fusion.gate_ref, bf16[1024,1024]{1,0:T(8,128)(2,1)} %fusion.51.dout_ref, ...), custom_call_target="tpu_custom_call" | custom-call | flops 1024 | bytes 1024 | tf_op jit(solution)/shard_map/mix_forward/pallas_call | solution.py:252
  264.0 10.0 %gated_middle.4 = (bf16[1024,1024]{1,0:T(8,128)(2,1)S(1)}, bf16[1024,1024]{1,0:T(8,128)(2,1)}, bf16[1024,1024]{1,0:T(8,128)(2,1)}, f32[1024,128]{1,0:T(8,128)S(1)}) custom-call(bf16[1024,1024]{1,0:T(8,128)(2,1)} %convert_bitcast_fusion.2.gate_ref, f32[1024,1024]{1,0:T(8,128)} %get-tuple-element.107.mixed_ref, bf16[1024,1024]{1,0:T(8,128)(2,1)} %fusion.48.dout_ref, ...), custom_call_target="tpu_custom_call" | custom-call | flops 1024 | bytes 1024 | tf_op jit(solution)/shard_map/gated_middle/pallas_call | solution.py:491
  274.1 7.7 %fusion.30 = f32[1,1024,1024]{2,1,0:T(8,128)S(1)} fusion(bf16[1024,1024]{1,0:T(8,128)(2,1)} %get-tuple-element.128, bf16[1024,1024]{1,0:T(8,128)(2,1)} %get-tuple-element.93, bf16[1024,1024]{1,0:T(8,128)(2,1)S(1)} %copy-done.36, bf16[1024,1024]{1,0:T(8,128)(2,1)S(1)} %copy-done.40), kind=kOutput, calls=%fused_computation.40 | convolution fusion | flops 4311744512 | bytes 12582912 | tf_op jit(solution)/shard_map/dot_general | solution.py:513
  281.9 4.6 fusion.27
  286.4 4.6 pad_maximum_fusion
  293.3 1.8 reduce_sum.265
  295.2 1.8 collective-permute-start.7
  296.9 6.9 %fusion.151.branch_ref = f32[1024,1024]{1,0:T(8,128)} fusion(bf16[1024,1024]{1,0:T(8,128)(2,1)} %copy-done.25, bf16[1024,1024]{1,0:T(8,128)(2,1)} %param.32), kind=kOutput, calls=%fused_computation.296 | convolution fusion | flops 2147483648 | bytes 8388608 | tf_op jit(solution)/shard_map/dot_general | solution.py:505
  303.8 30.3 %mix_backward.4 = (bf16[1024,1024]{1,0:T(8,128)(2,1)}, f32[8,8,16,128]{3,2,1,0:T(8,128)S(1)}, f32[1024,256]{1,0:T(8,128)S(1)}, f32[5,1024,128]{2,1,0:T(8,128)}) custom-call(bf16[1024,1024]{1,0:T(8,128)(2,1)} %convert_bitcast_fusion.1.raw_ref.before_ref, bf16[1024,1024]{1,0:T(8,128)(2,1)} %convert_bitcast_fusion.1.raw_ref.before_ref, ...), custom_call_target="tpu_custom_call" | custom-call | flops 1024 | bytes 1024 | tf_op jit(solution)/shard_map/mix_backward/pallas_call | solution.py:294
  337.5 9.9 %gated_middle.5 = (bf16[1024,1024]{1,0:T(8,128)(2,1)S(1)}, bf16[1024,1024]{1,0:T(8,128)(2,1)}, bf16[1024,1024]{1,0:T(8,128)(2,1)}, f32[1024,128]{1,0:T(8,128)}) custom-call(bf16[1024,1024]{1,0:T(8,128)(2,1)} %convolution_convert_fusion.gate_ref, f32[1024,1024]{1,0:T(8,128)} %get-tuple-element.136.mixed_ref, bf16[1024,1024]{1,0:T(8,128)(2,1)} %fusion.51.dout_ref, ...), custom_call_target="tpu_custom_call" | custom-call | flops 1024 | bytes 1024 | tf_op jit(solution)/shard_map/gated_middle/pallas_call | solution.py:491
  350.4 3.1 fusion.87
  361.5 4.5 fusion.23
  366.0 3.2 pad_maximum_fusion.1
  369.7 4.5 fusion.150
  374.2 14.2 %collective-permute-done.7.other_ref = f32[1024,1024]{1,0:T(8,128)} collective-permute-done((f32[1024,1024]{1,0:T(8,128)}, f32[1024,1024]{1,0:T(8,128)}, u32[]{:S(2)}, u32[]{:S(2)}) %collective-permute-start.7) | collective-permute-done | bytes 4194336 | tf_op jit(solution)/shard_map/ppermute | solution.py:533
  388.4 29.9 %mix_backward.5 = (bf16[1024,1024]{1,0:T(8,128)(2,1)}, f32[8,8,16,128]{3,2,1,0:T(8,128)S(1)}, f32[1024,256]{1,0:T(8,128)S(1)}, f32[5,1024,128]{2,1,0:T(8,128)}) custom-call(bf16[1024,1024]{1,0:T(8,128)(2,1)} %convolution_convert_fusion.1.raw_ref.before_ref, bf16[1024,1024]{1,0:T(8,128)(2,1)} %convolution_convert_fusion.1.raw_ref.before_ref, ...), custom_call_target="tpu_custom_call" | custom-call | flops 1024 | bytes 1024 | tf_op jit(solution)/shard_map/mix_backward/pallas_call | solution.py:294
  419.3 6.3 %copy.224 = f32[1024,1296]{1,0:T(8,128)} copy(f32[1024,1296]{0,1:T(8,128)} %pad_maximum_fusion.1) | data formatting | bytes 10616832
  428.8 2.4 fusion.152
  432.1 3.1 copy-done.27
  438.3 1.8 collective-permute-start.16
  442.6 4.5 fusion.155.received_ref
  455.9 1.7 collective-permute-start.19
  457.6 2.4 fusion.154
  460.0 4.5 add_add_fusion.other_ref
  464.5 2.7 collective-permute-start.20
  468.0 10.2 %finish.2 = (bf16[2,1024,1024]{2,1,0:T(8,128)(2,1)}, f32[2,1024,1024]{2,1,0:T(8,128)}) custom-call(f32[1024,1024]{1,0:T(8,128)} %copy-done.33, f32[1024,1024]{1,0:T(8,128)} %add_add_fusion.other_ref, f32[1024,1024]{1,0:T(8,128)} %fusion.151.branch_ref, f32[1024,1024]{1,0:T(8,128)} %fusion.155.received_ref, bf16[2,1024,1024]{2,1,0:T(8,128)(2,1)} %hidden_ref.3, ...), custom_call_target="tpu_custom_call" | custom-call | flops 1024 | bytes 1024 | tf_op jit(solution)/shard_map/finish/pallas_call | solution.py:437
  478.9 29.9 %reduce-scatter.7.cloned.1.call-done = f32[64,1296]{1,0:T(8,128)} async-done(((f32[1024,1296]{1,0:T(8,128)}), f32[64,1296]{1,0:T(8,128)}) %reduce-scatter.7.cloned.1.call-update) | async-done | bytes 331792
  511.9 10.1 %finish.3 = (bf16[2,1024,1024]{2,1,0:T(8,128)(2,1)}, f32[2,1024,1024]{2,1,0:T(8,128)}) custom-call(f32[1024,1024]{1,0:T(8,128)} %add_add_fusion.2.part_ref, f32[1024,1024]{1,0:T(8,128)} %collective-permute-done.7.other_ref, f32[1024,1024]{1,0:T(8,128)} %fusion.145.branch_ref, ...), custom_call_target="tpu_custom_call", output_to_operand_aliasing={{0}: (7, {}), {1}: (8, {})} | custom-call | flops 1024 | bytes 1024 | tf_op jit(solution)/shard_map/finish/pallas_call | solution.py:437
  (541 shorter events, 105.2 us)
Async XLA Ops:
  7.2 24.0 %copy-start = (bf16[1024,256]{1,0:T(8,128)(2,1)S(1)}, bf16[1024,256]{1,0:T(8,128)(2,1)}, u32[]{:S(2)}) copy-start(bf16[1024,256]{1,0:T(8,128)(2,1)} %param.22) | copy-start | bytes 1572868
  7.2 412.1 %reduce-scatter.5.cloned.1.call-start = ((), (), s32[]{:S(2)}) async-start(), calls=%async_computation.2 | async-start | bytes 8912896 | tf_op jit(solution)/shard_map/reduce_scatter | solution.py:789
  10.6 62.4 %collective-permute-start.15 = (f32[22576]{0:T(1024)}, f32[22576]{0:T(1024)}, u32[]{:S(2)}, u32[]{:S(2)}) collective-permute-start(f32[22576]{0:T(1024)} %concatenate.163), channel_id=1, source_target_pairs={{0,1},{1,0},{2,3},{3,2},{4,5},{5,4},{6,7},{7,6},{8,9},{9,8},{10,11... | collective-permute-start | bytes 270920 | tf_op jit(solution)/shard_map/ppermute | solution.py:602
  13.5 8.6 %copy-start.26 = (bf16[2,1024,1024]{2,1,0:T(8,128)(2,1)S(1)}, bf16[2,1024,1024]{2,1,0:T(8,128)(2,1)}, u32[]{:S(2)}) copy-start(bf16[2,1024,1024]{2,1,0:T(8,128)(2,1)} %hidden_ref.3) | copy-start | bytes 12582916
  15.8 93.9 %collective-permute-start.1 = (f32[256,1024]{1,0:T(8,128)}, f32[256,1024]{1,0:T(8,128)}, u32[]{:S(2)}, u32[]{:S(2)}) collective-permute-start(f32[256,1024]{1,0:T(8,128)} %dynamic-slice_convert_fusion.2), channel_id=1, source_target_pairs={{0,1},{1,0},{2,3},{3,2},{4,5},{5,4},{6,7},{7,6},{8,9},{9,8},{10,11... | collective-permute-start | bytes 3145736 | tf_op jit(solution)/shard_map/ppermute | solution.py:563
  18.0 93.3 %collective-permute-start.3 = (f32[256,1024]{1,0:T(8,128)}, f32[256,1024]{1,0:T(8,128)}, u32[]{:S(2)}, u32[]{:S(2)}) collective-permute-start(f32[256,1024]{1,0:T(8,128)} %dynamic-slice_convert_fusion.1), channel_id=1, source_target_pairs={{0,1},{1,0},{2,3},{3,2},{4,5},{5,4},{6,7},{7,6},{8,9},{9,8},{10,11... | collective-permute-start | bytes 3145736 | tf_op jit(solution)/shard_map/ppermute | solution.py:563
  22.1 165.9 %collective-permute-start.5 = (f32[256,1024]{1,0:T(8,128)}, f32[256,1024]{1,0:T(8,128)}, u32[]{:S(2)}, u32[]{:S(2)}) collective-permute-start(f32[256,1024]{1,0:T(8,128)} %dynamic-slice_convert_fusion), channel_id=1, source_target_pairs={{0,1},{1,0},{2,3},{3,2},{4,5},{5,4},{6,7},{7,6},{8,9},{9,8},{10,11... | collective-permute-start | bytes 3145736 | tf_op jit(solution)/shard_map/ppermute | solution.py:563
  28.5 23.1 %copy-start.141 = (f32[16]{0:T(128)}, f32[16]{0:T(128)S(1)}, u32[]{:S(2)}) copy-start(f32[16]{0:T(128)S(1)} %exponential_negate_fusion) | copy-start | bytes 196
  29.2 22.4 %copy-start.79 = (f32[16,1024]{1,0:T(8,128)}, f32[16,1024]{1,0:T(8,128)S(1)}, u32[]{:S(2)}) copy-start(f32[16,1024]{1,0:T(8,128)S(1)} %fusion.60) | copy-start | bytes 196612
  30.5 26.4 %copy-start.105 = (s32[1,1024]{1,0:T(1,128)}, s32[1,1024]{1,0:T(1,128)S(1)}, u32[]{:S(2)}) copy-start(s32[1,1024]{1,0:T(1,128)S(1)} %get-tuple-element.307) | copy-start | bytes 12292
  31.2 20.3 %copy-start.77 = (f32[16,1024]{1,0:T(8,128)}, f32[16,1024]{1,0:T(8,128)S(1)}, u32[]{:S(2)}) copy-start(f32[16,1024]{1,0:T(8,128)S(1)} %fusion.59) | copy-start | bytes 196612
  33.7 23.2 %copy-start.28 = (f32[1024,256]{0,1:T(8,128)}, f32[1024,256]{0,1:T(8,128)S(1)}, u32[]{:S(2)}) copy-start(f32[1024,256]{0,1:T(8,128)S(1)} %fusion.149) | copy-start | bytes 3145732
  47.3 8.8 %copy-start.152 = (f32[4,256]{1,0:T(4,128)S(1)}, f32[4,256]{1,0:T(4,128)}, u32[]{:S(2)}) copy-start(f32[4,256]{1,0:T(4,128)} %param.26) | copy-start | bytes 12292
  47.3 9.6 %copy-start.156 = (f32[256]{0:T(256)S(1)}, f32[256]{0:T(256)}, u32[]{:S(2)}) copy-start(f32[256]{0:T(256)} %param.27) | copy-start | bytes 3076
  51.6 30.0 %copy-start.69 = (f32[2,8,8,128]{3,2,1,0:T(8,128)}, f32[2,8,8,128]{3,2,1,0:T(8,128)S(1)}, u32[]{:S(2)}) copy-start(f32[2,8,8,128]{3,2,1,0:T(8,128)S(1)} %copy.234) | copy-start | bytes 196612
  51.7 19.9 %copy-start.71 = (f32[2,8,8,128]{3,2,1,0:T(8,128)}, f32[2,8,8,128]{3,2,1,0:T(8,128)S(1)}, u32[]{:S(2)}) copy-start(f32[2,8,8,128]{3,2,1,0:T(8,128)S(1)} %copy.231) | copy-start | bytes 196612
  56.1 6.4 %copy-start.115 = (f32[1,256]{1,0:T(1,128)}, f32[1,256]{1,0:T(1,128)S(1)}, u32[]{:S(2)}) copy-start(f32[1,256]{1,0:T(1,128)S(1)} %get-tuple-element.324) | copy-start | bytes 3076
  56.1 6.4 %copy-start.118 = (f32[1,256]{1,0:T(1,128)}, f32[1,256]{1,0:T(1,128)S(1)}, u32[]{:S(2)}) copy-start(f32[1,256]{1,0:T(1,128)S(1)} %get-tuple-element.326) | copy-start | bytes 3076
  56.2 6.4 %copy-start.121 = (f32[1,256]{1,0:T(1,128)}, f32[1,256]{1,0:T(1,128)S(1)}, u32[]{:S(2)}) copy-start(f32[1,256]{1,0:T(1,128)S(1)} %get-tuple-element.327) | copy-start | bytes 3076
  57.0 234.2 %copy-start.100 = (f32[1024]{0:T(1024)}, f32[1024]{0:T(1024)S(1)}, u32[]{:S(2)}) copy-start(f32[1024]{0:T(1024)S(1)} %get-tuple-element.321) | copy-start | bytes 12292
  63.4 21.6 %copy-start.3 = (bf16[128,1024]{1,0:T(8,128)(2,1)}, bf16[128,1024]{1,0:T(8,128)(2,1)S(1)}, u32[]{:S(2)}) copy-start(bf16[128,1024]{1,0:T(8,128)(2,1)S(1)} %get-tuple-element.272.outt_ref) | copy-start | bytes 786436
  63.6 21.4 %copy-start.1 = (bf16[1024,128]{1,0:T(8,128)(2,1)}, bf16[1024,128]{1,0:T(8,128)(2,1)S(1)}, u32[]{:S(2)}) copy-start(bf16[1024,128]{1,0:T(8,128)(2,1)S(1)} %copy.166.into_ref) | copy-start | bytes 786436
  85.0 17.5 %copy-start.87 = (f32[16,8,128]{2,1,0:T(8,128)S(1)}, f32[16,8,128]{2,1,0:T(8,128)}, u32[]{:S(2)}) copy-start(f32[16,8,128]{2,1,0:T(8,128)} %get-tuple-element.300) | copy-start | bytes 196612
  100.4 28.4 %collective-permute-start = (f32[2,1024]{1,0:T(2,128)}, f32[2,1024]{1,0:T(2,128)}, u32[]{:S(2)}, u32[]{:S(2)}) collective-permute-start(f32[2,1024]{1,0:T(2,128)} %slice_bitcast_fusion.3), channel_id=1, source_target_pairs={{0,1},{1,0},{2,3},{3,2},{4,5},{5,4},{6,7},{7,6},{8,9},{9,8},{10,11... | collective-permute-start | bytes 24584 | tf_op jit(solution)/shard_map/ppermute | solution.py:533
  109.7 65.7 %collective-permute-start.2 = (f32[256,1024]{1,0:T(8,128)}, f32[256,1024]{1,0:T(8,128)}, u32[]{:S(2)}, u32[]{:S(2)}) collective-permute-start(f32[256,1024]{1,0:T(8,128)} %collective-permute-done.1.first_ref), channel_id=1, source_target_pairs={{0,4},{2,6},{4,0},{6,2},{8,12},{10,14},{12,8},{14,10},{16,20},{18,... | collective-permute-start | bytes 3145736 | tf_op jit(solution)/shard_map/ppermute | solution.py:567
  111.3 64.1 %collective-permute-start.4 = (f32[256,1024]{1,0:T(8,128)}, f32[256,1024]{1,0:T(8,128)}, u32[]{:S(2)}, u32[]{:S(2)}) collective-permute-start(f32[256,1024]{1,0:T(8,128)} %collective-permute-done.3.first_ref), channel_id=1, source_target_pairs={{0,4},{2,6},{4,0},{6,2},{8,12},{10,14},{12,8},{14,10},{16,20},{18,... | collective-permute-start | bytes 3145736 | tf_op jit(solution)/shard_map/ppermute | solution.py:567
  129.6 9.6 %copy-start.94 = (bf16[1024,1024]{1,0:T(8,128)(2,1)S(1)}, bf16[1024,1024]{1,0:T(8,128)(2,1)}, u32[]{:S(2)}) copy-start(bf16[1024,1024]{1,0:T(8,128)(2,1)} %param.32) | copy-start | bytes 6291460
  143.5 99.7 %collective-permute-start.8 = (f32[1024,1024]{1,0:T(8,128)}, f32[1024,1024]{1,0:T(8,128)}, u32[]{:S(2)}, u32[]{:S(2)}) collective-permute-start(f32[1024,1024]{1,0:T(8,128)} %fusion.145.branch_ref), channel_id=1, source_target_pairs={{0,1},{1,0},{2,3},{3,2},{4,5},{5,4},{6,7},{7,6},{8,9},{9,8},{10,11... | collective-permute-start | bytes 12582920 | tf_op jit(solution)/shard_map/ppermute | solution.py:533
  143.6 33.7 %copy-start.104 = (f32[1024]{0:T(1024)S(1)}, f32[1024]{0:T(1024)}, u32[]{:S(2)}) copy-start(f32[1024]{0:T(1024)} %copy-done.102) | copy-start | bytes 12292
  175.4 40.7 %collective-permute-start.9 = (f32[256,1024]{1,0:T(8,128)}, f32[256,1024]{1,0:T(8,128)}, u32[]{:S(2)}, u32[]{:S(2)}) collective-permute-start(f32[256,1024]{1,0:T(8,128)} %collective-permute-done.1.first_ref), channel_id=1, source_target_pairs={{0,2},{2,0},{4,6},{6,4},{8,10},{10,8},{12,14},{14,12},{16,18},{18,... | collective-permute-start | bytes 3145736 | tf_op jit(solution)/shard_map/ppermute | solution.py:567
  175.4 41.3 %collective-permute-start.10 = (f32[256,1024]{1,0:T(8,128)}, f32[256,1024]{1,0:T(8,128)}, u32[]{:S(2)}, u32[]{:S(2)}) collective-permute-start(f32[256,1024]{1,0:T(8,128)} %collective-permute-done.2.second_ref), channel_id=1, source_target_pairs={{0,2},{2,0},{4,6},{6,4},{8,10},{10,8},{12,14},{14,12},{16,18},{18,... | collective-permute-start | bytes 3145736 | tf_op jit(solution)/shard_map/ppermute | solution.py:567
  183.1 7.0 %copy-start.142 = (f32[16]{0:T(128)S(1)}, f32[16]{0:T(128)}, u32[]{:S(2)}) copy-start(f32[16]{0:T(128)} %copy-done.141) | copy-start | bytes 196
  183.1 10.8 %copy-start.75 = (bf16[1024,16]{0,1:T(8,128)(2,1)S(1)}, bf16[1024,16]{0,1:T(8,128)(2,1)}, u32[]{:S(2)}) copy-start(bf16[1024,16]{0,1:T(8,128)(2,1)} %param.23) | copy-start | bytes 98308
  188.1 25.6 %collective-permute-start.6 = (f32[256,1024]{1,0:T(8,128)}, f32[256,1024]{1,0:T(8,128)S(1)}, u32[]{:S(2)}, u32[]{:S(2)}) collective-permute-start(f32[256,1024]{1,0:T(8,128)} %collective-permute-done.5.first_ref), channel_id=1, source_target_pairs={{0,4},{2,6},{4,0},{6,2},{8,12},{10,14},{12,8},{14,10},{16,20},{18,... | collective-permute-start | bytes 3145736 | tf_op jit(solution)/shard_map/ppermute | solution.py:567
  193.2 28.0 %collective-permute-start.11 = (f32[256,1024]{1,0:T(8,128)}, f32[256,1024]{1,0:T(8,128)S(1)}, u32[]{:S(2)}, u32[]{:S(2)}) collective-permute-start(f32[256,1024]{1,0:T(8,128)} %collective-permute-done.3.first_ref), channel_id=1, source_target_pairs={{0,2},{2,0},{4,6},{6,4},{8,10},{10,8},{12,14},{14,12},{16,18},{18,... | collective-permute-start | bytes 3145736 | tf_op jit(solution)/shard_map/ppermute | solution.py:567
  198.2 15.4 %copy-start.96 = (bf16[1024,1024]{1,0:T(8,128)(2,1)S(1)}, bf16[1024,1024]{1,0:T(8,128)(2,1)}, u32[]{:S(2)}) copy-start(bf16[1024,1024]{1,0:T(8,128)(2,1)} %param.21) | copy-start | bytes 6291460
  198.2 15.4 %copy-start.161 = (bf16[1024,1024]{1,0:T(8,128)(2,1)S(1)}, bf16[1024,1024]{1,0:T(8,128)(2,1)}, u32[]{:S(2)}) copy-start(bf16[1024,1024]{1,0:T(8,128)(2,1)} %get-tuple-element.104) | copy-start | bytes 6291460
  199.0 17.7 %copy-start.54 = (bf16[1024,1024]{1,0:T(8,128)(2,1)S(1)}, bf16[1024,1024]{1,0:T(8,128)(2,1)}, u32[]{:S(2)}) copy-start(bf16[1024,1024]{1,0:T(8,128)(2,1)} %param.20) | copy-start | bytes 6291460
  199.0 17.7 %copy-start.62 = (bf16[1024,1024]{1,0:T(8,128)(2,1)S(1)}, bf16[1024,1024]{1,0:T(8,128)(2,1)}, u32[]{:S(2)}) copy-start(bf16[1024,1024]{1,0:T(8,128)(2,1)} %get-tuple-element.93) | copy-start | bytes 6291460
  213.6 7.6 %collective-permute-start.12 = (f32[256,1024]{1,0:T(8,128)}, f32[256,1024]{1,0:T(8,128)}, u32[]{:S(2)}, u32[]{:S(2)}) collective-permute-start(f32[256,1024]{1,0:T(8,128)} %collective-permute-done.4.second_ref), channel_id=1, source_target_pairs={{0,2},{2,0},{4,6},{6,4},{8,10},{10,8},{12,14},{14,12},{16,18},{18,... | collective-permute-start | bytes 3145736 | tf_op jit(solution)/shard_map/ppermute | solution.py:567
  216.1 18.0 %collective-permute-start.13 = (f32[256,1024]{1,0:T(8,128)}, f32[256,1024]{1,0:T(8,128)S(1)}, u32[]{:S(2)}, u32[]{:S(2)}) collective-permute-start(f32[256,1024]{1,0:T(8,128)} %collective-permute-done.5.first_ref), channel_id=1, source_target_pairs={{0,2},{2,0},{4,6},{6,4},{8,10},{10,8},{12,14},{14,12},{16,18},{18,... | collective-permute-start | bytes 3145736 | tf_op jit(solution)/shard_map/ppermute | solution.py:567
  216.6 17.5 %collective-permute-start.14 = (f32[256,1024]{1,0:T(8,128)S(1)}, f32[256,1024]{1,0:T(8,128)}, u32[]{:S(2)}, u32[]{:S(2)}) collective-permute-start(f32[256,1024]{1,0:T(8,128)S(1)} %collective-permute-done.6.second_ref), channel_id=1, source_target_pairs={{0,2},{2,0},{4,6},{6,4},{8,10},{10,8},{12,14},{14,12},{16,18},{18,... | collective-permute-start | bytes 3145736 | tf_op jit(solution)/shard_map/ppermute | solution.py:567
  264.0 10.0 %copy-start.40 = (bf16[1024,1024]{1,0:T(8,128)(2,1)S(1)}, bf16[1024,1024]{1,0:T(8,128)(2,1)}, u32[]{:S(2)}) copy-start(bf16[1024,1024]{1,0:T(8,128)(2,1)} %copy-done.38) | copy-start | bytes 6291460
  274.0 7.8 %copy-start.14 = (f32[1024,128]{1,0:T(8,128)}, f32[1024,128]{1,0:T(8,128)S(1)}, u32[]{:S(2)}) copy-start(f32[1024,128]{1,0:T(8,128)S(1)} %get-tuple-element.157) | copy-start | bytes 1572868
  274.0 7.8 %copy-start.25 = (bf16[1024,1024]{1,0:T(8,128)(2,1)}, bf16[1024,1024]{1,0:T(8,128)(2,1)S(1)}, u32[]{:S(2)}) copy-start(bf16[1024,1024]{1,0:T(8,128)(2,1)S(1)} %get-tuple-element.130) | copy-start | bytes 6291460
  274.0 7.8 %copy-start.22 = (bf16[1024,1024]{1,0:T(8,128)(2,1)S(1)}, bf16[1024,1024]{1,0:T(8,128)(2,1)}, u32[]{:S(2)}) copy-start(bf16[1024,1024]{1,0:T(8,128)(2,1)} %copy-done.21) | copy-start | bytes 6291460
  274.0 7.8 %copy-start.43 = (bf16[2,1024,1024]{2,1,0:T(8,128)(2,1)S(1)}, bf16[2,1024,1024]{2,1,0:T(8,128)(2,1)}, u32[]{:S(2)}) copy-start(bf16[2,1024,1024]{2,1,0:T(8,128)(2,1)} %cotangent_ref.3) | copy-start | bytes 12582916
  291.1 217.7 %reduce-scatter.7.cloned.1.call-start = ((), (), s32[]{:S(2)}) async-start(), calls=%async_computation.3 | async-start | bytes 6127616
  295.2 93.2 %collective-permute-start.7 = (f32[1024,1024]{1,0:T(8,128)}, f32[1024,1024]{1,0:T(8,128)}, u32[]{:S(2)}, u32[]{:S(2)}) collective-permute-start(f32[1024,1024]{1,0:T(8,128)} %add_add_fusion.2.part_ref), channel_id=1, source_target_pairs={{0,1},{1,0},{2,3},{3,2},{4,5},{5,4},{6,7},{7,6},{8,9},{9,8},{10,11... | collective-permute-start | bytes 12582920 | tf_op jit(solution)/shard_map/ppermute | solution.py:533
  303.8 32.2 %copy-start.70 = (f32[2,8,8,128]{3,2,1,0:T(8,128)S(1)}, f32[2,8,8,128]{3,2,1,0:T(8,128)}, u32[]{:S(2)}) copy-start(f32[2,8,8,128]{3,2,1,0:T(8,128)} %copy-done.69) | copy-start | bytes 196612
  303.8 32.2 %copy-start.72 = (f32[2,8,8,128]{3,2,1,0:T(8,128)S(1)}, f32[2,8,8,128]{3,2,1,0:T(8,128)}, u32[]{:S(2)}) copy-start(f32[2,8,8,128]{3,2,1,0:T(8,128)} %copy-done.71) | copy-start | bytes 196612
  303.8 32.2 %copy-start.88 = (f32[16,8,128]{2,1,0:T(8,128)S(1)}, f32[16,8,128]{2,1,0:T(8,128)}, u32[]{:S(2)}) copy-start(f32[16,8,128]{2,1,0:T(8,128)} %get-tuple-element.342) | copy-start | bytes 196612
  337.5 12.7 %copy-start.78 = (f32[16,1024]{1,0:T(8,128)S(1)}, f32[16,1024]{1,0:T(8,128)}, u32[]{:S(2)}) copy-start(f32[16,1024]{1,0:T(8,128)} %copy-done.77) | copy-start | bytes 196612
  337.5 12.9 %copy-start.91 = (bf16[16,1024]{1,0:T(8,128)(2,1)S(1)}, bf16[16,1024]{1,0:T(8,128)(2,1)}, u32[]{:S(2)}) copy-start(bf16[16,1024]{1,0:T(8,128)(2,1)} %copy-done.90) | copy-start | bytes 98308
  438.3 9.3 %collective-permute-start.16 = (f32[2304]{0:T(1024)S(1)}, f32[2304]{0:T(1024)S(1)}, u32[]{:S(2)}, u32[]{:S(2)}) collective-permute-start(f32[2304]{0:T(1024)S(1)} %pad_maximum_fusion.5), channel_id=1, source_target_pairs={{0,1},{1,0},{2,3},{3,2},{4,5},{5,4},{6,7},{7,6},{8,9},{9,8},{10,11... | collective-permute-start | bytes 27656 | tf_op jit(solution)/shard_map/ppermute | solution.py:533
  447.7 4.1 collective-permute-start.17
  451.8 4.0 collective-permute-start.18
  455.9 8.6 %collective-permute-start.19 = (f32[8496]{0:T(1024)S(1)}, f32[8496]{0:T(1024)S(1)}, u32[]{:S(2)}, u32[]{:S(2)}) collective-permute-start(f32[8496]{0:T(1024)S(1)} %add.395), channel_id=1, source_target_pairs={{0,8},{2,10},{4,12},{6,14},{8,0},{10,2},{12,4},{14,6},{16,24},{18,... | collective-permute-start | bytes 101960 | tf_op jit(solution)/shard_map/ppermute | solution.py:567
  460.0 7.2 %copy-start.81 = (f32[2,64,1024]{2,1,0:T(8,128)S(1)}, f32[2,64,1024]{2,1,0:T(8,128)}, u32[]{:S(2)}) copy-start(f32[2,64,1024]{2,1,0:T(8,128)} %reduce-scatter.5.cloned.1.call-done) | copy-start | bytes 1572868
  460.0 8.0 %copy-start.20 = (f32[1024]{0:T(1024)S(1)}, f32[1024]{0:T(1024)}, u32[]{:S(2)}) copy-start(f32[1024]{0:T(1024)} %param.19) | copy-start | bytes 12292
  464.5 13.7 %collective-permute-start.20 = (f32[8496]{0:T(1024)S(1)}, f32[8496]{0:T(1024)S(1)}, u32[]{:S(2)}, u32[]{:S(2)}) collective-permute-start(f32[8496]{0:T(1024)S(1)} %add.396), channel_id=1, source_target_pairs={{0,16},{2,18},{4,20},{6,22},{8,24},{10,26},{12,28},{14,30},{16,0},... | collective-permute-start | bytes 101960 | tf_op jit(solution)/shard_map/ppermute | solution.py:567
  509.7 15.6 %collective-permute-start.21 = (f32[64,256]{0,1:T(8,128)S(1)}, f32[64,256]{0,1:T(8,128)S(1)}, u32[]{:S(2)}, u32[]{:S(2)}) collective-permute-start(f32[64,256]{0,1:T(8,128)S(1)} %copy.229), channel_id=1, source_target_pairs={{0,1},{1,0},{2,3},{3,2},{4,5},{5,4},{6,7},{7,6},{8,9},{9,8},{10,11... | collective-permute-start | bytes 196616 | tf_op jit(solution)/shard_map/ppermute | solution.py:533
  511.9 12.0 %slice-start = ((f32[64,1296]{1,0:T(8,128)}), f32[64,16]{1,0:T(8,128)S(1)}, s32[]{:S(2)}) async-start(f32[64,1296]{1,0:T(8,128)} %reduce-scatter.7.cloned.1.call-done), calls=%async_computation.4 | async-start | bytes 65536 | tf_op jit(solution)/shard_map/slice | solution.py:862
  511.9 12.7 %copy-start.82 = (f32[64,1296]{1,0:T(8,128)S(1)}, f32[64,1296]{1,0:T(8,128)}, u32[]{:S(2)}) copy-start(f32[64,1296]{1,0:T(8,128)} %reduce-scatter.7.cloned.1.call-done) | copy-start | bytes 995332
  (128 other events, 343.0 us)
Sparse Core Ops, SparseCore 0:
  291.2 106.1 reduce-scatter.4
  425.7 83.0 reduce-scatter.6

commit v6 on v5

--- a/solution.py
+++ b/solution.py
@@ -798,16 +798,16 @@
         ],
         axis=1,
     )
-    waits, extra_backs = (later_part, *others), []
+    waits, extra_backs = (later_part,), []
     for s in range(whole_from, seq_count):
         d_gate = middles[s][1]
-        back = unit_backward(extras[s], other, d_gate, after(middles[s][2], *waits), state_backs[s])
+        back = unit_backward(
+            extras[s], other, d_gate, after(middles[s][2], *waits), state_backs[s],
+            tuple(others[:whole_from]),
+        )
         extra_backs.append(back)
     later_part = after(later_part, early, *[back[0] for back in extra_backs])
     later = lax.psum_scatter(later_part, "dp", scatter_dimension=0, tiled=True)
-    later_value = later[:, :local_inner]
-    edge = local_inner + state_width
-    state_part = later[:, local_inner:edge]
     for s, back in zip(range(whole_from, seq_count), extra_backs):
         d_value = after(back[0], later_part)
         others.append(
@@ -842,6 +842,10 @@
     packed = sum_dp(jnp.concatenate([own_flat, shared_flat]), *between)
     own_sum, shared_sum = packed[: own_flat.shape[0]], packed[own_flat.shape[0] :]
 
+    later = after(later, stacked[1])
+    later_value = later[:, :local_inner]
+    edge = local_inner + state_width
+    state_part = later[:, local_inner:edge]
     grad_proj_state = tensor_join(state_part, tensor_others(state_part))
 
     def split(flat, like):

time: 538 us -> 510 us (0.948)
  waiting for transfers between devices: 60.4 us -> 34.9 us
    ppermute x5, waiting for transfers between devices: 14.2 us -> 1.2 us  [tensor_others(): return lax.ppermute(part, 'tensor', [(0, 1), (1, 0)])]
    unnamed x3, waiting for transfers between devices: 29.9 us -> 18.4 us
    unnamed x364 -> x351, local copies, waits for them, and re-layouts: 40.7 us -> 37.6 us
  transfers between devices with their start and end apart: 24 -> 24, of which waited for: 4 -> 3; matrix products, arithmetic and copies ran while one was open for 34% -> 36% of each run, Pallas kernels for 31% -> 33%
where the time goes in v6:
time: 510 us; the launch traced here: 505 us
  Pallas kernels  192 us (38%)
  matrix products  119 us (23%)
  local copies, waits for them, and re-layouts  68.6 us (13%)
  other arithmetic  52.1 us (10%)
  waiting for transfers between devices  34.9 us (7%)
  starting transfers between devices  20.9 us (4%)
  between operations  16.7 us (3%)
    pallas_call x3, Pallas kernels, mix_backward(): pl.pallas_call(back_kernel, grid=(seqs, chunks), in_specs=[slab, spec((ch...  90.7 us
    dot_general x12, matrix products, in_product(): lax.dot_general(weight, tokens, (((0,), (1,)), ((), ())), preferred_eleme...  45.8 us
    dot_general x12, matrix products, out_product(): lax.dot_general(left, weight, (((0,), (1,)), ((), ())), preferred_element...  41.7 us
    pallas_call x3, Pallas kernels, mix_forward(): pl.pallas_call(mix_kernel, grid=(seqs, chunks), in_specs=[slab, slab, sla...  40.6 us
    unnamed x351, local copies, waits for them, and re-layouts  37.6 us
    pallas_call x3, Pallas kernels, middle(): pl.pallas_call(functools.partial(middle_kernel, 1.0 / inner_total), grid=...  29.4 us
    pallas_call x2, Pallas kernels, finish(): pl.pallas_call(finish_kernel, grid=(length // tile,), in_specs=[flat] * 4...  20.7 us
    dot_general x4, matrix products, grad_product(): lax.dot_general(tokens, channels, (((0,), (1,)), ((), ())), preferred_ele...  19.9 us
  transfers between devices with their start and end apart: 24, of which 3 were waited for; matrix products, arithmetic and copies ran while one was open for 36% of the time, Pallas kernels for 33%

profile of v6, /device:TPU:0, one launch (start us, length us, event | category | flops | bytes accessed | tf_op | source)
XLA Modules:
  0.0 504.8 jit_solution(13794242801633737238)
XLA Ops:
  10.6 3.0 collective-permute-start.15
  13.5 2.3 dynamic-slice_convert_fusion.2
  15.8 2.2 dynamic-slice_convert_fusion.1
  18.0 2.0 collective-permute-start.3
  20.1 2.2 dynamic-slice_convert_fusion
  23.2 2.3 fusion.5
  25.6 3.7 convert_bitcast_fusion.4.gate_ref
  31.3 2.2 fusion.59
  33.6 2.5 fusion.149
  38.2 3.7 convert_bitcast_fusion.2.gate_ref
  41.9 3.7 fusion.45.dout_ref
  45.7 3.8 fusion.48.dout_ref
  49.5 4.2 convert_bitcast_fusion.3.raw_ref.before_ref
  59.2 3.3 multiply_convert_fusion
  64.4 6.0 %convert_bitcast_fusion.1.raw_ref.before_ref = bf16[1024,1024]{1,0:T(8,128)(2,1)} fusion(bf16[1024,1024]{1,0:T(8,128)(2,1)} %get-tuple-element.113, bf16[1024,1024]{1,0:T(8,128)(2,1)} %param.21), kind=kOutput, calls=%fused_computation.51 | convolution fusion | flops 2148532224 | bytes 6291456 | tf_op jit(solution)/shard_map/dot_general | solution.py:509
  74.8 2.4 fusion.61
  80.9 1.9 broadcast_in_dim.15.conv_ref
  83.7 13.5 %mix_forward.3 = (f32[1024,1024]{1,0:T(8,128)}, bf16[8,1024,128]{2,1,0:T(8,128)(2,1)S(1)}, f32[8,8,128]{2,1,0:T(8,128)S(1)}) custom-call(bf16[1024,1024]{1,0:T(8,128)(2,1)} %convert_bitcast_fusion.3.raw_ref.before_ref, bf16[1024,1024]{1,0:T(8,128)(2,1)} %convert_bitcast_fusion.4.gate_ref, bf16[1024,1024]{1,0:T(8,128)(2,1)} %fusion.45.dout_ref, ...), custom_call_target="tpu_custom_call" | custom-call | flops 1024 | bytes 1024 | tf_op jit(solution)/shard_map/mix_forward/pallas_call | solution.py:252
  99.2 2.0 collective-permute-start
  112.7 13.5 %mix_forward.4 = (f32[1024,1024]{1,0:T(8,128)}, bf16[8,1024,128]{2,1,0:T(8,128)(2,1)S(1)}, f32[8,8,128]{2,1,0:T(8,128)S(1)}) custom-call(bf16[1024,1024]{1,0:T(8,128)(2,1)} %convert_bitcast_fusion.1.raw_ref.before_ref, bf16[1024,1024]{1,0:T(8,128)(2,1)} %convert_bitcast_fusion.2.gate_ref, bf16[1024,1024]{1,0:T(8,128)(2,1)} %fusion.48.dout_ref, ...), custom_call_target="tpu_custom_call" | custom-call | flops 1024 | bytes 1024 | tf_op jit(solution)/shard_map/mix_forward/pallas_call | solution.py:252
  128.3 9.6 %gated_middle.3 = (bf16[1024,1024]{1,0:T(8,128)(2,1)S(1)}, bf16[1024,1024]{1,0:T(8,128)(2,1)}, bf16[1024,1024]{1,0:T(8,128)(2,1)}, f32[1024,128]{1,0:T(8,128)S(1)}) custom-call(bf16[1024,1024]{1,0:T(8,128)(2,1)} %convert_bitcast_fusion.4.gate_ref, f32[1024,1024]{1,0:T(8,128)} %get-tuple-element.89.mixed_ref, bf16[1024,1024]{1,0:T(8,128)(2,1)} %fusion.45.dout_ref, ...), custom_call_target="tpu_custom_call" | custom-call | flops 1024 | bytes 1024 | tf_op jit(solution)/shard_map/gated_middle/pallas_call | solution.py:491
  138.0 4.3 fusion.145.branch_ref
  142.4 30.0 %mix_backward.3 = (bf16[1024,1024]{1,0:T(8,128)(2,1)}, f32[8,8,16,128]{3,2,1,0:T(8,128)S(1)}, f32[1024,256]{1,0:T(8,128)S(1)}, f32[5,1024,128]{2,1,0:T(8,128)}) custom-call(bf16[1024,1024]{1,0:T(8,128)(2,1)} %convert_bitcast_fusion.3.raw_ref.before_ref, bf16[1024,1024]{1,0:T(8,128)(2,1)} %convert_bitcast_fusion.3.raw_ref.before_ref, ...), custom_call_target="tpu_custom_call" | custom-call | flops 1024 | bytes 1024 | tf_op jit(solution)/shard_map/mix_backward/pallas_call | solution.py:294
  176.1 2.9 multiply_reduce_fusion.7
  186.0 2.0 collective-permute-start.6
  188.0 1.7 copy_add_fusion.1
  193.4 2.2 multiply_reduce_fusion.4
  196.3 15.3 %collective-permute-done.6.second_ref = f32[256,1024]{1,0:T(8,128)S(1)} collective-permute-done((f32[256,1024]{1,0:T(8,128)}, f32[256,1024]{1,0:T(8,128)S(1)}, u32[]{:S(2)}, u32[]{:S(2)}) %collective-permute-start.6) | collective-permute-done | bytes 1048608 | tf_op jit(solution)/shard_map/ppermute | solution.py:567
  211.6 2.4 fusion.146
  214.7 4.8 add_add_fusion.2.part_ref
  219.5 4.1 assemble.3
  223.6 3.5 assemble.4
  227.1 5.5 %convolution_convert_fusion.gate_ref = bf16[1024,1024]{1,0:T(8,128)(2,1)} fusion(bf16[1024,1024]{1,0:T(8,128)(2,1)} %assemble.4, bf16[1024,1024]{1,0:T(8,128)(2,1)S(1)} %copy-done.37), kind=kOutput, calls=%fused_computation.59 | convolution fusion | flops 2148532224 | bytes 6291456 | tf_op jit(solution)/shard_map/dot_general | solution.py:509
  232.7 3.0 assemble.5
  235.7 6.1 %fusion.51.dout_ref = bf16[1024,1024]{1,0:T(8,128)(2,1)} fusion(bf16[1024,1024]{1,0:T(8,128)(2,1)} %assemble.5, bf16[2,1024,1024]{2,1,0:T(8,128)(2,1)} %cotangent_ref.3), kind=kOutput, calls=%fused_computation.58 | convolution fusion | flops 2148532224 | bytes 6291456 | tf_op jit(solution)/shard_map/dot_general | solution.py:509
  241.8 3.7 convolution_convert_fusion.1.raw_ref.before_ref
  245.5 1.9 broadcast_in_dim.19.conv_ref
  247.6 13.5 %mix_forward.5 = (f32[1024,1024]{1,0:T(8,128)}, bf16[8,1024,128]{2,1,0:T(8,128)(2,1)S(1)}, f32[8,8,128]{2,1,0:T(8,128)S(1)}) custom-call(bf16[1024,1024]{1,0:T(8,128)(2,1)} %convolution_convert_fusion.1.raw_ref.before_ref, bf16[1024,1024]{1,0:T(8,128)(2,1)} %convolution_convert_fusion.gate_ref, bf16[1024,1024]{1,0:T(8,128)(2,1)} %fusion.51.dout_ref, ...), custom_call_target="tpu_custom_call" | custom-call | flops 1024 | bytes 1024 | tf_op jit(solution)/shard_map/mix_forward/pallas_call | solution.py:252
  262.5 10.0 %gated_middle.4 = (bf16[1024,1024]{1,0:T(8,128)(2,1)S(1)}, bf16[1024,1024]{1,0:T(8,128)(2,1)}, bf16[1024,1024]{1,0:T(8,128)(2,1)}, f32[1024,128]{1,0:T(8,128)S(1)}) custom-call(bf16[1024,1024]{1,0:T(8,128)(2,1)} %convert_bitcast_fusion.2.gate_ref, f32[1024,1024]{1,0:T(8,128)} %get-tuple-element.105.mixed_ref, bf16[1024,1024]{1,0:T(8,128)(2,1)} %fusion.48.dout_ref, ...), custom_call_target="tpu_custom_call" | custom-call | flops 1024 | bytes 1024 | tf_op jit(solution)/shard_map/gated_middle/pallas_call | solution.py:491
  272.5 7.7 %fusion.30 = f32[1,1024,1024]{2,1,0:T(8,128)S(1)} fusion(bf16[1024,1024]{1,0:T(8,128)(2,1)} %get-tuple-element.126, bf16[1024,1024]{1,0:T(8,128)(2,1)} %get-tuple-element.91, bf16[1024,1024]{1,0:T(8,128)(2,1)S(1)} %copy-done.37, bf16[1024,1024]{1,0:T(8,128)(2,1)S(1)} %copy-done.41), kind=kOutput, calls=%fused_computation.40 | convolution fusion | flops 4311744512 | bytes 12582912 | tf_op jit(solution)/shard_map/dot_general | solution.py:513
  280.3 4.6 fusion.27
  284.9 4.6 pad_maximum_fusion
  293.0 1.8 collective-permute-start.7
  294.8 6.9 %fusion.151.branch_ref = f32[1024,1024]{1,0:T(8,128)} fusion(bf16[1024,1024]{1,0:T(8,128)(2,1)} %copy-done.26, bf16[1024,1024]{1,0:T(8,128)(2,1)} %param.32), kind=kOutput, calls=%fused_computation.297 | convolution fusion | flops 2147483648 | bytes 8388608 | tf_op jit(solution)/shard_map/dot_general | solution.py:505
  301.7 30.5 %mix_backward.4 = (bf16[1024,1024]{1,0:T(8,128)(2,1)}, f32[8,8,16,128]{3,2,1,0:T(8,128)S(1)}, f32[1024,256]{1,0:T(8,128)S(1)}, f32[5,1024,128]{2,1,0:T(8,128)}) custom-call(bf16[1024,1024]{1,0:T(8,128)(2,1)} %convert_bitcast_fusion.1.raw_ref.before_ref, bf16[1024,1024]{1,0:T(8,128)(2,1)} %convert_bitcast_fusion.1.raw_ref.before_ref, ...), custom_call_target="tpu_custom_call" | custom-call | flops 1024 | bytes 1024 | tf_op jit(solution)/shard_map/mix_backward/pallas_call | solution.py:294
  333.5 1.8 fusion.84
  335.2 9.8 %gated_middle.5 = (bf16[1024,1024]{1,0:T(8,128)(2,1)S(1)}, bf16[1024,1024]{1,0:T(8,128)(2,1)}, bf16[1024,1024]{1,0:T(8,128)(2,1)}, f32[1024,128]{1,0:T(8,128)}) custom-call(bf16[1024,1024]{1,0:T(8,128)(2,1)} %convolution_convert_fusion.gate_ref, f32[1024,1024]{1,0:T(8,128)} %get-tuple-element.134.mixed_ref, bf16[1024,1024]{1,0:T(8,128)(2,1)} %fusion.51.dout_ref, ...), custom_call_target="tpu_custom_call" | custom-call | flops 1024 | bytes 1024 | tf_op jit(solution)/shard_map/gated_middle/pallas_call | solution.py:491
  346.4 2.3 copy.200
  348.9 3.1 fusion.87
  359.9 4.5 fusion.23
  364.4 2.9 pad_maximum_fusion.1
  367.4 30.2 %mix_backward.5 = (bf16[1024,1024]{1,0:T(8,128)(2,1)}, f32[8,8,16,128]{3,2,1,0:T(8,128)S(1)}, f32[1024,256]{1,0:T(8,128)S(1)}, f32[5,1024,128]{2,1,0:T(8,128)}) custom-call(bf16[1024,1024]{1,0:T(8,128)(2,1)} %convolution_convert_fusion.1.raw_ref.before_ref, bf16[1024,1024]{1,0:T(8,128)(2,1)} %convolution_convert_fusion.1.raw_ref.before_ref, ...), custom_call_target="tpu_custom_call" | custom-call | flops 1024 | bytes 1024 | tf_op jit(solution)/shard_map/mix_backward/pallas_call | solution.py:294
  397.6 4.4 fusion.150
  402.1 6.1 %copy.224 = f32[1024,1296]{1,0:T(8,128)} copy(f32[1024,1296]{0,1:T(8,128)} %pad_maximum_fusion.1) | data formatting | bytes 10616832
  411.5 2.4 fusion.152
  414.8 2.8 copy-done.28
  417.6 1.7 copy-done.34
  425.0 7.1 %fusion.155.received_ref = f32[1024,1024]{1,0:T(8,128)} fusion(bf16[1024,1024]{1,0:T(8,128)(2,1)} %copy-done.23, bf16[1024,1024]{1,0:T(8,128)(2,1)} %assemble.5), kind=kOutput, calls=%fused_computation.301 | convolution fusion | flops 2147483648 | bytes 8388608 | tf_op jit(solution)/shard_map/dot_general | solution.py:505
  439.6 2.4 fusion.154
  442.1 4.9 add_add_fusion.other_ref
  446.9 2.4 collective-permute-start.20
  450.2 10.4 %finish.2 = (bf16[2,1024,1024]{2,1,0:T(8,128)(2,1)}, f32[2,1024,1024]{2,1,0:T(8,128)}) custom-call(f32[1024,1024]{1,0:T(8,128)} %copy-done.35, f32[1024,1024]{1,0:T(8,128)} %add_add_fusion.other_ref, f32[1024,1024]{1,0:T(8,128)} %fusion.151.branch_ref, f32[1024,1024]{1,0:T(8,128)} %fusion.155.received_ref, bf16[2,1024,1024]{2,1,0:T(8,128)(2,1)} %hidden_ref.3, ...), custom_call_target="tpu_custom_call" | custom-call | flops 1024 | bytes 1024 | tf_op jit(solution)/shard_map/finish/pallas_call | solution.py:437
  460.6 10.3 %finish.3 = (bf16[2,1024,1024]{2,1,0:T(8,128)(2,1)}, f32[2,1024,1024]{2,1,0:T(8,128)}) custom-call(f32[1024,1024]{1,0:T(8,128)} %add_add_fusion.2.part_ref, f32[1024,1024]{1,0:T(8,128)} %collective-permute-done.7.other_ref, f32[1024,1024]{1,0:T(8,128)} %fusion.145.branch_ref, ...), custom_call_target="tpu_custom_call", output_to_operand_aliasing={{0}: (7, {}), {1}: (8, {})} | custom-call | flops 1024 | bytes 1024 | tf_op jit(solution)/shard_map/finish/pallas_call | solution.py:437
  471.6 18.4 %reduce-scatter.7.cloned.1.call-done = f32[64,1296]{1,0:T(8,128)} async-done(((f32[1024,1296]{1,0:T(8,128)}), f32[64,1296]{1,0:T(8,128)}) %reduce-scatter.7.cloned.1.call-update) | async-done | bytes 331792
  (528 shorter events, 96.9 us)
Async XLA Ops:
  7.2 26.4 %copy-start = (bf16[1024,256]{1,0:T(8,128)(2,1)S(1)}, bf16[1024,256]{1,0:T(8,128)(2,1)}, u32[]{:S(2)}) copy-start(bf16[1024,256]{1,0:T(8,128)(2,1)} %param.22) | copy-start | bytes 1572868
  7.2 394.9 %reduce-scatter.5.cloned.1.call-start = ((), (), s32[]{:S(2)}) async-start(), calls=%async_computation.2 | async-start | bytes 8912896 | tf_op jit(solution)/shard_map/reduce_scatter | solution.py:789
  10.6 61.7 %collective-permute-start.15 = (f32[22576]{0:T(1024)}, f32[22576]{0:T(1024)}, u32[]{:S(2)}, u32[]{:S(2)}) collective-permute-start(f32[22576]{0:T(1024)} %concatenate.163), channel_id=1, source_target_pairs={{0,1},{1,0},{2,3},{3,2},{4,5},{5,4},{6,7},{7,6},{8,9},{9,8},{10,11... | collective-permute-start | bytes 270920 | tf_op jit(solution)/shard_map/ppermute | solution.py:602
  13.5 8.7 %copy-start.27 = (bf16[2,1024,1024]{2,1,0:T(8,128)(2,1)S(1)}, bf16[2,1024,1024]{2,1,0:T(8,128)(2,1)}, u32[]{:S(2)}) copy-start(bf16[2,1024,1024]{2,1,0:T(8,128)(2,1)} %hidden_ref.3) | copy-start | bytes 12582916
  15.8 92.6 %collective-permute-start.1 = (f32[256,1024]{1,0:T(8,128)}, f32[256,1024]{1,0:T(8,128)}, u32[]{:S(2)}, u32[]{:S(2)}) collective-permute-start(f32[256,1024]{1,0:T(8,128)} %dynamic-slice_convert_fusion.2), channel_id=1, source_target_pairs={{0,1},{1,0},{2,3},{3,2},{4,5},{5,4},{6,7},{7,6},{8,9},{9,8},{10,11... | collective-permute-start | bytes 3145736 | tf_op jit(solution)/shard_map/ppermute | solution.py:563
  18.0 92.0 %collective-permute-start.3 = (f32[256,1024]{1,0:T(8,128)}, f32[256,1024]{1,0:T(8,128)}, u32[]{:S(2)}, u32[]{:S(2)}) collective-permute-start(f32[256,1024]{1,0:T(8,128)} %dynamic-slice_convert_fusion.1), channel_id=1, source_target_pairs={{0,1},{1,0},{2,3},{3,2},{4,5},{5,4},{6,7},{7,6},{8,9},{9,8},{10,11... | collective-permute-start | bytes 3145736 | tf_op jit(solution)/shard_map/ppermute | solution.py:563
  22.2 163.8 %collective-permute-start.5 = (f32[256,1024]{1,0:T(8,128)}, f32[256,1024]{1,0:T(8,128)}, u32[]{:S(2)}, u32[]{:S(2)}) collective-permute-start(f32[256,1024]{1,0:T(8,128)} %dynamic-slice_convert_fusion), channel_id=1, source_target_pairs={{0,1},{1,0},{2,3},{3,2},{4,5},{5,4},{6,7},{7,6},{8,9},{9,8},{10,11... | collective-permute-start | bytes 3145736 | tf_op jit(solution)/shard_map/ppermute | solution.py:563
  29.3 24.5 %copy-start.135 = (f32[16]{0:T(128)}, f32[16]{0:T(128)S(1)}, u32[]{:S(2)}) copy-start(f32[16]{0:T(128)S(1)} %exponential_negate_fusion) | copy-start | bytes 196
  30.0 23.7 %copy-start.84 = (f32[16,1024]{1,0:T(8,128)}, f32[16,1024]{1,0:T(8,128)S(1)}, u32[]{:S(2)}) copy-start(f32[16,1024]{1,0:T(8,128)S(1)} %fusion.60) | copy-start | bytes 196612
  33.6 20.1 %copy-start.82 = (f32[16,1024]{1,0:T(8,128)}, f32[16,1024]{1,0:T(8,128)S(1)}, u32[]{:S(2)}) copy-start(f32[16,1024]{1,0:T(8,128)S(1)} %fusion.59) | copy-start | bytes 196612
  36.1 23.0 %copy-start.29 = (f32[1024,256]{0,1:T(8,128)}, f32[1024,256]{0,1:T(8,128)S(1)}, u32[]{:S(2)}) copy-start(f32[1024,256]{0,1:T(8,128)S(1)} %fusion.149) | copy-start | bytes 3145732
  38.2 20.9 %copy-start.31 = (f32[1024,256]{0,1:T(8,128)}, f32[1024,256]{0,1:T(8,128)S(1)}, u32[]{:S(2)}) copy-start(f32[1024,256]{0,1:T(8,128)S(1)} %fusion.144) | copy-start | bytes 3145732
  49.5 8.9 %copy-start.146 = (f32[4,256]{1,0:T(4,128)S(1)}, f32[4,256]{1,0:T(4,128)}, u32[]{:S(2)}) copy-start(f32[4,256]{1,0:T(4,128)} %param.26) | copy-start | bytes 12292
  49.5 9.7 %copy-start.150 = (f32[256]{0:T(256)S(1)}, f32[256]{0:T(256)}, u32[]{:S(2)}) copy-start(f32[256]{0:T(256)} %param.27) | copy-start | bytes 3076
  53.7 26.5 %copy-start.72 = (f32[2,8,8,128]{3,2,1,0:T(8,128)}, f32[2,8,8,128]{3,2,1,0:T(8,128)S(1)}, u32[]{:S(2)}) copy-start(f32[2,8,8,128]{3,2,1,0:T(8,128)S(1)} %copy.231) | copy-start | bytes 196612
  53.8 8.6 %copy-start.74 = (f32[2,8,8,128]{3,2,1,0:T(8,128)}, f32[2,8,8,128]{3,2,1,0:T(8,128)S(1)}, u32[]{:S(2)}) copy-start(f32[2,8,8,128]{3,2,1,0:T(8,128)S(1)} %copy.228) | copy-start | bytes 196612
  59.1 13.0 %copy-start.102 = (f32[1024]{0:T(1024)}, f32[1024]{0:T(1024)S(1)}, u32[]{:S(2)}) copy-start(f32[1024]{0:T(1024)S(1)} %get-tuple-element.347) | copy-start | bytes 12292
  63.3 20.4 %copy-start.3 = (bf16[128,1024]{1,0:T(8,128)(2,1)}, bf16[128,1024]{1,0:T(8,128)(2,1)S(1)}, u32[]{:S(2)}) copy-start(bf16[128,1024]{1,0:T(8,128)(2,1)S(1)} %get-tuple-element.271.outt_ref) | copy-start | bytes 786436
  63.5 20.2 %copy-start.1 = (bf16[1024,128]{1,0:T(8,128)(2,1)}, bf16[1024,128]{1,0:T(8,128)(2,1)S(1)}, u32[]{:S(2)}) copy-start(bf16[1024,128]{1,0:T(8,128)(2,1)S(1)} %copy.166.into_ref) | copy-start | bytes 786436
  64.4 6.1 %copy-start.67 = (bf16[1024,256]{0,1:T(8,128)(2,1)S(1)}, bf16[1024,256]{0,1:T(8,128)(2,1)}, u32[]{:S(2)}) copy-start(bf16[1024,256]{0,1:T(8,128)(2,1)} %get-tuple-element.244) | copy-start | bytes 1572868
  83.7 17.5 %copy-start.91 = (f32[16,8,128]{2,1,0:T(8,128)S(1)}, f32[16,8,128]{2,1,0:T(8,128)}, u32[]{:S(2)}) copy-start(f32[16,8,128]{2,1,0:T(8,128)} %get-tuple-element.299) | copy-start | bytes 196612
  99.2 28.4 %collective-permute-start = (f32[2,1024]{1,0:T(2,128)}, f32[2,1024]{1,0:T(2,128)}, u32[]{:S(2)}, u32[]{:S(2)}) collective-permute-start(f32[2,1024]{1,0:T(2,128)} %slice_bitcast_fusion.3), channel_id=1, source_target_pairs={{0,1},{1,0},{2,3},{3,2},{4,5},{5,4},{6,7},{7,6},{8,9},{9,8},{10,11... | collective-permute-start | bytes 24584 | tf_op jit(solution)/shard_map/ppermute | solution.py:533
  108.4 65.7 %collective-permute-start.2 = (f32[256,1024]{1,0:T(8,128)}, f32[256,1024]{1,0:T(8,128)}, u32[]{:S(2)}, u32[]{:S(2)}) collective-permute-start(f32[256,1024]{1,0:T(8,128)} %collective-permute-done.1.first_ref), channel_id=1, source_target_pairs={{0,4},{2,6},{4,0},{6,2},{8,12},{10,14},{12,8},{14,10},{16,20},{18,... | collective-permute-start | bytes 3145736 | tf_op jit(solution)/shard_map/ppermute | solution.py:567
  110.0 64.2 %collective-permute-start.4 = (f32[256,1024]{1,0:T(8,128)}, f32[256,1024]{1,0:T(8,128)}, u32[]{:S(2)}, u32[]{:S(2)}) collective-permute-start(f32[256,1024]{1,0:T(8,128)} %collective-permute-done.3.first_ref), channel_id=1, source_target_pairs={{0,4},{2,6},{4,0},{6,2},{8,12},{10,14},{12,8},{14,10},{16,20},{18,... | collective-permute-start | bytes 3145736 | tf_op jit(solution)/shard_map/ppermute | solution.py:567
  128.3 9.6 %copy-start.97 = (bf16[1024,1024]{1,0:T(8,128)(2,1)S(1)}, bf16[1024,1024]{1,0:T(8,128)(2,1)}, u32[]{:S(2)}) copy-start(bf16[1024,1024]{1,0:T(8,128)(2,1)} %param.32) | copy-start | bytes 6291460
  142.3 99.5 %collective-permute-start.8 = (f32[1024,1024]{1,0:T(8,128)}, f32[1024,1024]{1,0:T(8,128)}, u32[]{:S(2)}, u32[]{:S(2)}) collective-permute-start(f32[1024,1024]{1,0:T(8,128)} %fusion.145.branch_ref), channel_id=1, source_target_pairs={{0,1},{1,0},{2,3},{3,2},{4,5},{5,4},{6,7},{7,6},{8,9},{9,8},{10,11... | collective-permute-start | bytes 12582920 | tf_op jit(solution)/shard_map/ppermute | solution.py:533
  142.4 33.7 %copy-start.103 = (f32[1024]{0:T(1024)S(1)}, f32[1024]{0:T(1024)}, u32[]{:S(2)}) copy-start(f32[1024]{0:T(1024)} %copy-done.102) | copy-start | bytes 12292
  174.1 39.9 %collective-permute-start.9 = (f32[256,1024]{1,0:T(8,128)}, f32[256,1024]{1,0:T(8,128)}, u32[]{:S(2)}, u32[]{:S(2)}) collective-permute-start(f32[256,1024]{1,0:T(8,128)} %collective-permute-done.1.first_ref), channel_id=1, source_target_pairs={{0,2},{2,0},{4,6},{6,4},{8,10},{10,8},{12,14},{14,12},{16,18},{18,... | collective-permute-start | bytes 3145736 | tf_op jit(solution)/shard_map/ppermute | solution.py:567
  174.2 40.4 %collective-permute-start.10 = (f32[256,1024]{1,0:T(8,128)}, f32[256,1024]{1,0:T(8,128)}, u32[]{:S(2)}, u32[]{:S(2)}) collective-permute-start(f32[256,1024]{1,0:T(8,128)} %collective-permute-done.2.second_ref), channel_id=1, source_target_pairs={{0,2},{2,0},{4,6},{6,4},{8,10},{10,8},{12,14},{14,12},{16,18},{18,... | collective-permute-start | bytes 3145736 | tf_op jit(solution)/shard_map/ppermute | solution.py:567
  181.8 9.3 %copy-start.79 = (bf16[1024,16]{0,1:T(8,128)(2,1)S(1)}, bf16[1024,16]{0,1:T(8,128)(2,1)}, u32[]{:S(2)}) copy-start(bf16[1024,16]{0,1:T(8,128)(2,1)} %param.23) | copy-start | bytes 98308
  186.0 25.6 %collective-permute-start.6 = (f32[256,1024]{1,0:T(8,128)}, f32[256,1024]{1,0:T(8,128)S(1)}, u32[]{:S(2)}, u32[]{:S(2)}) collective-permute-start(f32[256,1024]{1,0:T(8,128)} %collective-permute-done.5.first_ref), channel_id=1, source_target_pairs={{0,4},{2,6},{4,0},{6,2},{8,12},{10,14},{12,8},{14,10},{16,20},{18,... | collective-permute-start | bytes 3145736 | tf_op jit(solution)/shard_map/ppermute | solution.py:567
  191.2 28.3 %collective-permute-start.11 = (f32[256,1024]{1,0:T(8,128)}, f32[256,1024]{1,0:T(8,128)S(1)}, u32[]{:S(2)}, u32[]{:S(2)}) collective-permute-start(f32[256,1024]{1,0:T(8,128)} %collective-permute-done.3.first_ref), channel_id=1, source_target_pairs={{0,2},{2,0},{4,6},{6,4},{8,10},{10,8},{12,14},{14,12},{16,18},{18,... | collective-permute-start | bytes 3145736 | tf_op jit(solution)/shard_map/ppermute | solution.py:567
  195.5 16.1 %copy-start.99 = (bf16[1024,1024]{1,0:T(8,128)(2,1)S(1)}, bf16[1024,1024]{1,0:T(8,128)(2,1)}, u32[]{:S(2)}) copy-start(bf16[1024,1024]{1,0:T(8,128)(2,1)} %param.21) | copy-start | bytes 6291460
  195.5 16.1 %copy-start.155 = (bf16[1024,1024]{1,0:T(8,128)(2,1)S(1)}, bf16[1024,1024]{1,0:T(8,128)(2,1)}, u32[]{:S(2)}) copy-start(bf16[1024,1024]{1,0:T(8,128)(2,1)} %get-tuple-element.102) | copy-start | bytes 6291460
  196.3 18.3 %copy-start.55 = (bf16[1024,1024]{1,0:T(8,128)(2,1)S(1)}, bf16[1024,1024]{1,0:T(8,128)(2,1)}, u32[]{:S(2)}) copy-start(bf16[1024,1024]{1,0:T(8,128)(2,1)} %param.20) | copy-start | bytes 6291460
  196.3 18.3 %copy-start.62 = (bf16[1024,1024]{1,0:T(8,128)(2,1)S(1)}, bf16[1024,1024]{1,0:T(8,128)(2,1)}, u32[]{:S(2)}) copy-start(bf16[1024,1024]{1,0:T(8,128)(2,1)} %get-tuple-element.91) | copy-start | bytes 6291460
  211.6 7.9 %collective-permute-start.12 = (f32[256,1024]{1,0:T(8,128)}, f32[256,1024]{1,0:T(8,128)S(1)}, u32[]{:S(2)}, u32[]{:S(2)}) collective-permute-start(f32[256,1024]{1,0:T(8,128)} %collective-permute-done.4.second_ref), channel_id=1, source_target_pairs={{0,2},{2,0},{4,6},{6,4},{8,10},{10,8},{12,14},{14,12},{16,18},{18,... | collective-permute-start | bytes 3145736 | tf_op jit(solution)/shard_map/ppermute | solution.py:567
  214.0 18.6 %collective-permute-start.13 = (f32[256,1024]{1,0:T(8,128)}, f32[256,1024]{1,0:T(8,128)S(1)}, u32[]{:S(2)}, u32[]{:S(2)}) collective-permute-start(f32[256,1024]{1,0:T(8,128)} %collective-permute-done.5.first_ref), channel_id=1, source_target_pairs={{0,2},{2,0},{4,6},{6,4},{8,10},{10,8},{12,14},{14,12},{16,18},{18,... | collective-permute-start | bytes 3145736 | tf_op jit(solution)/shard_map/ppermute | solution.py:567
  214.6 18.1 %collective-permute-start.14 = (f32[256,1024]{1,0:T(8,128)S(1)}, f32[256,1024]{1,0:T(8,128)}, u32[]{:S(2)}, u32[]{:S(2)}) collective-permute-start(f32[256,1024]{1,0:T(8,128)S(1)} %collective-permute-done.6.second_ref), channel_id=1, source_target_pairs={{0,2},{2,0},{4,6},{6,4},{8,10},{10,8},{12,14},{14,12},{16,18},{18,... | collective-permute-start | bytes 3145736 | tf_op jit(solution)/shard_map/ppermute | solution.py:567
  262.5 10.0 %copy-start.41 = (bf16[1024,1024]{1,0:T(8,128)(2,1)S(1)}, bf16[1024,1024]{1,0:T(8,128)(2,1)}, u32[]{:S(2)}) copy-start(bf16[1024,1024]{1,0:T(8,128)(2,1)} %copy-done.39) | copy-start | bytes 6291460
  272.5 7.8 %copy-start.14 = (f32[1024,128]{1,0:T(8,128)}, f32[1024,128]{1,0:T(8,128)S(1)}, u32[]{:S(2)}) copy-start(f32[1024,128]{1,0:T(8,128)S(1)} %get-tuple-element.155) | copy-start | bytes 1572868
  272.5 7.8 %copy-start.26 = (bf16[1024,1024]{1,0:T(8,128)(2,1)}, bf16[1024,1024]{1,0:T(8,128)(2,1)S(1)}, u32[]{:S(2)}) copy-start(bf16[1024,1024]{1,0:T(8,128)(2,1)S(1)} %get-tuple-element.128) | copy-start | bytes 6291460
  272.5 7.8 %copy-start.25 = (bf16[1024,1024]{1,0:T(8,128)(2,1)S(1)}, bf16[1024,1024]{1,0:T(8,128)(2,1)}, u32[]{:S(2)}) copy-start(bf16[1024,1024]{1,0:T(8,128)(2,1)} %copy-done.24) | copy-start | bytes 6291460
  272.5 7.8 %copy-start.44 = (bf16[2,1024,1024]{2,1,0:T(8,128)(2,1)S(1)}, bf16[2,1024,1024]{2,1,0:T(8,128)(2,1)}, u32[]{:S(2)}) copy-start(bf16[2,1024,1024]{2,1,0:T(8,128)(2,1)} %cotangent_ref.3) | copy-start | bytes 12582916
  289.5 200.4 %reduce-scatter.7.cloned.1.call-start = ((), (), s32[]{:S(2)}) async-start(), calls=%async_computation.3 | async-start | bytes 6127616
  293.0 109.1 %collective-permute-start.7 = (f32[1024,1024]{1,0:T(8,128)}, f32[1024,1024]{1,0:T(8,128)}, u32[]{:S(2)}, u32[]{:S(2)}) collective-permute-start(f32[1024,1024]{1,0:T(8,128)} %add_add_fusion.2.part_ref), channel_id=1, source_target_pairs={{0,1},{1,0},{2,3},{3,2},{4,5},{5,4},{6,7},{7,6},{8,9},{9,8},{10,11... | collective-permute-start | bytes 12582920 | tf_op jit(solution)/shard_map/ppermute | solution.py:533
  301.7 31.7 %copy-start.73 = (f32[2,8,8,128]{3,2,1,0:T(8,128)S(1)}, f32[2,8,8,128]{3,2,1,0:T(8,128)}, u32[]{:S(2)}) copy-start(f32[2,8,8,128]{3,2,1,0:T(8,128)} %copy-done.72) | copy-start | bytes 196612
  301.7 31.7 %copy-start.76 = (f32[2,8,8,128]{3,2,1,0:T(8,128)S(1)}, f32[2,8,8,128]{3,2,1,0:T(8,128)}, u32[]{:S(2)}) copy-start(f32[2,8,8,128]{3,2,1,0:T(8,128)} %copy-done.74) | copy-start | bytes 196612
  301.7 31.7 %copy-start.136 = (f32[16]{0:T(128)S(1)}, f32[16]{0:T(128)}, u32[]{:S(2)}) copy-start(f32[16]{0:T(128)} %copy-done.135) | copy-start | bytes 196
  335.2 13.5 %copy-start.83 = (f32[16,1024]{1,0:T(8,128)S(1)}, f32[16,1024]{1,0:T(8,128)}, u32[]{:S(2)}) copy-start(f32[16,1024]{1,0:T(8,128)} %copy-done.82) | copy-start | bytes 196612
  335.2 13.6 %copy-start.94 = (bf16[16,1024]{1,0:T(8,128)(2,1)S(1)}, bf16[16,1024]{1,0:T(8,128)(2,1)}, u32[]{:S(2)}) copy-start(bf16[16,1024]{1,0:T(8,128)(2,1)} %copy-done.93) | copy-start | bytes 98308
  367.4 30.3 %copy-start.56 = (bf16[1024,1024]{1,0:T(8,128)(2,1)S(1)}, bf16[1024,1024]{1,0:T(8,128)(2,1)}, u32[]{:S(2)}) copy-start(bf16[1024,1024]{1,0:T(8,128)(2,1)} %param.20) | copy-start | bytes 6291460
  367.4 30.3 %copy-start.158 = (bf16[1024,1024]{1,0:T(8,128)(2,1)S(1)}, bf16[1024,1024]{1,0:T(8,128)(2,1)}, u32[]{:S(2)}) copy-start(bf16[1024,1024]{1,0:T(8,128)(2,1)} %get-tuple-element.126) | copy-start | bytes 6291460
  414.7 6.3 %copy-start.35 = (f32[1024,1024]{1,0:T(8,128)}, f32[1024,1024]{1,0:T(8,128)S(1)}, u32[]{:S(2)}) copy-start(f32[1024,1024]{1,0:T(8,128)S(1)} %add_add_fusion.1.part_ref) | copy-start | bytes 12582916
  421.1 3.8 collective-permute-start.16
  424.9 7.1 %collective-permute-start.17 = (f32[8496]{0:T(1024)S(1)}, f32[8496]{0:T(1024)S(1)}, u32[]{:S(2)}, u32[]{:S(2)}) collective-permute-start(f32[8496]{0:T(1024)S(1)} %concatenate.173), channel_id=1, source_target_pairs={{0,2},{2,0},{4,6},{6,4},{8,10},{10,8},{12,14},{14,12},{16,18},{18,... | collective-permute-start | bytes 101960 | tf_op jit(solution)/shard_map/ppermute | solution.py:567
  425.0 8.2 %copy-start.20 = (f32[8,8,16,128]{3,2,1,0:T(8,128)S(1)}, f32[8,8,16,128]{3,2,1,0:T(8,128)}, u32[]{:S(2)}) copy-start(f32[8,8,16,128]{3,2,1,0:T(8,128)} %copy-done.19) | copy-start | bytes 1572868
  425.0 8.5 %copy-start.11 = (f32[1024,256]{1,0:T(8,128)S(1)}, f32[1024,256]{1,0:T(8,128)}, u32[]{:S(2)}) copy-start(f32[1024,256]{1,0:T(8,128)} %copy-done.10) | copy-start | bytes 3145732
  432.1 5.5 %collective-permute-start.18 = (f32[8496]{0:T(1024)S(1)}, f32[8496]{0:T(1024)S(1)}, u32[]{:S(2)}, u32[]{:S(2)}) collective-permute-start(f32[8496]{0:T(1024)S(1)} %add.394), channel_id=1, source_target_pairs={{0,4},{2,6},{4,0},{6,2},{8,12},{10,14},{12,8},{14,10},{16,20},{18,... | collective-permute-start | bytes 101960 | tf_op jit(solution)/shard_map/ppermute | solution.py:567
  437.7 9.3 %collective-permute-start.19 = (f32[8496]{0:T(1024)S(1)}, f32[8496]{0:T(1024)S(1)}, u32[]{:S(2)}, u32[]{:S(2)}) collective-permute-start(f32[8496]{0:T(1024)S(1)} %add.395), channel_id=1, source_target_pairs={{0,8},{2,10},{4,12},{6,14},{8,0},{10,2},{12,4},{14,6},{16,24},{18,... | collective-permute-start | bytes 101960 | tf_op jit(solution)/shard_map/ppermute | solution.py:567
  442.0 7.3 %copy-start.86 = (f32[2,64,1024]{2,1,0:T(8,128)S(1)}, f32[2,64,1024]{2,1,0:T(8,128)}, u32[]{:S(2)}) copy-start(f32[2,64,1024]{2,1,0:T(8,128)} %reduce-scatter.5.cloned.1.call-done) | copy-start | bytes 1572868
  442.1 8.1 %copy-start.22 = (f32[1024]{0:T(1024)S(1)}, f32[1024]{0:T(1024)}, u32[]{:S(2)}) copy-start(f32[1024]{0:T(1024)} %param.19) | copy-start | bytes 12292
  446.9 13.7 %collective-permute-start.20 = (f32[8496]{0:T(1024)S(1)}, f32[8496]{0:T(1024)S(1)}, u32[]{:S(2)}, u32[]{:S(2)}) collective-permute-start(f32[8496]{0:T(1024)S(1)} %add.396), channel_id=1, source_target_pairs={{0,16},{2,18},{4,20},{6,22},{8,24},{10,26},{12,28},{14,30},{16,0},... | collective-permute-start | bytes 101960 | tf_op jit(solution)/shard_map/ppermute | solution.py:567
  491.2 5.5 %collective-permute-start.21 = (f32[64,256]{0,1:T(8,128)S(1)}, f32[64,256]{0,1:T(8,128)S(1)}, u32[]{:S(2)}, u32[]{:S(2)}) collective-permute-start(f32[64,256]{0,1:T(8,128)S(1)} %slice.356), channel_id=1, source_target_pairs={{0,1},{1,0},{2,3},{3,2},{4,5},{5,4},{6,7},{7,6},{8,9},{9,8},{10,11... | collective-permute-start | bytes 196616 | tf_op jit(solution)/shard_map/ppermute | solution.py:533
  (121 other events, 291.8 us)
Sparse Core Ops, SparseCore 0:
  289.6 106.3 reduce-scatter.4
  408.3 81.5 reduce-scatter.6

commit v7 on v6

--- a/solution.py
+++ b/solution.py
@@ -555,9 +555,9 @@
         whole_ref[part, :] = piece_ref[...].astype(whole_ref.dtype)
 
 
-def gather_first(weight):
+def gather_first(weight, flip=0):
     rows, columns = weight.shape[0] // 4, weight.shape[1]
-    quarter = lax.rem(lax.axis_index("dp"), 4)
+    quarter = jnp.bitwise_xor(lax.rem(lax.axis_index("dp"), 4), flip)
     mine = lax.dynamic_slice(weight, (quarter * rows, 0), (rows, columns))
     mine = lax.optimization_barrier(mine.astype(jnp.float32))
     return lax.ppermute(mine, "tensor", [(0, 1), (1, 0)])
@@ -703,6 +703,7 @@
         sent = dict(value=proj_value, gate=proj_gate, out=proj_out)
         first = {k: gather_first(w) for k, w in sent.items()}
         second = {k: along_dp(first[k], 2) for k in ("value", "gate")}
+        second["out"] = gather_first(proj_out, 2)
         other["conv"] = wide_lanes(jnp.concatenate([c_w, c_b[None, :]], axis=0))
         other["gain_wide"] = wide_lanes(g_g)
 
@@ -744,16 +745,14 @@
 
     def own_backward(s, earlier, last_hops=False):
         d_mixed = after(d_mixeds[s], *earlier)
-        between = tuple(second.values()) if last_hops else ()
+        between = (second["value"], second["gate"]) if last_hops else ()
         d_value, *rest = unit_backward(
             units[s], own, d_gates[s], d_mixed, state_backs[s], between
         )
         if last_hops:
-            second["out"] = along_dp(after(first["out"], d_value), 2)
             for k in sent:
                 third[k] = along_dp(after(first[k], d_value), 1)
                 fourth[k] = along_dp(after(second[k], units[-1]["mixed"]), 1)
-            d_value = after(d_value, second["out"])
         backs.append((d_value, *rest))
         parts.append(lax.optimization_barrier(normed_part(own, d_gates[s], *backs[s][:3])))
 

time: 510 us -> 495 us (0.971)
  waiting for transfers between devices: 34.9 us -> 26.1 us
    ppermute x13 -> x12, waiting for transfers between devices: 15.3 us -> 3.48 us  [along_dp(): lax.ppermute(piece, 'dp', [(j, j ^ flip) for j in range(lax.axis_size('dp...]
    unnamed x351 -> x339, local copies, waits for them, and re-layouts: 37.6 us -> 35.3 us
    ppermute x13 -> x12, starting transfers between devices: 10.3 us -> 9.34 us  [along_dp(): lax.ppermute(piece, 'dp', [(j, j ^ flip) for j in range(lax.axis_size('dp...]
  transfers between devices with their start and end apart: 24 -> 24, of which waited for: 3 -> 4; matrix products, arithmetic and copies ran while one was open for 36% -> 36% of each run, Pallas kernels for 33% -> 34%
where the time goes in v7:
time: 495 us; the launch traced here: 490 us
  Pallas kernels  192 us (39%)
  matrix products  118 us (24%)
  local copies, waits for them, and re-layouts  64.6 us (13%)
  other arithmetic  50.9 us (10%)
  waiting for transfers between devices  26.1 us (5%)
  starting transfers between devices  21.9 us (4%)
  between operations  16.7 us (3%)
    pallas_call x3, Pallas kernels, mix_backward(): pl.pallas_call(back_kernel, grid=(seqs, chunks), in_specs=[slab, spec((ch...  90.7 us
    dot_general x12, matrix products, out_product(): lax.dot_general(left, weight, (((0,), (1,)), ((), ())), preferred_element...  43.8 us
    dot_general x12, matrix products, in_product(): lax.dot_general(weight, tokens, (((0,), (1,)), ((), ())), preferred_eleme...  41.8 us
    pallas_call x3, Pallas kernels, mix_forward(): pl.pallas_call(mix_kernel, grid=(seqs, chunks), in_specs=[slab, slab, sla...  40.6 us
    unnamed x339, local copies, waits for them, and re-layouts  35.3 us
    pallas_call x3, Pallas kernels, middle(): pl.pallas_call(functools.partial(middle_kernel, 1.0 / inner_total), grid=...  29.5 us
    pallas_call x2, Pallas kernels, finish(): pl.pallas_call(finish_kernel, grid=(length // tile,), in_specs=[flat] * 4...  21 us
    dot_general x4, matrix products, grad_product(): lax.dot_general(tokens, channels, (((0,), (1,)), ((), ())), preferred_ele...  19.2 us
  transfers between devices with their start and end apart: 24, of which 4 were waited for; matrix products, arithmetic and copies ran while one was open for 36% of the time, Pallas kernels for 34%

profile of v7, /device:TPU:0, one launch (start us, length us, event | category | flops | bytes accessed | tf_op | source)
XLA Modules:
  0.0 490.4 jit_solution(8038679539223803717)
XLA Ops:
  10.7 3.0 collective-permute-start.15
  13.7 2.1 dynamic-slice_convert_fusion.3
  15.8 2.1 dynamic-slice_convert_fusion.2
  17.9 2.0 collective-permute-start.3
  21.5 2.0 collective-permute-start.12
  23.6 3.1 fusion.3
  28.3 3.7 convert_bitcast_fusion.4.gate_ref
  34.8 2.5 fusion.149
  37.3 1.8 fusion.144
  39.8 3.7 convert_bitcast_fusion.2.gate_ref
  43.4 3.7 fusion.45.dout_ref
  47.1 3.7 fusion.48.dout_ref
  50.9 4.2 convert_bitcast_fusion.3.raw_ref.before_ref
  57.7 5.6 %multiply_convert_fusion = (bf16[1024,256]{0,1:T(8,128)(2,1)}, f32[1024,256]{0,1:T(8,128)}, bf16[1024,256]{0,1:T(8,128)(2,1)S(1)}, f32[1024,256]{0,1:T(8,128)}) fusion(f32[1024]{0:T(1024)S(1)} %get-tuple-element.321, f32[1021,256]{0,1:T(8,128)S(1)} %bitcast.342, f32[256]{0:T(256)S(1)} %bitcast.412, f32[1024]{0:T(1024)S(1)} %get-tuple-element.322, ...), kind=kLoop, calls=%fused_computation.114 | loop fusion | flops 8388608 | bytes 11551744 | tf_op jit(solution)/shard_map/convert_element_type | solution.py:723
  65.9 6.0 %convert_bitcast_fusion.1.raw_ref.before_ref = bf16[1024,1024]{1,0:T(8,128)(2,1)} fusion(bf16[1024,1024]{1,0:T(8,128)(2,1)} %copy-done.35, bf16[1024,1024]{1,0:T(8,128)(2,1)} %param.21), kind=kOutput, calls=%fused_computation.51 | convolution fusion | flops 2148532224 | bytes 6291456 | tf_op jit(solution)/shard_map/dot_general | solution.py:509
  75.6 2.4 fusion.61
  81.0 2.0 broadcast_in_dim.15.conv_ref
  85.1 13.5 %mix_forward.3 = (f32[1024,1024]{1,0:T(8,128)}, bf16[8,1024,128]{2,1,0:T(8,128)(2,1)S(1)}, f32[8,8,128]{2,1,0:T(8,128)S(1)}) custom-call(bf16[1024,1024]{1,0:T(8,128)(2,1)} %convert_bitcast_fusion.3.raw_ref.before_ref, bf16[1024,1024]{1,0:T(8,128)(2,1)} %convert_bitcast_fusion.4.gate_ref, bf16[1024,1024]{1,0:T(8,128)(2,1)} %fusion.45.dout_ref, ...), custom_call_target="tpu_custom_call" | custom-call | flops 1024 | bytes 1024 | tf_op jit(solution)/shard_map/mix_forward/pallas_call | solution.py:252
  105.1 13.5 %mix_forward.4 = (f32[1024,1024]{1,0:T(8,128)}, bf16[8,1024,128]{2,1,0:T(8,128)(2,1)S(1)}, f32[8,8,128]{2,1,0:T(8,128)S(1)}) custom-call(bf16[1024,1024]{1,0:T(8,128)(2,1)} %convert_bitcast_fusion.1.raw_ref.before_ref, bf16[1024,1024]{1,0:T(8,128)(2,1)} %convert_bitcast_fusion.2.gate_ref, bf16[1024,1024]{1,0:T(8,128)(2,1)} %fusion.48.dout_ref, ...), custom_call_target="tpu_custom_call" | custom-call | flops 1024 | bytes 1024 | tf_op jit(solution)/shard_map/mix_forward/pallas_call | solution.py:252
  120.8 9.6 %gated_middle.3 = (bf16[1024,1024]{1,0:T(8,128)(2,1)S(1)}, bf16[1024,1024]{1,0:T(8,128)(2,1)}, bf16[1024,1024]{1,0:T(8,128)(2,1)}, f32[1024,128]{1,0:T(8,128)S(1)}) custom-call(bf16[1024,1024]{1,0:T(8,128)(2,1)} %convert_bitcast_fusion.4.gate_ref, f32[1024,1024]{1,0:T(8,128)} %get-tuple-element.88.mixed_ref, bf16[1024,1024]{1,0:T(8,128)(2,1)} %fusion.45.dout_ref, ...), custom_call_target="tpu_custom_call" | custom-call | flops 1024 | bytes 1024 | tf_op jit(solution)/shard_map/gated_middle/pallas_call | solution.py:491
  130.4 2.0 collective-permute-start.2
  132.5 4.3 fusion.146.branch_ref
  138.6 30.1 %mix_backward.3 = (bf16[1024,1024]{1,0:T(8,128)(2,1)}, f32[8,8,16,128]{3,2,1,0:T(8,128)S(1)}, f32[1024,256]{1,0:T(8,128)S(1)}, f32[5,1024,128]{2,1,0:T(8,128)}) custom-call(bf16[1024,1024]{1,0:T(8,128)(2,1)} %convert_bitcast_fusion.3.raw_ref.before_ref, bf16[1024,1024]{1,0:T(8,128)(2,1)} %convert_bitcast_fusion.3.raw_ref.before_ref, ...), custom_call_target="tpu_custom_call" | custom-call | flops 1024 | bytes 1024 | tf_op jit(solution)/shard_map/mix_backward/pallas_call | solution.py:294
  168.8 4.4 fusion.145
  173.3 3.5 collective-permute-done.4.second_ref
  178.7 3.8 multiply_reduce_fusion.7
  182.5 2.3 multiply_reduce_fusion.6
  187.7 1.8 copy_add_fusion.1
  189.5 1.7 slice_multiply_fusion.7
  198.0 4.8 add_add_fusion.2.part_ref
  203.8 3.7 assemble.3
  207.5 3.4 assemble.4
  210.9 3.5 assemble.5
  214.4 5.7 %convolution_convert_fusion.gate_ref = bf16[1024,1024]{1,0:T(8,128)(2,1)} fusion(bf16[1024,1024]{1,0:T(8,128)(2,1)} %assemble.4, bf16[1024,1024]{1,0:T(8,128)(2,1)S(1)} %copy-done.37), kind=kOutput, calls=%fused_computation.59 | convolution fusion | flops 2148532224 | bytes 6291456 | tf_op jit(solution)/shard_map/dot_general | solution.py:509
  220.1 3.7 fusion.51.dout_ref
  223.8 3.7 collective-permute-done.6.received_ref
  227.5 3.7 convolution_convert_fusion.1.raw_ref.before_ref
  231.2 1.9 broadcast_in_dim.19.conv_ref
  233.3 13.5 %mix_forward.5 = (f32[1024,1024]{1,0:T(8,128)}, bf16[8,1024,128]{2,1,0:T(8,128)(2,1)S(1)}, f32[8,8,128]{2,1,0:T(8,128)S(1)}) custom-call(bf16[1024,1024]{1,0:T(8,128)(2,1)} %convolution_convert_fusion.1.raw_ref.before_ref, bf16[1024,1024]{1,0:T(8,128)(2,1)} %convolution_convert_fusion.gate_ref, bf16[1024,1024]{1,0:T(8,128)(2,1)} %fusion.51.dout_ref, ...), custom_call_target="tpu_custom_call" | custom-call | flops 1024 | bytes 1024 | tf_op jit(solution)/shard_map/mix_forward/pallas_call | solution.py:252
  248.2 10.0 %gated_middle.4 = (bf16[1024,1024]{1,0:T(8,128)(2,1)S(1)}, bf16[1024,1024]{1,0:T(8,128)(2,1)}, bf16[1024,1024]{1,0:T(8,128)(2,1)}, f32[1024,128]{1,0:T(8,128)S(1)}) custom-call(bf16[1024,1024]{1,0:T(8,128)(2,1)} %convert_bitcast_fusion.2.gate_ref, f32[1024,1024]{1,0:T(8,128)} %get-tuple-element.102.mixed_ref, bf16[1024,1024]{1,0:T(8,128)(2,1)} %fusion.48.dout_ref, ...), custom_call_target="tpu_custom_call" | custom-call | flops 1024 | bytes 1024 | tf_op jit(solution)/shard_map/gated_middle/pallas_call | solution.py:491
  258.3 7.1 %fusion.30 = f32[1,1024,1024]{2,1,0:T(8,128)S(1)} fusion(bf16[1024,1024]{1,0:T(8,128)(2,1)} %get-tuple-element.124, bf16[1024,1024]{1,0:T(8,128)(2,1)S(1)} %copy-done.150, bf16[1024,1024]{1,0:T(8,128)(2,1)S(1)} %copy-done.37, bf16[1024,1024]{1,0:T(8,128)(2,1)S(1)} %copy-done.41), kind=kOutput, calls=%fused_computation.40 | convolution fusion | flops 4311744512 | bytes 12582912 | tf_op jit(solution)/shard_map/dot_general | solution.py:513
  265.4 4.6 fusion.27
  270.0 4.6 pad_maximum_fusion
  279.6 6.9 %fusion.151.branch_ref = f32[1024,1024]{1,0:T(8,128)} fusion(bf16[1024,1024]{1,0:T(8,128)(2,1)} %copy-done.26, bf16[1024,1024]{1,0:T(8,128)(2,1)} %param.32), kind=kOutput, calls=%fused_computation.298 | convolution fusion | flops 2147483648 | bytes 8388608 | tf_op jit(solution)/shard_map/dot_general | solution.py:505
  286.5 30.5 %mix_backward.4 = (bf16[1024,1024]{1,0:T(8,128)(2,1)}, f32[8,8,16,128]{3,2,1,0:T(8,128)S(1)}, f32[1024,256]{1,0:T(8,128)S(1)}, f32[5,1024,128]{2,1,0:T(8,128)}) custom-call(bf16[1024,1024]{1,0:T(8,128)(2,1)} %convert_bitcast_fusion.1.raw_ref.before_ref, bf16[1024,1024]{1,0:T(8,128)(2,1)} %convert_bitcast_fusion.1.raw_ref.before_ref, ...), custom_call_target="tpu_custom_call" | custom-call | flops 1024 | bytes 1024 | tf_op jit(solution)/shard_map/mix_backward/pallas_call | solution.py:294
  318.3 2.3 fusion.84
  320.6 9.9 %gated_middle.5 = (bf16[1024,1024]{1,0:T(8,128)(2,1)S(1)}, bf16[1024,1024]{1,0:T(8,128)(2,1)}, bf16[1024,1024]{1,0:T(8,128)(2,1)}, f32[1024,128]{1,0:T(8,128)}) custom-call(bf16[1024,1024]{1,0:T(8,128)(2,1)} %convolution_convert_fusion.gate_ref, f32[1024,1024]{1,0:T(8,128)} %get-tuple-element.132.mixed_ref, bf16[1024,1024]{1,0:T(8,128)(2,1)} %fusion.51.dout_ref, ...), custom_call_target="tpu_custom_call" | custom-call | flops 1024 | bytes 1024 | tf_op jit(solution)/shard_map/gated_middle/pallas_call | solution.py:491
  331.9 2.3 copy.200
  334.4 3.0 fusion.87
  345.2 4.5 fusion.23
  349.8 2.9 pad_maximum_fusion.1
  352.7 30.1 %mix_backward.5 = (bf16[1024,1024]{1,0:T(8,128)(2,1)}, f32[8,8,16,128]{3,2,1,0:T(8,128)S(1)}, f32[1024,256]{1,0:T(8,128)S(1)}, f32[5,1024,128]{2,1,0:T(8,128)}) custom-call(bf16[1024,1024]{1,0:T(8,128)(2,1)} %convolution_convert_fusion.1.raw_ref.before_ref, bf16[1024,1024]{1,0:T(8,128)(2,1)} %convolution_convert_fusion.1.raw_ref.before_ref, ...), custom_call_target="tpu_custom_call" | custom-call | flops 1024 | bytes 1024 | tf_op jit(solution)/shard_map/mix_backward/pallas_call | solution.py:294
  382.9 4.4 fusion.150
  387.3 6.1 %copy.224 = f32[1024,1296]{1,0:T(8,128)} copy(f32[1024,1296]{0,1:T(8,128)} %pad_maximum_fusion.1) | data formatting | bytes 10616832
  396.7 2.4 fusion.152
  400.1 2.8 copy-done.28
  410.2 7.1 %fusion.155.received_ref = f32[1024,1024]{1,0:T(8,128)} fusion(bf16[1024,1024]{1,0:T(8,128)(2,1)} %copy-done.25, bf16[1024,1024]{1,0:T(8,128)(2,1)} %assemble.5), kind=kOutput, calls=%fused_computation.302 | convolution fusion | flops 2147483648 | bytes 8388608 | tf_op jit(solution)/shard_map/dot_general | solution.py:505
  423.3 1.8 collective-permute-start.19
  425.3 2.4 fusion.154
  427.8 4.8 add_add_fusion.other_ref
  432.6 2.7 collective-permute-start.20
  436.1 10.6 %finish.2 = (bf16[2,1024,1024]{2,1,0:T(8,128)(2,1)}, f32[2,1024,1024]{2,1,0:T(8,128)}) custom-call(f32[1024,1024]{1,0:T(8,128)} %copy-done.34, f32[1024,1024]{1,0:T(8,128)} %add_add_fusion.other_ref, f32[1024,1024]{1,0:T(8,128)} %fusion.151.branch_ref, f32[1024,1024]{1,0:T(8,128)} %fusion.155.received_ref, bf16[2,1024,1024]{2,1,0:T(8,128)(2,1)} %hidden_ref.3, ...), custom_call_target="tpu_custom_call" | custom-call | flops 1024 | bytes 1024 | tf_op jit(solution)/shard_map/finish/pallas_call | solution.py:437
  446.8 10.4 %finish.3 = (bf16[2,1024,1024]{2,1,0:T(8,128)(2,1)}, f32[2,1024,1024]{2,1,0:T(8,128)}) custom-call(f32[1024,1024]{1,0:T(8,128)} %add_add_fusion.2.part_ref, f32[1024,1024]{1,0:T(8,128)} %collective-permute-done.5.other_ref, f32[1024,1024]{1,0:T(8,128)} %fusion.146.branch_ref, ...), custom_call_target="tpu_custom_call", output_to_operand_aliasing={{0}: (7, {}), {1}: (8, {})} | custom-call | flops 1024 | bytes 1024 | tf_op jit(solution)/shard_map/finish/pallas_call | solution.py:437
  457.9 17.7 %reduce-scatter.7.cloned.1.call-done = f32[64,1296]{1,0:T(8,128)} async-done(((f32[1024,1296]{1,0:T(8,128)}), f32[64,1296]{1,0:T(8,128)}) %reduce-scatter.7.cloned.1.call-update) | async-done | bytes 331792
  (516 shorter events, 89.9 us)
Async XLA Ops:
  7.2 27.6 %copy-start = (bf16[1024,256]{1,0:T(8,128)(2,1)S(1)}, bf16[1024,256]{1,0:T(8,128)(2,1)}, u32[]{:S(2)}) copy-start(bf16[1024,256]{1,0:T(8,128)(2,1)} %param.22) | copy-start | bytes 1572868
  7.2 380.1 %reduce-scatter.5.cloned.1.call-start = ((), (), s32[]{:S(2)}) async-start(), calls=%async_computation.2 | async-start | bytes 8912896 | tf_op jit(solution)/shard_map/reduce_scatter | solution.py:788
  8.9 11.0 %copy-start.85 = (bf16[1024,1024]{1,0:T(8,128)(2,1)S(1)}, bf16[1024,1024]{1,0:T(8,128)(2,1)}, u32[]{:S(2)}) copy-start(bf16[1024,1024]{1,0:T(8,128)(2,1)} %param.32) | copy-start | bytes 6291460
  10.7 63.0 %collective-permute-start.15 = (f32[22576]{0:T(1024)}, f32[22576]{0:T(1024)}, u32[]{:S(2)}, u32[]{:S(2)}) collective-permute-start(f32[22576]{0:T(1024)} %concatenate.163), channel_id=1, source_target_pairs={{0,1},{1,0},{2,3},{3,2},{4,5},{5,4},{6,7},{7,6},{8,9},{9,8},{10,11... | collective-permute-start | bytes 270920 | tf_op jit(solution)/shard_map/ppermute | solution.py:602
  15.8 114.6 %collective-permute-start.1 = (f32[256,1024]{1,0:T(8,128)}, f32[256,1024]{1,0:T(8,128)}, u32[]{:S(2)}, u32[]{:S(2)}) collective-permute-start(f32[256,1024]{1,0:T(8,128)} %dynamic-slice_convert_fusion.3), channel_id=1, source_target_pairs={{0,1},{1,0},{2,3},{3,2},{4,5},{5,4},{6,7},{7,6},{8,9},{9,8},{10,11... | collective-permute-start | bytes 3145736 | tf_op jit(solution)/shard_map/ppermute | solution.py:563
  17.9 114.5 %collective-permute-start.3 = (f32[256,1024]{1,0:T(8,128)}, f32[256,1024]{1,0:T(8,128)}, u32[]{:S(2)}, u32[]{:S(2)}) collective-permute-start(f32[256,1024]{1,0:T(8,128)} %dynamic-slice_convert_fusion.2), channel_id=1, source_target_pairs={{0,1},{1,0},{2,3},{3,2},{4,5},{5,4},{6,7},{7,6},{8,9},{9,8},{10,11... | collective-permute-start | bytes 3145736 | tf_op jit(solution)/shard_map/ppermute | solution.py:563
  21.5 166.1 %collective-permute-start.11 = (f32[256,1024]{1,0:T(8,128)}, f32[256,1024]{1,0:T(8,128)}, u32[]{:S(2)}, u32[]{:S(2)}) collective-permute-start(f32[256,1024]{1,0:T(8,128)} %get-tuple-element.249), channel_id=1, source_target_pairs={{0,1},{1,0},{2,3},{3,2},{4,5},{5,4},{6,7},{7,6},{8,9},{9,8},{10,11... | collective-permute-start | bytes 3145736 | tf_op jit(solution)/shard_map/ppermute | solution.py:563
  21.5 151.6 %collective-permute-start.12 = (f32[256,1024]{1,0:T(8,128)}, f32[256,1024]{1,0:T(8,128)}, u32[]{:S(2)}, u32[]{:S(2)}) collective-permute-start(f32[256,1024]{1,0:T(8,128)} %get-tuple-element.248), channel_id=1, source_target_pairs={{0,1},{1,0},{2,3},{3,2},{4,5},{5,4},{6,7},{7,6},{8,9},{9,8},{10,11... | collective-permute-start | bytes 3145736 | tf_op jit(solution)/shard_map/ppermute | solution.py:563
  26.7 49.0 %copy-start.106 = (f32[1024]{0:T(1024)}, f32[1024]{0:T(1024)S(1)}, u32[]{:S(2)}) copy-start(f32[1024]{0:T(1024)S(1)} %add_rsqrt_fusion) | copy-start | bytes 12292
  32.1 23.1 %copy-start.132 = (f32[16]{0:T(128)}, f32[16]{0:T(128)S(1)}, u32[]{:S(2)}) copy-start(f32[16]{0:T(128)S(1)} %exponential_negate_fusion) | copy-start | bytes 196
  32.8 22.4 %copy-start.84 = (f32[16,1024]{1,0:T(8,128)}, f32[16,1024]{1,0:T(8,128)S(1)}, u32[]{:S(2)}) copy-start(f32[16,1024]{1,0:T(8,128)S(1)} %fusion.60) | copy-start | bytes 196612
  34.8 20.3 %copy-start.82 = (f32[16,1024]{1,0:T(8,128)}, f32[16,1024]{1,0:T(8,128)S(1)}, u32[]{:S(2)}) copy-start(f32[16,1024]{1,0:T(8,128)S(1)} %fusion.59) | copy-start | bytes 196612
  37.3 20.4 %copy-start.29 = (f32[1024,256]{0,1:T(8,128)}, f32[1024,256]{0,1:T(8,128)S(1)}, u32[]{:S(2)}) copy-start(f32[1024,256]{0,1:T(8,128)S(1)} %fusion.149) | copy-start | bytes 3145732
  50.9 6.6 %copy-start.142 = (f32[4,256]{1,0:T(4,128)S(1)}, f32[4,256]{1,0:T(4,128)}, u32[]{:S(2)}) copy-start(f32[4,256]{1,0:T(4,128)} %param.26) | copy-start | bytes 12292
  50.9 6.9 %copy-start.144 = (f32[256]{0:T(256)S(1)}, f32[256]{0:T(256)}, u32[]{:S(2)}) copy-start(f32[256]{0:T(256)} %param.27) | copy-start | bytes 3076
  55.1 24.7 %copy-start.75 = (f32[2,8,8,128]{3,2,1,0:T(8,128)}, f32[2,8,8,128]{3,2,1,0:T(8,128)S(1)}, u32[]{:S(2)}) copy-start(f32[2,8,8,128]{3,2,1,0:T(8,128)S(1)} %copy.231) | copy-start | bytes 196612
  55.2 17.7 %copy-start.77 = (f32[2,8,8,128]{3,2,1,0:T(8,128)}, f32[2,8,8,128]{3,2,1,0:T(8,128)S(1)}, u32[]{:S(2)}) copy-start(f32[2,8,8,128]{3,2,1,0:T(8,128)S(1)} %copy.228) | copy-start | bytes 196612
  57.7 15.8 %copy-start.101 = (f32[1024]{0:T(1024)}, f32[1024]{0:T(1024)S(1)}, u32[]{:S(2)}) copy-start(f32[1024]{0:T(1024)S(1)} %get-tuple-element.347) | copy-start | bytes 12292
  101.2 18.8 %collective-permute-start = (f32[2,1024]{1,0:T(2,128)}, f32[2,1024]{1,0:T(2,128)}, u32[]{:S(2)}, u32[]{:S(2)}) collective-permute-start(f32[2,1024]{1,0:T(2,128)} %slice_bitcast_fusion.3), channel_id=1, source_target_pairs={{0,1},{1,0},{2,3},{3,2},{4,5},{5,4},{6,7},{7,6},{8,9},{9,8},{10,11... | collective-permute-start | bytes 24584 | tf_op jit(solution)/shard_map/ppermute | solution.py:533
  120.8 11.8 %copy-start.87 = (bf16[1024,1024]{1,0:T(8,128)(2,1)S(1)}, bf16[1024,1024]{1,0:T(8,128)(2,1)}, u32[]{:S(2)}) copy-start(bf16[1024,1024]{1,0:T(8,128)(2,1)} %param.32) | copy-start | bytes 6291460
  130.4 6.5 %copy-start.16 = (f32[1024,128]{1,0:T(8,128)}, f32[1024,128]{1,0:T(8,128)S(1)}, u32[]{:S(2)}) copy-start(f32[1024,128]{1,0:T(8,128)S(1)} %get-tuple-element.152) | copy-start | bytes 1572868
  130.4 6.5 %copy-start.23 = (bf16[1024,1024]{1,0:T(8,128)(2,1)}, bf16[1024,1024]{1,0:T(8,128)(2,1)S(1)}, u32[]{:S(2)}) copy-start(bf16[1024,1024]{1,0:T(8,128)(2,1)S(1)} %get-tuple-element.92) | copy-start | bytes 6291460
  130.4 42.9 %collective-permute-start.2 = (f32[256,1024]{1,0:T(8,128)}, f32[256,1024]{1,0:T(8,128)}, u32[]{:S(2)}, u32[]{:S(2)}) collective-permute-start(f32[256,1024]{1,0:T(8,128)} %collective-permute-done.1.first_ref), channel_id=1, source_target_pairs={{0,4},{2,6},{4,0},{6,2},{8,12},{10,14},{12,8},{14,10},{16,20},{18,... | collective-permute-start | bytes 3145736 | tf_op jit(solution)/shard_map/ppermute | solution.py:567
  132.4 44.3 %collective-permute-start.4 = (f32[256,1024]{1,0:T(8,128)}, f32[256,1024]{1,0:T(8,128)}, u32[]{:S(2)}, u32[]{:S(2)}) collective-permute-start(f32[256,1024]{1,0:T(8,128)} %collective-permute-done.3.first_ref), channel_id=1, source_target_pairs={{0,4},{2,6},{4,0},{6,2},{8,12},{10,14},{12,8},{14,10},{16,20},{18,... | collective-permute-start | bytes 3145736 | tf_op jit(solution)/shard_map/ppermute | solution.py:567
  136.9 90.6 %collective-permute-start.6 = (f32[1024,1024]{1,0:T(8,128)}, f32[1024,1024]{1,0:T(8,128)}, u32[]{:S(2)}, u32[]{:S(2)}) collective-permute-start(f32[1024,1024]{1,0:T(8,128)} %fusion.146.branch_ref), channel_id=1, source_target_pairs={{0,1},{1,0},{2,3},{3,2},{4,5},{5,4},{6,7},{7,6},{8,9},{9,8},{10,11... | collective-permute-start | bytes 12582920 | tf_op jit(solution)/shard_map/ppermute | solution.py:533
  138.6 30.2 %copy-start.98 = (bf16[1024,1024]{1,0:T(8,128)(2,1)S(1)}, bf16[1024,1024]{1,0:T(8,128)(2,1)}, u32[]{:S(2)}) copy-start(bf16[1024,1024]{1,0:T(8,128)(2,1)} %param.20) | copy-start | bytes 6291460
  138.6 30.2 %copy-start.149 = (bf16[1024,1024]{1,0:T(8,128)(2,1)S(1)}, bf16[1024,1024]{1,0:T(8,128)(2,1)}, u32[]{:S(2)}) copy-start(bf16[1024,1024]{1,0:T(8,128)(2,1)} %get-tuple-element.90) | copy-start | bytes 6291460
  168.8 9.9 %copy-start.102 = (f32[1024]{0:T(1024)S(1)}, f32[1024]{0:T(1024)}, u32[]{:S(2)}) copy-start(f32[1024]{0:T(1024)} %copy-done.101) | copy-start | bytes 12292
  173.2 29.6 %collective-permute-start.14 = (f32[256,1024]{1,0:T(8,128)}, f32[256,1024]{1,0:T(8,128)}, u32[]{:S(2)}, u32[]{:S(2)}) collective-permute-start(f32[256,1024]{1,0:T(8,128)} %collective-permute-done.12.second_ref), channel_id=1, source_target_pairs={{0,2},{2,0},{4,6},{6,4},{8,10},{10,8},{12,14},{14,12},{16,18},{18,... | collective-permute-start | bytes 3145736 | tf_op jit(solution)/shard_map/ppermute | solution.py:567
  176.7 18.2 %collective-permute-start.7 = (f32[256,1024]{1,0:T(8,128)}, f32[256,1024]{1,0:T(8,128)}, u32[]{:S(2)}, u32[]{:S(2)}) collective-permute-start(f32[256,1024]{1,0:T(8,128)} %collective-permute-done.1.first_ref), channel_id=1, source_target_pairs={{0,2},{2,0},{4,6},{6,4},{8,10},{10,8},{12,14},{14,12},{16,18},{18,... | collective-permute-start | bytes 3145736 | tf_op jit(solution)/shard_map/ppermute | solution.py:567
  176.7 18.7 %collective-permute-start.8 = (f32[256,1024]{1,0:T(8,128)}, f32[256,1024]{1,0:T(8,128)}, u32[]{:S(2)}, u32[]{:S(2)}) collective-permute-start(f32[256,1024]{1,0:T(8,128)} %collective-permute-done.2.second_ref), channel_id=1, source_target_pairs={{0,2},{2,0},{4,6},{6,4},{8,10},{10,8},{12,14},{14,12},{16,18},{18,... | collective-permute-start | bytes 3145736 | tf_op jit(solution)/shard_map/ppermute | solution.py:567
  184.8 8.0 %copy-start.113 = (f32[1,256]{1,0:T(1,128)S(1)}, f32[1,256]{1,0:T(1,128)}, u32[]{:S(2)}) copy-start(f32[1,256]{1,0:T(1,128)} %copy-done.112) | copy-start | bytes 3076
  187.6 15.2 %collective-permute-start.9 = (f32[256,1024]{1,0:T(8,128)}, f32[256,1024]{1,0:T(8,128)S(1)}, u32[]{:S(2)}, u32[]{:S(2)}) collective-permute-start(f32[256,1024]{1,0:T(8,128)} %collective-permute-done.3.first_ref), channel_id=1, source_target_pairs={{0,2},{2,0},{4,6},{6,4},{8,10},{10,8},{12,14},{14,12},{16,18},{18,... | collective-permute-start | bytes 3145736 | tf_op jit(solution)/shard_map/ppermute | solution.py:567
  194.9 7.9 %collective-permute-start.10 = (f32[256,1024]{1,0:T(8,128)}, f32[256,1024]{1,0:T(8,128)S(1)}, u32[]{:S(2)}, u32[]{:S(2)}) collective-permute-start(f32[256,1024]{1,0:T(8,128)} %collective-permute-done.4.second_ref), channel_id=1, source_target_pairs={{0,2},{2,0},{4,6},{6,4},{8,10},{10,8},{12,14},{14,12},{16,18},{18,... | collective-permute-start | bytes 3145736 | tf_op jit(solution)/shard_map/ppermute | solution.py:567
  195.4 7.4 %collective-permute-start.13 = (f32[256,1024]{1,0:T(8,128)}, f32[256,1024]{1,0:T(8,128)S(1)}, u32[]{:S(2)}, u32[]{:S(2)}) collective-permute-start(f32[256,1024]{1,0:T(8,128)} %collective-permute-done.11.first_ref), channel_id=1, source_target_pairs={{0,2},{2,0},{4,6},{6,4},{8,10},{10,8},{12,14},{14,12},{16,18},{18,... | collective-permute-start | bytes 3145736 | tf_op jit(solution)/shard_map/ppermute | solution.py:567
  220.1 7.4 %copy-start.60 = (bf16[1024,1024]{1,0:T(8,128)(2,1)S(1)}, bf16[1024,1024]{1,0:T(8,128)(2,1)}, u32[]{:S(2)}) copy-start(bf16[1024,1024]{1,0:T(8,128)(2,1)} %assemble.3) | copy-start | bytes 6291460
  223.8 7.4 %copy-start.100 = (f32[5,1024]{1,0:T(8,128)S(1)}, f32[5,1024]{1,0:T(8,128)}, u32[]{:S(2)}) copy-start(f32[5,1024]{1,0:T(8,128)} %pad_maximum_fusion.4) | copy-start | bytes 61444
  248.2 10.0 %copy-start.41 = (bf16[1024,1024]{1,0:T(8,128)(2,1)S(1)}, bf16[1024,1024]{1,0:T(8,128)(2,1)}, u32[]{:S(2)}) copy-start(bf16[1024,1024]{1,0:T(8,128)(2,1)} %copy-done.39) | copy-start | bytes 6291460
  248.2 10.0 %copy-start.150 = (bf16[1024,1024]{1,0:T(8,128)(2,1)S(1)}, bf16[1024,1024]{1,0:T(8,128)(2,1)}, u32[]{:S(2)}) copy-start(bf16[1024,1024]{1,0:T(8,128)(2,1)} %get-tuple-element.90) | copy-start | bytes 6291460
  258.2 7.2 %copy-start.14 = (f32[1024,128]{1,0:T(8,128)}, f32[1024,128]{1,0:T(8,128)S(1)}, u32[]{:S(2)}) copy-start(f32[1024,128]{1,0:T(8,128)S(1)} %get-tuple-element.153) | copy-start | bytes 1572868
  258.2 7.2 %copy-start.26 = (bf16[1024,1024]{1,0:T(8,128)(2,1)}, bf16[1024,1024]{1,0:T(8,128)(2,1)S(1)}, u32[]{:S(2)}) copy-start(bf16[1024,1024]{1,0:T(8,128)(2,1)S(1)} %get-tuple-element.126) | copy-start | bytes 6291460
  258.2 7.1 %copy-start.24 = (bf16[1024,1024]{1,0:T(8,128)(2,1)S(1)}, bf16[1024,1024]{1,0:T(8,128)(2,1)}, u32[]{:S(2)}) copy-start(bf16[1024,1024]{1,0:T(8,128)(2,1)} %copy-done.23) | copy-start | bytes 6291460
  258.3 7.1 %copy-start.45 = (bf16[2,1024,1024]{2,1,0:T(8,128)(2,1)S(1)}, bf16[2,1024,1024]{2,1,0:T(8,128)(2,1)}, u32[]{:S(2)}) copy-start(bf16[2,1024,1024]{2,1,0:T(8,128)(2,1)} %cotangent_ref.3) | copy-start | bytes 12582916
  274.6 200.9 %reduce-scatter.7.cloned.1.call-start = ((), (), s32[]{:S(2)}) async-start(), calls=%async_computation.3 | async-start | bytes 6127616
  278.1 109.2 %collective-permute-start.5 = (f32[1024,1024]{1,0:T(8,128)}, f32[1024,1024]{1,0:T(8,128)}, u32[]{:S(2)}, u32[]{:S(2)}) collective-permute-start(f32[1024,1024]{1,0:T(8,128)} %add_add_fusion.2.part_ref), channel_id=1, source_target_pairs={{0,1},{1,0},{2,3},{3,2},{4,5},{5,4},{6,7},{7,6},{8,9},{9,8},{10,11... | collective-permute-start | bytes 12582920 | tf_op jit(solution)/shard_map/ppermute | solution.py:533
  286.5 31.8 %copy-start.76 = (f32[2,8,8,128]{3,2,1,0:T(8,128)S(1)}, f32[2,8,8,128]{3,2,1,0:T(8,128)}, u32[]{:S(2)}) copy-start(f32[2,8,8,128]{3,2,1,0:T(8,128)} %copy-done.75) | copy-start | bytes 196612
  286.5 31.8 %copy-start.78 = (f32[2,8,8,128]{3,2,1,0:T(8,128)S(1)}, f32[2,8,8,128]{3,2,1,0:T(8,128)}, u32[]{:S(2)}) copy-start(f32[2,8,8,128]{3,2,1,0:T(8,128)} %copy-done.77) | copy-start | bytes 196612
  286.5 31.8 %copy-start.134 = (f32[16]{0:T(128)S(1)}, f32[16]{0:T(128)}, u32[]{:S(2)}) copy-start(f32[16]{0:T(128)} %copy-done.132) | copy-start | bytes 196
  320.6 13.6 %copy-start.83 = (f32[16,1024]{1,0:T(8,128)S(1)}, f32[16,1024]{1,0:T(8,128)}, u32[]{:S(2)}) copy-start(f32[16,1024]{1,0:T(8,128)} %copy-done.82) | copy-start | bytes 196612
  320.6 13.6 %copy-start.92 = (f32[16,8,128]{2,1,0:T(8,128)S(1)}, f32[16,8,128]{2,1,0:T(8,128)}, u32[]{:S(2)}) copy-start(f32[16,8,128]{2,1,0:T(8,128)} %get-tuple-element.278) | copy-start | bytes 196612
  320.6 13.7 %copy-start.95 = (bf16[16,1024]{1,0:T(8,128)(2,1)S(1)}, bf16[16,1024]{1,0:T(8,128)(2,1)}, u32[]{:S(2)}) copy-start(bf16[16,1024]{1,0:T(8,128)(2,1)} %copy-done.94) | copy-start | bytes 98308
  352.7 30.2 %copy-start.99 = (bf16[1024,1024]{1,0:T(8,128)(2,1)S(1)}, bf16[1024,1024]{1,0:T(8,128)(2,1)}, u32[]{:S(2)}) copy-start(bf16[1024,1024]{1,0:T(8,128)(2,1)} %param.20) | copy-start | bytes 6291460
  352.7 30.2 %copy-start.152 = (bf16[1024,1024]{1,0:T(8,128)(2,1)S(1)}, bf16[1024,1024]{1,0:T(8,128)(2,1)}, u32[]{:S(2)}) copy-start(bf16[1024,1024]{1,0:T(8,128)(2,1)} %get-tuple-element.124) | copy-start | bytes 6291460
  400.0 6.3 %copy-start.34 = (f32[1024,1024]{1,0:T(8,128)}, f32[1024,1024]{1,0:T(8,128)S(1)}, u32[]{:S(2)}) copy-start(f32[1024,1024]{1,0:T(8,128)S(1)} %add_add_fusion.1.part_ref) | copy-start | bytes 12582916
  406.3 3.8 collective-permute-start.16
  410.2 7.2 %collective-permute-start.17 = (f32[8496]{0:T(1024)S(1)}, f32[8496]{0:T(1024)S(1)}, u32[]{:S(2)}, u32[]{:S(2)}) collective-permute-start(f32[8496]{0:T(1024)S(1)} %concatenate.173), channel_id=1, source_target_pairs={{0,2},{2,0},{4,6},{6,4},{8,10},{10,8},{12,14},{14,12},{16,18},{18,... | collective-permute-start | bytes 101960 | tf_op jit(solution)/shard_map/ppermute | solution.py:567
  410.2 8.7 %copy-start.20 = (f32[8,8,16,128]{3,2,1,0:T(8,128)S(1)}, f32[8,8,16,128]{3,2,1,0:T(8,128)}, u32[]{:S(2)}) copy-start(f32[8,8,16,128]{3,2,1,0:T(8,128)} %copy-done.19) | copy-start | bytes 1572868
  410.2 8.9 %copy-start.11 = (f32[1024,256]{1,0:T(8,128)S(1)}, f32[1024,256]{1,0:T(8,128)}, u32[]{:S(2)}) copy-start(f32[1024,256]{1,0:T(8,128)} %copy-done.10) | copy-start | bytes 3145732
  417.3 5.9 %collective-permute-start.18 = (f32[8496]{0:T(1024)S(1)}, f32[8496]{0:T(1024)S(1)}, u32[]{:S(2)}, u32[]{:S(2)}) collective-permute-start(f32[8496]{0:T(1024)S(1)} %add.398), channel_id=1, source_target_pairs={{0,4},{2,6},{4,0},{6,2},{8,12},{10,14},{12,8},{14,10},{16,20},{18,... | collective-permute-start | bytes 101960 | tf_op jit(solution)/shard_map/ppermute | solution.py:567
  423.3 9.3 %collective-permute-start.19 = (f32[8496]{0:T(1024)S(1)}, f32[8496]{0:T(1024)S(1)}, u32[]{:S(2)}, u32[]{:S(2)}) collective-permute-start(f32[8496]{0:T(1024)S(1)} %add.399), channel_id=1, source_target_pairs={{0,8},{2,10},{4,12},{6,14},{8,0},{10,2},{12,4},{14,6},{16,24},{18,... | collective-permute-start | bytes 101960 | tf_op jit(solution)/shard_map/ppermute | solution.py:567
  427.7 7.6 %copy-start.88 = (f32[2,64,1024]{2,1,0:T(8,128)S(1)}, f32[2,64,1024]{2,1,0:T(8,128)}, u32[]{:S(2)}) copy-start(f32[2,64,1024]{2,1,0:T(8,128)} %reduce-scatter.5.cloned.1.call-done) | copy-start | bytes 1572868
  427.7 8.4 %copy-start.22 = (f32[1024]{0:T(1024)S(1)}, f32[1024]{0:T(1024)}, u32[]{:S(2)}) copy-start(f32[1024]{0:T(1024)} %param.19) | copy-start | bytes 12292
  432.6 14.2 %collective-permute-start.20 = (f32[8496]{0:T(1024)S(1)}, f32[8496]{0:T(1024)S(1)}, u32[]{:S(2)}, u32[]{:S(2)}) collective-permute-start(f32[8496]{0:T(1024)S(1)} %add.400), channel_id=1, source_target_pairs={{0,16},{2,18},{4,20},{6,22},{8,24},{10,26},{12,28},{14,30},{16,0},... | collective-permute-start | bytes 101960 | tf_op jit(solution)/shard_map/ppermute | solution.py:567
  476.8 5.5 %collective-permute-start.21 = (f32[64,256]{0,1:T(8,128)S(1)}, f32[64,256]{0,1:T(8,128)S(1)}, u32[]{:S(2)}, u32[]{:S(2)}) collective-permute-start(f32[64,256]{0,1:T(8,128)S(1)} %slice.356), channel_id=1, source_target_pairs={{0,1},{1,0},{2,3},{3,2},{4,5},{5,4},{6,7},{7,6},{8,9},{9,8},{10,11... | collective-permute-start | bytes 196616 | tf_op jit(solution)/shard_map/ppermute | solution.py:533
  (115 other events, 326.5 us)
Sparse Core Ops, SparseCore 0:
  274.8 105.8 reduce-scatter.4
  393.6 81.9 reduce-scatter.6
